TPU v7x, 128 devices: a whole 4x4x4 slice. The times are simulated.
128 devices in a mesh: section: 2 (over core), seq: 4 (over y), shard: 16 (over z, x).
Axes of the slice: x: 4, y: 4, z: 4, core: 2. Of those that a mesh axis runs over, the one named last changes fastest.
Arguments:
- images_in: bfloat16 [2, 16, 576, 768], P(None, 'shard', 'seq'), may hold values from -6 to 6
- out_grad: bfloat16 [2, 16, 576, 768], P(None, 'shard', 'seq'), may hold values from -6 to 6
- routes: int32 [2, 2, 16, 576, 2], P('section', None, 'shard', 'seq'), may hold values from 0 to 3, all different within a row; in each aligned block of 144 rows (0 to 143, 144 to 287, ..., all dimensions but the last counted through in order) at most 80 rows name the same one
- w_qkv: bfloat16 [2, 768, 2304], P('section', ('seq', 'shard')), may hold values from -0.21875 to 0.21875
- w_proj: bfloat16 [2, 768, 768], P('section', ('seq', 'shard')), may hold values from -2.5 to 2.5
- w_route: bfloat16 [2, 768, 4], P('section', ('seq', 'shard')), may hold values from -0.21875 to 0.21875
- gain_attn: bfloat16 [2, 768], P('section', ('seq', 'shard')), may hold values from 0.5 to 1.5
- gain_ffn: bfloat16 [2, 768], P('section', ('seq', 'shard')), may hold values from 0.5 to 1.5
- w_in: bfloat16 [2, 4, 768, 3072], P('section', 'seq', 'shard'), may hold values from -0.21875 to 0.21875
- w_out: bfloat16 [2, 4, 3072, 768], P('section', 'seq', 'shard'), may hold values from -0.21875 to 0.21875
Outputs:
- layer_out: bfloat16 [2, 2, 16, 576, 768], P('section', None, 'shard', 'seq')
- in_grad: bfloat16 [2, 2, 16, 576, 768], P('section', None, 'shard', 'seq')
- grad_qkv: float32 [2, 768, 2304], P('section', ('seq', 'shard'))
- grad_proj: float32 [2, 768, 768], P('section', ('seq', 'shard'))
- grad_route: float32 [2, 768, 4], P('section', ('seq', 'shard'))
- grad_gain_attn: float32 [2, 768], P('section', ('seq', 'shard'))
- grad_gain_ffn: float32 [2, 768], P('section', ('seq', 'shard'))
- grad_expert_in: float32 [2, 4, 768, 3072], P('section', 'seq', 'shard')
- grad_expert_out: float32 [2, 4, 3072, 768], P('section', 'seq', 'shard')
Inputs may be any that keep to these rules, and one draw needn't show every extreme that they name: `routes`: within the tokens of one image on one index of seq (aligned blocks of rows), no expert is named more than 80 times, and the two experts of a token differ.
All inputs are finite; a program needn't handle non-finite values.
Results may differ from a plain program's by a relative error of at most 0.02.
Values may be sent and summed in bfloat16 or wider, within the bound.
No kernel may reach another device: no remote copies, remote signals or barrier semaphores. Data moves between devices by JAX's collectives and lax.ppermute only.
A program may use at most 320 MiB of HBM per device.

v0:
```python
from functools import partial

import jax
import jax.numpy as jnp
from jax import lax
from jax.sharding import PartitionSpec as P

HEAD_DIM = 64
CAP = 80


EPSILON = 1e-06
HIGHEST = lax.Precision.HIGHEST


def partner(block, axis, apart):
    count = lax.axis_size(axis)
    route = []
    for low in range(count):
        high = low | 1 << apart
        if high != low and high < count:
            route += [(low, high), (high, low)]
    return lax.ppermute(block, axis, route)


def norm_rows(values, gain_vec):
    centred = values - jnp.mean(values, axis=-1, keepdims=True)
    inverse = lax.rsqrt(jnp.mean(centred * centred, axis=-1, keepdims=True) + EPSILON)
    return centred * inverse * gain_vec


def slot_table(route_ids, experts, capacity):
    images, length, pick_count = route_ids.shape
    flattened = route_ids.reshape(images, length * pick_count)
    expert_ids = jnp.arange(experts, dtype=jnp.int32)
    matches = (flattened[:, :, None] == expert_ids).astype(jnp.int32)
    before = jnp.cumsum(matches, axis=1) - matches
    ranking = jnp.sum(before * matches, axis=2)
    columns = flattened * capacity + ranking
    targets = jnp.arange(experts * capacity, dtype=jnp.int32)
    table = (columns[:, :, None] == targets).astype(jnp.bfloat16)
    return table.reshape(images, length, pick_count, experts * capacity)


def attend(head_rows, head_dim):
    images, length, triple, group_width = head_rows.shape
    divided = head_rows.reshape(images, length, triple, group_width // head_dim, head_dim)
    queries = divided[:, :, 0]
    key_rows = divided[:, :, 1]
    value_rows = divided[:, :, 2]
    scores = jnp.einsum(
        "bqhd,bkhd->bhqk", queries, key_rows, preferred_element_type=jnp.float32
    ) * head_dim ** (-0.5)
    row_max = jnp.max(scores, axis=-1, keepdims=True)
    exponent = jnp.exp(scores - row_max)
    totals = jnp.sum(exponent, axis=-1, keepdims=True)
    attention = exponent / totals
    log_total = row_max + jnp.log(totals)
    mixture = jnp.einsum(
        "bhqk,bkhd->bqhd",
        attention.astype(jnp.bfloat16),
        value_rows,
        preferred_element_type=jnp.float32,
    )
    return (mixture.astype(jnp.bfloat16).reshape(images, length, group_width), log_total)


def attend_back(head_rows, log_total, d_mixture, head_dim):
    images, length, triple, group_width = head_rows.shape
    head_count = group_width // head_dim
    divided = head_rows.reshape(images, length, triple, head_count, head_dim)
    queries = divided[:, :, 0]
    key_rows = divided[:, :, 1]
    value_rows = divided[:, :, 2]
    scaling = head_dim ** (-0.5)
    scores = (
        jnp.einsum("bqhd,bkhd->bhqk", queries, key_rows, preferred_element_type=jnp.float32)
        * scaling
    )
    attention = jnp.exp(scores - log_total)
    d_head_out = d_mixture.reshape(images, length, head_count, head_dim)
    d_values = jnp.einsum(
        "bhqk,bqhd->bkhd",
        attention.astype(jnp.bfloat16),
        d_head_out,
        preferred_element_type=jnp.float32,
    )
    d_attention = jnp.einsum(
        "bqhd,bkhd->bhqk", d_head_out, value_rows, preferred_element_type=jnp.float32
    )
    centre = jnp.sum(attention * d_attention, axis=-1, keepdims=True)
    d_scores = (attention * (d_attention - centre)).astype(jnp.bfloat16) * jnp.asarray(
        scaling, jnp.bfloat16
    )
    d_queries = jnp.einsum(
        "bhqk,bkhd->bqhd", d_scores, key_rows, preferred_element_type=jnp.float32
    )
    d_keys = jnp.einsum("bhqk,bqhd->bkhd", d_scores, queries, preferred_element_type=jnp.float32)
    joined = jnp.stack([d_queries, d_keys, d_values], axis=2)
    return joined.reshape(images, length, triple, group_width).astype(jnp.bfloat16)


def expert_run(slab_rows, w_first, w_second):
    hidden = jnp.einsum("erd,edf->erf", slab_rows, w_first, preferred_element_type=jnp.float32)
    active = jax.nn.gelu(hidden, approximate=False).astype(jnp.bfloat16)
    result = jnp.einsum(
        "erf,efd->erd", active, w_second, preferred_element_type=jnp.float32
    ).astype(jnp.bfloat16)
    return (result, hidden)


def expert_back(slab_rows, hidden, d_result, w_first, w_second):
    active, gelu_back = jax.vjp(partial(jax.nn.gelu, approximate=False), hidden)
    d_active = jnp.einsum("erd,efd->erf", d_result, w_second, preferred_element_type=jnp.float32)
    grad_second = jnp.einsum(
        "erf,erd->efd", active.astype(jnp.bfloat16), d_result, preferred_element_type=jnp.float32
    )
    d_hidden = gelu_back(d_active)[0].astype(jnp.bfloat16)
    grad_first = jnp.einsum("erd,erf->edf", slab_rows, d_hidden, preferred_element_type=jnp.float32)
    d_slab = jnp.einsum(
        "erf,edf->erd", d_hidden, w_first, preferred_element_type=jnp.float32
    ).astype(jnp.bfloat16)
    return (d_slab, grad_first, grad_second)


def hand_over(outgoing):
    return partner(outgoing, "section", 0)


def layer_forward(tokens, route_ids, attn_weights, expert_weights, is_live, head_dim):
    w_mix, w_back, w_router, gain_one, gain_two = attn_weights
    w_first, w_second = expert_weights
    images, length, features = tokens.shape
    experts = w_router.shape[1]
    normed = norm_rows(tokens, gain_one.astype(jnp.float32)).astype(jnp.bfloat16)
    packed = jnp.einsum("itd,de->ite", normed, w_mix, preferred_element_type=jnp.float32).astype(
        jnp.bfloat16
    )
    head_rows = lax.all_to_all(
        packed.reshape(images, length, 3, features), "seq", split_axis=3, concat_axis=1, tiled=True
    )
    mixture, log_total = attend(head_rows, head_dim)
    gathered = lax.all_to_all(mixture, "seq", split_axis=1, concat_axis=2, tiled=True)
    branch = jnp.einsum("itd,de->ite", gathered, w_back, preferred_element_type=jnp.float32)
    residual = tokens + branch
    normed_two = norm_rows(residual, gain_two.astype(jnp.float32)).astype(jnp.bfloat16)
    logits = jnp.einsum(
        "itd,de->ite",
        normed_two.astype(jnp.float32),
        w_router.astype(jnp.float32),
        precision=HIGHEST,
    )
    gate_probs = jax.nn.softmax(logits, axis=-1)
    expert_ids = jnp.arange(experts, dtype=jnp.int32)
    matches = (route_ids[..., None] == expert_ids).astype(jnp.float32)
    chosen = jnp.sum(matches * gate_probs[:, :, None, :], axis=-1)
    selector = slot_table(route_ids, experts, CAP)
    buffer = jnp.einsum("itkc,itd->cid", selector, normed_two, preferred_element_type=jnp.float32)
    buffer = buffer.astype(jnp.bfloat16).reshape(experts, CAP * images, features)
    arrived = lax.all_to_all(buffer, "seq", split_axis=0, concat_axis=1, tiled=True)

    def run_experts(slab_rows):
        return expert_run(slab_rows, w_first, w_second)

    def skip_experts(slab_rows):
        return (
            jnp.zeros_like(slab_rows),
            jnp.zeros(slab_rows.shape[:2] + (w_first.shape[2],), jnp.float32),
        )

    result, hidden = lax.cond(is_live, run_experts, skip_experts, arrived)
    returned = lax.all_to_all(result, "seq", split_axis=1, concat_axis=0, tiled=True)
    picked = jnp.einsum(
        "itkc,cid->itkd",
        selector,
        returned.reshape(experts * CAP, images, features),
        preferred_element_type=jnp.float32,
    )
    output = residual + jnp.sum(chosen[..., None] * picked, axis=2)
    saved_state = (
        tokens,
        head_rows,
        log_total,
        gathered,
        residual,
        normed_two,
        gate_probs,
        chosen,
        arrived,
        hidden,
        returned,
    )
    return (output, saved_state)


def layer_backward(
    saved_state, d_output, route_ids, attn_weights, expert_weights, is_live, head_dim
):
    (
        tokens,
        head_rows,
        log_total,
        gathered,
        residual,
        normed_two,
        gate_probs,
        chosen,
        arrived,
        hidden,
        returned,
    ) = saved_state
    w_mix, w_back, w_router, gain_one, gain_two = attn_weights
    w_first, w_second = expert_weights
    images, length, features = tokens.shape
    experts = w_router.shape[1]
    selector = slot_table(route_ids, experts, CAP)
    picked = jnp.einsum(
        "itkc,cid->itkd",
        selector,
        returned.reshape(experts * CAP, images, features),
        preferred_element_type=jnp.float32,
    )
    d_chosen = jnp.sum(d_output[:, :, None, :] * picked, axis=-1)
    d_picked = (chosen[..., None] * d_output[:, :, None, :]).astype(jnp.bfloat16)
    d_buffer = jnp.einsum("itkc,itkd->cid", selector, d_picked, preferred_element_type=jnp.float32)
    d_buffer = d_buffer.astype(jnp.bfloat16).reshape(experts, CAP * images, features)
    d_result = lax.all_to_all(d_buffer, "seq", split_axis=0, concat_axis=1, tiled=True)

    def run_back(operands):
        return expert_back(operands[0], operands[1], operands[2], w_first, w_second)

    def skip_back(operands):
        return (
            jnp.zeros_like(operands[0]),
            jnp.zeros(w_first.shape, jnp.float32),
            jnp.zeros(w_second.shape, jnp.float32),
        )

    d_slab, grad_first, grad_second = lax.cond(
        is_live, run_back, skip_back, (arrived, hidden, d_result)
    )
    d_returned = lax.all_to_all(d_slab, "seq", split_axis=1, concat_axis=0, tiled=True)
    d_from_experts = jnp.einsum(
        "itkc,cid->itd",
        selector,
        d_returned.reshape(experts * CAP, images, features),
        preferred_element_type=jnp.float32,
    )
    expert_ids = jnp.arange(experts, dtype=jnp.int32)
    matches = (route_ids[..., None] == expert_ids).astype(jnp.float32)
    d_gates = jnp.sum(matches * d_chosen[..., None], axis=2)
    d_logits = gate_probs * (d_gates - jnp.sum(gate_probs * d_gates, axis=-1, keepdims=True))
    grad_router = jnp.einsum(
        "itd,ite->de", normed_two.astype(jnp.float32), d_logits, precision=HIGHEST
    )
    d_normed_two = d_from_experts + jnp.einsum(
        "ite,de->itd", d_logits, w_router.astype(jnp.float32), precision=HIGHEST
    )
    unused, norm_back_two = jax.vjp(norm_rows, residual, gain_two.astype(jnp.float32))
    d_resid_part, d_gain_two = norm_back_two(d_normed_two)
    d_residual = d_output + d_resid_part
    d_branch = d_residual.astype(jnp.bfloat16)
    grad_back = jnp.einsum("itd,ite->de", gathered, d_branch, preferred_element_type=jnp.float32)
    d_mixture = jnp.einsum(
        "ite,de->itd", d_branch, w_back, preferred_element_type=jnp.float32
    ).astype(jnp.bfloat16)
    d_head_in = lax.all_to_all(d_mixture, "seq", split_axis=2, concat_axis=1, tiled=True)
    d_heads = attend_back(head_rows, log_total, d_head_in, head_dim)
    d_packed = lax.all_to_all(d_heads, "seq", split_axis=1, concat_axis=3, tiled=True).reshape(
        images, length, 3 * features
    )
    normed, norm_back_one = jax.vjp(norm_rows, tokens, gain_one.astype(jnp.float32))
    grad_mix = jnp.einsum(
        "itd,ite->de", normed.astype(jnp.bfloat16), d_packed, preferred_element_type=jnp.float32
    )
    d_normed = jnp.einsum("ite,de->itd", d_packed, w_mix, preferred_element_type=jnp.float32)
    d_token_part, d_gain_one = norm_back_one(d_normed)
    d_tokens = d_residual + d_token_part
    return (
        d_tokens,
        (grad_mix, grad_back, grad_router, d_gain_one, d_gain_two),
        (grad_first, grad_second),
    )


def shards(images_in, out_grad, routes, w_qkv, w_proj, w_route, gain_attn, gain_ffn, w_in, w_out):
    section_index = lax.axis_index("section")
    micro_count = images_in.shape[0]
    attn_weights = (
        lax.all_gather(w_qkv[0], ("seq", "shard"), axis=0, tiled=True),
        lax.all_gather(w_proj[0], ("seq", "shard"), axis=0, tiled=True),
        lax.all_gather(w_route[0], ("seq", "shard"), axis=0, tiled=True),
        lax.all_gather(gain_attn[0], ("seq", "shard"), axis=0, tiled=True),
        lax.all_gather(gain_ffn[0], ("seq", "shard"), axis=0, tiled=True),
    )
    expert_weights = (
        lax.all_gather(w_in[0], "shard", axis=1, tiled=True),
        lax.all_gather(w_out[0], "shard", axis=1, tiled=True),
    )
    route_set = routes[0]
    waiting = jnp.zeros(images_in.shape[1:], jnp.bfloat16)
    layer_outs = []
    kept_state = []
    for step_num in range(micro_count + 1):
        offset = step_num - section_index
        is_live = jnp.logical_and(offset >= 0, offset < micro_count)
        route_ids = lax.dynamic_index_in_dim(
            route_set, jnp.clip(offset, 0, micro_count - 1), 0, keepdims=False
        )
        tokens = jnp.where(
            section_index == 0, images_in[min(step_num, micro_count - 1)], waiting
        ).astype(jnp.float32)
        output, saved_state = layer_forward(
            tokens, route_ids, attn_weights, expert_weights, is_live, HEAD_DIM
        )
        outgoing = output.astype(jnp.bfloat16)
        layer_outs.append(outgoing)
        kept_state.append((saved_state, route_ids))
        if step_num < micro_count:
            waiting = hand_over(outgoing)
    waiting = jnp.zeros(images_in.shape[1:], jnp.bfloat16)
    attn_total = None
    expert_total = None
    in_grads = []
    for step_num in range(micro_count + 1):
        saved_state, route_ids = kept_state[micro_count - step_num]
        is_live = jnp.logical_or(
            jnp.logical_and(section_index == 1, step_num < micro_count),
            jnp.logical_and(section_index == 0, step_num >= 1),
        )
        incoming = jnp.where(
            section_index == 1, out_grad[max(micro_count - 1 - step_num, 0)], waiting
        ).astype(jnp.float32)
        d_output = jnp.where(is_live, incoming, 0.0)
        d_tokens, attn_grads, expert_grads = layer_backward(
            saved_state, d_output, route_ids, attn_weights, expert_weights, is_live, HEAD_DIM
        )
        attn_total = (
            attn_grads if attn_total is None else jax.tree.map(jnp.add, attn_total, attn_grads)
        )
        expert_total = (
            expert_grads
            if expert_total is None
            else jax.tree.map(jnp.add, expert_total, expert_grads)
        )
        outgoing = d_tokens.astype(jnp.bfloat16)
        in_grads.append(outgoing)
        if step_num < micro_count:
            waiting = hand_over(outgoing)
    grad_first, grad_second = (
        lax.psum_scatter(
            expert_total[0].astype(jnp.bfloat16), "shard", scatter_dimension=1, tiled=True
        ).astype(jnp.float32),
        lax.psum_scatter(
            expert_total[1].astype(jnp.bfloat16), "shard", scatter_dimension=1, tiled=True
        ).astype(jnp.float32),
    )
    summed = (
        lax.psum_scatter(attn_total[0], ("seq", "shard"), scatter_dimension=0, tiled=True),
        lax.psum_scatter(attn_total[1], ("seq", "shard"), scatter_dimension=0, tiled=True),
        lax.psum_scatter(attn_total[2], ("seq", "shard"), scatter_dimension=0, tiled=True),
        lax.psum_scatter(attn_total[3], ("seq", "shard"), scatter_dimension=0, tiled=True),
        lax.psum_scatter(attn_total[4], ("seq", "shard"), scatter_dimension=0, tiled=True),
    )
    layer_out = lax.dynamic_slice_in_dim(jnp.stack(layer_outs), section_index, micro_count, 0)[None]
    in_grad = lax.dynamic_slice_in_dim(jnp.stack(in_grads[::-1]), section_index, micro_count, 0)[
        None
    ]
    return (
        layer_out,
        in_grad,
        summed[0][None],
        summed[1][None],
        summed[2][None],
        summed[3][None],
        summed[4][None],
        grad_first[None],
        grad_second[None],
    )


def solution(mesh):
    return jax.shard_map(
        shards,
        mesh=mesh,
        in_specs=(
            P(None, "shard", "seq", None),
            P(None, "shard", "seq", None),
            P("section", None, "shard", "seq", None),
            P("section", ("seq", "shard"), None),
            P("section", ("seq", "shard"), None),
            P("section", ("seq", "shard"), None),
            P("section", ("seq", "shard")),
            P("section", ("seq", "shard")),
            P("section", "seq", "shard", None),
            P("section", "seq", "shard", None),
        ),
        out_specs=(
            P("section", None, "shard", "seq", None),
            P("section", None, "shard", "seq", None),
            P("section", ("seq", "shard"), None),
            P("section", ("seq", "shard"), None),
            P("section", ("seq", "shard"), None),
            P("section", ("seq", "shard")),
            P("section", ("seq", "shard")),
            P("section", "seq", "shard", None),
            P("section", "seq", "shard", None),
        ),
        check_vma=False,
    )
```

profile of v0, /device:TPU:64, one launch (start us, length us, event | category | flops | bytes accessed | tf_op | source)
XLA Modules:
  0.0 2106.4 jit_solution(1496131316656891660)
XLA Ops:
  17.8 160.5 %all-reduce.13 = (bf16[768]{0:T(1024)(128)(2,1)S(1)}, bf16[768]{0:T(1024)(128)(2,1)}) all-reduce(bf16[768]{0:T(1024)(128)(2,1)S(1)} %dynamic-update-slice, bf16[768]{0:T(1024)(128)(2,1)S(1)} %dynamic-update-slice.1), channel_id=2, replica_groups=mesh['section'=2,'seq'=4,'shard'=16] {'seq','shard'}, use_global_device_ids=true, to_apply=%add.3 | all-reduce | flops 1536 | bytes 6144
  278.0 181.2 %all-gather.4 = bf16[1,768,4]{2,0,1:T(2,128)(2,1)} all-gather(bf16[1,12,4]{2,0,1:T(2,128)(2,1)S(1)} %copy.432), channel_id=6, replica_groups=mesh['section'=2,'seq'=4,'shard'=16] {'seq','shard'}, dimensions={1}, use_global_device_ids=true | all-gather | bytes 6240 | tf_op jit(solution)/shard_map/all_gather | solution.py:292
  470.1 18.2 conditional.6
  476.7 11.5 fusion.52
  613.0 17.9 conditional.7
  619.3 11.5 fusion.138
  680.8 11.6 all-to-all-done.8
  768.4 19.9 conditional.9
  911.1 14.2 all_to_all.300
  935.7 27.6 %collective-permute-start.2 = (bf16[1,144,768]{2,1,0:T(8,128)(2,1)}, bf16[1,144,768]{2,1,0:T(8,128)(2,1)}, u32[]{:S(2)}, u32[]{:S(2)}) collective-permute-start(bf16[1,144,768]{2,1,0:T(8,128)(2,1)} %add_convert_fusion.6), channel_id=1, source_target_pairs={{0,64},{64,0},{1,65},{65,1},{2,66},{66,2},{3,67},{67,3},{4,68},{68... | collective-permute-start | bytes 663560 | tf_op jit(solution)/shard_map/ppermute | solution.py:23
  973.5 9.9 all-to-all-done.16
  983.3 43.2 %conditional.10 = (bf16[1,320,768]{2,1,0:T(8,128)(2,1)}, f32[1,3072,768]{2,1,0:T(8,128)}, f32[1,768,3072]{2,1,0:T(8,128)}) conditional(s32[]{:T(128)} %convert_element_type.624, () %tuple.64, (f32[1,320,3072]{2,1,0:T(8,128)}, bf16[4,80,768]{2,1,0:T(8,128)(2,1)}, bf16[1,3072,768]{2,1,0:T(8,128)(2,1)}, bf16[1,768,3072]{2,1,0:T(8,128)(2,1)}, ...), branch_computations={%region_58.59_spmd, %region_59.60_spmd} | conditional | flops 6117703680 | bytes 92799048 | solution.py:239
  1130.7 16.9 all_to_all.301
  1165.9 9.7 all-to-all-done.20
  1175.6 42.7 %conditional.11 = (bf16[1,320,768]{2,1,0:T(8,128)(2,1)}, f32[1,3072,768]{2,1,0:T(8,128)}, f32[1,768,3072]{2,1,0:T(8,128)}) conditional(s32[]{:T(128)} %convert_element_type.636, () %tuple.66, (f32[1,320,3072]{2,1,0:T(8,128)}, bf16[4,80,768]{2,1,0:T(8,128)(2,1)}, bf16[1,3072,768]{2,1,0:T(8,128)(2,1)}, bf16[1,768,3072]{2,1,0:T(8,128)(2,1)}, ...), branch_computations={%region_68.69_spmd, %region_69.70_spmd} | conditional | flops 6117703680 | bytes 92799048 | solution.py:239
  1218.3 12.3 add_convert_fusion.4
  1303.3 12.1 add_convert_fusion.3
  1395.6 207.8 %fusion.686 = (f32[16,2304]{1,0:T(8,128)}, f32[16,768]{1,0:T(8,128)}) fusion(f32[768,2304]{1,0:T(8,128)} %add_add_fusion, f32[768,768]{1,0:T(8,128)} %add_add_fusion.1), kind=kCustom, calls=%all-reduce-scatter.2 | all-reduce-scatter fusion | flops 3145729 | bytes 9634304
  1613.5 21.1 %collective-permute-start.31 = (f32[16,768]{1,0:T(8,128)}, f32[16,768]{1,0:T(8,128)S(1)}, u32[]{:S(2)}, u32[]{:S(2)}) collective-permute-start(f32[16,768]{1,0:T(8,128)} %get-tuple-element.193), channel_id=1, source_target_pairs={{0,12},{1,13},{2,14},{3,15},{4,16},{5,17},{6,18},{7,19},{8,20},{9,... | collective-permute-start | bytes 147464
  1692.0 323.5 %all-reduce.12 = (f32[768,4]{0,1:T(4,128)S(1)}, f32[768]{0:T(1024)S(1)}, f32[768]{0:T(1024)S(1)}) all-reduce(f32[768,4]{0,1:T(4,128)} %convolution_add_fusion.4, f32[768]{0:T(1024)S(1)} %add_add_fusion.10, f32[768]{0:T(1024)S(1)} %copy-done.110), channel_id=11, replica_groups=mesh['section'=2,'seq'=4,'shard'=16] {'seq','shard'}, use_global_device_ids=true, to_apply=%region_80.81.clone | all-reduce | flops 4608 | bytes 36864
  2027.2 9.9 collective-permute-start.8
  2037.1 10.2 collective-permute-start.7
  2047.4 12.9 collective-permute-start.6
  2083.2 11.5 concatenate.27
  (772 shorter events, 1003.9 us)
Async XLA Ops:
  7.2 178.3 %all-gather.12.cloned.1.call-start = ((), (), s32[]{:S(2)}) async-start(), calls=%async_computation.28 | async-start | bytes 7188480 | tf_op jit(solution)/shard_map/all_gather | solution.py:290
  8.9 242.3 %all-gather.14.cloned.1.call-start = ((), (), s32[]{:S(2)}) async-start(), calls=%async_computation.29 | async-start | bytes 2396160 | tf_op jit(solution)/shard_map/all_gather | solution.py:291
  10.3 459.7 %all-gather.16.cloned.1.call-start = ((), (), s32[]{:S(2)}) async-start(), calls=%async_computation.30 | async-start | bytes 5013504 | tf_op jit(solution)/shard_map/all_gather | solution.py:297
  11.1 459.0 %all-gather.18.cloned.1.call-start = ((), (), s32[]{:S(2)}) async-start(), calls=%async_computation.31 | async-start | bytes 5013504 | tf_op jit(solution)/shard_map/all_gather | solution.py:298
  267.6 202.4 %all-to-all-start.2 = ((bf16[4,80,768]{2,1,0:T(8,128)(2,1)}), bf16[4,80,768]{2,1,0:T(8,128)(2,1)}, u32[]{:S(2)}, u32[]{:S(2)}) async-start(bf16[4,80,768]{2,1,0:T(8,128)(2,1)} %bitcast.861), calls=%async_computation.2 | async-start | bytes 983040 | tf_op jit(solution)/shard_map/all_to_all | solution.py:160
  935.7 29.0 %collective-permute-start.2 = (bf16[1,144,768]{2,1,0:T(8,128)(2,1)}, bf16[1,144,768]{2,1,0:T(8,128)(2,1)}, u32[]{:S(2)}, u32[]{:S(2)}) collective-permute-start(bf16[1,144,768]{2,1,0:T(8,128)(2,1)} %add_convert_fusion.6), channel_id=1, source_target_pairs={{0,64},{64,0},{1,65},{65,1},{2,66},{66,2},{3,67},{67,3},{4,68},{68... | collective-permute-start | bytes 663560 | tf_op jit(solution)/shard_map/ppermute | solution.py:23
  1165.8 929.6 %reduce-scatter.8.cloned.1.call-start = ((), (), s32[]{:S(2)}) async-start(), calls=%async_computation.26 | async-start | bytes 5013504 | tf_op jit(solution)/shard_map/reduce_scatter | solution.py:351
  1303.0 794.3 %reduce-scatter.10.cloned.1.call-start = ((), (), s32[]{:S(2)}) async-start(), calls=%async_computation.27 | async-start | bytes 5013504 | tf_op jit(solution)/shard_map/reduce_scatter | solution.py:354
  1604.3 40.3 %collective-permute-start.34 = (f32[16,768]{1,0:T(8,128)}, f32[16,768]{1,0:T(8,128)S(1)}, u32[]{:S(2)}, u32[]{:S(2)}) collective-permute-start(f32[16,768]{1,0:T(8,128)} %get-tuple-element.193), channel_id=1, source_target_pairs={{0,15},{1,16},{2,17},{3,18},{4,19},{5,20},{6,21},{7,22},{8,23},{9,... | collective-permute-start | bytes 147464
  1605.6 41.6 %collective-permute-start.33 = (f32[16,768]{1,0:T(8,128)}, f32[16,768]{1,0:T(8,128)S(1)}, u32[]{:S(2)}, u32[]{:S(2)}) collective-permute-start(f32[16,768]{1,0:T(8,128)} %get-tuple-element.193), channel_id=1, source_target_pairs={{0,14},{1,15},{2,16},{3,17},{4,18},{5,19},{6,20},{7,21},{8,22},{9,... | collective-permute-start | bytes 147464
  1606.9 46.9 %collective-permute-start.32 = (f32[16,768]{1,0:T(8,128)}, f32[16,768]{1,0:T(8,128)S(1)}, u32[]{:S(2)}, u32[]{:S(2)}) collective-permute-start(f32[16,768]{1,0:T(8,128)} %get-tuple-element.193), channel_id=1, source_target_pairs={{0,13},{1,14},{2,15},{3,16},{4,17},{5,18},{6,19},{7,20},{8,21},{9,... | collective-permute-start | bytes 147464
  1613.5 42.9 %collective-permute-start.31 = (f32[16,768]{1,0:T(8,128)}, f32[16,768]{1,0:T(8,128)S(1)}, u32[]{:S(2)}, u32[]{:S(2)}) collective-permute-start(f32[16,768]{1,0:T(8,128)} %get-tuple-element.193), channel_id=1, source_target_pairs={{0,12},{1,13},{2,14},{3,15},{4,16},{5,17},{6,18},{7,19},{8,20},{9,... | collective-permute-start | bytes 147464
  1681.0 335.2 %collective-permute-start.18 = (f32[16,2304]{1,0:T(8,128)}, f32[16,2304]{1,0:T(8,128)S(1)}, u32[]{:S(2)}, u32[]{:S(2)}) collective-permute-start(f32[16,2304]{1,0:T(8,128)} %get-tuple-element.192), channel_id=1, source_target_pairs={{0,15},{1,16},{2,17},{3,18},{4,19},{5,20},{6,21},{7,22},{8,23},{9,... | collective-permute-start | bytes 442376
  1683.0 334.5 %collective-permute-start.17 = (f32[16,2304]{1,0:T(8,128)}, f32[16,2304]{1,0:T(8,128)S(1)}, u32[]{:S(2)}, u32[]{:S(2)}) collective-permute-start(f32[16,2304]{1,0:T(8,128)} %get-tuple-element.192), channel_id=1, source_target_pairs={{0,14},{1,15},{2,16},{3,17},{4,18},{5,19},{6,20},{7,21},{8,22},{9,... | collective-permute-start | bytes 442376
  1684.6 334.1 %collective-permute-start.16 = (f32[16,2304]{1,0:T(8,128)}, f32[16,2304]{1,0:T(8,128)S(1)}, u32[]{:S(2)}, u32[]{:S(2)}) collective-permute-start(f32[16,2304]{1,0:T(8,128)} %get-tuple-element.192), channel_id=1, source_target_pairs={{0,13},{1,14},{2,15},{3,16},{4,17},{5,18},{6,19},{7,20},{8,21},{9,... | collective-permute-start | bytes 442376
  1686.0 334.7 %collective-permute-start.15 = (f32[16,2304]{1,0:T(8,128)}, f32[16,2304]{1,0:T(8,128)S(1)}, u32[]{:S(2)}, u32[]{:S(2)}) collective-permute-start(f32[16,2304]{1,0:T(8,128)} %get-tuple-element.192), channel_id=1, source_target_pairs={{0,12},{1,13},{2,14},{3,15},{4,16},{5,17},{6,18},{7,19},{8,20},{9,... | collective-permute-start | bytes 442376
  1687.3 335.4 %collective-permute-start.14 = (f32[16,2304]{1,0:T(8,128)}, f32[16,2304]{1,0:T(8,128)S(1)}, u32[]{:S(2)}, u32[]{:S(2)}) collective-permute-start(f32[16,2304]{1,0:T(8,128)} %get-tuple-element.192), channel_id=1, source_target_pairs={{0,11},{1,12},{2,13},{3,14},{4,15},{5,16},{6,17},{7,18},{8,19},{9,... | collective-permute-start | bytes 442376
  2018.8 28.6 %collective-permute-start.11 = (f32[16,2304]{1,0:T(8,128)}, f32[16,2304]{1,0:T(8,128)S(1)}, u32[]{:S(2)}, u32[]{:S(2)}) collective-permute-start(f32[16,2304]{1,0:T(8,128)} %get-tuple-element.192), channel_id=1, source_target_pairs={{0,8},{1,9},{2,10},{3,11},{4,12},{5,13},{6,14},{7,15},{8,16},{9,17... | collective-permute-start | bytes 442376
  2020.7 39.6 %collective-permute-start.10 = (f32[16,2304]{1,0:T(8,128)}, f32[16,2304]{1,0:T(8,128)S(1)}, u32[]{:S(2)}, u32[]{:S(2)}) collective-permute-start(f32[16,2304]{1,0:T(8,128)} %get-tuple-element.192), channel_id=1, source_target_pairs={{0,7},{1,8},{2,9},{3,10},{4,11},{5,12},{6,13},{7,14},{8,15},{9,16}... | collective-permute-start | bytes 442376
  2022.6 45.0 %collective-permute-start.9 = (f32[16,2304]{1,0:T(8,128)}, f32[16,2304]{1,0:T(8,128)S(1)}, u32[]{:S(2)}, u32[]{:S(2)}) collective-permute-start(f32[16,2304]{1,0:T(8,128)} %get-tuple-element.192), channel_id=1, source_target_pairs={{0,6},{1,7},{2,8},{3,9},{4,10},{5,11},{6,12},{7,13},{8,14},{9,15},... | collective-permute-start | bytes 442376
  2027.2 54.5 %collective-permute-start.8 = (f32[16,2304]{1,0:T(8,128)}, f32[16,2304]{1,0:T(8,128)S(1)}, u32[]{:S(2)}, u32[]{:S(2)}) collective-permute-start(f32[16,2304]{1,0:T(8,128)} %get-tuple-element.192), channel_id=1, source_target_pairs={{0,5},{1,6},{2,7},{3,8},{4,9},{5,10},{6,11},{7,12},{8,13},{9,14},{... | collective-permute-start | bytes 442376
  2037.1 44.6 %collective-permute-start.7 = (f32[16,2304]{1,0:T(8,128)}, f32[16,2304]{1,0:T(8,128)S(1)}, u32[]{:S(2)}, u32[]{:S(2)}) collective-permute-start(f32[16,2304]{1,0:T(8,128)} %get-tuple-element.192), channel_id=1, source_target_pairs={{0,4},{1,5},{2,6},{3,7},{4,8},{5,9},{6,10},{7,11},{8,12},{9,13},{1... | collective-permute-start | bytes 442376
  2047.4 34.4 %collective-permute-start.6 = (f32[16,2304]{1,0:T(8,128)}, f32[16,2304]{1,0:T(8,128)S(1)}, u32[]{:S(2)}, u32[]{:S(2)}) collective-permute-start(f32[16,2304]{1,0:T(8,128)} %get-tuple-element.192), channel_id=1, source_target_pairs={{0,3},{1,4},{2,5},{3,6},{4,7},{5,8},{6,9},{7,10},{8,11},{9,12},{10... | collective-permute-start | bytes 442376
  2060.3 21.4 %collective-permute-start.5 = (f32[16,2304]{1,0:T(8,128)}, f32[16,2304]{1,0:T(8,128)S(1)}, u32[]{:S(2)}, u32[]{:S(2)}) collective-permute-start(f32[16,2304]{1,0:T(8,128)} %get-tuple-element.192), channel_id=1, source_target_pairs={{0,2},{1,3},{2,4},{3,5},{4,6},{5,7},{6,8},{7,9},{8,10},{9,11},{10,... | collective-permute-start | bytes 442376
  (183 other events, 2509.0 us)
Sparse Core Ops, SparseCore 0:
  11.3 76.1 all-gather.11
  90.9 64.0 all-gather.13
  157.1 52.8 all-gather.15
  212.1 53.8 all-gather.17
  1230.7 94.4 reduce-scatter.7
  1328.4 87.4 reduce-scatter.9
where the time goes:
time: 2120 us; the launch traced here: 2110 us
  blocking collectives  904 us (43%)
  local copies, waits for them, and re-layouts  353 us (17%)
  matrix products  267 us (13%)
  starting transfers between devices  260 us (12%)
  other arithmetic  197 us (9%)
  waiting for transfers between devices  95.6 us (5%)
    unnamed x3, blocking collectives  692 us
    all_gather x1, blocking collectives, shards(): lax.all_gather(w_route[0], ('seq', 'shard'), axis=0, tiled=True)  181 us
    unnamed x324, local copies, waits for them, and re-layouts  144 us
    unnamed x32, starting transfers between devices  138 us
    unnamed x12, other arithmetic  58.4 us
  transfers between devices with their start and end apart: 64, of which 22 were waited for; matrix products, arithmetic and copies ran while one was open for 25% of the time, Pallas kernels for 0%

commit v1 on v0

v1 whole, which is shorter than its diff:
```python
from functools import partial

import jax
import jax.numpy as jnp
from jax import lax
from jax.sharding import PartitionSpec as P

D = 768
FF = 3072
HEAD_DIM = 64
CAP = 80
N_SEQ = 4
N_SHARD = 16
GROUP = 3
ROWS = 144
SEQ = 576
WIDE = 896
EPSILON = 1e-06
F32 = jnp.float32
BF16 = jnp.bfloat16


def dot(a, b, ca, cb):
    return lax.dot_general(a, b, (((ca,), (cb,)), ((), ())), preferred_element_type=F32)


def swap(v):
    return lax.ppermute(v, "section", [(0, 1), (1, 0)])


def turn(v, d):
    return lax.ppermute(v, "seq", [(i, (i + d) % N_SEQ) for i in range(N_SEQ)])


def hop(v, axis, d):
    route = []
    for z in range(4):
        for x in range(4):
            to = ((z + d) % 4) * 4 + x if axis == "z" else z * 4 + (x + d) % 4
            route.append((z * 4 + x, to))
    return lax.ppermute(v, "shard", route)


def place(axis):
    i = lax.axis_index("shard")
    return i // 4 if axis == "z" else lax.rem(i, 4)


def pick(v, i):
    return lax.dynamic_index_in_dim(v, i, 0, keepdims=False)


def gather_four(v, axis):
    blocks = [v] + [hop(v, axis, -d) for d in (1, 2, 3)]
    joined = jnp.stack(blocks + blocks[:3])
    return lax.dynamic_slice_in_dim(joined, lax.rem(4 - place(axis), 4), 4, 0)


def gather_shard(v):
    along = gather_four(v, "x")
    return gather_four(along, "z").reshape((N_SHARD,) + v.shape)


def scatter_four(v, axis):
    me = place(axis)
    total = pick(v, me).astype(F32)
    for d in (1, 2, 3):
        total = total + hop(pick(v, lax.rem(me + d, 4)), axis, d).astype(F32)
    return total


def scatter_shard(v):
    parts = v.reshape((4, 4) + v.shape[1:])
    first = scatter_four(parts[:, :, 0].swapaxes(0, 1), "x").astype(BF16)
    second = scatter_four(parts[:, :, 1], "z").astype(BF16)
    return jnp.stack([scatter_four(first, "z"), scatter_four(second, "x")])


def norm_parts(values):
    centred = values - jnp.mean(values, axis=-1, keepdims=True)
    inverse = lax.rsqrt(jnp.mean(centred * centred, axis=-1, keepdims=True) + EPSILON)
    return centred * inverse, inverse


def norm_back(n, inverse, gain, dy):
    gdy = dy * gain
    return (
        gdy
        - jnp.mean(gdy, axis=-1, keepdims=True)
        - n * jnp.mean(gdy * n, axis=-1, keepdims=True)
    ) * inverse


def gather_tokens(x):
    return jnp.concatenate([x] + [turn(x, -d) for d in (1, 2, 3)], axis=0)


def attend(x_all, w_mix, gain):
    normed = (norm_parts(x_all.astype(F32))[0] * gain).astype(BF16)
    packed = dot(normed, w_mix, 1, 0).astype(BF16)
    heads = packed.reshape(SEQ, 3, GROUP, HEAD_DIM)
    scores = jnp.einsum("qhd,khd->hqk", heads[:, 0], heads[:, 1], preferred_element_type=F32)
    scores = scores * HEAD_DIM ** (-0.5)
    top = jnp.max(scores, axis=-1, keepdims=True)
    exponent = jnp.exp(scores - top)
    totals = jnp.sum(exponent, axis=-1, keepdims=True)
    attention = (exponent / totals).astype(BF16)
    mixture = jnp.einsum("hqk,khd->qhd", attention, heads[:, 2], preferred_element_type=F32)
    return mixture.astype(BF16).reshape(SEQ, GROUP * HEAD_DIM), normed, packed, top + jnp.log(totals)


def attend_back(packed, log_total, d_mixture):
    heads = packed.reshape(SEQ, 3, GROUP, HEAD_DIM)
    scores = jnp.einsum("qhd,khd->hqk", heads[:, 0], heads[:, 1], preferred_element_type=F32)
    attention = jnp.exp(scores * HEAD_DIM ** (-0.5) - log_total)
    d_out = d_mixture.reshape(SEQ, GROUP, HEAD_DIM)
    d_values = jnp.einsum(
        "hqk,qhd->khd", attention.astype(BF16), d_out, preferred_element_type=F32
    )
    d_att = jnp.einsum("qhd,khd->hqk", d_out, heads[:, 2], preferred_element_type=F32)
    centre = jnp.sum(attention * d_att, axis=-1, keepdims=True)
    d_scores = (attention * (d_att - centre)).astype(BF16) * jnp.asarray(HEAD_DIM ** (-0.5), BF16)
    d_queries = jnp.einsum("hqk,khd->qhd", d_scores, heads[:, 1], preferred_element_type=F32)
    d_keys = jnp.einsum("hqk,qhd->khd", d_scores, heads[:, 0], preferred_element_type=F32)
    return jnp.stack([d_queries, d_keys, d_values], axis=1).reshape(SEQ, 576).astype(BF16)


def exchange_mixture(mixture):
    blocks = [mixture[ROWS * d : ROWS * (d + 1)] for d in range(N_SEQ)]
    return jnp.concatenate([blocks[0]] + [turn(blocks[d], d) for d in (1, 2, 3)], axis=1)


def selector_of(route_ids, me):
    relative = lax.rem(route_ids - me + N_SEQ, N_SEQ)
    experts = jnp.arange(N_SEQ, dtype=jnp.int32)
    named = (relative[:, 0:1] == experts) | (relative[:, 1:2] == experts)
    rank = jnp.cumsum(named.astype(jnp.int32), axis=0) - 1
    slots = jnp.arange(CAP, dtype=jnp.int32)
    chosen = named[:, :, None] & (rank[:, :, None] == slots)
    return chosen.reshape(ROWS, N_SEQ * CAP)


def two_parts(v):
    high = v.astype(BF16)
    return high, (v - high.astype(F32)).astype(BF16)


def middle(x, gathered, w_back, w_router, gain, route_ids, me):
    residual = x.astype(F32) + dot(gathered, w_back, 1, 0)
    n, inverse = norm_parts(residual)
    normed = (n * gain).astype(BF16)
    logits = dot(normed, w_router, 1, 0)
    gate_probs = jax.nn.softmax(logits, axis=-1)
    chosen = selector_of(route_ids, me)
    relative_gates = jnp.concatenate([gate_probs, gate_probs], axis=1)
    relative_gates = lax.dynamic_slice_in_dim(relative_gates, me, N_SEQ, 1)
    spread = jnp.broadcast_to(relative_gates[:, :, None], (ROWS, N_SEQ, CAP)).reshape(ROWS, -1)
    weights = two_parts(jnp.where(chosen, spread, 0.0))
    chosen = chosen.astype(BF16)
    buffer = dot(chosen, normed, 0, 0).astype(BF16)
    return residual, normed, gate_probs, chosen, weights, buffer


def send_out(buffer):
    blocks = [buffer[CAP * d : CAP * (d + 1)] for d in range(N_SEQ)]
    return jnp.concatenate([blocks[0]] + [turn(blocks[d], d) for d in (1, 2, 3)], axis=0)


def send_back(buffer):
    blocks = [buffer[CAP * d : CAP * (d + 1)] for d in range(N_SEQ)]
    return jnp.concatenate([blocks[0]] + [turn(blocks[d], -d) for d in (1, 2, 3)], axis=0)


def gelu_parts(h):
    cdf = 0.5 * (1.0 + lax.erf(h * 0.7071067811865476))
    return cdf


def expert_run(rows, packs):
    total = 0.0
    for pack in packs:
        for i in range(2):
            first = pack[:, 2 * i].reshape(D, 768)
            second = pack[:, 2 * i + 1].reshape(768, D)
            hidden = dot(rows, first, 1, 0)
            active = (hidden * gelu_parts(hidden)).astype(BF16)
            total = total + dot(active, second, 1, 0)
    return total.astype(BF16)


def expert_back(rows, d_result, packs):
    d_rows = 0.0
    grads = []
    for pack in packs:
        blocks = []
        for i in range(2):
            first = pack[:, 2 * i].reshape(D, 768)
            second = pack[:, 2 * i + 1].reshape(768, D)
            hidden = dot(rows, first, 1, 0)
            cdf = gelu_parts(hidden)
            active = (hidden * cdf).astype(BF16)
            slope = cdf + hidden * jnp.exp(-0.5 * hidden * hidden) * 0.3989422804014327
            d_active = dot(d_result, second, 1, 1)
            d_hidden = (d_active * slope).astype(BF16)
            d_rows = d_rows + dot(d_hidden, first, 1, 1)
            blocks.append(dot(rows, d_hidden, 0, 0).astype(BF16).reshape(N_SHARD, 48, 768))
            blocks.append(dot(active, d_result, 0, 0).astype(BF16).reshape(N_SHARD, 48, 768))
        grads.append(jnp.stack(blocks, axis=1))
    return d_rows.astype(BF16), grads


def combine(residual, weights, returned):
    return residual + dot(weights[0], returned, 1, 0) + dot(weights[1], returned, 1, 0)


def router_back(d_out, returned, chosen, gate_probs, me):
    products = jnp.where(chosen > 0, dot(d_out, returned, 1, 1), 0.0)
    d_gates = jnp.sum(products.reshape(ROWS, N_SEQ, CAP), axis=-1)
    d_gates = jnp.concatenate([d_gates, d_gates], axis=1)
    d_gates = lax.dynamic_slice_in_dim(d_gates, lax.rem(N_SEQ - me, N_SEQ), N_SEQ, 1)
    return gate_probs * (d_gates - jnp.sum(gate_probs * d_gates, axis=-1, keepdims=True))


def middle_back(d_out, d_returned, chosen, d_logits, w_router, residual, normed, gain, gathered, w_back):
    d_normed = dot(chosen, d_returned, 1, 0)
    for e in range(4):
        d_normed = d_normed + d_logits[:, e : e + 1] * w_router[:, e].astype(F32)[None, :]
    n, inverse = norm_parts(residual)
    d_residual = d_out.astype(F32) + norm_back(n, inverse, gain, d_normed)
    grad_gain = jnp.sum(d_normed * n, axis=0)
    high, low = two_parts(d_logits)
    grad_router = dot(normed, high, 0, 0) + dot(normed, low, 0, 0)
    d_branch = d_residual.astype(BF16)
    grad_back = dot(gathered, d_branch, 0, 0)
    d_mixture = dot(d_branch, w_back, 1, 1).astype(BF16)
    return d_residual, grad_gain, grad_router, grad_back, d_mixture


def exchange_d_mixture(d_mixture):
    blocks = [d_mixture[:, 192 * d : 192 * (d + 1)] for d in range(N_SEQ)]
    return jnp.concatenate([blocks[0]] + [turn(blocks[d], -d) for d in (1, 2, 3)], axis=0)


def attention_weights(w_qkv, w_proj, w_route, gain_attn, gain_ffn):
    mine = w_qkv.reshape(12, 3, N_SEQ, 192).transpose(2, 0, 1, 3).reshape(N_SEQ, 12, 576)
    small = jnp.concatenate(
        [w_route, gain_attn[:, None], gain_ffn[:, None], jnp.zeros((12, 122), BF16)], axis=1
    )
    mine = jnp.concatenate([mine, jnp.broadcast_to(small, (N_SEQ, 12, 128))], axis=2)
    arrived = lax.all_to_all(mine, "seq", 0, 0, tiled=True)
    back = w_proj.reshape(12, N_SEQ, 192).transpose(1, 0, 2)
    pack = jnp.concatenate([arrived[:, :, :576], back, arrived[:, :, 576:]], axis=2)
    whole = gather_shard(pack)
    other = swap(whole)
    core = lax.axis_index("section")
    layers = []
    for s in range(2):
        both = jnp.where(core == s, whole, other)
        rows = both.swapaxes(0, 1).reshape(D, WIDE)
        back_rows = both[:, :, :, 576:768].transpose(0, 2, 1, 3).reshape(192, D)
        layers.append((rows, back_rows))
    out = []
    for rows, back_rows in layers:
        w_back = jnp.concatenate([back_rows] + [turn(back_rows, d) for d in (1, 2, 3)], axis=0)
        out.append(
            (
                rows[:, :576],
                w_back,
                rows[:, 768:772],
                rows[:, 772].astype(F32),
                rows[:, 773].astype(F32),
            )
        )
    return out


def expert_weights(w_in, w_out):
    core = lax.axis_index("section")
    first = w_in.reshape(48, N_SHARD, 4, 48).transpose(2, 0, 1, 3).reshape(4, 48, 768)
    second = w_out.reshape(4, 48, 768)
    quarters = jnp.stack([first, second], axis=1).reshape(2, 4, 48, 768)
    mine = pick(quarters, core)
    arrived = swap(pick(quarters, 1 - core))
    out = []
    for s in range(2):
        own = jnp.where(core == s, mine, arrived)
        whole = lax.all_gather(own, "shard", axis=0, tiled=False)
        out.append((whole, swap(whole)))
    return out


def finish_experts(grads):
    own, other = grads
    total = (own.astype(F32) + swap(other).astype(F32)).astype(BF16)
    return scatter_shard(total.reshape(N_SHARD, 2, 2, 48, 768))


def finish_attention(grad_mix, small, grad_back):
    core = lax.axis_index("section")
    blocks = [grad_back[192 * d : 192 * (d + 1)] for d in range(N_SEQ)]
    back = blocks[0]
    for d in (1, 2, 3):
        back = back + turn(blocks[d].astype(BF16), -d).astype(F32)
    back = back.reshape(N_SHARD, 12, N_SEQ, 192).transpose(2, 0, 1, 3)
    rows = jnp.concatenate([grad_mix, small], axis=1).reshape(N_SEQ, N_SHARD, 12, 704)
    pack = jnp.concatenate([rows, back], axis=3).astype(BF16)
    pack = pack.reshape(2, 2, N_SHARD, 12, WIDE)
    total = pick(pack, core).astype(F32) + swap(pick(pack, 1 - core)).astype(F32)
    total = total.astype(BF16).transpose(1, 0, 2, 3)
    return scatter_shard(total)


def shards(images_in, out_grad, routes, w_qkv, w_proj, w_route, gain_attn, gain_ffn, w_in, w_out):
    core = lax.axis_index("section")
    me = lax.axis_index("seq")
    own_routes = routes[0, :, 0]
    mine = pick(own_routes, core)
    arrived = swap(pick(own_routes, 1 - core))
    route_of = (jnp.where(core == 0, mine, arrived), jnp.where(core == 0, arrived, mine))
    x0 = pick(images_in, core)[0]
    d_last = pick(out_grad, core)[0]
    attn = attention_weights(w_qkv[0], w_proj[0], w_route[0], gain_attn[0], gain_ffn[0])
    experts = expert_weights(w_in[0, 0], w_out[0, 0])

    saved = []
    x = x0
    layer_outs = []
    for s in range(2):
        w_mix, w_back, w_router, gain_one, gain_two = attn[s]
        x_all = gather_tokens(x)
        mixture, normed_one, packed, log_total = attend(x_all, w_mix, gain_one)
        gathered = exchange_mixture(mixture)
        residual, normed_two, gates, chosen, weights, buffer = middle(
            x, gathered, w_back, w_router, gain_two, route_of[s], me
        )
        rows = send_out(buffer)
        result = expert_run(rows, experts[s])
        returned = send_back(result)
        output = combine(residual, weights, returned).astype(BF16)
        saved.append(
            (x, normed_one, packed, log_total, gathered, residual, normed_two, gates, chosen, weights, rows, returned)
        )
        layer_outs.append(output)
        x = output

    d_out = d_last
    in_grads = [None, None]
    finished = [None, None]
    for s in (1, 0):
        w_mix, w_back, w_router, gain_one, gain_two = attn[s]
        (x, normed_one, packed, log_total, gathered, residual, normed_two, gates, chosen, weights, rows, returned) = saved[s]
        d_buffer = (dot(weights[0], d_out, 0, 0) + dot(weights[1], d_out, 0, 0)).astype(BF16)
        d_result = send_out(d_buffer)
        d_rows, expert_grads = expert_back(rows, d_result, experts[s])
        d_returned = send_back(d_rows)
        d_logits = router_back(d_out, returned, chosen, gates, me)
        d_residual, grad_gain_two, grad_router, grad_back, d_mixture = middle_back(
            d_out, d_returned, chosen, d_logits, w_router, residual, normed_two, gain_two, gathered, w_back
        )
        expert_total = finish_experts(expert_grads)
        d_heads = exchange_d_mixture(d_mixture)
        d_packed = attend_back(packed, log_total, d_heads)
        d_normed_all = dot(d_packed, w_mix, 1, 1)
        d_normed = d_normed_all[:ROWS]
        for d in (1, 2, 3):
            d_normed = d_normed + turn(d_normed_all[ROWS * d : ROWS * (d + 1)].astype(BF16), d).astype(F32)
        grad_mix = dot(normed_one, d_packed, 0, 0)
        n, inverse = norm_parts(x.astype(F32))
        d_out = (d_residual + norm_back(n, inverse, gain_one, d_normed)).astype(BF16)
        grad_gain_one = jnp.sum(d_normed * n, axis=0)
        small = jnp.concatenate(
            [grad_router, grad_gain_one[:, None], grad_gain_two[:, None], jnp.zeros((D, 122), F32)], axis=1
        )
        attn_total = finish_attention(grad_mix, small, grad_back)
        in_grads[s] = d_out
        finished[s] = (expert_total, attn_total)

    def settle(pair):
        keep = jnp.where(core == 0, pair[0], pair[1])
        give = jnp.where(core == 0, pair[1], pair[0])
        return keep, swap(give)

    def in_order(keep, got):
        return jnp.where(core == 0, jnp.stack([keep, got]), jnp.stack([got, keep]))

    layer_out = in_order(*settle(layer_outs))
    in_grad = in_order(*settle(in_grads))
    expert_sum = in_order(*settle([finished[s][0] for s in range(2)]))
    attn_sum = in_order(*settle([finished[s][1] for s in range(2)]))
    quarters = expert_sum.reshape(4, 2, 48, 768)
    grad_in = quarters[:, 0].reshape(4, 48, N_SHARD, 48).transpose(1, 2, 0, 3).reshape(48, FF)
    grad_out = quarters[:, 1].reshape(192, D)
    attn_sum = attn_sum.reshape(N_SEQ, 12, WIDE)
    back = attn_sum[:, :, 704:].transpose(1, 0, 2).reshape(12, D)
    mix = lax.all_to_all(attn_sum[:, :, :704].astype(BF16), "seq", 0, 0, tiled=True).astype(F32)
    grad_qkv = mix[:, :, :576].reshape(N_SEQ, 12, 3, 192).transpose(1, 2, 0, 3).reshape(12, 3 * D)
    small = jnp.sum(mix[:, :, 576:], axis=0)
    return (
        layer_out[None, :, None],
        in_grad[None, :, None],
        grad_qkv[None],
        back[None],
        small[None, :, 0:4],
        small[None, :, 4],
        small[None, :, 5],
        grad_in[None],
        grad_out[None],
    )


def solution(mesh):
    def run(*args):
        outs = shards(*args)
        outs = list(outs)
        outs[7] = outs[7][:, None]
        outs[8] = outs[8][:, None]
        return tuple(outs)

    return jax.shard_map(
        run,
        mesh=mesh,
        in_specs=(
            P(None, "shard", "seq", None),
            P(None, "shard", "seq", None),
            P("section", None, "shard", "seq", None),
            P("section", ("seq", "shard"), None),
            P("section", ("seq", "shard"), None),
            P("section", ("seq", "shard"), None),
            P("section", ("seq", "shard")),
            P("section", ("seq", "shard")),
            P("section", "seq", "shard", None),
            P("section", "seq", "shard", None),
        ),
        out_specs=(
            P("section", None, "shard", "seq", None),
            P("section", None, "shard", "seq", None),
            P("section", ("seq", "shard"), None),
            P("section", ("seq", "shard"), None),
            P("section", ("seq", "shard"), None),
            P("section", ("seq", "shard")),
            P("section", ("seq", "shard")),
            P("section", "seq", "shard", None),
            P("section", "seq", "shard", None),
        ),
        check_vma=False,
    )
```

time: 2120 us -> 727 us (0.34)
  the two profiles are of different devices: /device:TPU:64 before, /device:TPU:1 now
where the time goes in v1:
time: 727 us; the launch traced here: 717 us
  starting transfers between devices  186 us (26%)
  waiting for transfers between devices  172 us (24%)
  matrix products  154 us (21%)
  local copies, waits for them, and re-layouts  134 us (18%)
  other arithmetic  54.1 us (7%)
  between operations  17.8 us (2%)
    ppermute x54, waiting for transfers between devices, hop(): return lax.ppermute(v, 'shard', route)  116 us
    dot_general x80, matrix products, dot(): lax.dot_general(a, b, (((ca,), (cb,)), ((), ())), preferred_element_type=...  100 us
    ppermute x60, starting transfers between devices, turn(): return lax.ppermute(v, 'seq', [(i, (i + d) % N_SEQ) for i in range(N_SEQ)])  71.9 us
    ppermute x13, starting transfers between devices, swap(): return lax.ppermute(v, 'section', [(0, 1), (1, 0)])  51.5 us
    ppermute x54, starting transfers between devices, hop(): return lax.ppermute(v, 'shard', route)  51.1 us
    ppermute x60, waiting for transfers between devices, turn(): return lax.ppermute(v, 'seq', [(i, (i + d) % N_SEQ) for i in range(N_SEQ)])  48.3 us
    unnamed x414, local copies, waits for them, and re-layouts  32.9 us
    dot_general x2, matrix products, attend_back(): jnp.einsum('hqk,khd->qhd', d_scores, heads[:, 1], preferred_element_type=...  17.4 us
  transfers between devices with their start and end apart: 131, of which 63 were waited for; matrix products, arithmetic and copies ran while one was open for 39% of the time, Pallas kernels for 0%

profile of v1, /device:TPU:1, one launch (start us, length us, event | category | flops | bytes accessed | tf_op | source)
XLA Modules:
  0.0 717.1 jit_solution(1360421445324028367)
XLA Ops:
  42.7 4.4 collective-permute-start.6
  50.8 12.2 %collective-permute-done.6 = bf16[4,4,12,896]{3,2,1,0:T(8,128)(2,1)S(1)} collective-permute-done((bf16[4,4,12,896]{3,2,1,0:T(8,128)(2,1)S(1)}, bf16[4,4,12,896]{3,2,1,0:T(8,128)(2,1)S(1)}, u32[]{:S(2)}, u32[]{:S(2)}) %collective-permute-start.6) | collective-permute-done | bytes 344096 | tf_op jit(solution)/shard_map/ppermute | solution.py:41
  63.9 6.8 collective-permute-done.7
  71.5 16.3 %collective-permute-done.8 = bf16[4,4,12,896]{3,2,1,0:T(8,128)(2,1)S(1)} collective-permute-done((bf16[4,4,12,896]{3,2,1,0:T(8,128)(2,1)S(1)}, bf16[4,4,12,896]{3,2,1,0:T(8,128)(2,1)S(1)}, u32[]{:S(2)}, u32[]{:S(2)}) %collective-permute-start.8) | collective-permute-done | bytes 344096 | tf_op jit(solution)/shard_map/ppermute | solution.py:41
  93.3 4.9 collective-permute-start.9
  191.8 4.6 fusion.373
  205.4 5.0 collective-permute-done.26
  361.8 9.0 %fusion.91 = bf16[576,1,3,64]{0,3,2,1:T(8,128)(2,1)} fusion(f32[3,576,576]{1,2,0:T(8,128)} %fusion.256, f32[3,576,576]{1,2,0:T(8,128)} %copy-done.1, f32[3,576]{1,0:T(4,128)S(1)} %copy-done.121, bf16[576,3,3,64]{0,3,2,1:T(8,128)(2,1)} %bitcast.699), kind=kOutput, calls=%fused_computation.136 | convolution fusion | flops 139348224 | bytes 18182144 | tf_op jit(solution)/shard_map/hqk,qhd->khd/dot_general | solution.py:124
  370.9 9.1 %fusion.86 = bf16[576,1,3,64]{0,3,2,1:T(8,128)(2,1)} fusion(f32[3,576,576]{1,2,0:T(8,128)} %fusion.256, f32[3,576,576]{1,2,0:T(8,128)} %copy-done.1, f32[3,576]{1,0:T(4,128)S(1)} %copy-done.121, bf16[576,3,3,64]{0,3,2,1:T(8,128)(2,1)} %bitcast.700), kind=kOutput, calls=%fused_computation.135 | convolution fusion | flops 139348224 | bytes 18182144 | tf_op jit(solution)/shard_map/hqk,khd->qhd/dot_general | solution.py:123
  417.4 6.7 collective-permute-start.86
  477.1 8.3 %fusion.101 = bf16[576,1,3,64]{0,3,2,1:T(8,128)(2,1)S(1)} fusion(f32[3,576,576]{1,2,0:T(8,128)} %fusion.254, f32[3,576,576]{1,2,0:T(8,128)} %copy-done, f32[3,576]{1,0:T(4,128)S(1)} %copy-done.120, bf16[576,3,3,64]{0,3,2,1:T(8,128)(2,1)} %bitcast.694), kind=kOutput, calls=%fused_computation.138 | convolution fusion | flops 139348224 | bytes 18182144 | tf_op jit(solution)/shard_map/hqk,qhd->khd/dot_general | solution.py:124
  485.4 8.4 %fusion.96 = bf16[576,1,3,64]{0,3,2,1:T(8,128)(2,1)S(1)} fusion(f32[3,576,576]{1,2,0:T(8,128)} %fusion.254, f32[3,576,576]{1,2,0:T(8,128)} %copy-done, f32[3,576]{1,0:T(4,128)S(1)} %copy-done.120, bf16[576,3,3,64]{0,3,2,1:T(8,128)(2,1)} %bitcast.695), kind=kOutput, calls=%fused_computation.137 | convolution fusion | flops 139348224 | bytes 18182144 | tf_op jit(solution)/shard_map/hqk,khd->qhd/dot_general | solution.py:123
  503.5 4.9 collective-permute-done.63
  511.1 5.4 collective-permute-done.69
  538.9 4.4 collective-permute-start.66
  598.3 10.2 %collective-permute-start.109 = (bf16[4,2,48,768]{3,2,0,1:T(8,128)(2,1)S(1)}, bf16[4,2,48,768]{3,2,0,1:T(8,128)(2,1)S(1)}, u32[]{:S(2)}, u32[]{:S(2)}) collective-permute-start(bf16[4,2,48,768]{3,2,0,1:T(8,128)(2,1)S(1)} %get-tuple-element.101), channel_id=1, source_target_pairs={{0,12},{1,13},{2,14},{3,15},{4,0},{5,1},{6,2},{7,3},{8,4},{9,5},{1... | collective-permute-start | bytes 1769480 | tf_op jit(solution)/shard_map/ppermute | solution.py:41
  608.5 6.2 collective-permute-done.120
  616.1 6.5 collective-permute-done.125
  628.7 6.8 collective-permute-done.119
  638.1 7.7 %collective-permute-done.117 = bf16[2,48,768]{2,1,0:T(8,128)(2,1)S(1)} collective-permute-done((bf16[2,48,768]{2,1,0:T(8,128)(2,1)S(1)}, bf16[2,48,768]{2,1,0:T(8,128)(2,1)S(1)}, u32[]{:S(2)}, u32[]{:S(2)}) %collective-permute-start.117) | collective-permute-done | bytes 147488 | tf_op jit(solution)/shard_map/ppermute | solution.py:41
  646.0 11.6 %collective-permute-start.99 = (f32[2,12,896]{2,1,0:T(8,128)S(1)}, f32[2,12,896]{2,1,0:T(8,128)S(1)}, u32[]{:S(2)}, u32[]{:S(2)}) collective-permute-start(f32[2,12,896]{2,1,0:T(8,128)S(1)} %maximum_select_fusion.7), channel_id=1, source_target_pairs={{0,64},{64,0},{1,65},{65,1},{2,66},{66,2},{3,67},{67,3},{4,68},{68... | collective-permute-start | bytes 258056 | tf_op jit(solution)/shard_map/ppermute | solution.py:28
  661.4 10.3 %collective-permute-done.101 = bf16[4,2,48,768]{3,2,1,0:T(8,128)(2,1)S(1)} collective-permute-done((bf16[4,2,48,768]{3,2,1,0:T(8,128)(2,1)S(1)}, bf16[4,2,48,768]{3,2,1,0:T(8,128)(2,1)S(1)}, u32[]{:S(2)}, u32[]{:S(2)}) %collective-permute-start.101) | collective-permute-done | bytes 589856 | tf_op jit(solution)/shard_map/ppermute | solution.py:41
  679.9 8.8 %collective-permute-start.126 = (f32[2,2,48,768]{3,2,1,0:T(8,128)S(1)}, f32[2,2,48,768]{3,2,1,0:T(8,128)S(1)}, u32[]{:S(2)}, u32[]{:S(2)}) collective-permute-start(f32[2,2,48,768]{3,2,1,0:T(8,128)S(1)} %maximum_select_fusion.2), channel_id=1, source_target_pairs={{0,64},{64,0},{1,65},{65,1},{2,66},{66,2},{3,67},{67,3},{4,68},{68... | collective-permute-start | bytes 1769480 | tf_op jit(solution)/shard_map/ppermute | solution.py:28
  689.4 7.7 %all-to-all-start.1 = ((bf16[4,12,704]{2,1,0:T(8,128)(2,1)}), bf16[4,12,704]{2,1,0:T(8,128)(2,1)S(1)}, u32[]{:S(2)}, u32[]{:S(2)}) async-start(bf16[4,12,704]{2,1,0:T(8,128)(2,1)} %slice.869), calls=%async_computation.1 | async-start | bytes 196608 | tf_op jit(solution)/shard_map/all_to_all | solution.py:395
  (1020 shorter events, 513.1 us)
Async XLA Ops:
  7.2 133.6 %all-gather.5.cloned.1.call-start = ((), (), s32[]{:S(2)}) async-start(), calls=%async_computation.2 | async-start | bytes 5013504 | tf_op jit(solution)/shard_map/all_gather | solution.py:287
  13.8 85.7 %collective-permute-start.2 = (bf16[144,768]{1,0:T(8,128)(2,1)S(1)}, bf16[144,768]{1,0:T(8,128)(2,1)S(1)}, u32[]{:S(2)}, u32[]{:S(2)}) collective-permute-start(bf16[144,768]{1,0:T(8,128)(2,1)S(1)} %get-tuple-element.66), channel_id=1, source_target_pairs={{0,16},{16,32},{32,48},{48,0},{1,17},{17,33},{33,49},{49,1},{2,18}... | collective-permute-start | bytes 663560 | tf_op jit(solution)/shard_map/ppermute | solution.py:32
  15.3 84.2 %collective-permute-start.1 = (bf16[144,768]{1,0:T(8,128)(2,1)S(1)}, bf16[144,768]{1,0:T(8,128)(2,1)S(1)}, u32[]{:S(2)}, u32[]{:S(2)}) collective-permute-start(bf16[144,768]{1,0:T(8,128)(2,1)S(1)} %get-tuple-element.66), channel_id=1, source_target_pairs={{0,32},{16,48},{32,0},{48,16},{1,33},{17,49},{33,1},{49,17},{2,34}... | collective-permute-start | bytes 663560 | tf_op jit(solution)/shard_map/ppermute | solution.py:32
  17.9 81.6 %collective-permute-start = (bf16[144,768]{1,0:T(8,128)(2,1)S(1)}, bf16[144,768]{1,0:T(8,128)(2,1)S(1)}, u32[]{:S(2)}, u32[]{:S(2)}) collective-permute-start(bf16[144,768]{1,0:T(8,128)(2,1)S(1)} %get-tuple-element.66), channel_id=1, source_target_pairs={{0,48},{16,0},{32,16},{48,32},{1,49},{17,1},{33,17},{49,33},{2,50}... | collective-permute-start | bytes 663560 | tf_op jit(solution)/shard_map/ppermute | solution.py:32
  25.0 130.5 %all-gather.7.cloned.1.call-start = ((), (), s32[]{:S(2)}) async-start(), calls=%async_computation.3 | async-start | bytes 5013504 | tf_op jit(solution)/shard_map/all_gather | solution.py:287
  106.0 33.0 %collective-permute-start.13 = (bf16[192,768]{1,0:T(8,128)(2,1)}, bf16[192,768]{1,0:T(8,128)(2,1)}, u32[]{:S(2)}, u32[]{:S(2)}) collective-permute-start(bf16[192,768]{1,0:T(8,128)(2,1)} %reshape.956), channel_id=1, source_target_pairs={{0,16},{16,32},{32,48},{48,0},{1,17},{17,33},{33,49},{49,1},{2,18}... | collective-permute-start | bytes 884744 | tf_op jit(solution)/shard_map/ppermute | solution.py:32
  106.0 34.7 %collective-permute-start.14 = (bf16[192,768]{1,0:T(8,128)(2,1)}, bf16[192,768]{1,0:T(8,128)(2,1)}, u32[]{:S(2)}, u32[]{:S(2)}) collective-permute-start(bf16[192,768]{1,0:T(8,128)(2,1)} %reshape.956), channel_id=1, source_target_pairs={{0,32},{16,48},{32,0},{48,16},{1,33},{17,49},{33,1},{49,17},{2,34}... | collective-permute-start | bytes 884744 | tf_op jit(solution)/shard_map/ppermute | solution.py:32
  108.9 35.3 %collective-permute-start.15 = (bf16[192,768]{1,0:T(8,128)(2,1)}, bf16[192,768]{1,0:T(8,128)(2,1)}, u32[]{:S(2)}, u32[]{:S(2)}) collective-permute-start(bf16[192,768]{1,0:T(8,128)(2,1)} %reshape.956), channel_id=1, source_target_pairs={{0,48},{16,0},{32,16},{48,32},{1,49},{17,1},{33,17},{49,33},{2,50}... | collective-permute-start | bytes 884744 | tf_op jit(solution)/shard_map/ppermute | solution.py:32
  114.1 46.5 %collective-permute-start.31 = (bf16[192,768]{1,0:T(8,128)(2,1)}, bf16[192,768]{1,0:T(8,128)(2,1)}, u32[]{:S(2)}, u32[]{:S(2)}) collective-permute-start(bf16[192,768]{1,0:T(8,128)(2,1)} %reshape.963), channel_id=1, source_target_pairs={{0,16},{16,32},{32,48},{48,0},{1,17},{17,33},{33,49},{49,1},{2,18}... | collective-permute-start | bytes 884744 | tf_op jit(solution)/shard_map/ppermute | solution.py:32
  140.8 38.1 %collective-permute-start.21 = (bf16[16,4,48,768]{3,2,1,0:T(8,128)(2,1)}, bf16[16,4,48,768]{3,2,1,0:T(8,128)(2,1)}, u32[]{:S(2)}, u32[]{:S(2)}) collective-permute-start(bf16[16,4,48,768]{3,2,1,0:T(8,128)(2,1)} %bitcast.654), channel_id=1, source_target_pairs={{0,64},{64,0},{1,65},{65,1},{2,66},{66,2},{3,67},{67,3},{4,68},{68... | collective-permute-start | bytes 14155784 | tf_op jit(solution)/shard_map/ppermute | solution.py:28
  155.6 36.2 %collective-permute-start.37 = (bf16[16,4,48,768]{3,2,1,0:T(8,128)(2,1)}, bf16[16,4,48,768]{3,2,1,0:T(8,128)(2,1)}, u32[]{:S(2)}, u32[]{:S(2)}) collective-permute-start(bf16[16,4,48,768]{3,2,1,0:T(8,128)(2,1)} %bitcast.656), channel_id=1, source_target_pairs={{0,64},{64,0},{1,65},{65,1},{2,66},{66,2},{3,67},{67,3},{4,68},{68... | collective-permute-start | bytes 14155784 | tf_op jit(solution)/shard_map/ppermute | solution.py:28
  278.7 57.2 %collective-permute-start.41 = (bf16[144,768]{1,0:T(8,128)(2,1)}, bf16[144,768]{1,0:T(8,128)(2,1)}, u32[]{:S(2)}, u32[]{:S(2)}) collective-permute-start(bf16[144,768]{1,0:T(8,128)(2,1)} %get-tuple-element.184), channel_id=1, source_target_pairs={{0,64},{64,0},{1,65},{65,1},{2,66},{66,2},{3,67},{67,3},{4,68},{68... | collective-permute-start | bytes 663560 | tf_op jit(solution)/shard_map/ppermute | solution.py:28
  324.9 257.8 %collective-permute-start.113 = (bf16[16,4,48,768]{3,2,0,1:T(8,128)(2,1)}, bf16[16,4,48,768]{3,2,0,1:T(8,128)(2,1)}, u32[]{:S(2)}, u32[]{:S(2)}) collective-permute-start(bf16[16,4,48,768]{3,2,0,1:T(8,128)(2,1)} %pad_maximum_fusion.1), channel_id=1, source_target_pairs={{0,64},{64,0},{1,65},{65,1},{2,66},{66,2},{3,67},{67,3},{4,68},{68... | collective-permute-start | bytes 14155784 | tf_op jit(solution)/shard_map/ppermute | solution.py:28
  350.4 58.8 %collective-permute-start.85 = (bf16[192,768]{1,0:T(8,128)(2,1)}, bf16[192,768]{1,0:T(8,128)(2,1)}, u32[]{:S(2)}, u32[]{:S(2)}) collective-permute-start(bf16[192,768]{1,0:T(8,128)(2,1)} %get-tuple-element.117), channel_id=1, source_target_pairs={{0,16},{16,32},{32,48},{48,0},{1,17},{17,33},{33,49},{49,1},{2,18}... | collective-permute-start | bytes 884744 | tf_op jit(solution)/shard_map/ppermute | solution.py:32
  417.4 109.0 %collective-permute-start.86 = (bf16[2,16,12,896]{3,1,2,0:T(8,128)(2,1)}, bf16[2,16,12,896]{3,1,2,0:T(8,128)(2,1)}, u32[]{:S(2)}, u32[]{:S(2)}) collective-permute-start(bf16[2,16,12,896]{3,1,2,0:T(8,128)(2,1)} %dynamic-slice_bitcast_fusion), channel_id=1, source_target_pairs={{0,64},{64,0},{1,65},{65,1},{2,66},{66,2},{3,67},{67,3},{4,68},{68... | collective-permute-start | bytes 2064392 | tf_op jit(solution)/shard_map/ppermute | solution.py:28
  516.5 73.2 %collective-permute-start.100 = (bf16[16,4,48,768]{3,2,0,1:T(8,128)(2,1)}, bf16[16,4,48,768]{3,2,0,1:T(8,128)(2,1)}, u32[]{:S(2)}, u32[]{:S(2)}) collective-permute-start(bf16[16,4,48,768]{3,2,0,1:T(8,128)(2,1)} %pad_maximum_fusion), channel_id=1, source_target_pairs={{0,64},{64,0},{1,65},{65,1},{2,66},{66,2},{3,67},{67,3},{4,68},{68... | collective-permute-start | bytes 14155784 | tf_op jit(solution)/shard_map/ppermute | solution.py:28
  588.6 26.2 %collective-permute-start.120 = (bf16[4,2,48,768]{3,2,1,0:T(8,128)(2,1)S(1)}, bf16[4,2,48,768]{3,2,1,0:T(8,128)(2,1)S(1)}, u32[]{:S(2)}, u32[]{:S(2)}) collective-permute-start(bf16[4,2,48,768]{3,2,1,0:T(8,128)(2,1)S(1)} %bitcast.710), channel_id=1, source_target_pairs={{0,4},{1,5},{2,6},{3,7},{4,8},{5,9},{6,10},{7,11},{8,12},{9,13},{1... | collective-permute-start | bytes 1769480 | tf_op jit(solution)/shard_map/ppermute | solution.py:41
  588.9 26.5 %collective-permute-start.116 = (bf16[4,2,48,768]{3,2,1,0:T(8,128)(2,1)S(1)}, bf16[4,2,48,768]{3,2,1,0:T(8,128)(2,1)S(1)}, u32[]{:S(2)}, u32[]{:S(2)}) collective-permute-start(bf16[4,2,48,768]{3,2,1,0:T(8,128)(2,1)S(1)} %bitcast.709), channel_id=1, source_target_pairs={{0,3},{1,0},{2,1},{3,2},{4,7},{5,4},{6,5},{7,6},{8,11},{9,8},{10,9... | collective-permute-start | bytes 1769480 | tf_op jit(solution)/shard_map/ppermute | solution.py:41
  589.7 25.8 %collective-permute-start.115 = (bf16[4,2,48,768]{3,2,1,0:T(8,128)(2,1)S(1)}, bf16[4,2,48,768]{3,2,1,0:T(8,128)(2,1)S(1)}, u32[]{:S(2)}, u32[]{:S(2)}) collective-permute-start(bf16[4,2,48,768]{3,2,1,0:T(8,128)(2,1)S(1)} %bitcast.708), channel_id=1, source_target_pairs={{0,2},{1,3},{2,0},{3,1},{4,6},{5,7},{6,4},{7,5},{8,10},{9,11},{10,... | collective-permute-start | bytes 1769480 | tf_op jit(solution)/shard_map/ppermute | solution.py:41
  598.3 47.5 %collective-permute-start.109 = (bf16[4,2,48,768]{3,2,0,1:T(8,128)(2,1)S(1)}, bf16[4,2,48,768]{3,2,0,1:T(8,128)(2,1)S(1)}, u32[]{:S(2)}, u32[]{:S(2)}) collective-permute-start(bf16[4,2,48,768]{3,2,0,1:T(8,128)(2,1)S(1)} %get-tuple-element.101), channel_id=1, source_target_pairs={{0,12},{1,13},{2,14},{3,15},{4,0},{5,1},{6,2},{7,3},{8,4},{9,5},{1... | collective-permute-start | bytes 1769480 | tf_op jit(solution)/shard_map/ppermute | solution.py:41
  614.8 31.3 %collective-permute-start.108 = (bf16[4,2,48,768]{3,2,0,1:T(8,128)(2,1)S(1)}, bf16[4,2,48,768]{3,2,0,1:T(8,128)(2,1)S(1)}, u32[]{:S(2)}, u32[]{:S(2)}) collective-permute-start(bf16[4,2,48,768]{3,2,0,1:T(8,128)(2,1)S(1)} %get-tuple-element.102), channel_id=1, source_target_pairs={{0,8},{1,9},{2,10},{3,11},{4,12},{5,13},{6,14},{7,15},{8,0},{9,1},... | collective-permute-start | bytes 1769480 | tf_op jit(solution)/shard_map/ppermute | solution.py:41
  615.5 42.2 %collective-permute-start.107 = (bf16[4,2,48,768]{3,2,0,1:T(8,128)(2,1)S(1)}, bf16[4,2,48,768]{3,2,0,1:T(8,128)(2,1)S(1)}, u32[]{:S(2)}, u32[]{:S(2)}) collective-permute-start(bf16[4,2,48,768]{3,2,0,1:T(8,128)(2,1)S(1)} %get-tuple-element.100), channel_id=1, source_target_pairs={{0,4},{1,5},{2,6},{3,7},{4,8},{5,9},{6,10},{7,11},{8,12},{9,13},{1... | collective-permute-start | bytes 1769480 | tf_op jit(solution)/shard_map/ppermute | solution.py:41
  645.8 26.0 %collective-permute-start.101 = (bf16[4,2,48,768]{3,2,1,0:T(8,128)(2,1)S(1)}, bf16[4,2,48,768]{3,2,1,0:T(8,128)(2,1)S(1)}, u32[]{:S(2)}, u32[]{:S(2)}) collective-permute-start(bf16[4,2,48,768]{3,2,1,0:T(8,128)(2,1)S(1)} %bitcast.704), channel_id=1, source_target_pairs={{0,1},{1,2},{2,3},{3,0},{4,5},{5,6},{6,7},{7,4},{8,9},{9,10},{10,1... | collective-permute-start | bytes 1769480 | tf_op jit(solution)/shard_map/ppermute | solution.py:41
  646.0 42.7 %collective-permute-start.99 = (f32[2,12,896]{2,1,0:T(8,128)S(1)}, f32[2,12,896]{2,1,0:T(8,128)S(1)}, u32[]{:S(2)}, u32[]{:S(2)}) collective-permute-start(f32[2,12,896]{2,1,0:T(8,128)S(1)} %maximum_select_fusion.7), channel_id=1, source_target_pairs={{0,64},{64,0},{1,65},{65,1},{2,66},{66,2},{3,67},{67,3},{4,68},{68... | collective-permute-start | bytes 258056 | tf_op jit(solution)/shard_map/ppermute | solution.py:28
  (294 other events, 2080.7 us)
Sparse Core Ops, SparseCore 0:
  13.8 75.9 all-gather.4
  92.5 54.2 all-gather.6

commit v2 on v1

--- a/solution.py
+++ b/solution.py
@@ -50,30 +50,8 @@
     return lax.dynamic_index_in_dim(v, i, 0, keepdims=False)
 
 
-def gather_four(v, axis):
-    blocks = [v] + [hop(v, axis, -d) for d in (1, 2, 3)]
-    joined = jnp.stack(blocks + blocks[:3])
-    return lax.dynamic_slice_in_dim(joined, lax.rem(4 - place(axis), 4), 4, 0)
-
-
-def gather_shard(v):
-    along = gather_four(v, "x")
-    return gather_four(along, "z").reshape((N_SHARD,) + v.shape)
-
-
-def scatter_four(v, axis):
-    me = place(axis)
-    total = pick(v, me).astype(F32)
-    for d in (1, 2, 3):
-        total = total + hop(pick(v, lax.rem(me + d, 4)), axis, d).astype(F32)
-    return total
-
-
-def scatter_shard(v):
-    parts = v.reshape((4, 4) + v.shape[1:])
-    first = scatter_four(parts[:, :, 0].swapaxes(0, 1), "x").astype(BF16)
-    second = scatter_four(parts[:, :, 1], "z").astype(BF16)
-    return jnp.stack([scatter_four(first, "z"), scatter_four(second, "x")])
+def tie(value, other):
+    return lax.optimization_barrier((value, other))[0]
 
 
 def norm_parts(values):
@@ -161,13 +139,13 @@
     return residual, normed, gate_probs, chosen, weights, buffer
 
 
-def send_out(buffer):
-    blocks = [buffer[CAP * d : CAP * (d + 1)] for d in range(N_SEQ)]
+def send_out(buffer, height=CAP):
+    blocks = [buffer[height * d : height * (d + 1)] for d in range(N_SEQ)]
     return jnp.concatenate([blocks[0]] + [turn(blocks[d], d) for d in (1, 2, 3)], axis=0)
 
 
-def send_back(buffer):
-    blocks = [buffer[CAP * d : CAP * (d + 1)] for d in range(N_SEQ)]
+def send_back(buffer, height=CAP):
+    blocks = [buffer[height * d : height * (d + 1)] for d in range(N_SEQ)]
     return jnp.concatenate([blocks[0]] + [turn(blocks[d], -d) for d in (1, 2, 3)], axis=0)
 
 
@@ -188,8 +166,9 @@
     return total.astype(BF16)
 
 
-def expert_back(rows, d_result, packs):
+def expert_back(rows, d_result, packs, forward):
     d_rows = 0.0
+    result = 0.0
     grads = []
     for pack in packs:
         blocks = []
@@ -200,12 +179,16 @@
             cdf = gelu_parts(hidden)
             active = (hidden * cdf).astype(BF16)
             slope = cdf + hidden * jnp.exp(-0.5 * hidden * hidden) * 0.3989422804014327
+            if forward:
+                result = result + dot(active, second, 1, 0)
             d_active = dot(d_result, second, 1, 1)
             d_hidden = (d_active * slope).astype(BF16)
             d_rows = d_rows + dot(d_hidden, first, 1, 1)
             blocks.append(dot(rows, d_hidden, 0, 0).astype(BF16).reshape(N_SHARD, 48, 768))
             blocks.append(dot(active, d_result, 0, 0).astype(BF16).reshape(N_SHARD, 48, 768))
         grads.append(jnp.stack(blocks, axis=1))
+    if forward:
+        return result.astype(BF16), d_rows.astype(BF16), grads
     return d_rows.astype(BF16), grads
 
 
@@ -242,33 +225,30 @@
 
 
 def attention_weights(w_qkv, w_proj, w_route, gain_attn, gain_ffn):
+    core = lax.axis_index("section")
     mine = w_qkv.reshape(12, 3, N_SEQ, 192).transpose(2, 0, 1, 3).reshape(N_SEQ, 12, 576)
     small = jnp.concatenate(
-        [w_route, gain_attn[:, None], gain_ffn[:, None], jnp.zeros((12, 122), BF16)], axis=1
+        [w_route, gain_attn[:, None], gain_ffn[:, None], jnp.zeros((12, 58), BF16)], axis=1
     )
-    mine = jnp.concatenate([mine, jnp.broadcast_to(small, (N_SEQ, 12, 128))], axis=2)
-    arrived = lax.all_to_all(mine, "seq", 0, 0, tiled=True)
-    back = w_proj.reshape(12, N_SEQ, 192).transpose(1, 0, 2)
-    pack = jnp.concatenate([arrived[:, :, :576], back, arrived[:, :, 576:]], axis=2)
-    whole = gather_shard(pack)
+    mine = jnp.concatenate([mine, jnp.broadcast_to(small, (N_SEQ, 12, 64))], axis=2)
+    spread = jnp.broadcast_to(mine[:, None], (N_SEQ, N_SHARD, 12, 640))
+    spread = spread.reshape(N_SEQ * N_SHARD, 12, 640)
+    whole = lax.all_to_all(spread, ("seq", "shard"), 0, 0, tiled=True).reshape(D, 640)
     other = swap(whole)
-    core = lax.axis_index("section")
-    layers = []
+    spread = jnp.broadcast_to(w_proj[None], (N_SHARD, 12, D))
+    back_rows = lax.all_to_all(spread, "shard", 0, 0, tiled=True).reshape(192, D)
+    w_back = jnp.concatenate([back_rows] + [turn(back_rows, d) for d in (1, 2, 3)], axis=0)
+    other_back = swap(w_back)
+    out = []
     for s in range(2):
-        both = jnp.where(core == s, whole, other)
-        rows = both.swapaxes(0, 1).reshape(D, WIDE)
-        back_rows = both[:, :, :, 576:768].transpose(0, 2, 1, 3).reshape(192, D)
-        layers.append((rows, back_rows))
-    out = []
-    for rows, back_rows in layers:
-        w_back = jnp.concatenate([back_rows] + [turn(back_rows, d) for d in (1, 2, 3)], axis=0)
+        rows = jnp.where(core == s, whole, other)
         out.append(
             (
                 rows[:, :576],
-                w_back,
-                rows[:, 768:772],
-                rows[:, 772].astype(F32),
-                rows[:, 773].astype(F32),
+                jnp.where(core == s, w_back, other_back),
+                rows[:, 576:580],
+                rows[:, 580].astype(F32),
+                rows[:, 581].astype(F32),
             )
         )
     return out
@@ -289,25 +269,39 @@
     return out
 
 
-def finish_experts(grads):
+def join_experts(grads):
     own, other = grads
-    total = (own.astype(F32) + swap(other).astype(F32)).astype(BF16)
-    return scatter_shard(total.reshape(N_SHARD, 2, 2, 48, 768))
-
-
-def finish_attention(grad_mix, small, grad_back):
+    return (own.astype(F32) + swap(other).astype(F32)).astype(BF16)
+
+
+def scatter_now(v):
+    arrived = lax.all_to_all(v, "shard", 0, 0, tiled=True)
+    return jnp.sum(arrived.astype(F32), axis=0)
+
+
+def scatter_beside(v):
+    return lax.psum_scatter(v, "shard", scatter_dimension=0, tiled=True)[0].astype(F32)
+
+
+def join_attention(grad_mix, small, grad_back, me):
     core = lax.axis_index("section")
-    blocks = [grad_back[192 * d : 192 * (d + 1)] for d in range(N_SEQ)]
-    back = blocks[0]
-    for d in (1, 2, 3):
-        back = back + turn(blocks[d].astype(BF16), -d).astype(F32)
-    back = back.reshape(N_SHARD, 12, N_SEQ, 192).transpose(2, 0, 1, 3)
-    rows = jnp.concatenate([grad_mix, small], axis=1).reshape(N_SEQ, N_SHARD, 12, 704)
-    pack = jnp.concatenate([rows, back], axis=3).astype(BF16)
-    pack = pack.reshape(2, 2, N_SHARD, 12, WIDE)
-    total = pick(pack, core).astype(F32) + swap(pick(pack, 1 - core)).astype(F32)
-    total = total.astype(BF16).transpose(1, 0, 2, 3)
-    return scatter_shard(total)
+    mix = jnp.concatenate([grad_mix, small], axis=1).astype(BF16)
+    twice = jnp.concatenate([grad_back, grad_back], axis=0).astype(BF16)
+    turned = [
+        lax.dynamic_slice_in_dim(twice, 192 * lax.rem(me - g + N_SEQ, N_SEQ), 192, 0)
+        for g in range(N_SEQ)
+    ]
+    back = jnp.concatenate(turned, axis=0)
+    keep = jnp.where(core == 0, mix, back)
+    give = jnp.where(core == 0, back, mix)
+    return (keep.astype(F32) + swap(give).astype(F32)).astype(BF16)
+
+
+def scatter_attention(total):
+    arrived = lax.all_to_all(
+        total.reshape(N_SEQ * N_SHARD, 12, D), ("seq", "shard"), 0, 0, tiled=True
+    )
+    return jnp.sum(arrived.reshape(N_SEQ, N_SHARD, 12, D).astype(F32), axis=1)
 
 
 def shards(images_in, out_grad, routes, w_qkv, w_proj, w_route, gain_attn, gain_ffn, w_in, w_out):
@@ -333,32 +327,55 @@
         residual, normed_two, gates, chosen, weights, buffer = middle(
             x, gathered, w_back, w_router, gain_two, route_of[s], me
         )
-        rows = send_out(buffer)
-        result = expert_run(rows, experts[s])
-        returned = send_back(result)
-        output = combine(residual, weights, returned).astype(BF16)
-        saved.append(
-            (x, normed_one, packed, log_total, gathered, residual, normed_two, gates, chosen, weights, rows, returned)
-        )
-        layer_outs.append(output)
-        x = output
+        kept = (x, normed_one, packed, log_total, gathered, residual, normed_two, gates, chosen, weights)
+        if s == 0:
+            rows = send_out(buffer)
+            result = expert_run(rows, experts[s])
+            returned = send_back(result)
+            x = combine(residual, weights, returned).astype(BF16)
+            layer_outs.append(x)
+            saved.append(kept + (rows, returned))
+        else:
+            saved.append(kept + (buffer,))
 
     d_out = d_last
     in_grads = [None, None]
-    finished = [None, None]
+    expert_sums = [None, None]
+    attn_sums = [None, None]
     for s in (1, 0):
         w_mix, w_back, w_router, gain_one, gain_two = attn[s]
-        (x, normed_one, packed, log_total, gathered, residual, normed_two, gates, chosen, weights, rows, returned) = saved[s]
+        (x, normed_one, packed, log_total, gathered, residual, normed_two, gates, chosen, weights) = saved[s][:10]
         d_buffer = (dot(weights[0], d_out, 0, 0) + dot(weights[1], d_out, 0, 0)).astype(BF16)
-        d_result = send_out(d_buffer)
-        d_rows, expert_grads = expert_back(rows, d_result, experts[s])
-        d_returned = send_back(d_rows)
+        if s == 1:
+            both = jnp.stack([saved[s][10].reshape(4, CAP, D), d_buffer.reshape(4, CAP, D)], axis=1)
+            both = send_out(both.reshape(8 * CAP, D), 2 * CAP).reshape(4, 2, CAP, D)
+            rows = both[:, 0].reshape(4 * CAP, D)
+            d_result = both[:, 1].reshape(4 * CAP, D)
+            result, d_rows, expert_grads = expert_back(rows, d_result, experts[s], True)
+            both = jnp.stack([result.reshape(4, CAP, D), d_rows.reshape(4, CAP, D)], axis=1)
+            both = send_back(both.reshape(8 * CAP, D), 2 * CAP).reshape(4, 2, CAP, D)
+            returned = both[:, 0].reshape(4 * CAP, D)
+            d_returned = both[:, 1].reshape(4 * CAP, D)
+            layer_outs.append(combine(residual, weights, returned).astype(BF16))
+        else:
+            rows, returned = saved[s][10:]
+            d_result = send_out(d_buffer)
+            d_rows, expert_grads = expert_back(rows, d_result, experts[s], False)
+            d_returned = send_back(d_rows)
+        joined = join_experts(expert_grads)
+        if s == 1:
+            expert_sums[s] = scatter_beside(joined)
+        else:
+            expert_sums[s] = scatter_now(joined)
         d_logits = router_back(d_out, returned, chosen, gates, me)
         d_residual, grad_gain_two, grad_router, grad_back, d_mixture = middle_back(
             d_out, d_returned, chosen, d_logits, w_router, residual, normed_two, gain_two, gathered, w_back
         )
-        expert_total = finish_experts(expert_grads)
         d_heads = exchange_d_mixture(d_mixture)
+        if s == 0:
+            d_heads, expert_sums[1], attn_sums[1] = lax.optimization_barrier(
+                (d_heads, expert_sums[1], attn_sums[1])
+            )
         d_packed = attend_back(packed, log_total, d_heads)
         d_normed_all = dot(d_packed, w_mix, 1, 1)
         d_normed = d_normed_all[:ROWS]
@@ -369,11 +386,10 @@
         d_out = (d_residual + norm_back(n, inverse, gain_one, d_normed)).astype(BF16)
         grad_gain_one = jnp.sum(d_normed * n, axis=0)
         small = jnp.concatenate(
-            [grad_router, grad_gain_one[:, None], grad_gain_two[:, None], jnp.zeros((D, 122), F32)], axis=1
+            [grad_router, grad_gain_one[:, None], grad_gain_two[:, None], jnp.zeros((D, 186), F32)], axis=1
         )
-        attn_total = finish_attention(grad_mix, small, grad_back)
+        attn_sums[s] = scatter_attention(join_attention(grad_mix, small, grad_back, me))
         in_grads[s] = d_out
-        finished[s] = (expert_total, attn_total)
 
     def settle(pair):
         keep = jnp.where(core == 0, pair[0], pair[1])
@@ -385,14 +401,13 @@
 
     layer_out = in_order(*settle(layer_outs))
     in_grad = in_order(*settle(in_grads))
-    expert_sum = in_order(*settle([finished[s][0] for s in range(2)]))
-    attn_sum = in_order(*settle([finished[s][1] for s in range(2)]))
+    expert_sum = in_order(*settle(expert_sums))
+    attn_sum = in_order(*settle(attn_sums))
     quarters = expert_sum.reshape(4, 2, 48, 768)
     grad_in = quarters[:, 0].reshape(4, 48, N_SHARD, 48).transpose(1, 2, 0, 3).reshape(48, FF)
     grad_out = quarters[:, 1].reshape(192, D)
-    attn_sum = attn_sum.reshape(N_SEQ, 12, WIDE)
-    back = attn_sum[:, :, 704:].transpose(1, 0, 2).reshape(12, D)
-    mix = lax.all_to_all(attn_sum[:, :, :704].astype(BF16), "seq", 0, 0, tiled=True).astype(F32)
+    mix = attn_sum[0]
+    back = jnp.sum(attn_sum[1], axis=0)
     grad_qkv = mix[:, :, :576].reshape(N_SEQ, 12, 3, 192).transpose(1, 2, 0, 3).reshape(12, 3 * D)
     small = jnp.sum(mix[:, :, 576:], axis=0)
     return (

time: 727 us -> 589 us (0.81)
  starting transfers between devices: 186 us -> 119 us
  local copies, waits for them, and re-layouts: 134 us -> 77.8 us
  waiting for transfers between devices: 172 us -> 139 us
  other arithmetic: 54.1 us -> 77.4 us
    ppermute x54 -> x0, waiting for transfers between devices: 116 us -> none  [hop(): return lax.ppermute(v, 'shard', route)]
    all_to_all x2 -> x5, waiting for transfers between devices: 5.43 us -> 57.3 us  [the longest x2 33.9 us: scatter_attention(): lax.all_to_all(total.reshape(N_SEQ * N_SHARD, 12, D), ('seq', 'shard'), 0...]
    ppermute x54 -> x0, starting transfers between devices: 51.1 us -> none  [hop(): return lax.ppermute(v, 'shard', route)]
    all_to_all x2 -> x5, starting transfers between devices: 11.1 us -> 37.9 us  [the longest x2 19.6 us: scatter_attention(): lax.all_to_all(total.reshape(N_SEQ * N_SHARD, 12, D), ('seq', 'shard'), 0...]
    all_gather x2, waiting for transfers between devices: 0.01 us -> 24.9 us  [expert_weights(): whole = lax.all_gather(own, 'shard', axis=0, tiled=False)]
    ppermute x13 -> x14, starting transfers between devices: 51.5 us -> 26.6 us  [swap(): return lax.ppermute(v, 'section', [(0, 1), (1, 0)])]
    unnamed x414 -> x392, local copies, waits for them, and re-layouts: 32.9 us -> 14 us
    ppermute x60 -> x45, starting transfers between devices: 71.9 us -> 54.2 us  [turn(): return lax.ppermute(v, 'seq', [(i, (i + d) % N_SEQ) for i in range(N_SEQ)])]
  transfers between devices with their start and end apart: 131 -> 67, of which waited for: 63 -> 28; matrix products, arithmetic and copies ran while one was open for 39% -> 42% of each run, Pallas kernels for 0% -> 0%
where the time goes in v2:
time: 589 us; the launch traced here: 578 us
  matrix products  147 us (25%)
  waiting for transfers between devices  139 us (24%)
  starting transfers between devices  119 us (20%)
  local copies, waits for them, and re-layouts  77.8 us (13%)
  other arithmetic  77.4 us (13%)
  between operations  17.5 us (3%)
    dot_general x80, matrix products, dot(): lax.dot_general(a, b, (((ca,), (cb,)), ((), ())), preferred_element_type=...  91.4 us
    ppermute x45, waiting for transfers between devices, turn(): return lax.ppermute(v, 'seq', [(i, (i + d) % N_SEQ) for i in range(N_SEQ)])  54.9 us
    ppermute x45, starting transfers between devices, turn(): return lax.ppermute(v, 'seq', [(i, (i + d) % N_SEQ) for i in range(N_SEQ)])  54.2 us
    all_to_all x2, waiting for transfers between devices, scatter_attention(): lax.all_to_all(total.reshape(N_SEQ * N_SHARD, 12, D), ('seq', 'shard'), 0...  33.9 us
    ppermute x14, starting transfers between devices, swap(): return lax.ppermute(v, 'section', [(0, 1), (1, 0)])  26.6 us
    all_gather x2, waiting for transfers between devices, expert_weights(): whole = lax.all_gather(own, 'shard', axis=0, tiled=False)  24.9 us
    all_to_all x2, starting transfers between devices, scatter_attention(): lax.all_to_all(total.reshape(N_SEQ * N_SHARD, 12, D), ('seq', 'shard'), 0...  19.6 us
    dot_general x2, matrix products, attend_back(): jnp.einsum('hqk,khd->qhd', d_scores, heads[:, 1], preferred_element_type=...  18.6 us
  transfers between devices with their start and end apart: 67, of which 28 were waited for; matrix products, arithmetic and copies ran while one was open for 42% of the time, Pallas kernels for 0%

profile of v2, /device:TPU:1, one launch (start us, length us, event | category | flops | bytes accessed | tf_op | source)
XLA Modules:
  0.0 578.1 jit_solution(960326820531119584)
XLA Ops:
  20.6 10.2 %all-to-all-start = ((bf16[64,12,640]{2,1,0:T(8,128)(2,1)}), bf16[64,12,640]{2,1,0:T(8,128)(2,1)S(1)}, u32[]{:S(2)}, u32[]{:S(2)}) async-start(bf16[64,12,640]{2,1,0:T(8,128)(2,1)} %bitcast.5), calls=%async_computation | async-start | bytes 2621440 | tf_op jit(solution)/shard_map/all_to_all | solution.py:236
  38.7 14.9 %all-to-all-done = bf16[64,12,640]{2,1,0:T(8,128)(2,1)S(1)} async-done(((bf16[64,12,640]{2,1,0:T(8,128)(2,1)}), bf16[64,12,640]{2,1,0:T(8,128)(2,1)S(1)}, u32[]{:S(2)}, u32[]{:S(2)}) %all-to-all-start) | async-done | bytes 983072 | tf_op jit(solution)/shard_map/all_to_all | solution.py:236
  62.3 8.5 %all-to-all-done.1 = bf16[16,12,768]{2,1,0:T(8,128)(2,1)S(1)} async-done(((bf16[16,12,768]{2,1,0:T(8,128)(2,1)}), bf16[16,12,768]{2,1,0:T(8,128)(2,1)S(1)}, u32[]{:S(2)}, u32[]{:S(2)}) %all-to-all-start.1) | async-done | bytes 294944 | tf_op jit(solution)/shard_map/all_to_all | solution.py:239
  74.2 16.1 %collective-permute-done.7 = bf16[192,768]{0,1:T(8,128)(2,1)S(1)} collective-permute-done((bf16[192,768]{0,1:T(8,128)(2,1)S(1)}, bf16[192,768]{0,1:T(8,128)(2,1)S(1)}, u32[]{:S(2)}, u32[]{:S(2)}) %collective-permute-start.7) | collective-permute-done | bytes 294944 | tf_op jit(solution)/shard_map/ppermute | solution.py:32
  115.3 24.9 %all-gather.7.cloned.1.call-done = bf16[64,48,768]{2,1,0:T(8,128)(2,1)} async-done(((bf16[4,48,768]{2,1,0:T(8,128)(2,1)}), bf16[64,48,768]{2,1,0:T(8,128)(2,1)}) %all-gather.7.cloned.1.call-update) | async-done | bytes 4718608 | tf_op jit(solution)/shard_map/all_gather | solution.py:267
  174.1 4.6 fusion.324
  190.4 6.9 %collective-permute-done.22 = bf16[144,768]{1,0:T(8,128)(2,1)S(1)} collective-permute-done((bf16[144,768]{1,0:T(8,128)(2,1)S(1)}, bf16[144,768]{1,0:T(8,128)(2,1)S(1)}, u32[]{:S(2)}, u32[]{:S(2)}) %collective-permute-start.22) | collective-permute-done | bytes 221216 | tf_op jit(solution)/shard_map/ppermute | solution.py:32
  231.8 4.9 collective-permute-done.27
  274.2 4.3 collective-permute-done.32
  298.3 9.0 %fusion.133 = bf16[576,1,3,64]{0,3,2,1:T(8,128)(2,1)} fusion(f32[3,576,576]{1,2,0:T(8,128)} %fusion.245, f32[3,576,576]{1,2,0:T(8,128)} %copy-done.1, f32[3,576]{1,0:T(4,128)S(1)} %copy-done.121, bf16[576,3,3,64]{0,3,2,1:T(8,128)(2,1)} %bitcast.472), kind=kOutput, calls=%fused_computation.198 | convolution fusion | flops 139458816 | bytes 18182144 | tf_op jit(solution)/shard_map/hqk,khd->qhd/dot_general | solution.py:101
  307.3 9.0 %fusion.128 = bf16[576,1,3,64]{0,3,2,1:T(8,128)(2,1)} fusion(f32[3,576,576]{1,2,0:T(8,128)} %fusion.245, f32[3,576,576]{1,2,0:T(8,128)} %copy-done.1, f32[3,576]{1,0:T(4,128)S(1)} %copy-done.121, bf16[576,3,3,64]{0,3,2,1:T(8,128)(2,1)} %bitcast.473), kind=kOutput, calls=%fused_computation.197 | convolution fusion | flops 139458816 | bytes 18182144 | tf_op jit(solution)/shard_map/hqk,qhd->khd/dot_general | solution.py:102
  334.2 4.8 collective-permute-start.41
  343.2 8.0 %concatenate.126 = bf16[768,768]{0,1:T(8,128)(2,1)} concatenate(bf16[768,576]{0,1:T(8,128)(2,1)} %convolution_convert_fusion.19, bf16[768,4]{0,1:T(4,128)(2,1)S(1)} %copy-done.134, bf16[768,1]{0,1:T(2,128)(2,1)S(1)} %broadcast_in_dim.48, bf16[768,1]{0,1:T(2,128)(2,1)S(1)} %broadcast_in_dim.49, bf16[768,186]{0,1:T(8,128)(2,1)S(1)} %broadcast.479), dimensions={1} | concatenate | bytes 2359296 | tf_op jit(solution)/shard_map/concatenate | solution.py:288
  354.8 6.4 %add_convert_fusion.1 = bf16[16,4,48,768]{3,2,1,0:T(8,128)(2,1)} fusion(bf16[16,4,48,768]{3,2,1,0:T(8,128)(2,1)} %collective-permute-done.49, bf16[16,1,48,768]{3,2,1,0:T(8,128)(2,1)} %bitcast.448, bf16[16,1,48,768]{3,2,1,0:T(8,128)(2,1)S(1)} %bitcast.447, bf16[16,1,48,768]{3,2,1,0:T(8,128)(2,1)S(1)} %bitcast.446, bf16[16,1,48,768]{3,2,1,0:T(8,128)(2,1)S(1)} %bitcast.445), kind=kLoop, calls=%fused_computation.4 | loop fusion | flops 16515072 | bytes 14155776 | tf_op jit(solution)/shard_map/convert_element_type | solution.py:274
  376.4 4.5 collective-permute-start.57
  412.0 9.6 %all-to-all-start.2 = ((bf16[64,12,768]{2,1,0:T(8,128)(2,1)}), bf16[64,12,768]{2,1,0:T(8,128)(2,1)}, u32[]{:S(2)}, u32[]{:S(2)}) async-start(bf16[64,12,768]{2,1,0:T(8,128)(2,1)} %reshape.744), calls=%async_computation.2 | async-start | bytes 3145728 | tf_op jit(solution)/shard_map/all_to_all | solution.py:301
  423.8 6.9 %add_convert_fusion = bf16[16,4,48,768]{3,2,1,0:T(8,128)(2,1)} fusion(bf16[16,4,48,768]{3,2,1,0:T(8,128)(2,1)} %collective-permute-done.57, bf16[16,1,48,768]{3,2,1,0:T(8,128)(2,1)} %bitcast.452, bf16[16,1,48,768]{3,2,1,0:T(8,128)(2,1)} %bitcast.451, bf16[16,1,48,768]{3,2,1,0:T(8,128)(2,1)} %bitcast.450, bf16[16,1,48,768]{3,2,1,0:T(8,128)(2,1)S(1)} %bitcast.449), kind=kLoop, calls=%fused_computation.3 | loop fusion | flops 16515072 | bytes 14155776 | tf_op jit(solution)/shard_map/convert_element_type | solution.py:274
  430.7 14.9 %all-to-all-done.2 = bf16[64,12,768]{2,1,0:T(8,128)(2,1)} async-done(((bf16[64,12,768]{2,1,0:T(8,128)(2,1)}), bf16[64,12,768]{2,1,0:T(8,128)(2,1)}, u32[]{:S(2)}, u32[]{:S(2)}) %all-to-all-start.2) | async-done | bytes 1179680 | tf_op jit(solution)/shard_map/all_to_all | solution.py:301
  445.7 4.6 all-to-all-start.4
  467.4 9.6 %fusion.123 = bf16[576,1,3,64]{0,3,2,1:T(8,128)(2,1)} fusion(f32[3,576,576]{1,2,0:T(8,128)} %fusion.243, f32[3,576,576]{1,2,0:T(8,128)} %copy-done, f32[3,576]{1,0:T(4,128)S(1)} %copy-done.120, bf16[576,3,3,64]{0,3,2,1:T(8,128)(2,1)S(1)} %bitcast.467), kind=kOutput, calls=%fused_computation.196 | convolution fusion | flops 139458816 | bytes 18182144 | tf_op jit(solution)/shard_map/hqk,khd->qhd/dot_general | solution.py:101
  476.9 9.5 %fusion.118 = bf16[576,1,3,64]{0,3,2,1:T(8,128)(2,1)} fusion(f32[3,576,576]{1,2,0:T(8,128)} %fusion.243, f32[3,576,576]{1,2,0:T(8,128)} %copy-done, f32[3,576]{1,0:T(4,128)S(1)} %copy-done.120, bf16[576,3,3,64]{0,3,2,1:T(8,128)(2,1)S(1)} %bitcast.468), kind=kOutput, calls=%fused_computation.195 | convolution fusion | flops 139458816 | bytes 18182144 | tf_op jit(solution)/shard_map/hqk,qhd->khd/dot_general | solution.py:102
  508.6 6.3 %collective-permute-start.55 = (bf16[768,768]{0,1:T(8,128)(2,1)}, bf16[768,768]{0,1:T(8,128)(2,1)}, u32[]{:S(2)}, u32[]{:S(2)}) collective-permute-start(bf16[768,768]{0,1:T(8,128)(2,1)} %broadcast_select_fusion.1), channel_id=1, source_target_pairs={{0,64},{64,0},{1,65},{65,1},{2,66},{66,2},{3,67},{67,3},{4,68},{68... | collective-permute-start | bytes 3538952 | tf_op jit(solution)/shard_map/ppermute | solution.py:28
  525.2 10.0 %all-to-all-start.3 = ((bf16[64,12,768]{2,1,0:T(8,128)(2,1)}), bf16[64,12,768]{2,1,0:T(8,128)(2,1)S(1)}, u32[]{:S(2)}, u32[]{:S(2)}) async-start(bf16[64,12,768]{2,1,0:T(8,128)(2,1)} %reshape.746), calls=%async_computation.3 | async-start | bytes 3145728 | tf_op jit(solution)/shard_map/all_to_all | solution.py:301
  539.7 18.9 %all-to-all-done.3 = bf16[64,12,768]{2,1,0:T(8,128)(2,1)S(1)} async-done(((bf16[64,12,768]{2,1,0:T(8,128)(2,1)}), bf16[64,12,768]{2,1,0:T(8,128)(2,1)S(1)}, u32[]{:S(2)}, u32[]{:S(2)}) %all-to-all-start.3) | async-done | bytes 1179680 | tf_op jit(solution)/shard_map/all_to_all | solution.py:301
  (806 shorter events, 333.2 us)
Async XLA Ops:
  7.2 95.4 %all-gather.5.cloned.1.call-start = ((), (), s32[]{:S(2)}) async-start(), calls=%async_computation.6 | async-start | bytes 5013504 | tf_op jit(solution)/shard_map/all_gather | solution.py:267
  13.6 126.6 %all-gather.7.cloned.1.call-start = ((), (), s32[]{:S(2)}) async-start(), calls=%async_computation.7 | async-start | bytes 5013504 | tf_op jit(solution)/shard_map/all_gather | solution.py:267
  14.6 47.5 %collective-permute-start = (bf16[144,768]{1,0:T(8,128)(2,1)S(1)}, bf16[144,768]{1,0:T(8,128)(2,1)S(1)}, u32[]{:S(2)}, u32[]{:S(2)}) collective-permute-start(bf16[144,768]{1,0:T(8,128)(2,1)S(1)} %get-tuple-element.72), channel_id=1, source_target_pairs={{0,48},{16,0},{32,16},{48,32},{1,49},{17,1},{33,17},{49,33},{2,50}... | collective-permute-start | bytes 663560 | tf_op jit(solution)/shard_map/ppermute | solution.py:32
  17.4 44.6 %collective-permute-start.1 = (bf16[144,768]{1,0:T(8,128)(2,1)S(1)}, bf16[144,768]{1,0:T(8,128)(2,1)S(1)}, u32[]{:S(2)}, u32[]{:S(2)}) collective-permute-start(bf16[144,768]{1,0:T(8,128)(2,1)S(1)} %get-tuple-element.72), channel_id=1, source_target_pairs={{0,32},{16,48},{32,0},{48,16},{1,33},{17,49},{33,1},{49,17},{2,34}... | collective-permute-start | bytes 663560 | tf_op jit(solution)/shard_map/ppermute | solution.py:32
  17.8 44.3 %collective-permute-start.2 = (bf16[144,768]{1,0:T(8,128)(2,1)S(1)}, bf16[144,768]{1,0:T(8,128)(2,1)S(1)}, u32[]{:S(2)}, u32[]{:S(2)}) collective-permute-start(bf16[144,768]{1,0:T(8,128)(2,1)S(1)} %get-tuple-element.72), channel_id=1, source_target_pairs={{0,16},{16,32},{32,48},{48,0},{1,17},{17,33},{33,49},{49,1},{2,18}... | collective-permute-start | bytes 663560 | tf_op jit(solution)/shard_map/ppermute | solution.py:32
  20.6 33.1 %all-to-all-start = ((bf16[64,12,640]{2,1,0:T(8,128)(2,1)}), bf16[64,12,640]{2,1,0:T(8,128)(2,1)S(1)}, u32[]{:S(2)}, u32[]{:S(2)}) async-start(bf16[64,12,640]{2,1,0:T(8,128)(2,1)} %bitcast.5), calls=%async_computation | async-start | bytes 2621440 | tf_op jit(solution)/shard_map/all_to_all | solution.py:236
  58.0 403.4 %reduce-scatter.4.cloned.1.call-start = ((), (), s32[]{:S(2)}) async-start(), calls=%async_computation.8 | async-start | bytes 5013504
  59.1 34.6 %collective-permute-start.3 = (bf16[768,640]{1,0:T(8,128)(2,1)}, bf16[768,640]{1,0:T(8,128)(2,1)}, u32[]{:S(2)}, u32[]{:S(2)}) collective-permute-start(bf16[768,640]{1,0:T(8,128)(2,1)} %reshape.729), channel_id=1, source_target_pairs={{0,64},{64,0},{1,65},{65,1},{2,66},{66,2},{3,67},{67,3},{4,68},{68... | collective-permute-start | bytes 2949128 | tf_op jit(solution)/shard_map/ppermute | solution.py:28
  71.1 19.3 %collective-permute-start.7 = (bf16[192,768]{0,1:T(8,128)(2,1)S(1)}, bf16[192,768]{0,1:T(8,128)(2,1)S(1)}, u32[]{:S(2)}, u32[]{:S(2)}) collective-permute-start(bf16[192,768]{0,1:T(8,128)(2,1)S(1)} %copy.189), channel_id=1, source_target_pairs={{0,16},{16,32},{32,48},{48,0},{1,17},{17,33},{33,49},{49,1},{2,18}... | collective-permute-start | bytes 884744 | tf_op jit(solution)/shard_map/ppermute | solution.py:32
  71.1 19.2 %collective-permute-start.8 = (bf16[192,768]{0,1:T(8,128)(2,1)S(1)}, bf16[192,768]{0,1:T(8,128)(2,1)S(1)}, u32[]{:S(2)}, u32[]{:S(2)}) collective-permute-start(bf16[192,768]{0,1:T(8,128)(2,1)S(1)} %copy.189), channel_id=1, source_target_pairs={{0,32},{16,48},{32,0},{48,16},{1,33},{17,49},{33,1},{49,17},{2,34}... | collective-permute-start | bytes 884744 | tf_op jit(solution)/shard_map/ppermute | solution.py:32
  71.2 19.4 %collective-permute-start.9 = (bf16[192,768]{0,1:T(8,128)(2,1)S(1)}, bf16[192,768]{0,1:T(8,128)(2,1)S(1)}, u32[]{:S(2)}, u32[]{:S(2)}) collective-permute-start(bf16[192,768]{0,1:T(8,128)(2,1)S(1)} %copy.189), channel_id=1, source_target_pairs={{0,48},{16,0},{32,16},{48,32},{1,49},{17,1},{33,17},{49,33},{2,50}... | collective-permute-start | bytes 884744 | tf_op jit(solution)/shard_map/ppermute | solution.py:32
  91.2 18.1 %collective-permute-start.10 = (bf16[768,768]{0,1:T(8,128)(2,1)S(1)}, bf16[768,768]{0,1:T(8,128)(2,1)}, u32[]{:S(2)}, u32[]{:S(2)}) collective-permute-start(bf16[768,768]{0,1:T(8,128)(2,1)S(1)} %pad_maximum_fusion.2), channel_id=1, source_target_pairs={{0,64},{64,0},{1,65},{65,1},{2,66},{66,2},{3,67},{67,3},{4,68},{68... | collective-permute-start | bytes 3538952 | tf_op jit(solution)/shard_map/ppermute | solution.py:28
  102.5 58.9 %collective-permute-start.16 = (bf16[16,4,48,768]{3,2,1,0:T(8,128)(2,1)}, bf16[16,4,48,768]{3,2,1,0:T(8,128)(2,1)}, u32[]{:S(2)}, u32[]{:S(2)}) collective-permute-start(bf16[16,4,48,768]{3,2,1,0:T(8,128)(2,1)} %bitcast.426), channel_id=1, source_target_pairs={{0,64},{64,0},{1,65},{65,1},{2,66},{66,2},{3,67},{67,3},{4,68},{68... | collective-permute-start | bytes 14155784 | tf_op jit(solution)/shard_map/ppermute | solution.py:28
  140.2 33.9 %collective-permute-start.29 = (bf16[16,4,48,768]{3,2,1,0:T(8,128)(2,1)}, bf16[16,4,48,768]{3,2,1,0:T(8,128)(2,1)}, u32[]{:S(2)}, u32[]{:S(2)}) collective-permute-start(bf16[16,4,48,768]{3,2,1,0:T(8,128)(2,1)} %bitcast.422), channel_id=1, source_target_pairs={{0,64},{64,0},{1,65},{65,1},{2,66},{66,2},{3,67},{67,3},{4,68},{68... | collective-permute-start | bytes 14155784 | tf_op jit(solution)/shard_map/ppermute | solution.py:28
  267.7 87.0 %collective-permute-start.49 = (bf16[16,4,48,768]{3,2,1,0:T(8,128)(2,1)}, bf16[16,4,48,768]{3,2,1,0:T(8,128)(2,1)}, u32[]{:S(2)}, u32[]{:S(2)}) collective-permute-start(bf16[16,4,48,768]{3,2,1,0:T(8,128)(2,1)} %pad_maximum_fusion), channel_id=1, source_target_pairs={{0,64},{64,0},{1,65},{65,1},{2,66},{66,2},{3,67},{67,3},{4,68},{68... | collective-permute-start | bytes 14155784 | tf_op jit(solution)/shard_map/ppermute | solution.py:28
  333.2 29.1 %collective-permute-start.40 = (bf16[80,768]{1,0:T(8,128)(2,1)}, bf16[80,768]{1,0:T(8,128)(2,1)}, u32[]{:S(2)}, u32[]{:S(2)}) collective-permute-start(bf16[80,768]{1,0:T(8,128)(2,1)} %get-tuple-element.133), channel_id=1, source_target_pairs={{0,16},{16,32},{32,48},{48,0},{1,17},{17,33},{33,49},{49,1},{2,18}... | collective-permute-start | bytes 368648 | tf_op jit(solution)/shard_map/ppermute | solution.py:32
  334.2 28.1 %collective-permute-start.41 = (bf16[80,768]{1,0:T(8,128)(2,1)}, bf16[80,768]{1,0:T(8,128)(2,1)}, u32[]{:S(2)}, u32[]{:S(2)}) collective-permute-start(bf16[80,768]{1,0:T(8,128)(2,1)} %get-tuple-element.132), channel_id=1, source_target_pairs={{0,32},{16,48},{32,0},{48,16},{1,33},{17,49},{33,1},{49,17},{2,34}... | collective-permute-start | bytes 368648 | tf_op jit(solution)/shard_map/ppermute | solution.py:32
  339.0 23.2 %collective-permute-start.42 = (bf16[80,768]{1,0:T(8,128)(2,1)}, bf16[80,768]{1,0:T(8,128)(2,1)}, u32[]{:S(2)}, u32[]{:S(2)}) collective-permute-start(bf16[80,768]{1,0:T(8,128)(2,1)} %get-tuple-element.131), channel_id=1, source_target_pairs={{0,48},{16,0},{32,16},{48,32},{1,49},{17,1},{33,17},{49,33},{2,50}... | collective-permute-start | bytes 368648 | tf_op jit(solution)/shard_map/ppermute | solution.py:32
  376.4 47.5 %collective-permute-start.57 = (bf16[16,4,48,768]{3,2,1,0:T(8,128)(2,1)}, bf16[16,4,48,768]{3,2,1,0:T(8,128)(2,1)}, u32[]{:S(2)}, u32[]{:S(2)}) collective-permute-start(bf16[16,4,48,768]{3,2,1,0:T(8,128)(2,1)} %pad_maximum_fusion.1), channel_id=1, source_target_pairs={{0,64},{64,0},{1,65},{65,1},{2,66},{66,2},{3,67},{67,3},{4,68},{68... | collective-permute-start | bytes 14155784 | tf_op jit(solution)/shard_map/ppermute | solution.py:28
  380.9 23.2 %collective-permute-start.50 = (bf16[768,768]{0,1:T(8,128)(2,1)S(1)}, bf16[768,768]{0,1:T(8,128)(2,1)S(1)}, u32[]{:S(2)}, u32[]{:S(2)}) collective-permute-start(bf16[768,768]{0,1:T(8,128)(2,1)S(1)} %copy-done.69), channel_id=1, source_target_pairs={{0,64},{64,0},{1,65},{65,1},{2,66},{66,2},{3,67},{67,3},{4,68},{68... | collective-permute-start | bytes 3538952 | tf_op jit(solution)/shard_map/ppermute | solution.py:28
  412.0 33.7 %all-to-all-start.2 = ((bf16[64,12,768]{2,1,0:T(8,128)(2,1)}), bf16[64,12,768]{2,1,0:T(8,128)(2,1)}, u32[]{:S(2)}, u32[]{:S(2)}) async-start(bf16[64,12,768]{2,1,0:T(8,128)(2,1)} %reshape.744), calls=%async_computation.2 | async-start | bytes 3145728 | tf_op jit(solution)/shard_map/all_to_all | solution.py:301
  445.7 70.6 %all-to-all-start.4 = ((bf16[16,4,48,768]{3,2,1,0:T(8,128)(2,1)}), bf16[16,4,48,768]{3,2,1,0:T(8,128)(2,1)}, u32[]{:S(2)}, u32[]{:S(2)}) async-start(bf16[16,4,48,768]{3,2,1,0:T(8,128)(2,1)} %add_convert_fusion), calls=%async_computation.4 | async-start | bytes 9437184 | tf_op jit(solution)/shard_map/all_to_all | solution.py:278
  516.2 20.1 %collective-permute-start.33 = (bf16[144,768]{1,0:T(8,128)(2,1)}, bf16[144,768]{1,0:T(8,128)(2,1)S(1)}, u32[]{:S(2)}, u32[]{:S(2)}) collective-permute-start(bf16[144,768]{1,0:T(8,128)(2,1)} %get-tuple-element.143), channel_id=1, source_target_pairs={{0,64},{64,0},{1,65},{65,1},{2,66},{66,2},{3,67},{67,3},{4,68},{68... | collective-permute-start | bytes 663560 | tf_op jit(solution)/shard_map/ppermute | solution.py:28
  525.2 33.4 %all-to-all-start.3 = ((bf16[64,12,768]{2,1,0:T(8,128)(2,1)}), bf16[64,12,768]{2,1,0:T(8,128)(2,1)S(1)}, u32[]{:S(2)}, u32[]{:S(2)}) async-start(bf16[64,12,768]{2,1,0:T(8,128)(2,1)} %reshape.746), calls=%async_computation.3 | async-start | bytes 3145728 | tf_op jit(solution)/shard_map/all_to_all | solution.py:301
  (238 other events, 1772.5 us)
Sparse Core Ops, SparseCore 0:
  13.8 71.7 all-gather.4
  88.3 51.8 all-gather.6
  361.3 89.9 reduce-scatter.3

commit v3 on v2

v3 whole, which is shorter than its diff:
```python
import math
from functools import partial

import jax
import jax.numpy as jnp
from jax import lax
from jax.experimental import pallas as pl
from jax.experimental.pallas import tpu as pltpu
from jax.sharding import PartitionSpec as P

D = 768
FF = 3072
HEAD_DIM = 64
CAP = 80
N_SEQ = 4
N_SHARD = 16
GROUP = 3
ROWS = 144
SEQ = 576
WIDE = 1472
LIMIT = 56 * 1024 * 1024
EPSILON = 1e-06
F32 = jnp.float32
BF16 = jnp.bfloat16


def dot(a, b, ca, cb):
    return lax.dot_general(a, b, (((ca,), (cb,)), ((), ())), preferred_element_type=F32)


def swap(v):
    return lax.ppermute(v, "section", [(0, 1), (1, 0)])


def turn(v, d):
    return lax.ppermute(v, "seq", [(i, (i + d) % N_SEQ) for i in range(N_SEQ)])


def hop(v, axis, d):
    route = []
    for z in range(4):
        for x in range(4):
            to = ((z + d) % 4) * 4 + x if axis == "z" else z * 4 + (x + d) % 4
            route.append((z * 4 + x, to))
    return lax.ppermute(v, "shard", route)


def place(axis):
    i = lax.axis_index("shard")
    return i // 4 if axis == "z" else lax.rem(i, 4)


def pick(v, i):
    return lax.dynamic_index_in_dim(v, i, 0, keepdims=False)


def tie(value, other):
    return lax.optimization_barrier((value, other))[0]


def norm_parts(values):
    centred = values - jnp.mean(values, axis=-1, keepdims=True)
    inverse = lax.rsqrt(jnp.mean(centred * centred, axis=-1, keepdims=True) + EPSILON)
    return centred * inverse, inverse


def norm_back(n, inverse, gain, dy):
    gdy = dy * gain
    return (
        gdy
        - jnp.mean(gdy, axis=-1, keepdims=True)
        - n * jnp.mean(gdy * n, axis=-1, keepdims=True)
    ) * inverse


def two_parts(v):
    high = v.astype(BF16)
    return high, (v - high.astype(F32)).astype(BF16)


def gather_tokens(x):
    return jnp.concatenate([x] + [turn(x, -d) for d in (1, 2, 3)], axis=0)


def send_out(blocks):
    return [blocks[0]] + [turn(blocks[d], d) for d in (1, 2, 3)]


def send_back(blocks):
    return [blocks[0]] + [turn(blocks[d], -d) for d in (1, 2, 3)]


def vmem():
    return pl.BlockSpec(memory_space=pltpu.VMEM)


def smem():
    return pl.BlockSpec(memory_space=pltpu.SMEM)


def shape(dims, kind):
    return jax.ShapeDtypeStruct(dims, kind)


def call(body, outs, ins, name, flops, scalars=0, scratch=()):
    specs = [smem()] * scalars + [vmem()] * (len(ins) - scalars)
    moved = sum(math.prod(v.shape) * v.dtype.itemsize for v in list(ins) + list(outs))
    return pl.pallas_call(
        body,
        out_shape=outs,
        in_specs=specs,
        out_specs=[vmem()] * len(outs),
        scratch_shapes=list(scratch),
        name=name,
        cost_estimate=pl.CostEstimate(flops=int(flops), bytes_accessed=moved, transcendentals=0),
        compiler_params=pltpu.CompilerParams(vmem_limit_bytes=LIMIT),
    )(*ins)


def attend_kernel(x_ref, w_ref, gain_ref, mix_ref, packed_ref, log_ref):
    n, _ = norm_parts(x_ref[...].astype(F32))
    normed = (n * gain_ref[4:5, :]).astype(BF16)
    packed_ref[...] = dot(normed, w_ref[...], 1, 0).astype(BF16)
    lane = lax.broadcasted_iota(jnp.int32, (SEQ, 128), 1)
    logs = jnp.zeros((SEQ, 128), F32)
    outs = []
    for h in range(GROUP):
        query = packed_ref[:, 64 * h : 64 * h + 64]
        key = packed_ref[:, 192 + 64 * h : 256 + 64 * h]
        value = packed_ref[:, 384 + 64 * h : 448 + 64 * h]
        scores = dot(query, key, 1, 1) * HEAD_DIM ** (-0.5)
        top = jnp.max(scores, axis=1, keepdims=True)
        exponent = jnp.exp(scores - top)
        total = jnp.sum(exponent, axis=1, keepdims=True)
        outs.append((dot(exponent.astype(BF16), value, 1, 0) / total).astype(BF16))
        logs = jnp.where(lane == h, top + jnp.log(total), logs)
    log_ref[...] = logs
    mixture = jnp.concatenate(outs, axis=1)
    for d in range(N_SEQ):
        mix_ref[d] = mixture[ROWS * d : ROWS * (d + 1)]


def attend(x_all, w_mix, gains):
    return call(
        attend_kernel,
        [shape((N_SEQ, ROWS, 192), BF16), shape((SEQ, 576), BF16), shape((SEQ, 128), F32)],
        [x_all, w_mix, gains],
        "attention",
        2 * SEQ * D * 576 + 3 * 4 * SEQ * SEQ * 64,
    )


def attend_back_kernel(
    x_ref, w_ref, gain_ref, packed_ref, log_ref, d0, d1, d2, d3, small_ref,
    d_normed_ref, grad_ref, d_packed_ref, d_mix_ref,
):
    for d, ref in enumerate((d0, d1, d2, d3)):
        d_mix_ref[ROWS * d : ROWS * (d + 1)] = ref[...]
    scaling = HEAD_DIM ** (-0.5)
    parts = [[], [], []]
    for h in range(GROUP):
        query = packed_ref[:, 64 * h : 64 * h + 64]
        key = packed_ref[:, 192 + 64 * h : 256 + 64 * h]
        value = packed_ref[:, 384 + 64 * h : 448 + 64 * h]
        d_out = d_mix_ref[:, 64 * h : 64 * h + 64]
        attention = jnp.exp(dot(query, key, 1, 1) * scaling - log_ref[:, h : h + 1])
        parts[2].append(dot(attention.astype(BF16), d_out, 0, 0).astype(BF16))
        d_att = dot(d_out, value, 1, 1)
        centre = jnp.sum(attention * d_att, axis=1, keepdims=True)
        d_scores = (attention * (d_att - centre) * scaling).astype(BF16)
        parts[0].append(dot(d_scores, key, 1, 0).astype(BF16))
        parts[1].append(dot(d_scores, query, 0, 0).astype(BF16))
    d_packed_ref[...] = jnp.concatenate(parts[0] + parts[1] + parts[2], axis=1)
    n, _ = norm_parts(x_ref[...].astype(F32))
    normed = (n * gain_ref[4:5, :]).astype(BF16)
    d_packed = d_packed_ref[...]
    d_normed = dot(d_packed, w_ref[...], 1, 1)
    for d in range(N_SEQ):
        d_normed_ref[d] = d_normed[ROWS * d : ROWS * (d + 1)].astype(BF16)
    column = (lax.broadcasted_iota(jnp.int32, (SEQ, 64), 1) == 4).astype(BF16)
    high, low = two_parts(d_normed * n)
    small = small_ref[...] + dot(high, column, 0, 0) + dot(low, column, 0, 0)
    grad = dot(normed, d_packed, 0, 0)
    grad = jnp.concatenate([grad, small, jnp.zeros((D, 128), F32)], axis=1)
    grad_ref[...] = grad.astype(BF16)


def attend_back(x_all, w_mix, gains, packed, logs, d_heads, small):
    return call(
        attend_back_kernel,
        [shape((N_SEQ, ROWS, D), BF16), shape((D, D), BF16)],
        [x_all, w_mix, gains, packed, logs, *d_heads, small],
        "attention_back",
        4 * SEQ * D * 576 + 3 * 10 * SEQ * SEQ * 64,
        scratch=[pltpu.VMEM((SEQ, 576), BF16), pltpu.VMEM((SEQ, 192), BF16)],
    )


def middle_kernel(
    extra, me_ref, x_ref, g0, g1, g2, g3, w_ref, router_ref, gain_ref, route_ref, *refs
):
    me = me_ref[0]
    if extra:
        d_out_ref, *refs = refs
    residual_ref, normed_ref, gates_ref, chosen_ref, high_ref, low_ref, buffer_ref = refs[:7]
    residual = x_ref[...].astype(F32)
    for d, ref in enumerate((g0, g1, g2, g3)):
        residual = residual + dot(ref[...], w_ref[lax.rem(me - d + N_SEQ, N_SEQ)], 1, 0)
    residual_ref[...] = residual
    n, _ = norm_parts(residual)
    normed = (n * gain_ref[5:6, :]).astype(BF16)
    normed_ref[...] = normed
    lane = lax.broadcasted_iota(jnp.int32, (ROWS, 128), 1)
    logits = jnp.where(lane < 4, dot(normed, router_ref[...], 1, 0), -1e30)
    logits = logits - jnp.max(logits, axis=1, keepdims=True)
    gates = jnp.exp(logits)
    gates = gates / jnp.sum(gates, axis=1, keepdims=True)
    gates_ref[...] = gates
    routes = route_ref[...]
    relative = lax.rem(routes - me + N_SEQ, N_SEQ)
    named = (lane == relative[:, 0:1]) | (lane == relative[:, 1:2])
    row = lax.broadcasted_iota(jnp.int32, (ROWS, ROWS), 0)
    column = lax.broadcasted_iota(jnp.int32, (ROWS, ROWS), 1)
    before = (row > column).astype(BF16)
    rank = dot(before, named.astype(BF16), 1, 0)
    slot = lax.broadcasted_iota(jnp.int32, (ROWS, 320), 1)
    own = jnp.where(slot >= 160, jnp.where(slot >= 240, 3, 2), jnp.where(slot >= 80, 1, 0))
    place = (slot - CAP * own).astype(F32)
    wanted = jnp.full((ROWS, 320), -1.0, F32)
    spread = jnp.zeros((ROWS, 320), F32)
    position = jnp.where(named, rank, -1.0)
    for e in range(N_SEQ):
        wanted = jnp.where(own == e, position[:, e : e + 1], wanted)
        spread = jnp.where(lax.rem(own + me, N_SEQ) == e, gates[:, e : e + 1], spread)
    taken = wanted == place
    chosen = taken.astype(BF16)
    high, low = two_parts(jnp.where(taken, spread, 0.0))
    chosen_ref[...] = chosen
    high_ref[...] = high
    low_ref[...] = low
    buffer = dot(chosen, normed, 0, 0).astype(BF16)
    if not extra:
        for d in range(N_SEQ):
            buffer_ref[d] = buffer[CAP * d : CAP * (d + 1)]
    else:
        d_out = d_out_ref[...]
        d_buffer = (dot(high, d_out, 0, 0) + dot(low, d_out, 0, 0)).astype(BF16)
        for d in range(N_SEQ):
            buffer_ref[d, 0] = buffer[CAP * d : CAP * (d + 1)]
            buffer_ref[d, 1] = d_buffer[CAP * d : CAP * (d + 1)]


def middle(me, x, gathered, w_back, router, gains, route_ids, d_out):
    extra = d_out is not None
    sent = (N_SEQ, 2, CAP, D) if extra else (N_SEQ, CAP, D)
    return call(
        partial(middle_kernel, extra),
        [
            shape((ROWS, D), F32),
            shape((ROWS, D), BF16),
            shape((ROWS, 128), F32),
            shape((ROWS, 320), BF16),
            shape((ROWS, 320), BF16),
            shape((ROWS, 320), BF16),
            shape(sent, BF16),
        ],
        [me, x, *gathered, w_back, router, gains, route_ids] + ([d_out] if extra else []),
        "middle",
        2 * ROWS * D * (D + 320),
        scalars=1,
    )


def gelu_of(hidden):
    cdf = 0.5 + 0.5 * lax.erf(hidden * 0.7071067811865476)
    return hidden * cdf, cdf


def quarter(ref, i):
    return ref[:, i].reshape(768, D)


def expert_kernel(r0, r1, r2, r3, own_ref, other_ref, out_ref, rows_ref, total):
    @pl.when(pl.program_id(0) == 0)
    def _():
        for d, ref in enumerate((r0, r1, r2, r3)):
            rows_ref[CAP * d : CAP * (d + 1)] = ref[...]
        total[...] = jnp.zeros_like(total)

    rows = rows_ref[...]
    for pack in (own_ref, other_ref):
        hidden = dot(rows, quarter(pack, 0), 1, 0)
        active = gelu_of(hidden)[0].astype(BF16)
        total[...] += dot(active, quarter(pack, 1), 1, 0)

    @pl.when(pl.program_id(0) == 1)
    def _():
        for d in range(N_SEQ):
            out_ref[d] = total[CAP * d : CAP * (d + 1)].astype(BF16)


def whole_block(dims):
    return pl.BlockSpec(dims, lambda i: (0,) * len(dims))


def pack_block():
    return pl.BlockSpec((N_SHARD, 2, 48, 768), lambda i: (0, i, 0, 0))


def grid_call(body, outs, out_specs, ins, in_specs, name, flops, scratch):
    moved = sum(math.prod(v.shape) * v.dtype.itemsize for v in list(ins) + outs)
    return pl.pallas_call(
        body,
        grid=(2,),
        out_shape=outs,
        in_specs=in_specs,
        out_specs=out_specs,
        scratch_shapes=scratch,
        name=name,
        cost_estimate=pl.CostEstimate(flops=flops, bytes_accessed=moved, transcendentals=0),
        compiler_params=pltpu.CompilerParams(
            vmem_limit_bytes=LIMIT, dimension_semantics=("arbitrary",)
        ),
    )(*ins)


def expert_run(blocks, packs):
    return grid_call(
        expert_kernel,
        [shape((N_SEQ, CAP, D), BF16)],
        [whole_block((N_SEQ, CAP, D))],
        [*blocks, *packs],
        [whole_block((CAP, D))] * 4 + [pack_block()] * 2,
        "expert",
        4 * 320 * D * FF,
        [pltpu.VMEM((320, D), BF16), pltpu.VMEM((320, D), F32)],
    )[0]


def expert_back_kernel(forward, *refs):
    ins, (own_ref, other_ref), refs = refs[: 4 if forward else 8], refs[4 if forward else 8 :][:2], refs[6 if forward else 10 :]
    out_ref, rows_out, d_result_out, act_own, act_other, dh_own, dh_other, d_total, total = refs
    step = pl.program_id(0)

    @pl.when(step == 0)
    def _():
        for d in range(N_SEQ):
            there = pl.ds(CAP * d, CAP)
            rows_out[there] = ins[d][0] if forward else ins[d][...]
            d_result_out[there] = ins[d][1] if forward else ins[4 + d][...]
        d_total[...] = jnp.zeros_like(d_total)
        if forward:
            total[...] = jnp.zeros_like(total)

    rows = rows_out[...]
    d_result = d_result_out[...]
    for pack, act_ref, dh_ref in ((own_ref, act_own, dh_own), (other_ref, act_other, dh_other)):
        hidden = dot(rows, quarter(pack, 0), 1, 0)
        value, cdf = gelu_of(hidden)
        active = value.astype(BF16)
        act_ref[...] = active
        slope = cdf + hidden * jnp.exp(-0.5 * hidden * hidden) * 0.3989422804014327
        d_hidden = (dot(d_result, quarter(pack, 1), 1, 1) * slope).astype(BF16)
        dh_ref[...] = d_hidden
        d_total[...] += dot(d_hidden, quarter(pack, 0), 1, 1)
        if forward:
            total[...] += dot(active, quarter(pack, 1), 1, 0)

    @pl.when(step == 1)
    def _():
        for d in range(N_SEQ):
            there = pl.ds(CAP * d, CAP)
            if forward:
                out_ref[d, 0] = total[there].astype(BF16)
                out_ref[d, 1] = d_total[there].astype(BF16)
            else:
                out_ref[d] = d_total[there].astype(BF16)


def expert_back(blocks, packs, forward):
    sent = (N_SEQ, 2, CAP, D) if forward else (N_SEQ, CAP, D)
    half = pl.BlockSpec((320, 768), lambda i: (0, i))
    block = whole_block((2, CAP, D)) if forward else whole_block((CAP, D))
    return grid_call(
        partial(expert_back_kernel, forward),
        [shape(sent, BF16)] + [shape((320, D), BF16)] * 2 + [shape((320, 1536), BF16)] * 4,
        [whole_block(sent)] + [whole_block((320, D))] * 2 + [half] * 4,
        [*blocks, *packs],
        [block] * len(blocks) + [pack_block()] * 2,
        "expert_back",
        8 * 320 * D * FF,
        [pltpu.VMEM((320, D), F32)] * 2,
    )


def expert_grad_kernel(rows_ref, d_result_ref, act_ref, dh_ref, out_ref):
    grad = dot(rows_ref[...], dh_ref[...], 0, 0).astype(BF16)
    out_ref[:, 0] = grad.reshape(N_SHARD, 48, 768)
    grad = dot(act_ref[...], d_result_ref[...], 0, 0).astype(BF16)
    out_ref[:, 1] = grad.reshape(N_SHARD, 48, 768)


def expert_grad(rows, d_result, active, d_hidden):
    half = pl.BlockSpec((320, 768), lambda i: (0, i))
    return grid_call(
        expert_grad_kernel,
        [shape((N_SHARD, 4, 48, 768), BF16)],
        [pack_block()],
        [rows, d_result, active, d_hidden],
        [whole_block((320, D))] * 2 + [half] * 2,
        "expert_grad",
        2 * 320 * D * FF,
        [],
    )[0]


def combine_kernel(residual_ref, high_ref, low_ref, r0, r1, r2, r3, out_ref, rows_ref):
    for d, ref in enumerate((r0, r1, r2, r3)):
        rows_ref[CAP * d : CAP * (d + 1)] = ref[...]
    rows = rows_ref[...]
    total = residual_ref[...] + dot(high_ref[...], rows, 1, 0) + dot(low_ref[...], rows, 1, 0)
    out_ref[...] = total.astype(BF16)


def combine(residual, high, low, blocks):
    return call(
        combine_kernel,
        [shape((ROWS, D), BF16)],
        [residual, high, low, *blocks],
        "combine",
        4 * ROWS * D * 320,
        scratch=[pltpu.VMEM((320, D), BF16)],
    )[0]


def send_grad_kernel(d_out_ref, high_ref, low_ref, out_ref):
    d_out = d_out_ref[...]
    total = dot(high_ref[...], d_out, 0, 0) + dot(low_ref[...], d_out, 0, 0)
    for d in range(N_SEQ):
        out_ref[d] = total[CAP * d : CAP * (d + 1)].astype(BF16)


def send_grad(d_out, high, low):
    return call(
        send_grad_kernel, [shape((N_SEQ, CAP, D), BF16)], [d_out, high, low], "send_grad", 4 * ROWS * D * 320
    )[0]


def middle_back_kernel(paired, me_ref, d_out_ref, *refs):
    me = me_ref[0]
    count = 4 if paired else 8
    blocks, refs = refs[:count], refs[count:]
    gathered, refs = refs[:4], refs[4:]
    (
        chosen_ref, gates_ref, residual_ref, normed_ref, gain_ref, w_ref,
        d_residual_ref, small_ref, grad_ref, d_mix_ref, rows_ref, d_rows_ref,
    ) = refs
    for d in range(N_SEQ):
        there = pl.ds(CAP * d, CAP)
        rows_ref[there] = blocks[d][0] if paired else blocks[d][...]
        d_rows_ref[there] = blocks[d][1] if paired else blocks[4 + d][...]
    d_out = d_out_ref[...]
    chosen = chosen_ref[...]
    gates = gates_ref[...]
    products = dot(d_out, rows_ref[...], 1, 1) * chosen.astype(F32)
    slot = lax.broadcasted_iota(jnp.int32, (ROWS, 320), 1)
    own = jnp.where(slot >= 160, jnp.where(slot >= 240, 3, 2), jnp.where(slot >= 80, 1, 0))
    own = lax.rem(own + me, N_SEQ)
    lane = lax.broadcasted_iota(jnp.int32, (ROWS, 128), 1)
    d_gates = jnp.zeros((ROWS, 128), F32)
    for e in range(N_SEQ):
        part = jnp.sum(jnp.where(own == e, products, 0.0), axis=1, keepdims=True)
        d_gates = jnp.where(lane == e, part, d_gates)
    d_logits = gates * (d_gates - jnp.sum(gates * d_gates, axis=1, keepdims=True))
    d_normed = dot(chosen, d_rows_ref[...], 1, 0)
    for e in range(N_SEQ):
        d_normed = d_normed + d_logits[:, e : e + 1] * gain_ref[e : e + 1, :]
    n, inverse = norm_parts(residual_ref[...])
    d_residual = d_out.astype(F32) + norm_back(n, inverse, gain_ref[5:6, :], d_normed)
    d_residual_ref[...] = d_residual
    d_branch = d_residual.astype(BF16)
    for d in range(N_SEQ):
        group = lax.rem(me - d + N_SEQ, N_SEQ)
        d_mix_ref[d] = dot(d_branch, w_ref[group], 1, 1).astype(BF16)
        grad_ref[group] = dot(gathered[d][...], d_branch, 0, 0).astype(BF16)
    high, low = two_parts(d_logits)
    small = dot(normed_ref[...], high, 0, 0) + dot(normed_ref[...], low, 0, 0)
    column = (lax.broadcasted_iota(jnp.int32, (ROWS, 128), 1) == 5).astype(BF16)
    high, low = two_parts(d_normed * n)
    small = small + dot(high, column, 0, 0) + dot(low, column, 0, 0)
    small_ref[...] = small[:, 0:64]


def middle_back(me, d_out, blocks, gathered, chosen, gates, residual, normed, gains, w_back, paired):
    return call(
        partial(middle_back_kernel, paired),
        [
            shape((ROWS, D), F32),
            shape((D, 64), F32),
            shape((N_SEQ, 192, D), BF16),
            shape((N_SEQ, ROWS, 192), BF16),
        ],
        [me, d_out, *blocks, *gathered, chosen, gates, residual, normed, gains, w_back],
        "middle_back",
        2 * ROWS * D * (2 * D + 640),
        scalars=1,
        scratch=[pltpu.VMEM((320, D), BF16)] * 2,
    )


def finish_kernel(d_residual_ref, x_ref, gain_ref, b0, b1, b2, b3, out_ref):
    d_normed = b0[...].astype(F32) + b1[...].astype(F32) + b2[...].astype(F32) + b3[...].astype(F32)
    n, inverse = norm_parts(x_ref[...].astype(F32))
    total = d_residual_ref[...] + norm_back(n, inverse, gain_ref[4:5, :], d_normed)
    out_ref[...] = total.astype(BF16)


def finish(d_residual, x, gains, blocks):
    return call(
        finish_kernel, [shape((ROWS, D), BF16)], [d_residual, x, gains, *blocks], "finish", 20 * ROWS * D
    )[0]


def attention_weights(w_qkv, w_proj, w_route, gain_attn, gain_ffn):
    core = lax.axis_index("section")
    mine = w_qkv.reshape(12, 3, N_SEQ, 192).transpose(2, 0, 1, 3).reshape(N_SEQ, 12, 576)
    small = jnp.concatenate(
        [w_route, gain_attn[:, None], gain_ffn[:, None], jnp.zeros((12, 122), BF16)], axis=1
    )
    whole = jnp.broadcast_to(w_proj, (N_SEQ, 12, D))
    mine = jnp.concatenate([whole, mine, jnp.broadcast_to(small, (N_SEQ, 12, 128))], axis=2)
    spread = jnp.broadcast_to(mine[:, None], (N_SEQ, N_SHARD, 12, WIDE))
    spread = spread.reshape(N_SEQ * N_SHARD, 12, WIDE)
    whole = lax.all_to_all(spread, ("seq", "shard"), 0, 0, tiled=True).reshape(D, WIDE)
    other = swap(whole)
    out = []
    for s in range(2):
        rows = jnp.where(core == s, whole, other)
        table = rows[:, 1344:1352].T.astype(F32)
        out.append((rows[:, 768:1344], rows[:, :768].reshape(N_SEQ, 192, D), rows[:, 1344:], table))
    return out


def expert_weights(w_in, w_out):
    core = lax.axis_index("section")
    first = w_in.reshape(48, N_SHARD, 4, 48).transpose(2, 0, 1, 3).reshape(4, 48, 768)
    second = w_out.reshape(4, 48, 768)
    quarters = jnp.stack([first, second], axis=1).reshape(2, 4, 48, 768)
    mine = pick(quarters, core)
    arrived = swap(pick(quarters, 1 - core))
    out = []
    for s in range(2):
        own = jnp.where(core == s, mine, arrived)
        if s == 1:
            own = tie(own, out[0][0])
        whole = lax.all_gather(own, "shard", axis=0, tiled=False)
        out.append((whole, swap(whole)))
    return out


def join_experts(own, other):
    return (own.astype(F32) + swap(other).astype(F32)).astype(BF16)


def scatter_beside(v):
    return lax.psum_scatter(v, "shard", scatter_dimension=0, tiled=True)[0]


def join_attention(mix, back):
    core = lax.axis_index("section")
    keep = jnp.where(core == 0, mix, back)
    give = jnp.where(core == 0, back, mix)
    return (keep.astype(F32) + swap(give).astype(F32)).astype(BF16)


def shards(images_in, out_grad, routes, w_qkv, w_proj, w_route, gain_attn, gain_ffn, w_in, w_out):
    core = lax.axis_index("section")
    me = lax.axis_index("seq").astype(jnp.int32).reshape(1)
    own_routes = routes[0, :, 0]
    mine = pick(own_routes, core)
    arrived = swap(pick(own_routes, 1 - core))
    route_of = (jnp.where(core == 0, mine, arrived), jnp.where(core == 0, arrived, mine))
    x0 = pick(images_in, core)[0]
    d_last = pick(out_grad, core)[0]
    attn = attention_weights(w_qkv[0], w_proj[0], w_route[0], gain_attn[0], gain_ffn[0])
    experts = expert_weights(w_in[0, 0], w_out[0, 0])

    saved = []
    x = x0
    layer_outs = []
    for s in range(2):
        w_mix, w_back, router, table = attn[s]
        x_all = gather_tokens(x)
        mixture, packed, logs = attend(x_all, w_mix, table)
        gathered = send_out(mixture)
        d_out = d_last if s == 1 else None
        residual, normed, gates, chosen, high, low, buffer = middle(
            me, x, gathered, w_back, router, table, route_of[s], d_out
        )
        blocks = send_out(buffer)
        kept = (x, x_all, packed, logs, gathered, residual, normed, gates, chosen, high, low, blocks)
        if s == 0:
            returned = send_back(expert_run(blocks, experts[s]))
            x = combine(residual, high, low, returned)
            layer_outs.append(x)
            saved.append((kept, returned))
        else:
            saved.append((kept, None))

    d_out = d_last
    in_grads = [None, None]
    expert_sums = [None, None]
    joined = [None, None]
    for s in (1, 0):
        w_mix, w_back, router, table = attn[s]
        kept, returned = saved[s]
        x, x_all, packed, logs, gathered, residual, normed, gates, chosen, high, low, blocks = kept
        if s == 1:
            sent, *states = expert_back(blocks, experts[s], True)
            arrived = send_back(sent)
            layer_outs.append(combine(residual, high, low, [v[0] for v in arrived]))
        else:
            d_blocks = send_out(send_grad(d_out, high, low))
            sent, *states = expert_back([*blocks, *d_blocks], experts[s], False)
            arrived = [*returned, *send_back(sent)]
        rows, d_result, act_own, act_other, dh_own, dh_other = states
        other = expert_grad(rows, d_result, act_other, dh_other)
        own = expert_grad(rows, d_result, act_own, dh_own)
        expert_sums[s] = scatter_beside(join_experts(own, other))
        d_residual, small, grad_back, d_mixture = middle_back(
            me, d_out, arrived, gathered, chosen, gates, residual, normed, table, w_back, s == 1
        )
        d_heads = send_back(d_mixture)
        d_normed, grad_mix = attend_back(x_all, w_mix, table, packed, logs, d_heads, small)
        d_parts = send_out(d_normed)
        joined[s] = join_attention(grad_mix, grad_back.reshape(D, D))
        d_out = finish(d_residual, x, table, d_parts)
        in_grads[s] = d_out

    pair = jnp.concatenate([joined[0], joined[1]], axis=1).reshape(N_SEQ * N_SHARD, 12, 2 * D)
    arrived = lax.all_to_all(pair, ("seq", "shard"), 0, 0, tiled=True)
    attn_sum = jnp.sum(arrived.reshape(N_SEQ, N_SHARD, 12, 2 * D).astype(F32), axis=1)
    attn_sums = [attn_sum[:, :, :D], attn_sum[:, :, D:]]

    def settle(pair):
        keep = jnp.where(core == 0, pair[0], pair[1])
        give = jnp.where(core == 0, pair[1], pair[0])
        return keep, swap(give)

    def in_order(keep, got):
        return jnp.where(core == 0, jnp.stack([keep, got]), jnp.stack([got, keep]))

    layer_out = in_order(*settle(layer_outs))
    in_grad = in_order(*settle(in_grads))
    expert_sum = in_order(*settle(expert_sums)).astype(F32)
    attn_sum = in_order(*settle(attn_sums))
    quarters = expert_sum.reshape(4, 2, 48, 768)
    grad_in = quarters[:, 0].reshape(4, 48, N_SHARD, 48).transpose(1, 2, 0, 3).reshape(48, FF)
    grad_out = quarters[:, 1].reshape(192, D)
    mix = attn_sum[0]
    back = jnp.sum(attn_sum[1], axis=0)
    grad_qkv = mix[:, :, :576].reshape(N_SEQ, 12, 3, 192).transpose(1, 2, 0, 3).reshape(12, 3 * D)
    small = jnp.sum(mix[:, :, 576:640], axis=0)
    return (
        layer_out[None, :, None],
        in_grad[None, :, None],
        grad_qkv[None],
        back[None],
        small[None, :, 0:4],
        small[None, :, 4],
        small[None, :, 5],
        grad_in[None],
        grad_out[None],
    )


def solution(mesh):
    def run(*args):
        outs = shards(*args)
        outs = list(outs)
        outs[7] = outs[7][:, None]
        outs[8] = outs[8][:, None]
        return tuple(outs)

    return jax.shard_map(
        run,
        mesh=mesh,
        in_specs=(
            P(None, "shard", "seq", None),
            P(None, "shard", "seq", None),
            P("section", None, "shard", "seq", None),
            P("section", ("seq", "shard"), None),
            P("section", ("seq", "shard"), None),
            P("section", ("seq", "shard"), None),
            P("section", ("seq", "shard")),
            P("section", ("seq", "shard")),
            P("section", "seq", "shard", None),
            P("section", "seq", "shard", None),
        ),
        out_specs=(
            P("section", None, "shard", "seq", None),
            P("section", None, "shard", "seq", None),
            P("section", ("seq", "shard"), None),
            P("section", ("seq", "shard"), None),
            P("section", ("seq", "shard"), None),
            P("section", ("seq", "shard")),
            P("section", ("seq", "shard")),
            P("section", "seq", "shard", None),
            P("section", "seq", "shard", None),
        ),
        check_vma=False,
    )
```

time: 589 us -> 563 us (0.956)
  matrix products: 147 us -> 0 us
  Pallas kernels: 0 us -> 115 us
  waiting for transfers between devices: 139 us -> 228 us
  other arithmetic: 77.4 us -> 34.5 us
  starting transfers between devices: 119 us -> 86.7 us
    dot_general x92 -> x0, matrix products: 147 us -> none  [the longest x80 91.4 us: dot(): lax.dot_general(a, b, (((ca,), (cb,)), ((), ())), preferred_element_type=...]
    pallas_call x0 -> x20, Pallas kernels: none -> 115 us  [the longest x13 62.4 us: call(): pl.pallas_call(body, out_shape=outs, in_specs=specs, out_specs=[vmem()] *...]
    all_gather x2, waiting for transfers between devices: 24.9 us -> 76.3 us  [expert_weights(): whole = lax.all_gather(own, 'shard', axis=0, tiled=False)]
    ppermute x45 -> x42, waiting for transfers between devices: 54.9 us -> 101 us  [turn(): return lax.ppermute(v, 'seq', [(i, (i + d) % N_SEQ) for i in range(N_SEQ)])]
    squeeze x0 -> x18, local copies, waits for them, and re-layouts: none -> 24.4 us  [the longest x7 11.7 us: send_out(): return [blocks[0]] + [turn(blocks[d], d) for d in (1, 2, 3)]]
    all_to_all x5 -> x2, starting transfers between devices: 37.9 us -> 15.4 us  [the longest x1 8.56 us: attention_weights(): lax.all_to_all(spread, ('seq', 'shard'), 0, 0, tiled=True).reshape(D, WIDE)]
    all_to_all x5 -> x2, waiting for transfers between devices: 57.3 us -> 43 us  [the longest x1 43 us: attention_weights(): lax.all_to_all(spread, ('seq', 'shard'), 0, 0, tiled=True).reshape(D, WIDE)]
    concatenate x4 -> x1, local copies, waits for them, and re-layouts: 14.1 us -> 0.09 us  [attention_weights(): jnp.concatenate([whole, mine, jnp.broadcast_to(small, (N_SEQ, 12, 128))],...]
  transfers between devices with their start and end apart: 67 -> 61, of which waited for: 28 -> 38; matrix products, arithmetic and copies ran while one was open for 42% -> 14% of each run, Pallas kernels for 0% -> 18%
where the time goes in v3:
time: 563 us; the launch traced here: 553 us
  waiting for transfers between devices  228 us (40%)
  Pallas kernels  115 us (20%)
  starting transfers between devices  86.7 us (15%)
  local copies, waits for them, and re-layouts  74 us (13%)
  other arithmetic  34.5 us (6%)
  between operations  14.8 us (3%)
    ppermute x42, waiting for transfers between devices, turn(): return lax.ppermute(v, 'seq', [(i, (i + d) % N_SEQ) for i in range(N_SEQ)])  101 us
    all_gather x2, waiting for transfers between devices, expert_weights(): whole = lax.all_gather(own, 'shard', axis=0, tiled=False)  76.3 us
    pallas_call x13, Pallas kernels, call(): pl.pallas_call(body, out_shape=outs, in_specs=specs, out_specs=[vmem()] *...  62.4 us
    pallas_call x7, Pallas kernels, grid_call(): pl.pallas_call(body, grid=(2,), out_shape=outs, in_specs=in_specs, out_sp...  52.1 us
    ppermute x42, starting transfers between devices, turn(): return lax.ppermute(v, 'seq', [(i, (i + d) % N_SEQ) for i in range(N_SEQ)])  48.2 us
    all_to_all x1, waiting for transfers between devices, attention_weights(): lax.all_to_all(spread, ('seq', 'shard'), 0, 0, tiled=True).reshape(D, WIDE)  43 us
    ppermute x13, starting transfers between devices, swap(): return lax.ppermute(v, 'section', [(0, 1), (1, 0)])  23 us
    convert_element_type x2, other arithmetic, join_experts(): return (own.astype(F32) + swap(other).astype(F32)).astype(BF16)  12 us
  transfers between devices with their start and end apart: 61, of which 38 were waited for; matrix products, arithmetic and copies ran while one was open for 14% of the time, Pallas kernels for 18%

profile of v3, /device:TPU:1, one launch (start us, length us, event | category | flops | bytes accessed | tf_op | source)
XLA Modules:
  0.0 552.7 jit_solution(7032433462867923918)
XLA Ops:
  13.8 56.4 %all-gather.5.cloned.1.call-done = bf16[64,48,768]{2,1,0:T(8,128)(2,1)} async-done(((bf16[4,48,768]{2,1,0:T(8,128)(2,1)}), bf16[64,48,768]{2,1,0:T(8,128)(2,1)}) %all-gather.5.cloned.1.call-update) | async-done | bytes 4718608 | tf_op jit(solution)/shard_map/all_gather | solution.py:556
  73.2 8.6 %all-to-all-start = ((bf16[64,12,1472]{2,1,0:T(8,128)(2,1)}), bf16[64,12,1472]{2,1,0:T(8,128)(2,1)}, u32[]{:S(2)}, u32[]{:S(2)}) async-start(bf16[64,12,1472]{2,1,0:T(8,128)(2,1)} %bitcast.188), calls=%async_computation | async-start | bytes 6291456 | tf_op jit(solution)/shard_map/all_to_all | solution.py:534
  82.8 43.0 %all-to-all-done = bf16[64,12,1472]{2,1,0:T(8,128)(2,1)} async-done(((bf16[64,12,1472]{2,1,0:T(8,128)(2,1)}), bf16[64,12,1472]{2,1,0:T(8,128)(2,1)}, u32[]{:S(2)}, u32[]{:S(2)}) %all-to-all-start) | async-done | bytes 2261024 | tf_op jit(solution)/shard_map/all_to_all | solution.py:534
  135.1 19.9 %all-gather.7.cloned.1.call-done = bf16[64,48,768]{2,1,0:T(8,128)(2,1)} async-done(((bf16[4,48,768]{2,1,0:T(8,128)(2,1)}), bf16[64,48,768]{2,1,0:T(8,128)(2,1)}) %all-gather.7.cloned.1.call-update) | async-done | bytes 4718608 | tf_op jit(solution)/shard_map/all_gather | solution.py:556
  179.6 5.6 %attention.2 = (bf16[4,144,192]{2,1,0:T(8,128)(2,1)}, bf16[576,576]{1,0:T(8,128)(2,1)}, f32[576,128]{1,0:T(8,128)}) custom-call(bf16[576,768]{1,0:T(8,128)(2,1)} %pad_maximum_fusion.1.x_ref, bf16[768,576]{1,0:T(8,128)(2,1)} %copy.108.w_ref, f32[8,768]{1,0:T(8,128)} %convert_bitcast_fusion.1.gain_ref.refs_16_), custom_call_target="tpu_custom_call" | custom-call | flops 764411904 | bytes 2973696 | tf_op jit(solution)/shard_map/attention/pallas_call | solution.py:108
  211.7 7.0 %expert.1 = bf16[4,80,768]{2,1,0:T(8,128)(2,1)} custom-call(bf16[80,768]{1,0:T(8,128)(2,1)} %get-tuple-element.171.r0.refs_0_, bf16[80,768]{1,0:T(8,128)(2,1)} %copy-done.44, bf16[80,768]{1,0:T(8,128)(2,1)} %copy-done.43, bf16[80,768]{1,0:T(8,128)(2,1)} %copy-done.42, bf16[16,4,48,768]{3,2,1,0:T(8,128)(2,1)} %bitcast.214, ...), custom_call_target="tpu_custom_call" | custom-call | flops 3019898880 | bytes 10420224 | tf_op jit(solution)/shard_map/expert/pallas_call | solution.py:312
  242.0 5.6 %attention.3 = (bf16[4,144,192]{2,1,0:T(8,128)(2,1)}, bf16[576,576]{1,0:T(8,128)(2,1)}, f32[576,128]{1,0:T(8,128)}) custom-call(bf16[576,768]{1,0:T(8,128)(2,1)} %pad_maximum_fusion.2.x_ref, bf16[768,576]{1,0:T(8,128)(2,1)} %copy.115.w_ref, f32[8,768]{1,0:T(8,128)} %convert_bitcast_fusion.gain_ref.refs_12_), custom_call_target="tpu_custom_call" | custom-call | flops 764411904 | bytes 2973696 | tf_op jit(solution)/shard_map/attention/pallas_call | solution.py:108
  276.4 11.6 %expert_back.2 = (bf16[4,2,80,768]{3,2,1,0:T(8,128)(2,1)}, bf16[320,768]{1,0:T(8,128)(2,1)}, bf16[320,768]{1,0:T(8,128)(2,1)}, bf16[320,1536]{1,0:T(8,128)(2,1)}...) custom-call(bf16[2,80,768]{2,1,0:T(8,128)(2,1)} %get-tuple-element.141.refs_0_, ...), custom_call_target="tpu_custom_call" | custom-call | flops 6039797760 | bytes 16318464 | tf_op jit(solution)/shard_map/expert_back/pallas_call | solution.py:312
  288.0 5.8 %expert_grad.7 = bf16[16,4,48,768]{3,2,1,0:T(8,128)(2,1)} custom-call(bf16[320,768]{1,0:T(8,128)(2,1)} %get-tuple-element.97.rows_ref, bf16[320,768]{1,0:T(8,128)(2,1)} %get-tuple-element.98.d_result_ref, bf16[320,1536]{1,0:T(8,128)(2,1)} %get-tuple-element.101.act_ref, bf16[320,1536]{1,0:T(8,128)(2,1)} %get-tuple-element.102.dh_ref), custom_call_target="tpu_custom_call" | custom-call | flops 1509949440 | bytes 7667712 | tf_op jit(solution)/shard_map/expert_grad/pallas_call | solution.py:312
  293.7 9.1 %collective-permute-start.53 = (bf16[16,4,48,768]{3,2,1,0:T(8,128)(2,1)}, bf16[16,4,48,768]{3,2,1,0:T(8,128)(2,1)S(1)}, u32[]{:S(2)}, u32[]{:S(2)}) collective-permute-start(bf16[16,4,48,768]{3,2,1,0:T(8,128)(2,1)} %expert_grad.7), channel_id=1, source_target_pairs={{0,64},{64,0},{1,65},{65,1},{2,66},{66,2},{3,67},{67,3},{4,68},{68... | collective-permute-start | bytes 14155784 | tf_op jit(solution)/shard_map/ppermute | solution.py:32
  302.8 5.8 %expert_grad.6 = bf16[16,4,48,768]{3,2,1,0:T(8,128)(2,1)} custom-call(bf16[320,768]{1,0:T(8,128)(2,1)} %get-tuple-element.97.rows_ref, bf16[320,768]{1,0:T(8,128)(2,1)} %get-tuple-element.98.d_result_ref, bf16[320,1536]{1,0:T(8,128)(2,1)} %get-tuple-element.99.act_ref, bf16[320,1536]{1,0:T(8,128)(2,1)} %get-tuple-element.100.dh_ref), custom_call_target="tpu_custom_call" | custom-call | flops 1509949440 | bytes 7667712 | tf_op jit(solution)/shard_map/expert_grad/pallas_call | solution.py:312
  310.6 5.9 %add_convert_fusion = bf16[16,4,48,768]{3,2,1,0:T(8,128)(2,1)} fusion(bf16[16,4,48,768]{3,2,1,0:T(8,128)(2,1)S(1)} %collective-permute-done.53, bf16[16,4,48,768]{3,2,1,0:T(8,128)(2,1)} %expert_grad.6), kind=kLoop, calls=%fused_computation | loop fusion | flops 9437184 | bytes 14155776 | tf_op jit(solution)/shard_map/convert_element_type | solution.py:562
  322.7 9.4 %collective-permute-done.28.refs_3_ = bf16[2,80,768]{2,1,0:T(8,128)(2,1)S(1)} collective-permute-done((bf16[2,80,768]{2,1,0:T(8,128)(2,1)S(1)}, bf16[2,80,768]{2,1,0:T(8,128)(2,1)S(1)}, u32[]{:S(2)}, u32[]{:S(2)}) %collective-permute-start.28) | collective-permute-done | bytes 245792 | tf_op jit(solution)/shard_map/ppermute | solution.py:36
  333.2 5.5 middle_back.2
  349.3 9.8 %attention_back.2 = (bf16[4,144,768]{2,1,0:T(8,128)(2,1)}, bf16[768,768]{1,0:T(8,128)(2,1)}) custom-call(bf16[576,768]{1,0:T(8,128)(2,1)} %pad_maximum_fusion.2.x_ref, bf16[768,576]{1,0:T(8,128)(2,1)} %copy.115.w_ref, f32[8,768]{1,0:T(8,128)} %convert_bitcast_fusion.gain_ref.refs_12_, bf16[576,576]{1,0:T(8,128)(2,1)} %get-tuple-element.72.packed_ref, ...), custom_call_target="tpu_custom_call" | custom-call | flops 1656225792 | bytes 5234688 | tf_op jit(solution)/shard_map/attention_back/pallas_call | solution.py:108
  370.0 6.0 %collective-permute-done.33.b1 = bf16[144,768]{1,0:T(8,128)(2,1)S(1)} collective-permute-done((bf16[144,768]{1,0:T(8,128)(2,1)S(1)}, bf16[144,768]{1,0:T(8,128)(2,1)S(1)}, u32[]{:S(2)}, u32[]{:S(2)}) %collective-permute-start.33) | collective-permute-done | bytes 221216 | tf_op jit(solution)/shard_map/ppermute | solution.py:36
  392.3 10.4 %expert_back.3 = (bf16[4,80,768]{2,1,0:T(8,128)(2,1)}, bf16[320,768]{1,0:T(8,128)(2,1)}, bf16[320,768]{1,0:T(8,128)(2,1)}, bf16[320,1536]{1,0:T(8,128)(2,1)}, bf...) custom-call(bf16[80,768]{1,0:T(8,128)(2,1)} %get-tuple-element.171.r0.refs_0_, ...), custom_call_target="tpu_custom_call" | custom-call | flops 6039797760 | bytes 15826944 | tf_op jit(solution)/shard_map/expert_back/pallas_call | solution.py:312
  402.7 5.8 %expert_grad.5 = bf16[16,4,48,768]{3,2,1,0:T(8,128)(2,1)} custom-call(bf16[320,768]{1,0:T(8,128)(2,1)} %get-tuple-element.91.rows_ref, bf16[320,768]{1,0:T(8,128)(2,1)} %get-tuple-element.92.d_result_ref, bf16[320,1536]{1,0:T(8,128)(2,1)} %get-tuple-element.95.act_ref, bf16[320,1536]{1,0:T(8,128)(2,1)} %get-tuple-element.96.dh_ref), custom_call_target="tpu_custom_call" | custom-call | flops 1509949440 | bytes 7667712 | tf_op jit(solution)/shard_map/expert_grad/pallas_call | solution.py:312
  410.3 5.8 %expert_grad.4 = bf16[16,4,48,768]{3,2,1,0:T(8,128)(2,1)} custom-call(bf16[320,768]{1,0:T(8,128)(2,1)} %get-tuple-element.91.rows_ref, bf16[320,768]{1,0:T(8,128)(2,1)} %get-tuple-element.92.d_result_ref, bf16[320,1536]{1,0:T(8,128)(2,1)} %get-tuple-element.93.act_ref, bf16[320,1536]{1,0:T(8,128)(2,1)} %get-tuple-element.94.dh_ref), custom_call_target="tpu_custom_call" | custom-call | flops 1509949440 | bytes 7667712 | tf_op jit(solution)/shard_map/expert_grad/pallas_call | solution.py:312
  418.0 6.1 %add_convert_fusion.1 = bf16[16,4,48,768]{3,2,1,0:T(8,128)(2,1)} fusion(bf16[16,4,48,768]{3,2,1,0:T(8,128)(2,1)S(1)} %collective-permute-done.52, bf16[16,4,48,768]{3,2,1,0:T(8,128)(2,1)} %expert_grad.4), kind=kLoop, calls=%fused_computation.1 | loop fusion | flops 9437184 | bytes 14155776 | tf_op jit(solution)/shard_map/convert_element_type | solution.py:562
  451.3 10.1 %attention_back.3 = (bf16[4,144,768]{2,1,0:T(8,128)(2,1)}, bf16[768,768]{1,0:T(8,128)(2,1)}) custom-call(bf16[576,768]{1,0:T(8,128)(2,1)} %pad_maximum_fusion.1.x_ref, bf16[768,576]{1,0:T(8,128)(2,1)} %copy.108.w_ref, f32[8,768]{1,0:T(8,128)} %convert_bitcast_fusion.1.gain_ref.refs_16_, bf16[576,576]{1,0:T(8,128)(2,1)} %get-tuple-element.82.packed_ref, ...), custom_call_target="tpu_custom_call" | custom-call | flops 1656225792 | bytes 5234688 | tf_op jit(solution)/shard_map/attention_back/pallas_call | solution.py:108
  468.8 6.8 %all-to-all-start.1 = ((bf16[64,12,1536]{2,1,0:T(8,128)(2,1)}), bf16[64,12,1536]{2,1,0:T(8,128)(2,1)S(1)}, u32[]{:S(2)}, u32[]{:S(2)}) async-start(bf16[64,12,1536]{2,1,0:T(8,128)(2,1)} %reshape.199), calls=%async_computation.1 | async-start | bytes 6291456 | tf_op jit(solution)/shard_map/all_to_all | solution.py:641
  491.1 24.9 %collective-permute-done.47.b3 = bf16[144,768]{1,0:T(8,128)(2,1)S(1)} collective-permute-done((bf16[144,768]{1,0:T(8,128)(2,1)S(1)}, bf16[144,768]{1,0:T(8,128)(2,1)S(1)}, u32[]{:S(2)}, u32[]{:S(2)}) %collective-permute-start.47) | collective-permute-done | bytes 221216 | tf_op jit(solution)/shard_map/ppermute | solution.py:36
  516.0 5.9 %collective-permute-done.45.b1 = bf16[144,768]{1,0:T(8,128)(2,1)S(1)} collective-permute-done((bf16[144,768]{1,0:T(8,128)(2,1)S(1)}, bf16[144,768]{1,0:T(8,128)(2,1)S(1)}, u32[]{:S(2)}, u32[]{:S(2)}) %collective-permute-start.45) | collective-permute-done | bytes 221216 | tf_op jit(solution)/shard_map/ppermute | solution.py:36
  (322 shorter events, 247.3 us)
Async XLA Ops:
  7.2 62.9 %all-gather.5.cloned.1.call-start = ((), (), s32[]{:S(2)}) async-start(), calls=%async_computation.4 | async-start | bytes 5013504 | tf_op jit(solution)/shard_map/all_gather | solution.py:556
  13.7 141.3 %all-gather.7.cloned.1.call-start = ((), (), s32[]{:S(2)}) async-start(), calls=%async_computation.5 | async-start | bytes 5013504 | tf_op jit(solution)/shard_map/all_gather | solution.py:556
  73.2 52.7 %all-to-all-start = ((bf16[64,12,1472]{2,1,0:T(8,128)(2,1)}), bf16[64,12,1472]{2,1,0:T(8,128)(2,1)}, u32[]{:S(2)}, u32[]{:S(2)}) async-start(bf16[64,12,1472]{2,1,0:T(8,128)(2,1)} %bitcast.188), calls=%async_computation | async-start | bytes 6291456 | tf_op jit(solution)/shard_map/all_to_all | solution.py:534
  81.7 451.1 %reduce-scatter.9.cloned.1.call-start = ((), (), s32[]{:S(2)}) async-start(), calls=%async_computation.7 | async-start | bytes 5013504
  81.8 129.3 %collective-permute-start.12 = (bf16[16,4,48,768]{3,2,1,0:T(8,128)(2,1)}, bf16[16,4,48,768]{3,2,1,0:T(8,128)(2,1)}, u32[]{:S(2)}, u32[]{:S(2)}) collective-permute-start(bf16[16,4,48,768]{3,2,1,0:T(8,128)(2,1)} %bitcast.213), channel_id=1, source_target_pairs={{0,64},{64,0},{1,65},{65,1},{2,66},{66,2},{3,67},{67,3},{4,68},{68... | collective-permute-start | bytes 14155784 | tf_op jit(solution)/shard_map/ppermute | solution.py:32
  132.4 39.2 %collective-permute-start.3 = (bf16[768,1472]{0,1:T(8,128)(2,1)}, bf16[768,1472]{0,1:T(8,128)(2,1)}, u32[]{:S(2)}, u32[]{:S(2)}) collective-permute-start(bf16[768,1472]{0,1:T(8,128)(2,1)} %copy.107), channel_id=1, source_target_pairs={{0,64},{64,0},{1,65},{65,1},{2,66},{66,2},{3,67},{67,3},{4,68},{68... | collective-permute-start | bytes 6782984 | tf_op jit(solution)/shard_map/ppermute | solution.py:32
  155.0 120.7 %collective-permute-start.25 = (bf16[16,4,48,768]{3,2,1,0:T(8,128)(2,1)}, bf16[16,4,48,768]{3,2,1,0:T(8,128)(2,1)}, u32[]{:S(2)}, u32[]{:S(2)}) collective-permute-start(bf16[16,4,48,768]{3,2,1,0:T(8,128)(2,1)} %bitcast.216), channel_id=1, source_target_pairs={{0,64},{64,0},{1,65},{65,1},{2,66},{66,2},{3,67},{67,3},{4,68},{68... | collective-permute-start | bytes 14155784 | tf_op jit(solution)/shard_map/ppermute | solution.py:32
  157.0 12.8 %collective-permute-start.1 = (bf16[144,768]{1,0:T(8,128)(2,1)S(1)}, bf16[144,768]{1,0:T(8,128)(2,1)S(1)}, u32[]{:S(2)}, u32[]{:S(2)}) collective-permute-start(bf16[144,768]{1,0:T(8,128)(2,1)S(1)} %dynamic-slice_bitcast_fusion.2.x_ref), channel_id=1, source_target_pairs={{0,32},{16,48},{32,0},{48,16},{1,33},{17,49},{33,1},{49,17},{2,34}... | collective-permute-start | bytes 663560 | tf_op jit(solution)/shard_map/ppermute | solution.py:36
  169.8 18.9 %collective-permute-start.7 = (s32[144,2]{1,0:T(8,128)S(1)}, s32[144,2]{1,0:T(8,128)S(1)}, u32[]{:S(2)}, u32[]{:S(2)}) collective-permute-start(s32[144,2]{1,0:T(8,128)S(1)} %bitcast.205), channel_id=1, source_target_pairs={{0,64},{64,0},{1,65},{65,1},{2,66},{66,2},{3,67},{67,3},{4,68},{68... | collective-permute-start | bytes 3464 | tf_op jit(solution)/shard_map/ppermute | solution.py:32
  186.9 9.3 %collective-permute-start.6 = (bf16[144,192]{1,0:T(8,128)(2,1)}, bf16[144,192]{1,0:T(8,128)(2,1)S(1)}, u32[]{:S(2)}, u32[]{:S(2)}) collective-permute-start(bf16[144,192]{1,0:T(8,128)(2,1)} %get-tuple-element.192), channel_id=1, source_target_pairs={{0,48},{16,0},{32,16},{48,32},{1,49},{17,1},{33,17},{49,33},{2,50}... | collective-permute-start | bytes 165896 | tf_op jit(solution)/shard_map/ppermute | solution.py:36
  231.7 8.4 %collective-permute-start.17 = (bf16[144,768]{1,0:T(8,128)(2,1)}, bf16[144,768]{1,0:T(8,128)(2,1)S(1)}, u32[]{:S(2)}, u32[]{:S(2)}) collective-permute-start(bf16[144,768]{1,0:T(8,128)(2,1)} %combine.2.x_ref), channel_id=1, source_target_pairs={{0,32},{16,48},{32,0},{48,16},{1,33},{17,49},{33,1},{49,17},{2,34}... | collective-permute-start | bytes 663560 | tf_op jit(solution)/shard_map/ppermute | solution.py:36
  293.7 16.8 %collective-permute-start.53 = (bf16[16,4,48,768]{3,2,1,0:T(8,128)(2,1)}, bf16[16,4,48,768]{3,2,1,0:T(8,128)(2,1)S(1)}, u32[]{:S(2)}, u32[]{:S(2)}) collective-permute-start(bf16[16,4,48,768]{3,2,1,0:T(8,128)(2,1)} %expert_grad.7), channel_id=1, source_target_pairs={{0,64},{64,0},{1,65},{65,1},{2,66},{66,2},{3,67},{67,3},{4,68},{68... | collective-permute-start | bytes 14155784 | tf_op jit(solution)/shard_map/ppermute | solution.py:32
  316.6 216.3 %reduce-scatter.7.cloned.1.call-start = ((), (), s32[]{:S(2)}) async-start(), calls=%async_computation.6 | async-start | bytes 5013504
  318.5 13.6 %collective-permute-start.28 = (bf16[2,80,768]{2,1,0:T(8,128)(2,1)S(1)}, bf16[2,80,768]{2,1,0:T(8,128)(2,1)S(1)}, u32[]{:S(2)}, u32[]{:S(2)}) collective-permute-start(bf16[2,80,768]{2,1,0:T(8,128)(2,1)S(1)} %get-tuple-element.135), channel_id=1, source_target_pairs={{0,16},{16,32},{32,48},{48,0},{1,17},{17,33},{33,49},{49,1},{2,18}... | collective-permute-start | bytes 737288 | tf_op jit(solution)/shard_map/ppermute | solution.py:36
  319.0 13.2 %collective-permute-start.27 = (bf16[2,80,768]{2,1,0:T(8,128)(2,1)S(1)}, bf16[2,80,768]{2,1,0:T(8,128)(2,1)S(1)}, u32[]{:S(2)}, u32[]{:S(2)}) collective-permute-start(bf16[2,80,768]{2,1,0:T(8,128)(2,1)S(1)} %get-tuple-element.136), channel_id=1, source_target_pairs={{0,32},{16,48},{32,0},{48,16},{1,33},{17,49},{33,1},{49,17},{2,34}... | collective-permute-start | bytes 737288 | tf_op jit(solution)/shard_map/ppermute | solution.py:36
  320.2 12.3 %collective-permute-start.26 = (bf16[2,80,768]{2,1,0:T(8,128)(2,1)S(1)}, bf16[2,80,768]{2,1,0:T(8,128)(2,1)S(1)}, u32[]{:S(2)}, u32[]{:S(2)}) collective-permute-start(bf16[2,80,768]{2,1,0:T(8,128)(2,1)S(1)} %get-tuple-element.137), channel_id=1, source_target_pairs={{0,48},{16,0},{32,16},{48,32},{1,49},{17,1},{33,17},{49,33},{2,50}... | collective-permute-start | bytes 737288 | tf_op jit(solution)/shard_map/ppermute | solution.py:36
  363.1 12.9 %collective-permute-start.33 = (bf16[144,768]{1,0:T(8,128)(2,1)S(1)}, bf16[144,768]{1,0:T(8,128)(2,1)S(1)}, u32[]{:S(2)}, u32[]{:S(2)}) collective-permute-start(bf16[144,768]{1,0:T(8,128)(2,1)S(1)} %get-tuple-element.148), channel_id=1, source_target_pairs={{0,16},{16,32},{32,48},{48,0},{1,17},{17,33},{33,49},{49,1},{2,18}... | collective-permute-start | bytes 663560 | tf_op jit(solution)/shard_map/ppermute | solution.py:36
  408.5 9.5 %collective-permute-start.52 = (bf16[16,4,48,768]{3,2,1,0:T(8,128)(2,1)}, bf16[16,4,48,768]{3,2,1,0:T(8,128)(2,1)S(1)}, u32[]{:S(2)}, u32[]{:S(2)}) collective-permute-start(bf16[16,4,48,768]{3,2,1,0:T(8,128)(2,1)} %expert_grad.5), channel_id=1, source_target_pairs={{0,64},{64,0},{1,65},{65,1},{2,66},{66,2},{3,67},{67,3},{4,68},{68... | collective-permute-start | bytes 14155784 | tf_op jit(solution)/shard_map/ppermute | solution.py:32
  446.5 16.4 %collective-permute-start.50 = (bf16[768,768]{1,0:T(8,128)(2,1)S(1)}, bf16[768,768]{1,0:T(8,128)(2,1)S(1)}, u32[]{:S(2)}, u32[]{:S(2)}) collective-permute-start(bf16[768,768]{1,0:T(8,128)(2,1)S(1)} %bitcast_select_fusion), channel_id=1, source_target_pairs={{0,64},{64,0},{1,65},{65,1},{2,66},{66,2},{3,67},{67,3},{4,68},{68... | collective-permute-start | bytes 3538952 | tf_op jit(solution)/shard_map/ppermute | solution.py:32
  468.8 59.5 %all-to-all-start.1 = ((bf16[64,12,1536]{2,1,0:T(8,128)(2,1)}), bf16[64,12,1536]{2,1,0:T(8,128)(2,1)S(1)}, u32[]{:S(2)}, u32[]{:S(2)}) async-start(bf16[64,12,1536]{2,1,0:T(8,128)(2,1)} %reshape.199), calls=%async_computation.1 | async-start | bytes 6291456 | tf_op jit(solution)/shard_map/all_to_all | solution.py:641
  484.2 31.8 %collective-permute-start.47 = (bf16[144,768]{1,0:T(8,128)(2,1)S(1)}, bf16[144,768]{1,0:T(8,128)(2,1)S(1)}, u32[]{:S(2)}, u32[]{:S(2)}) collective-permute-start(bf16[144,768]{1,0:T(8,128)(2,1)S(1)} %get-tuple-element.142), channel_id=1, source_target_pairs={{0,48},{16,0},{32,16},{48,32},{1,49},{17,1},{33,17},{49,33},{2,50}... | collective-permute-start | bytes 663560 | tf_op jit(solution)/shard_map/ppermute | solution.py:36
  486.6 29.4 %collective-permute-start.46 = (bf16[144,768]{1,0:T(8,128)(2,1)S(1)}, bf16[144,768]{1,0:T(8,128)(2,1)S(1)}, u32[]{:S(2)}, u32[]{:S(2)}) collective-permute-start(bf16[144,768]{1,0:T(8,128)(2,1)S(1)} %get-tuple-element.143), channel_id=1, source_target_pairs={{0,32},{16,48},{32,0},{48,16},{1,33},{17,49},{33,1},{49,17},{2,34}... | collective-permute-start | bytes 663560 | tf_op jit(solution)/shard_map/ppermute | solution.py:36
  487.0 34.9 %collective-permute-start.45 = (bf16[144,768]{1,0:T(8,128)(2,1)S(1)}, bf16[144,768]{1,0:T(8,128)(2,1)S(1)}, u32[]{:S(2)}, u32[]{:S(2)}) collective-permute-start(bf16[144,768]{1,0:T(8,128)(2,1)S(1)} %get-tuple-element.144), channel_id=1, source_target_pairs={{0,16},{16,32},{32,48},{48,0},{1,17},{17,33},{33,49},{49,1},{2,18}... | collective-permute-start | bytes 663560 | tf_op jit(solution)/shard_map/ppermute | solution.py:36
  489.3 39.7 %collective-permute-start.29 = (bf16[144,768]{1,0:T(8,128)(2,1)}, bf16[144,768]{1,0:T(8,128)(2,1)}, u32[]{:S(2)}, u32[]{:S(2)}) collective-permute-start(bf16[144,768]{1,0:T(8,128)(2,1)} %get-tuple-element.175), channel_id=1, source_target_pairs={{0,64},{64,0},{1,65},{65,1},{2,66},{66,2},{3,67},{67,3},{4,68},{68... | collective-permute-start | bytes 663560 | tf_op jit(solution)/shard_map/ppermute | solution.py:32
  (91 other events, 944.3 us)
Sparse Core Ops, SparseCore 0:
  13.8 56.2 all-gather.4
  72.8 82.1 all-gather.6
  316.7 75.2 reduce-scatter.8
  424.3 99.3 reduce-scatter.6

commit v4 on v3

--- a/solution.py
+++ b/solution.py
@@ -50,6 +50,28 @@
     return i // 4 if axis == "z" else lax.rem(i, 4)
 
 
+def hop(v, axis, d):
+    route = []
+    for z in range(4):
+        for x in range(4):
+            to = ((z + d) % 4) * 4 + x if axis == "z" else z * 4 + (x + d) % 4
+            route.append((z * 4 + x, to))
+    return lax.ppermute(v, "shard", route)
+
+
+def from_ring(v, axis):
+    return [v] + [hop(v, axis, -d) for d in (1, 2, 3)]
+
+
+def along_ring(blocks, axis):
+    return [blocks[0]] + [hop(blocks[d], axis, d) for d in (1, 2, 3)]
+
+
+def where_shard():
+    i = lax.axis_index("shard").astype(jnp.int32)
+    return jnp.stack([i // 4, lax.rem(i, 4)])
+
+
 def pick(v, i):
     return lax.dynamic_index_in_dim(v, i, 0, keepdims=False)
 
@@ -117,7 +139,9 @@
     )(*ins)
 
 
-def attend_kernel(x_ref, w_ref, gain_ref, mix_ref, packed_ref, log_ref):
+def attend_kernel(x0, x1, x2, x3, w_ref, gain_ref, m0, m1, m2, m3, x_ref, packed_ref, log_ref):
+    for d, ref in enumerate((x0, x1, x2, x3)):
+        x_ref[ROWS * d : ROWS * (d + 1)] = ref[...]
     n, _ = norm_parts(x_ref[...].astype(F32))
     normed = (n * gain_ref[4:5, :]).astype(BF16)
     packed_ref[...] = dot(normed, w_ref[...], 1, 0).astype(BF16)
@@ -136,23 +160,25 @@
         logs = jnp.where(lane == h, top + jnp.log(total), logs)
     log_ref[...] = logs
     mixture = jnp.concatenate(outs, axis=1)
-    for d in range(N_SEQ):
-        mix_ref[d] = mixture[ROWS * d : ROWS * (d + 1)]
-
-
-def attend(x_all, w_mix, gains):
-    return call(
+    for d, ref in enumerate((m0, m1, m2, m3)):
+        ref[...] = mixture[ROWS * d : ROWS * (d + 1)]
+
+
+def attend(x_blocks, w_mix, gains):
+    outs = call(
         attend_kernel,
-        [shape((N_SEQ, ROWS, 192), BF16), shape((SEQ, 576), BF16), shape((SEQ, 128), F32)],
-        [x_all, w_mix, gains],
+        [shape((ROWS, 192), BF16)] * 4
+        + [shape((SEQ, D), BF16), shape((SEQ, 576), BF16), shape((SEQ, 128), F32)],
+        [*x_blocks, w_mix, gains],
         "attention",
         2 * SEQ * D * 576 + 3 * 4 * SEQ * SEQ * 64,
     )
+    return outs[:4], *outs[4:]
 
 
 def attend_back_kernel(
     x_ref, w_ref, gain_ref, packed_ref, log_ref, d0, d1, d2, d3, small_ref,
-    d_normed_ref, grad_ref, d_packed_ref, d_mix_ref,
+    n0, n1, n2, n3, grad_ref, d_packed_ref, d_mix_ref,
 ):
     for d, ref in enumerate((d0, d1, d2, d3)):
         d_mix_ref[ROWS * d : ROWS * (d + 1)] = ref[...]
@@ -175,25 +201,151 @@
     normed = (n * gain_ref[4:5, :]).astype(BF16)
     d_packed = d_packed_ref[...]
     d_normed = dot(d_packed, w_ref[...], 1, 1)
-    for d in range(N_SEQ):
-        d_normed_ref[d] = d_normed[ROWS * d : ROWS * (d + 1)].astype(BF16)
+    for d, ref in enumerate((n0, n1, n2, n3)):
+        ref[...] = d_normed[ROWS * d : ROWS * (d + 1)].astype(BF16)
     column = (lax.broadcasted_iota(jnp.int32, (SEQ, 64), 1) == 4).astype(BF16)
     high, low = two_parts(d_normed * n)
     small = small_ref[...] + dot(high, column, 0, 0) + dot(low, column, 0, 0)
     grad = dot(normed, d_packed, 0, 0)
     grad = jnp.concatenate([grad, small, jnp.zeros((D, 128), F32)], axis=1)
-    grad_ref[...] = grad.astype(BF16)
+    grad_ref[...] = by_shard(grad.astype(BF16))
 
 
 def attend_back(x_all, w_mix, gains, packed, logs, d_heads, small):
-    return call(
+    outs = call(
         attend_back_kernel,
-        [shape((N_SEQ, ROWS, D), BF16), shape((D, D), BF16)],
+        [shape((ROWS, D), BF16)] * 4 + [shape((D, D), BF16)],
         [x_all, w_mix, gains, packed, logs, *d_heads, small],
         "attention_back",
         4 * SEQ * D * 576 + 3 * 10 * SEQ * SEQ * 64,
         scratch=[pltpu.VMEM((SEQ, 576), BF16), pltpu.VMEM((SEQ, 192), BF16)],
     )
+    return outs[:4], outs[4]
+
+
+def order_rows(first, second):
+    i = lax.broadcasted_iota(jnp.int32, (D, 1), 0)
+    outer = lax.div(i, 12 * first)
+    left = i - 12 * first * outer
+    inner = lax.div(left, 12)
+    source = inner * (12 * second) + outer * 12 + left - 12 * inner
+    return (lax.broadcasted_iota(jnp.int32, (D, D), 1) == source).astype(BF16)
+
+
+def by_shard(v):
+    return dot(order_rows(N_SEQ, N_SHARD), v, 1, 0).astype(BF16)
+
+
+def unpack_kernel(where_ref, b0, b1, b2, b3, rows_ref, back_ref, all_ref):
+    z, x = where_ref[0], where_ref[1]
+    for dz, ref in enumerate((b0, b1, b2, b3)):
+        for dx in range(4):
+            all_ref[lax.rem(z + dz, 4) * 4 + lax.rem(x + dx, 4)] = ref[dx]
+    order = order_rows(N_SHARD, N_SEQ)
+    whole = all_ref[...].reshape(D, 832)
+    ordered = dot(order, whole, 1, 0).astype(BF16)
+    rows_ref[...] = ordered[:, :640]
+    for chunk in range(N_SEQ):
+        back_ref[:, 192 * chunk : 192 * (chunk + 1)] = ordered[192 * chunk : 192 * (chunk + 1), 640:]
+
+
+def unpack(where, blocks):
+    return call(
+        unpack_kernel,
+        [shape((D, 640), BF16), shape((192, D), BF16)],
+        [where, *blocks],
+        "unpack",
+        2 * D * D * 832,
+        scalars=1,
+        scratch=[pltpu.VMEM((N_SHARD, 48, 832), BF16)],
+    )
+
+
+def order_kernel(where_ref, a0, a1, a2, a3, b0, b1, b2, b3, out_ref):
+    z, x = where_ref[0], where_ref[1]
+    firsts, seconds = (a0, a1, a2, a3), (b0, b1, b2, b3)
+    for dz in range(4):
+        for dx in range(4):
+            place = lax.rem(z + dz, 4) * 4 + lax.rem(x + dx, 4)
+            out_ref[place, 0:2] = firsts[dz][dx]
+            out_ref[place, 2:4] = seconds[dx][dz]
+
+
+def order(where, firsts, seconds):
+    return call(
+        order_kernel,
+        [shape((N_SHARD, 4, 48, D), BF16)],
+        [where, *firsts, *seconds],
+        "order",
+        0,
+        scalars=1,
+    )[0]
+
+
+def arrange_kernel(cut, where_ref, *refs):
+    z, x = where_ref[0], where_ref[1]
+    if cut:
+        ka, ga, *outs = refs
+        firsts, seconds = [(v, slice(0, 2)) for v in (ka, ga)], [(v, slice(2, 4)) for v in (ka, ga)]
+    else:
+        ka, ga, kb, gb, *outs = refs
+        firsts, seconds = [(v, slice(None)) for v in (ka, ga)], [(v, slice(None)) for v in (kb, gb)]
+    for d in range(4):
+        for o in range(4):
+            there = o * 4 + lax.rem(x + d, 4)
+            (keep, part), (got, _) = firsts
+            outs[d][o] = (keep[there, part].astype(F32) + got[there, part].astype(F32)).astype(BF16)
+            there = lax.rem(z + d, 4) * 4 + o
+            (keep, part), (got, _) = seconds
+            outs[4 + d][o] = (keep[there, part].astype(F32) + got[there, part].astype(F32)).astype(BF16)
+
+
+def arrange(where, pairs):
+    cut = len(pairs) == 2
+    dims = (4, 2, 48, D) if cut else (4, 48, D)
+    outs = call(
+        partial(arrange_kernel, cut), [shape(dims, BF16)] * 8, [where, *pairs], "arrange", 0, scalars=1
+    )
+    return outs[:4], outs[4:]
+
+
+def add_up_kernel(where_ref, *refs):
+    z, x = where_ref[0], where_ref[1]
+    for half, here in ((0, z), (1, x)):
+        blocks, outs = refs[4 * half : 4 * half + 4], refs[8 + 4 * half : 12 + 4 * half]
+        for d in range(4):
+            there = lax.rem(here + d, 4)
+            total = blocks[0][there].astype(F32)
+            for other in blocks[1:]:
+                total = total + other[there].astype(F32)
+            outs[d][...] = total.astype(BF16)
+
+
+def add_up(where, firsts, seconds):
+    dims = firsts[0].shape[1:]
+    outs = call(
+        add_up_kernel, [shape(dims, BF16)] * 8, [where, *firsts, *seconds], "add_up", 0, scalars=1
+    )
+    return outs[:4], outs[4:]
+
+
+def last_kernel(*refs):
+    for half in range(2):
+        total = refs[4 * half][...].astype(F32)
+        for d in (1, 2, 3):
+            total = total + refs[4 * half + d][...].astype(F32)
+        refs[8][half] = total.astype(BF16)
+
+
+def last(firsts, seconds):
+    dims = firsts[0].shape
+    return call(last_kernel, [shape((2,) + dims, BF16)], [*firsts, *seconds], "last", 0)[0]
+
+
+def scatter_pair(where, *pairs):
+    firsts, seconds = arrange(where, pairs)
+    firsts, seconds = add_up(where, along_ring(firsts, "x"), along_ring(seconds, "z"))
+    return last(along_ring(firsts, "z"), along_ring(seconds, "x"))
 
 
 def middle_kernel(
@@ -202,10 +354,10 @@
     me = me_ref[0]
     if extra:
         d_out_ref, *refs = refs
-    residual_ref, normed_ref, gates_ref, chosen_ref, high_ref, low_ref, buffer_ref = refs[:7]
+    residual_ref, normed_ref, gates_ref, chosen_ref, high_ref, low_ref, *sent = refs
     residual = x_ref[...].astype(F32)
     for d, ref in enumerate((g0, g1, g2, g3)):
-        residual = residual + dot(ref[...], w_ref[lax.rem(me - d + N_SEQ, N_SEQ)], 1, 0)
+        residual = residual + dot(ref[...], w_ref[d], 1, 0)
     residual_ref[...] = residual
     n, _ = norm_parts(residual)
     normed = (n * gain_ref[5:6, :]).astype(BF16)
@@ -241,19 +393,19 @@
     buffer = dot(chosen, normed, 0, 0).astype(BF16)
     if not extra:
         for d in range(N_SEQ):
-            buffer_ref[d] = buffer[CAP * d : CAP * (d + 1)]
+            sent[d][...] = buffer[CAP * d : CAP * (d + 1)]
     else:
         d_out = d_out_ref[...]
         d_buffer = (dot(high, d_out, 0, 0) + dot(low, d_out, 0, 0)).astype(BF16)
         for d in range(N_SEQ):
-            buffer_ref[d, 0] = buffer[CAP * d : CAP * (d + 1)]
-            buffer_ref[d, 1] = d_buffer[CAP * d : CAP * (d + 1)]
+            sent[d][0] = buffer[CAP * d : CAP * (d + 1)]
+            sent[d][1] = d_buffer[CAP * d : CAP * (d + 1)]
 
 
 def middle(me, x, gathered, w_back, router, gains, route_ids, d_out):
     extra = d_out is not None
-    sent = (N_SEQ, 2, CAP, D) if extra else (N_SEQ, CAP, D)
-    return call(
+    sent = (2, CAP, D) if extra else (CAP, D)
+    outs = call(
         partial(middle_kernel, extra),
         [
             shape((ROWS, D), F32),
@@ -262,13 +414,14 @@
             shape((ROWS, 320), BF16),
             shape((ROWS, 320), BF16),
             shape((ROWS, 320), BF16),
-            shape(sent, BF16),
-        ],
+        ]
+        + [shape(sent, BF16)] * 4,
         [me, x, *gathered, w_back, router, gains, route_ids] + ([d_out] if extra else []),
         "middle",
         2 * ROWS * D * (D + 320),
         scalars=1,
     )
+    return *outs[:6], outs[6:]
 
 
 def gelu_of(hidden):
@@ -280,7 +433,7 @@
     return ref[:, i].reshape(768, D)
 
 
-def expert_kernel(r0, r1, r2, r3, own_ref, other_ref, out_ref, rows_ref, total):
+def expert_kernel(r0, r1, r2, r3, own_ref, other_ref, o0, o1, o2, o3, rows_ref, total):
     @pl.when(pl.program_id(0) == 0)
     def _():
         for d, ref in enumerate((r0, r1, r2, r3)):
@@ -295,8 +448,8 @@
 
     @pl.when(pl.program_id(0) == 1)
     def _():
-        for d in range(N_SEQ):
-            out_ref[d] = total[CAP * d : CAP * (d + 1)].astype(BF16)
+        for d, ref in enumerate((o0, o1, o2, o3)):
+            ref[...] = total[CAP * d : CAP * (d + 1)].astype(BF16)
 
 
 def whole_block(dims):
@@ -327,19 +480,20 @@
 def expert_run(blocks, packs):
     return grid_call(
         expert_kernel,
-        [shape((N_SEQ, CAP, D), BF16)],
-        [whole_block((N_SEQ, CAP, D))],
+        [shape((CAP, D), BF16)] * 4,
+        [whole_block((CAP, D))] * 4,
         [*blocks, *packs],
         [whole_block((CAP, D))] * 4 + [pack_block()] * 2,
         "expert",
         4 * 320 * D * FF,
         [pltpu.VMEM((320, D), BF16), pltpu.VMEM((320, D), F32)],
-    )[0]
+    )
 
 
 def expert_back_kernel(forward, *refs):
     ins, (own_ref, other_ref), refs = refs[: 4 if forward else 8], refs[4 if forward else 8 :][:2], refs[6 if forward else 10 :]
-    out_ref, rows_out, d_result_out, act_own, act_other, dh_own, dh_other, d_total, total = refs
+    sent, refs = refs[:4], refs[4:]
+    rows_out, d_result_out, act_own, act_other, dh_own, dh_other, d_total, total = refs
     step = pl.program_id(0)
 
     @pl.when(step == 0)
@@ -371,26 +525,27 @@
         for d in range(N_SEQ):
             there = pl.ds(CAP * d, CAP)
             if forward:
-                out_ref[d, 0] = total[there].astype(BF16)
-                out_ref[d, 1] = d_total[there].astype(BF16)
+                sent[d][0] = total[there].astype(BF16)
+                sent[d][1] = d_total[there].astype(BF16)
             else:
-                out_ref[d] = d_total[there].astype(BF16)
+                sent[d][...] = d_total[there].astype(BF16)
 
 
 def expert_back(blocks, packs, forward):
-    sent = (N_SEQ, 2, CAP, D) if forward else (N_SEQ, CAP, D)
     half = pl.BlockSpec((320, 768), lambda i: (0, i))
     block = whole_block((2, CAP, D)) if forward else whole_block((CAP, D))
-    return grid_call(
+    sent = (2, CAP, D) if forward else (CAP, D)
+    outs = grid_call(
         partial(expert_back_kernel, forward),
-        [shape(sent, BF16)] + [shape((320, D), BF16)] * 2 + [shape((320, 1536), BF16)] * 4,
-        [whole_block(sent)] + [whole_block((320, D))] * 2 + [half] * 4,
+        [shape(sent, BF16)] * 4 + [shape((320, D), BF16)] * 2 + [shape((320, 1536), BF16)] * 4,
+        [whole_block(sent)] * 4 + [whole_block((320, D))] * 2 + [half] * 4,
         [*blocks, *packs],
         [block] * len(blocks) + [pack_block()] * 2,
         "expert_back",
         8 * 320 * D * FF,
         [pltpu.VMEM((320, D), F32)] * 2,
     )
+    return outs[:4], *outs[4:]
 
 
 def expert_grad_kernel(rows_ref, d_result_ref, act_ref, dh_ref, out_ref):
@@ -433,19 +588,6 @@
     )[0]
 
 
-def send_grad_kernel(d_out_ref, high_ref, low_ref, out_ref):
-    d_out = d_out_ref[...]
-    total = dot(high_ref[...], d_out, 0, 0) + dot(low_ref[...], d_out, 0, 0)
-    for d in range(N_SEQ):
-        out_ref[d] = total[CAP * d : CAP * (d + 1)].astype(BF16)
-
-
-def send_grad(d_out, high, low):
-    return call(
-        send_grad_kernel, [shape((N_SEQ, CAP, D), BF16)], [d_out, high, low], "send_grad", 4 * ROWS * D * 320
-    )[0]
-
-
 def middle_back_kernel(paired, me_ref, d_out_ref, *refs):
     me = me_ref[0]
     count = 4 if paired else 8
@@ -453,7 +595,7 @@
     gathered, refs = refs[:4], refs[4:]
     (
         chosen_ref, gates_ref, residual_ref, normed_ref, gain_ref, w_ref,
-        d_residual_ref, small_ref, grad_ref, d_mix_ref, rows_ref, d_rows_ref,
+        d_residual_ref, small_ref, grad_ref, m0, m1, m2, m3, rows_ref, d_rows_ref, back_ref,
     ) = refs
     for d in range(N_SEQ):
         there = pl.ds(CAP * d, CAP)
@@ -479,10 +621,11 @@
     d_residual = d_out.astype(F32) + norm_back(n, inverse, gain_ref[5:6, :], d_normed)
     d_residual_ref[...] = d_residual
     d_branch = d_residual.astype(BF16)
-    for d in range(N_SEQ):
+    for d, ref in enumerate((m0, m1, m2, m3)):
         group = lax.rem(me - d + N_SEQ, N_SEQ)
-        d_mix_ref[d] = dot(d_branch, w_ref[group], 1, 1).astype(BF16)
-        grad_ref[group] = dot(gathered[d][...], d_branch, 0, 0).astype(BF16)
+        ref[...] = dot(d_branch, w_ref[d], 1, 1).astype(BF16)
+        back_ref[group] = dot(gathered[d][...], d_branch, 0, 0).astype(BF16)
+    grad_ref[...] = by_shard(back_ref[...].reshape(D, D))
     high, low = two_parts(d_logits)
     small = dot(normed_ref[...], high, 0, 0) + dot(normed_ref[...], low, 0, 0)
     column = (lax.broadcasted_iota(jnp.int32, (ROWS, 128), 1) == 5).astype(BF16)
@@ -492,70 +635,77 @@
 
 
 def middle_back(me, d_out, blocks, gathered, chosen, gates, residual, normed, gains, w_back, paired):
-    return call(
+    outs = call(
         partial(middle_back_kernel, paired),
         [
             shape((ROWS, D), F32),
             shape((D, 64), F32),
-            shape((N_SEQ, 192, D), BF16),
-            shape((N_SEQ, ROWS, 192), BF16),
-        ],
+            shape((D, D), BF16),
+        ]
+        + [shape((ROWS, 192), BF16)] * 4,
         [me, d_out, *blocks, *gathered, chosen, gates, residual, normed, gains, w_back],
         "middle_back",
         2 * ROWS * D * (2 * D + 640),
         scalars=1,
-        scratch=[pltpu.VMEM((320, D), BF16)] * 2,
-    )
-
-
-def finish_kernel(d_residual_ref, x_ref, gain_ref, b0, b1, b2, b3, out_ref):
+        scratch=[pltpu.VMEM((320, D), BF16)] * 2 + [pltpu.VMEM((N_SEQ, 192, D), BF16)],
+    )
+    return *outs[:3], outs[3:]
+
+
+def finish_kernel(further, d_residual_ref, x_ref, gain_ref, b0, b1, b2, b3, *refs):
     d_normed = b0[...].astype(F32) + b1[...].astype(F32) + b2[...].astype(F32) + b3[...].astype(F32)
     n, inverse = norm_parts(x_ref[...].astype(F32))
     total = d_residual_ref[...] + norm_back(n, inverse, gain_ref[4:5, :], d_normed)
-    out_ref[...] = total.astype(BF16)
-
-
-def finish(d_residual, x, gains, blocks):
-    return call(
-        finish_kernel, [shape((ROWS, D), BF16)], [d_residual, x, gains, *blocks], "finish", 20 * ROWS * D
-    )[0]
-
-
-def attention_weights(w_qkv, w_proj, w_route, gain_attn, gain_ffn):
-    core = lax.axis_index("section")
+    if not further:
+        refs[0][...] = total.astype(BF16)
+        return
+    high_ref, low_ref, out_ref, *sent = refs
+    d_out = total.astype(BF16)
+    out_ref[...] = d_out
+    rows = dot(high_ref[...], d_out, 0, 0) + dot(low_ref[...], d_out, 0, 0)
+    for d in range(N_SEQ):
+        sent[d][...] = rows[CAP * d : CAP * (d + 1)].astype(BF16)
+
+
+def finish(d_residual, x, gains, blocks, weights):
+    further = weights is not None
+    outs = call(
+        partial(finish_kernel, further),
+        [shape((ROWS, D), BF16)] + [shape((CAP, D), BF16)] * (4 if further else 0),
+        [d_residual, x, gains, *blocks] + (list(weights) if further else []),
+        "finish",
+        4 * ROWS * D * 320,
+    )
+    return outs[0], outs[1:]
+
+
+def attention_weights(where, w_qkv, w_proj, w_route, gain_attn, gain_ffn):
     mine = w_qkv.reshape(12, 3, N_SEQ, 192).transpose(2, 0, 1, 3).reshape(N_SEQ, 12, 576)
     small = jnp.concatenate(
-        [w_route, gain_attn[:, None], gain_ffn[:, None], jnp.zeros((12, 122), BF16)], axis=1
-    )
-    whole = jnp.broadcast_to(w_proj, (N_SEQ, 12, D))
-    mine = jnp.concatenate([whole, mine, jnp.broadcast_to(small, (N_SEQ, 12, 128))], axis=2)
-    spread = jnp.broadcast_to(mine[:, None], (N_SEQ, N_SHARD, 12, WIDE))
-    spread = spread.reshape(N_SEQ * N_SHARD, 12, WIDE)
-    whole = lax.all_to_all(spread, ("seq", "shard"), 0, 0, tiled=True).reshape(D, WIDE)
-    other = swap(whole)
-    out = []
-    for s in range(2):
-        rows = jnp.where(core == s, whole, other)
-        table = rows[:, 1344:1352].T.astype(F32)
-        out.append((rows[:, 768:1344], rows[:, :768].reshape(N_SEQ, 192, D), rows[:, 1344:], table))
-    return out
-
-
-def expert_weights(w_in, w_out):
+        [w_route, gain_attn[:, None], gain_ffn[:, None], jnp.zeros((12, 58), BF16)], axis=1
+    )
+    mine = jnp.concatenate([mine, jnp.broadcast_to(small, (N_SEQ, 12, 64))], axis=2)
+    arrived = lax.all_to_all(mine, "seq", 0, 0, tiled=True).reshape(48, 640)
+    back = w_proj.reshape(12, N_SEQ, 192).transpose(1, 0, 2).reshape(48, 192)
+    pack = jnp.concatenate([arrived, back], axis=1)
+    near = jnp.stack(from_ring(pack, "x"))
+    return unpack(where, from_ring(near, "z"))
+
+
+def both_layers(mine):
+    core = lax.axis_index("section")
+    other = swap(mine)
+    return [jnp.where(core == s, mine, other) for s in range(2)]
+
+
+def half_packs(w_in, w_out):
     core = lax.axis_index("section")
     first = w_in.reshape(48, N_SHARD, 4, 48).transpose(2, 0, 1, 3).reshape(4, 48, 768)
     second = w_out.reshape(4, 48, 768)
     quarters = jnp.stack([first, second], axis=1).reshape(2, 4, 48, 768)
     mine = pick(quarters, core)
     arrived = swap(pick(quarters, 1 - core))
-    out = []
-    for s in range(2):
-        own = jnp.where(core == s, mine, arrived)
-        if s == 1:
-            own = tie(own, out[0][0])
-        whole = lax.all_gather(own, "shard", axis=0, tiled=False)
-        out.append((whole, swap(whole)))
-    return out
+    return [jnp.where(core == s, mine, arrived) for s in range(2)]
 
 
 def join_experts(own, other):
@@ -564,13 +714,6 @@
 
 def scatter_beside(v):
     return lax.psum_scatter(v, "shard", scatter_dimension=0, tiled=True)[0]
-
-
-def join_attention(mix, back):
-    core = lax.axis_index("section")
-    keep = jnp.where(core == 0, mix, back)
-    give = jnp.where(core == 0, back, mix)
-    return (keep.astype(F32) + swap(give).astype(F32)).astype(BF16)
 
 
 def shards(images_in, out_grad, routes, w_qkv, w_proj, w_route, gain_attn, gain_ffn, w_in, w_out):
@@ -582,20 +725,37 @@
     route_of = (jnp.where(core == 0, mine, arrived), jnp.where(core == 0, arrived, mine))
     x0 = pick(images_in, core)[0]
     d_last = pick(out_grad, core)[0]
-    attn = attention_weights(w_qkv[0], w_proj[0], w_route[0], gain_attn[0], gain_ffn[0])
-    experts = expert_weights(w_in[0, 0], w_out[0, 0])
+    where = where_shard()
+    halves = half_packs(w_in[0, 0], w_out[0, 0])
+    near_a = jnp.stack(from_ring(halves[0][0:2], "x"))
+    near_b = jnp.stack(from_ring(halves[0][2:4], "z"))
+    rows, back_rows = attention_weights(
+        where, w_qkv[0], w_proj[0], w_route[0], gain_attn[0], gain_ffn[0]
+    )
+    near_a, near_b, rows = lax.optimization_barrier((near_a, near_b, rows))
+    own = order(where, from_ring(near_a, "z"), from_ring(near_b, "x"))
+    experts = [(own, swap(own)), None]
+    attn_rows = both_layers(rows)
+    w_mix = [v[:, :576] for v in attn_rows]
+    routers = [jnp.pad(v[:, 576:], ((0, 0), (0, 64))) for v in attn_rows]
+    tables = [v[:, 576:584].T.astype(F32) for v in attn_rows]
+    w_back = both_layers(jnp.stack([back_rows] + [turn(back_rows, d) for d in (1, 2, 3)]))
 
     saved = []
     x = x0
     layer_outs = []
     for s in range(2):
-        w_mix, w_back, router, table = attn[s]
-        x_all = gather_tokens(x)
-        mixture, packed, logs = attend(x_all, w_mix, table)
+        mixture, x_all, packed, logs = attend([x] + [turn(x, -d) for d in (1, 2, 3)], w_mix[s], tables[s])
+        if s == 0:
+            later = tie(halves[1], (mixture[0], own))
+            later = lax.all_gather(later, "shard", axis=0, tiled=False)
+        else:
+            later = tie(later, mixture[0])
+            experts[1] = (later, swap(later))
         gathered = send_out(mixture)
         d_out = d_last if s == 1 else None
         residual, normed, gates, chosen, high, low, buffer = middle(
-            me, x, gathered, w_back, router, table, route_of[s], d_out
+            me, x, gathered, w_back[s], routers[s], tables[s], route_of[s], d_out
         )
         blocks = send_out(buffer)
         kept = (x, x_all, packed, logs, gathered, residual, normed, gates, chosen, high, low, blocks)
@@ -608,38 +768,51 @@
             saved.append((kept, None))
 
     d_out = d_last
+    d_buffer = None
     in_grads = [None, None]
     expert_sums = [None, None]
-    joined = [None, None]
+    attn_grads = [None, None]
     for s in (1, 0):
-        w_mix, w_back, router, table = attn[s]
         kept, returned = saved[s]
         x, x_all, packed, logs, gathered, residual, normed, gates, chosen, high, low, blocks = kept
         if s == 1:
             sent, *states = expert_back(blocks, experts[s], True)
             arrived = send_back(sent)
+            first_arrival = arrived[1]
             layer_outs.append(combine(residual, high, low, [v[0] for v in arrived]))
         else:
-            d_blocks = send_out(send_grad(d_out, high, low))
-            sent, *states = expert_back([*blocks, *d_blocks], experts[s], False)
-            arrived = [*returned, *send_back(sent)]
+            sent, *states = expert_back([*blocks, *send_out(d_buffer)], experts[s], False)
+            back = send_back(sent)
+            first_arrival = back[1]
+            arrived = [*returned, *back]
         rows, d_result, act_own, act_other, dh_own, dh_other = states
-        other = expert_grad(rows, d_result, act_other, dh_other)
-        own = expert_grad(rows, d_result, act_own, dh_own)
-        expert_sums[s] = scatter_beside(join_experts(own, other))
+        if s == 1:
+            rows = tie(rows, first_arrival)
+        other = swap(expert_grad(rows, d_result, act_other, dh_other))
         d_residual, small, grad_back, d_mixture = middle_back(
-            me, d_out, arrived, gathered, chosen, gates, residual, normed, table, w_back, s == 1
+            me, d_out, arrived, gathered, chosen, gates, residual, normed, tables[s], w_back[s], s == 1
         )
         d_heads = send_back(d_mixture)
-        d_normed, grad_mix = attend_back(x_all, w_mix, table, packed, logs, d_heads, small)
+        if s == 1:
+            rows = tie(rows, d_heads[1])
+        own = expert_grad(rows, d_result, act_own, dh_own)
+        if s == 1:
+            expert_sums[s] = scatter_beside((own.astype(F32) + other.astype(F32)).astype(BF16))
+        else:
+            expert_sums[s] = scatter_pair(where, own, other)
+            expert_sums[s] = expert_sums[s].reshape(4, 48, D)
+        d_normed, grad_mix = attend_back(x_all, w_mix[s], tables[s], packed, logs, d_heads, small)
         d_parts = send_out(d_normed)
-        joined[s] = join_attention(grad_mix, grad_back.reshape(D, D))
-        d_out = finish(d_residual, x, table, d_parts)
+        keep = jnp.where(core == 0, grad_mix, grad_back)
+        give = jnp.where(core == 0, grad_back, grad_mix)
+        attn_grads[s] = (keep.reshape(N_SHARD, 48, D), swap(give).reshape(N_SHARD, 48, D))
+        weights = saved[0][0][9:11] if s == 1 else None
+        d_out, d_buffer = finish(d_residual, x, tables[s], d_parts, weights)
         in_grads[s] = d_out
 
-    pair = jnp.concatenate([joined[0], joined[1]], axis=1).reshape(N_SEQ * N_SHARD, 12, 2 * D)
-    arrived = lax.all_to_all(pair, ("seq", "shard"), 0, 0, tiled=True)
-    attn_sum = jnp.sum(arrived.reshape(N_SEQ, N_SHARD, 12, 2 * D).astype(F32), axis=1)
+    attn_sum = scatter_pair(where, *attn_grads[0], *attn_grads[1])
+    attn_sum = attn_sum.reshape(2, N_SEQ, 12, D).transpose(1, 2, 0, 3).reshape(N_SEQ, 12, 2 * D)
+    attn_sum = lax.all_to_all(attn_sum, "seq", 0, 0, tiled=True).astype(F32)
     attn_sums = [attn_sum[:, :, :D], attn_sum[:, :, D:]]
 
     def settle(pair):

time: 563 us -> 581 us (1.032)
  starting transfers between devices: 86.7 us -> 150 us
  waiting for transfers between devices: 228 us -> 191 us
  Pallas kernels: 115 us -> 150 us
  local copies, waits for them, and re-layouts: 74 us -> 42.1 us
  other arithmetic: 34.5 us -> 23.7 us
    ppermute x0 -> x42, waiting for transfers between devices: none -> 81.9 us  [hop(): return lax.ppermute(v, 'shard', route)]
    all_gather x2 -> x1, waiting for transfers between devices: 76.3 us -> 0.01 us  [shards(): later = lax.all_gather(later, 'shard', axis=0, tiled=False)]
    ppermute x0 -> x42, starting transfers between devices: none -> 55.4 us  [hop(): return lax.ppermute(v, 'shard', route)]
    all_to_all x2, waiting for transfers between devices: 43 us -> 4.43 us  [the longest x1 4.42 us: attention_weights(): arrived = lax.all_to_all(mine, 'seq', 0, 0, tiled=True).reshape(48, 640)]
    pallas_call x13 -> x20, Pallas kernels: 62.4 us -> 96.6 us  [call(): pl.pallas_call(body, out_shape=outs, in_specs=specs, out_specs=[vmem()] *...]
    squeeze x12 -> x0, local copies, waits for them, and re-layouts: 18.3 us -> none  [the longest x7 11.7 us: send_out(): return [blocks[0]] + [turn(blocks[d], d) for d in (1, 2, 3)]]
    slice x12 -> x6, local copies, waits for them, and re-layouts: 14.2 us -> 2.78 us  [the longest x4 2.76 us: shards(): w_mix = [v[:, :576] for v in attn_rows]]
    ppermute x13 -> x14, starting transfers between devices: 23 us -> 33.3 us  [swap(): return lax.ppermute(v, 'section', [(0, 1), (1, 0)])]
  transfers between devices with their start and end apart: 61 -> 105, of which waited for: 38 -> 54; matrix products, arithmetic and copies ran while one was open for 14% -> 6% of each run, Pallas kernels for 18% -> 21%
where the time goes in v4:
time: 581 us; the launch traced here: 572 us
  waiting for transfers between devices  191 us (33%)
  starting transfers between devices  150 us (26%)
  Pallas kernels  150 us (26%)
  local copies, waits for them, and re-layouts  42.1 us (7%)
  other arithmetic  23.7 us (4%)
  between operations  15.5 us (3%)
    ppermute x45, waiting for transfers between devices, turn(): return lax.ppermute(v, 'seq', [(i, (i + d) % N_SEQ) for i in range(N_SEQ)])  100 us
    pallas_call x20, Pallas kernels, call(): pl.pallas_call(body, out_shape=outs, in_specs=specs, out_specs=[vmem()] *...  96.6 us
    ppermute x42, waiting for transfers between devices, hop(): return lax.ppermute(v, 'shard', route)  81.9 us
    ppermute x42, starting transfers between devices, hop(): return lax.ppermute(v, 'shard', route)  55.4 us
    pallas_call x7, Pallas kernels, grid_call(): pl.pallas_call(body, grid=(2,), out_shape=outs, in_specs=in_specs, out_sp...  52.9 us
    ppermute x45, starting transfers between devices, turn(): return lax.ppermute(v, 'seq', [(i, (i + d) % N_SEQ) for i in range(N_SEQ)])  52.8 us
    ppermute x14, starting transfers between devices, swap(): return lax.ppermute(v, 'section', [(0, 1), (1, 0)])  33.3 us
    unnamed x235, local copies, waits for them, and re-layouts  15 us
  transfers between devices with their start and end apart: 105, of which 54 were waited for; matrix products, arithmetic and copies ran while one was open for 6% of the time, Pallas kernels for 21%

profile of v4, /device:TPU:1, one launch (start us, length us, event | category | flops | bytes accessed | tf_op | source)
XLA Modules:
  0.0 571.8 jit_solution(3681634680892338157)
XLA Ops:
  45.4 7.4 %collective-permute-done.14.b2 = bf16[4,48,832]{2,1,0:T(8,128)(2,1)S(1)} collective-permute-done((bf16[4,48,832]{2,1,0:T(8,128)(2,1)S(1)}, bf16[4,48,832]{2,1,0:T(8,128)(2,1)S(1)}, u32[]{:S(2)}, u32[]{:S(2)}) %collective-permute-start.14) | collective-permute-done | bytes 319520 | tf_op jit(solution)/shard_map/ppermute | solution.py:59
  72.1 11.4 %collective-permute-done.29.a2 = bf16[4,2,48,768]{3,2,1,0:T(8,128)(2,1)} collective-permute-done((bf16[4,2,48,768]{3,2,1,0:T(8,128)(2,1)S(1)}, bf16[4,2,48,768]{3,2,1,0:T(8,128)(2,1)}, u32[]{:S(2)}, u32[]{:S(2)}) %collective-permute-start.29) | collective-permute-done | bytes 589856 | tf_op jit(solution)/shard_map/ppermute | solution.py:59
  88.9 7.5 %collective-permute-start.1 = (bf16[144,768]{1,0:T(8,128)(2,1)}, bf16[144,768]{1,0:T(8,128)(2,1)}, u32[]{:S(2)}, u32[]{:S(2)}) collective-permute-start(bf16[144,768]{1,0:T(8,128)(2,1)} %dynamic-slice_bitcast_fusion.2.x0.x_ref), channel_id=1, source_target_pairs={{0,32},{16,48},{32,0},{48,16},{1,33},{17,49},{33,1},{49,17},{2,34}... | collective-permute-start | bytes 663560 | tf_op jit(solution)/shard_map/ppermute | solution.py:36
  96.4 6.8 %collective-permute-done.31.b1 = bf16[4,2,48,768]{3,2,1,0:T(8,128)(2,1)S(1)} collective-permute-done((bf16[4,2,48,768]{3,2,1,0:T(8,128)(2,1)S(1)}, bf16[4,2,48,768]{3,2,1,0:T(8,128)(2,1)S(1)}, u32[]{:S(2)}, u32[]{:S(2)}) %collective-permute-start.31) | collective-permute-done | bytes 589856 | tf_op jit(solution)/shard_map/ppermute | solution.py:59
  111.0 6.0 %attention.2 = (bf16[144,192]{1,0:T(8,128)(2,1)}, bf16[144,192]{1,0:T(8,128)(2,1)}, bf16[144,192]{1,0:T(8,128)(2,1)}, bf16[144,192]{1,0:T(8,128)(2,1)}, bf16[576...) custom-call(bf16[144,768]{1,0:T(8,128)(2,1)} %dynamic-slice_bitcast_fusion.2.x0.x_ref, ...), custom_call_target="tpu_custom_call" | custom-call | flops 764411904 | bytes 3858432 | tf_op jit(solution)/shard_map/attention/pallas_call | solution.py:130
  122.7 6.5 %collective-permute-done.22 = bf16[192,768]{1,0:T(8,128)(2,1)S(1)} collective-permute-done((bf16[192,768]{1,0:T(8,128)(2,1)S(1)}, bf16[192,768]{1,0:T(8,128)(2,1)S(1)}, u32[]{:S(2)}, u32[]{:S(2)}) %collective-permute-start.22) | collective-permute-done | bytes 294944 | tf_op jit(solution)/shard_map/ppermute | solution.py:36
  131.2 7.1 %collective-permute-done.20 = bf16[192,768]{1,0:T(8,128)(2,1)S(1)} collective-permute-done((bf16[192,768]{1,0:T(8,128)(2,1)S(1)}, bf16[192,768]{1,0:T(8,128)(2,1)S(1)}, u32[]{:S(2)}, u32[]{:S(2)}) %collective-permute-start.20) | collective-permute-done | bytes 294944 | tf_op jit(solution)/shard_map/ppermute | solution.py:36
  165.3 7.1 %expert.1 = (bf16[80,768]{1,0:T(8,128)(2,1)}, bf16[80,768]{1,0:T(8,128)(2,1)}, bf16[80,768]{1,0:T(8,128)(2,1)}, bf16[80,768]{1,0:T(8,128)(2,1)}) custom-call(bf16[80,768]{1,0:T(8,128)(2,1)} %get-tuple-element.147.r0.refs_0_, bf16[80,768]{1,0:T(8,128)(2,1)} %copy-done.97, bf16[80,768]{1,0:T(8,128)(2,1)} %copy-done.98, bf16[80,768]{1,0:T(8,128)(2,1)} %copy-done.99, ...), custom_call_target="tpu_custom_call" | custom-call | flops 3019898880 | bytes 10420224 | tf_op jit(solution)/shard_map/expert/pallas_call | solution.py:465
  198.9 6.0 %attention.3 = (bf16[144,192]{1,0:T(8,128)(2,1)}, bf16[144,192]{1,0:T(8,128)(2,1)}, bf16[144,192]{1,0:T(8,128)(2,1)}, bf16[144,192]{1,0:T(8,128)(2,1)}, bf16[576...) custom-call(bf16[144,768]{1,0:T(8,128)(2,1)} %combine.2.x0.x_ref, bf16[144,768]{1,0:T(8,128)(2,1)} %copy-done.91, ...), custom_call_target="tpu_custom_call" | custom-call | flops 764411904 | bytes 3858432 | tf_op jit(solution)/shard_map/attention/pallas_call | solution.py:130
  227.7 6.8 %collective-permute-done.45.refs_2_ = bf16[2,80,768]{2,1,0:T(8,128)(2,1)S(1)} collective-permute-done((bf16[2,80,768]{2,1,0:T(8,128)(2,1)}, bf16[2,80,768]{2,1,0:T(8,128)(2,1)S(1)}, u32[]{:S(2)}, u32[]{:S(2)}) %collective-permute-start.45) | collective-permute-done | bytes 245792 | tf_op jit(solution)/shard_map/ppermute | solution.py:36
  235.3 11.6 %expert_back.2 = (bf16[2,80,768]{2,1,0:T(8,128)(2,1)}, bf16[2,80,768]{2,1,0:T(8,128)(2,1)}, bf16[2,80,768]{2,1,0:T(8,128)(2,1)}, bf16[2,80,768]{2,1,0:T(8,128)(2...) custom-call(bf16[2,80,768]{2,1,0:T(8,128)(2,1)} %get-tuple-element.1, ...), custom_call_target="tpu_custom_call" | custom-call | flops 6039797760 | bytes 16318464 | tf_op jit(solution)/shard_map/expert_back/pallas_call | solution.py:465
  277.4 6.6 %middle_back.2 = (f32[144,768]{1,0:T(8,128)}, f32[768,64]{1,0:T(8,128)}, bf16[768,768]{1,0:T(8,128)(2,1)}, bf16[144,192]{1,0:T(8,128)(2,1)}, bf16[144,192]{1,0:T...) custom-call(s32[1]{0:T(128)} %bitcast.me_ref, ...), custom_call_target="tpu_custom_call" | custom-call | flops 481296384 | bytes 5498884 | tf_op jit(solution)/shard_map/middle_back/pallas_call | solution.py:130
  293.2 6.0 %add_convert_fusion = bf16[16,4,48,768]{3,2,1,0:T(8,128)(2,1)} fusion(bf16[16,4,48,768]{3,2,1,0:T(8,128)(2,1)S(1)} %collective-permute-done.99, bf16[16,4,48,768]{3,2,1,0:T(8,128)(2,1)} %expert_grad.6), kind=kLoop, calls=%fused_computation | loop fusion | flops 9437184 | bytes 14155776 | tf_op jit(solution)/shard_map/convert_element_type | solution.py:800
  308.0 11.1 %attention_back.2 = (bf16[144,768]{1,0:T(8,128)(2,1)}, bf16[144,768]{1,0:T(8,128)(2,1)}, bf16[144,768]{1,0:T(8,128)(2,1)}, bf16[144,768]{1,0:T(8,128)(2,1)}, bf16[768,768]{1,0:T(8,128)(2,1)}) custom-call(bf16[576,768]{1,0:T(8,128)(2,1)} %get-tuple-element.178.x_ref, bf16[768,576]{1,0:T(8,128)(2,1)} %copy.127.w_ref, ...), custom_call_target="tpu_custom_call" | custom-call | flops 1656225792 | bytes 5234688 | tf_op jit(solution)/shard_map/attention_back/pallas_call | solution.py:130
  321.8 9.6 %collective-permute-done.55.b1 = bf16[144,768]{1,0:T(8,128)(2,1)S(1)} collective-permute-done((bf16[144,768]{1,0:T(8,128)(2,1)}, bf16[144,768]{1,0:T(8,128)(2,1)S(1)}, u32[]{:S(2)}, u32[]{:S(2)}) %collective-permute-start.55) | collective-permute-done | bytes 221216 | tf_op jit(solution)/shard_map/ppermute | solution.py:36
  345.9 10.4 %expert_back.3 = (bf16[80,768]{1,0:T(8,128)(2,1)}, bf16[80,768]{1,0:T(8,128)(2,1)}, bf16[80,768]{1,0:T(8,128)(2,1)}, bf16[80,768]{1,0:T(8,128)(2,1)}, bf16[320,7...) custom-call(bf16[80,768]{1,0:T(8,128)(2,1)} %get-tuple-element.147.r, ...), custom_call_target="tpu_custom_call" | custom-call | flops 6039797760 | bytes 15826944 | tf_op jit(solution)/shard_map/expert_back/pallas_call | solution.py:465
  375.4 6.7 %middle_back.3 = (f32[144,768]{1,0:T(8,128)}, f32[768,64]{1,0:T(8,128)}, bf16[768,768]{1,0:T(8,128)(2,1)}, bf16[144,192]{1,0:T(8,128)(2,1)}, bf16[144,192]{1,0:T...) custom-call(s32[1]{0:T(128)} %bitcast.me_ref, bf16[144,768]{1,0:T(8,128)(2,1)} %get-tuple-element.190.d_out_ref, ...), custom_call_target="tpu_custom_call" | custom-call | flops 481296384 | bytes 5498884 | tf_op jit(solution)/shard_map/middle_back/pallas_call | solution.py:130
  388.7 11.1 %attention_back.3 = (bf16[144,768]{1,0:T(8,128)(2,1)}, bf16[144,768]{1,0:T(8,128)(2,1)}, bf16[144,768]{1,0:T(8,128)(2,1)}, bf16[144,768]{1,0:T(8,128)(2,1)}, bf16[768,768]{1,0:T(8,128)(2,1)}) custom-call(bf16[576,768]{1,0:T(8,128)(2,1)} %get-tuple-element.203.x_ref, bf16[768,576]{1,0:T(8,128)(2,1)} %copy.122.w_ref, ...), custom_call_target="tpu_custom_call" | custom-call | flops 1656225792 | bytes 5234688 | tf_op jit(solution)/shard_map/attention_back/pallas_call | solution.py:130
  427.7 6.3 %expert_grad.4.refs_0_ = bf16[16,4,48,768]{3,2,1,0:T(8,128)(2,1)} custom-call(bf16[320,768]{1,0:T(8,128)(2,1)} %get-tuple-element.235.rows_ref, bf16[320,768]{1,0:T(8,128)(2,1)} %get-tuple-element.236.d_result_ref, bf16[320,1536]{1,0:T(8,128)(2,1)} %get-tuple-element.237.act_ref, bf16[320,1536]{1,0:T(8,128)(2,1)} %get-tuple-element.238.dh_ref), custom_call_target="tpu_custom_call" | custom-call | flops 1509949440 | bytes 7667712 | tf_op jit(solution)/shard_map/expert_grad/pallas_call | solution.py:465
  434.1 7.0 %arrange.3 = (bf16[4,2,48,768]{3,2,1,0:T(8,128)(2,1)}, bf16[4,2,48,768]{3,2,1,0:T(8,128)(2,1)}, bf16[4,2,48,768]{3,2,1,0:T(8,128)(2,1)}, bf16[4,2,48,768]{3,2,1,...) custom-call(s32[2]{0:T(128)} %pad_add_fusion.where_ref, ...), custom_call_target="tpu_custom_call" | custom-call | bytes 14155784 | tf_op jit(solution)/shard_map/arrange/pallas_call | solution.py:130
  456.7 7.4 %collective-permute-start.51 = (bf16[144,768]{1,0:T(8,128)(2,1)}, bf16[144,768]{1,0:T(8,128)(2,1)}, u32[]{:S(2)}, u32[]{:S(2)}) collective-permute-start(bf16[144,768]{1,0:T(8,128)(2,1)} %get-tuple-element.309), channel_id=1, source_target_pairs={{0,64},{64,0},{1,65},{65,1},{2,66},{66,2},{3,67},{67,3},{4,68},{68... | collective-permute-start | bytes 663560 | tf_op jit(solution)/shard_map/ppermute | solution.py:32
  467.7 7.8 %collective-permute-done.82.refs_5_ = bf16[48,768]{1,0:T(8,128)(2,1)S(1)} collective-permute-done((bf16[48,768]{1,0:T(8,128)(2,1)}, bf16[48,768]{1,0:T(8,128)(2,1)S(1)}, u32[]{:S(2)}, u32[]{:S(2)}) %collective-permute-start.82) | collective-permute-done | bytes 73760 | tf_op jit(solution)/shard_map/ppermute | solution.py:59
  479.3 11.1 %collective-permute-done.84.refs_7_ = bf16[48,768]{1,0:T(8,128)(2,1)S(1)} collective-permute-done((bf16[48,768]{1,0:T(8,128)(2,1)}, bf16[48,768]{1,0:T(8,128)(2,1)S(1)}, u32[]{:S(2)}, u32[]{:S(2)}) %collective-permute-start.84) | collective-permute-done | bytes 73760 | tf_op jit(solution)/shard_map/ppermute | solution.py:59
  512.7 13.5 %collective-permute-done.91.refs_6_ = bf16[4,2,48,768]{3,2,1,0:T(8,128)(2,1)} collective-permute-done((bf16[4,2,48,768]{3,2,1,0:T(8,128)(2,1)}, bf16[4,2,48,768]{3,2,1,0:T(8,128)(2,1)}, u32[]{:S(2)}, u32[]{:S(2)}) %collective-permute-start.91) | collective-permute-done | bytes 589856 | tf_op jit(solution)/shard_map/ppermute | solution.py:59
  (532 shorter events, 357.3 us)
Async XLA Ops:
  17.5 187.5 %all-gather.3.cloned.1.call-start = ((), (), s32[]{:S(2)}) async-start(), calls=%async_computation.3 | async-start | bytes 5013504 | tf_op jit(solution)/shard_map/all_gather | solution.py:751
  58.8 24.7 %collective-permute-start.29 = (bf16[4,2,48,768]{3,2,1,0:T(8,128)(2,1)S(1)}, bf16[4,2,48,768]{3,2,1,0:T(8,128)(2,1)}, u32[]{:S(2)}, u32[]{:S(2)}) collective-permute-start(bf16[4,2,48,768]{3,2,1,0:T(8,128)(2,1)S(1)} %pad_maximum_fusion.2.a0), channel_id=1, source_target_pairs={{0,8},{1,9},{2,10},{3,11},{4,12},{5,13},{6,14},{7,15},{8,0},{9,1},... | collective-permute-start | bytes 1769480 | tf_op jit(solution)/shard_map/ppermute | solution.py:59
  61.9 47.0 %collective-permute-start.16 = (bf16[768,640]{0,1:T(8,128)(2,1)S(1)}, bf16[768,640]{0,1:T(8,128)(2,1)S(1)}, u32[]{:S(2)}, u32[]{:S(2)}) collective-permute-start(bf16[768,640]{0,1:T(8,128)(2,1)S(1)} %copy.121), channel_id=1, source_target_pairs={{0,64},{64,0},{1,65},{65,1},{2,66},{66,2},{3,67},{67,3},{4,68},{68... | collective-permute-start | bytes 2949128 | tf_op jit(solution)/shard_map/ppermute | solution.py:32
  65.4 22.0 %collective-permute-start.28 = (bf16[4,2,48,768]{3,2,1,0:T(8,128)(2,1)S(1)}, bf16[4,2,48,768]{3,2,1,0:T(8,128)(2,1)S(1)}, u32[]{:S(2)}, u32[]{:S(2)}) collective-permute-start(bf16[4,2,48,768]{3,2,1,0:T(8,128)(2,1)S(1)} %pad_maximum_fusion.2.a0), channel_id=1, source_target_pairs={{0,12},{1,13},{2,14},{3,15},{4,0},{5,1},{6,2},{7,3},{8,4},{9,5},{1... | collective-permute-start | bytes 1769480 | tf_op jit(solution)/shard_map/ppermute | solution.py:59
  66.8 22.1 %collective-permute-start.33 = (bf16[4,2,48,768]{3,2,1,0:T(8,128)(2,1)S(1)}, bf16[4,2,48,768]{3,2,1,0:T(8,128)(2,1)S(1)}, u32[]{:S(2)}, u32[]{:S(2)}) collective-permute-start(bf16[4,2,48,768]{3,2,1,0:T(8,128)(2,1)S(1)} %pad_maximum_fusion.3.b0), channel_id=1, source_target_pairs={{0,1},{1,2},{2,3},{3,0},{4,5},{5,6},{6,7},{7,4},{8,9},{9,10},{10,1... | collective-permute-start | bytes 1769480 | tf_op jit(solution)/shard_map/ppermute | solution.py:59
  72.1 24.3 %collective-permute-start.32 = (bf16[4,2,48,768]{3,2,1,0:T(8,128)(2,1)S(1)}, bf16[4,2,48,768]{3,2,1,0:T(8,128)(2,1)S(1)}, u32[]{:S(2)}, u32[]{:S(2)}) collective-permute-start(bf16[4,2,48,768]{3,2,1,0:T(8,128)(2,1)S(1)} %pad_maximum_fusion.3.b0), channel_id=1, source_target_pairs={{0,2},{1,3},{2,0},{3,1},{4,6},{5,7},{6,4},{7,5},{8,10},{9,11},{10,... | collective-permute-start | bytes 1769480 | tf_op jit(solution)/shard_map/ppermute | solution.py:59
  87.4 23.5 %collective-permute-start.2 = (bf16[144,768]{1,0:T(8,128)(2,1)}, bf16[144,768]{1,0:T(8,128)(2,1)}, u32[]{:S(2)}, u32[]{:S(2)}) collective-permute-start(bf16[144,768]{1,0:T(8,128)(2,1)} %dynamic-slice_bitcast_fusion.2.x0.x_ref), channel_id=1, source_target_pairs={{0,16},{16,32},{32,48},{48,0},{1,17},{17,33},{33,49},{49,1},{2,18}... | collective-permute-start | bytes 663560 | tf_op jit(solution)/shard_map/ppermute | solution.py:36
  88.9 22.0 %collective-permute-start.1 = (bf16[144,768]{1,0:T(8,128)(2,1)}, bf16[144,768]{1,0:T(8,128)(2,1)}, u32[]{:S(2)}, u32[]{:S(2)}) collective-permute-start(bf16[144,768]{1,0:T(8,128)(2,1)} %dynamic-slice_bitcast_fusion.2.x0.x_ref), channel_id=1, source_target_pairs={{0,32},{16,48},{32,0},{48,16},{1,33},{17,49},{33,1},{49,17},{2,34}... | collective-permute-start | bytes 663560 | tf_op jit(solution)/shard_map/ppermute | solution.py:36
  117.0 431.1 %reduce-scatter.4.cloned.1.call-start = ((), (), s32[]{:S(2)}) async-start(), calls=%async_computation.4 | async-start | bytes 5013504
  117.1 47.6 %collective-permute-start.34 = (bf16[16,4,48,768]{3,2,1,0:T(8,128)(2,1)}, bf16[16,4,48,768]{3,2,1,0:T(8,128)(2,1)}, u32[]{:S(2)}, u32[]{:S(2)}) collective-permute-start(bf16[16,4,48,768]{3,2,1,0:T(8,128)(2,1)} %order.1.own_ref.refs_8_), channel_id=1, source_target_pairs={{0,64},{64,0},{1,65},{65,1},{2,66},{66,2},{3,67},{67,3},{4,68},{68... | collective-permute-start | bytes 14155784 | tf_op jit(solution)/shard_map/ppermute | solution.py:32
  205.0 29.6 %collective-permute-start.47 = (bf16[16,4,48,768]{3,2,1,0:T(8,128)(2,1)}, bf16[16,4,48,768]{3,2,1,0:T(8,128)(2,1)}, u32[]{:S(2)}, u32[]{:S(2)}) collective-permute-start(bf16[16,4,48,768]{3,2,1,0:T(8,128)(2,1)} %bitcast.152), channel_id=1, source_target_pairs={{0,64},{64,0},{1,65},{65,1},{2,66},{66,2},{3,67},{67,3},{4,68},{68... | collective-permute-start | bytes 14155784 | tf_op jit(solution)/shard_map/ppermute | solution.py:32
  260.6 32.6 %collective-permute-start.99 = (bf16[16,4,48,768]{3,2,1,0:T(8,128)(2,1)}, bf16[16,4,48,768]{3,2,1,0:T(8,128)(2,1)S(1)}, u32[]{:S(2)}, u32[]{:S(2)}) collective-permute-start(bf16[16,4,48,768]{3,2,1,0:T(8,128)(2,1)} %expert_grad.7), channel_id=1, source_target_pairs={{0,64},{64,0},{1,65},{65,1},{2,66},{66,2},{3,67},{67,3},{4,68},{68... | collective-permute-start | bytes 14155784 | tf_op jit(solution)/shard_map/ppermute | solution.py:32
  362.2 64.5 %collective-permute-start.86 = (bf16[16,4,48,768]{3,2,1,0:T(8,128)(2,1)}, bf16[16,4,48,768]{3,2,1,0:T(8,128)(2,1)S(1)}, u32[]{:S(2)}, u32[]{:S(2)}) collective-permute-start(bf16[16,4,48,768]{3,2,1,0:T(8,128)(2,1)} %expert_grad.5), channel_id=1, source_target_pairs={{0,64},{64,0},{1,65},{65,1},{2,66},{66,2},{3,67},{67,3},{4,68},{68... | collective-permute-start | bytes 14155784 | tf_op jit(solution)/shard_map/ppermute | solution.py:32
  414.7 26.4 %collective-permute-start.74 = (bf16[4,48,768]{2,1,0:T(8,128)(2,1)}, bf16[4,48,768]{2,1,0:T(8,128)(2,1)S(1)}, u32[]{:S(2)}, u32[]{:S(2)}) collective-permute-start(bf16[4,48,768]{2,1,0:T(8,128)(2,1)} %get-tuple-element.221), channel_id=1, source_target_pairs={{0,2},{1,3},{2,0},{3,1},{4,6},{5,7},{6,4},{7,5},{8,10},{9,11},{10,... | collective-permute-start | bytes 884744 | tf_op jit(solution)/shard_map/ppermute | solution.py:59
  419.0 22.2 %collective-permute-start.75 = (bf16[4,48,768]{2,1,0:T(8,128)(2,1)}, bf16[4,48,768]{2,1,0:T(8,128)(2,1)S(1)}, u32[]{:S(2)}, u32[]{:S(2)}) collective-permute-start(bf16[4,48,768]{2,1,0:T(8,128)(2,1)} %get-tuple-element.222), channel_id=1, source_target_pairs={{0,3},{1,0},{2,1},{3,2},{4,7},{5,4},{6,5},{7,6},{8,11},{9,8},{10,9... | collective-permute-start | bytes 884744 | tf_op jit(solution)/shard_map/ppermute | solution.py:59
  419.0 24.5 %collective-permute-start.76 = (bf16[4,48,768]{2,1,0:T(8,128)(2,1)}, bf16[4,48,768]{2,1,0:T(8,128)(2,1)S(1)}, u32[]{:S(2)}, u32[]{:S(2)}) collective-permute-start(bf16[4,48,768]{2,1,0:T(8,128)(2,1)} %get-tuple-element.224), channel_id=1, source_target_pairs={{0,4},{1,5},{2,6},{3,7},{4,8},{5,9},{6,10},{7,11},{8,12},{9,13},{1... | collective-permute-start | bytes 884744 | tf_op jit(solution)/shard_map/ppermute | solution.py:59
  444.3 57.5 %collective-permute-start.87 = (bf16[4,2,48,768]{3,2,1,0:T(8,128)(2,1)}, bf16[4,2,48,768]{3,2,1,0:T(8,128)(2,1)S(1)}, u32[]{:S(2)}, u32[]{:S(2)}) collective-permute-start(bf16[4,2,48,768]{3,2,1,0:T(8,128)(2,1)} %get-tuple-element.242), channel_id=1, source_target_pairs={{0,1},{1,2},{2,3},{3,0},{4,5},{5,6},{6,7},{7,4},{8,9},{9,10},{10,1... | collective-permute-start | bytes 1769480 | tf_op jit(solution)/shard_map/ppermute | solution.py:59
  454.1 50.4 %collective-permute-start.88 = (bf16[4,2,48,768]{3,2,1,0:T(8,128)(2,1)}, bf16[4,2,48,768]{3,2,1,0:T(8,128)(2,1)S(1)}, u32[]{:S(2)}, u32[]{:S(2)}) collective-permute-start(bf16[4,2,48,768]{3,2,1,0:T(8,128)(2,1)} %get-tuple-element.243), channel_id=1, source_target_pairs={{0,2},{1,3},{2,0},{3,1},{4,6},{5,7},{6,4},{7,5},{8,10},{9,11},{10,... | collective-permute-start | bytes 1769480 | tf_op jit(solution)/shard_map/ppermute | solution.py:59
  456.7 42.0 %collective-permute-start.51 = (bf16[144,768]{1,0:T(8,128)(2,1)}, bf16[144,768]{1,0:T(8,128)(2,1)}, u32[]{:S(2)}, u32[]{:S(2)}) collective-permute-start(bf16[144,768]{1,0:T(8,128)(2,1)} %get-tuple-element.309), channel_id=1, source_target_pairs={{0,64},{64,0},{1,65},{65,1},{2,66},{66,2},{3,67},{67,3},{4,68},{68... | collective-permute-start | bytes 663560 | tf_op jit(solution)/shard_map/ppermute | solution.py:32
  475.5 32.1 %collective-permute-start.89 = (bf16[4,2,48,768]{3,2,1,0:T(8,128)(2,1)}, bf16[4,2,48,768]{3,2,1,0:T(8,128)(2,1)S(1)}, u32[]{:S(2)}, u32[]{:S(2)}) collective-permute-start(bf16[4,2,48,768]{3,2,1,0:T(8,128)(2,1)} %get-tuple-element.244), channel_id=1, source_target_pairs={{0,3},{1,0},{2,1},{3,2},{4,7},{5,4},{6,5},{7,6},{8,11},{9,8},{10,9... | collective-permute-start | bytes 1769480 | tf_op jit(solution)/shard_map/ppermute | solution.py:59
  498.8 27.4 %collective-permute-start.91 = (bf16[4,2,48,768]{3,2,1,0:T(8,128)(2,1)}, bf16[4,2,48,768]{3,2,1,0:T(8,128)(2,1)}, u32[]{:S(2)}, u32[]{:S(2)}) collective-permute-start(bf16[4,2,48,768]{3,2,1,0:T(8,128)(2,1)} %get-tuple-element.247), channel_id=1, source_target_pairs={{0,8},{1,9},{2,10},{3,11},{4,12},{5,13},{6,14},{7,15},{8,0},{9,1},... | collective-permute-start | bytes 1769480 | tf_op jit(solution)/shard_map/ppermute | solution.py:59
  501.8 26.0 %collective-permute-start.92 = (bf16[4,2,48,768]{3,2,1,0:T(8,128)(2,1)}, bf16[4,2,48,768]{3,2,1,0:T(8,128)(2,1)}, u32[]{:S(2)}, u32[]{:S(2)}) collective-permute-start(bf16[4,2,48,768]{3,2,1,0:T(8,128)(2,1)} %get-tuple-element.248), channel_id=1, source_target_pairs={{0,12},{1,13},{2,14},{3,15},{4,0},{5,1},{6,2},{7,3},{8,4},{9,5},{1... | collective-permute-start | bytes 1769480 | tf_op jit(solution)/shard_map/ppermute | solution.py:59
  504.5 28.8 %collective-permute-start.70 = (bf16[144,768]{1,0:T(8,128)(2,1)}, bf16[144,768]{1,0:T(8,128)(2,1)S(1)}, u32[]{:S(2)}, u32[]{:S(2)}) collective-permute-start(bf16[144,768]{1,0:T(8,128)(2,1)} %get-tuple-element.307), channel_id=1, source_target_pairs={{0,64},{64,0},{1,65},{65,1},{2,66},{66,2},{3,67},{67,3},{4,68},{68... | collective-permute-start | bytes 663560 | tf_op jit(solution)/shard_map/ppermute | solution.py:32
  507.6 26.6 %collective-permute-start.85 = (f32[4,12,768]{2,1,0:T(8,128)S(1)}, f32[4,12,768]{2,1,0:T(8,128)S(1)}, u32[]{:S(2)}, u32[]{:S(2)}) collective-permute-start(f32[4,12,768]{2,1,0:T(8,128)S(1)} %get-tuple-element.313), channel_id=1, source_target_pairs={{0,64},{64,0},{1,65},{65,1},{2,66},{66,2},{3,67},{67,3},{4,68},{68... | collective-permute-start | bytes 442376 | tf_op jit(solution)/shard_map/ppermute | solution.py:32
  (197 other events, 1675.6 us)
Sparse Core Ops, SparseCore 0:
  117.2 54.3 all-gather.2
  299.4 76.7 reduce-scatter.3

commit v5 on v4

--- a/solution.py
+++ b/solution.py
@@ -1,4 +1,3 @@
-import math
 from functools import partial
 
 import jax
@@ -36,42 +35,6 @@
     return lax.ppermute(v, "seq", [(i, (i + d) % N_SEQ) for i in range(N_SEQ)])
 
 
-def hop(v, axis, d):
-    route = []
-    for z in range(4):
-        for x in range(4):
-            to = ((z + d) % 4) * 4 + x if axis == "z" else z * 4 + (x + d) % 4
-            route.append((z * 4 + x, to))
-    return lax.ppermute(v, "shard", route)
-
-
-def place(axis):
-    i = lax.axis_index("shard")
-    return i // 4 if axis == "z" else lax.rem(i, 4)
-
-
-def hop(v, axis, d):
-    route = []
-    for z in range(4):
-        for x in range(4):
-            to = ((z + d) % 4) * 4 + x if axis == "z" else z * 4 + (x + d) % 4
-            route.append((z * 4 + x, to))
-    return lax.ppermute(v, "shard", route)
-
-
-def from_ring(v, axis):
-    return [v] + [hop(v, axis, -d) for d in (1, 2, 3)]
-
-
-def along_ring(blocks, axis):
-    return [blocks[0]] + [hop(blocks[d], axis, d) for d in (1, 2, 3)]
-
-
-def where_shard():
-    i = lax.axis_index("shard").astype(jnp.int32)
-    return jnp.stack([i // 4, lax.rem(i, 4)])
-
-
 def pick(v, i):
     return lax.dynamic_index_in_dim(v, i, 0, keepdims=False)
 
@@ -124,9 +87,8 @@
     return jax.ShapeDtypeStruct(dims, kind)
 
 
-def call(body, outs, ins, name, flops, scalars=0, scratch=()):
+def call(body, outs, ins, name, scalars=0, scratch=()):
     specs = [smem()] * scalars + [vmem()] * (len(ins) - scalars)
-    moved = sum(math.prod(v.shape) * v.dtype.itemsize for v in list(ins) + list(outs))
     return pl.pallas_call(
         body,
         out_shape=outs,
@@ -134,7 +96,6 @@
         out_specs=[vmem()] * len(outs),
         scratch_shapes=list(scratch),
         name=name,
-        cost_estimate=pl.CostEstimate(flops=int(flops), bytes_accessed=moved, transcendentals=0),
         compiler_params=pltpu.CompilerParams(vmem_limit_bytes=LIMIT),
     )(*ins)
 
@@ -171,9 +132,8 @@
         + [shape((SEQ, D), BF16), shape((SEQ, 576), BF16), shape((SEQ, 128), F32)],
         [*x_blocks, w_mix, gains],
         "attention",
-        2 * SEQ * D * 576 + 3 * 4 * SEQ * SEQ * 64,
-    )
-    return outs[:4], *outs[4:]
+    )
+    return list(outs[:4]), *outs[4:]
 
 
 def attend_back_kernel(
@@ -208,7 +168,7 @@
     small = small_ref[...] + dot(high, column, 0, 0) + dot(low, column, 0, 0)
     grad = dot(normed, d_packed, 0, 0)
     grad = jnp.concatenate([grad, small, jnp.zeros((D, 128), F32)], axis=1)
-    grad_ref[...] = by_shard(grad.astype(BF16))
+    grad_ref[...] = grad.astype(BF16)
 
 
 def attend_back(x_all, w_mix, gains, packed, logs, d_heads, small):
@@ -217,7 +177,6 @@
         [shape((ROWS, D), BF16)] * 4 + [shape((D, D), BF16)],
         [x_all, w_mix, gains, packed, logs, *d_heads, small],
         "attention_back",
-        4 * SEQ * D * 576 + 3 * 10 * SEQ * SEQ * 64,
         scratch=[pltpu.VMEM((SEQ, 576), BF16), pltpu.VMEM((SEQ, 192), BF16)],
     )
     return outs[:4], outs[4]
@@ -232,132 +191,28 @@
     return (lax.broadcasted_iota(jnp.int32, (D, D), 1) == source).astype(BF16)
 
 
-def by_shard(v):
-    return dot(order_rows(N_SEQ, N_SHARD), v, 1, 0).astype(BF16)
-
-
-def unpack_kernel(where_ref, b0, b1, b2, b3, rows_ref, back_ref, all_ref):
-    z, x = where_ref[0], where_ref[1]
-    for dz, ref in enumerate((b0, b1, b2, b3)):
-        for dx in range(4):
-            all_ref[lax.rem(z + dz, 4) * 4 + lax.rem(x + dx, 4)] = ref[dx]
-    order = order_rows(N_SHARD, N_SEQ)
+def unpack_kernel(all_ref, rows_ref, back_ref):
     whole = all_ref[...].reshape(D, 832)
-    ordered = dot(order, whole, 1, 0).astype(BF16)
+    ordered = dot(order_rows(N_SHARD, N_SEQ), whole, 1, 0).astype(BF16)
     rows_ref[...] = ordered[:, :640]
     for chunk in range(N_SEQ):
         back_ref[:, 192 * chunk : 192 * (chunk + 1)] = ordered[192 * chunk : 192 * (chunk + 1), 640:]
 
 
-def unpack(where, blocks):
-    return call(
-        unpack_kernel,
-        [shape((D, 640), BF16), shape((192, D), BF16)],
-        [where, *blocks],
-        "unpack",
-        2 * D * D * 832,
-        scalars=1,
-        scratch=[pltpu.VMEM((N_SHARD, 48, 832), BF16)],
-    )
-
-
-def order_kernel(where_ref, a0, a1, a2, a3, b0, b1, b2, b3, out_ref):
-    z, x = where_ref[0], where_ref[1]
-    firsts, seconds = (a0, a1, a2, a3), (b0, b1, b2, b3)
-    for dz in range(4):
-        for dx in range(4):
-            place = lax.rem(z + dz, 4) * 4 + lax.rem(x + dx, 4)
-            out_ref[place, 0:2] = firsts[dz][dx]
-            out_ref[place, 2:4] = seconds[dx][dz]
-
-
-def order(where, firsts, seconds):
-    return call(
-        order_kernel,
-        [shape((N_SHARD, 4, 48, D), BF16)],
-        [where, *firsts, *seconds],
-        "order",
-        0,
-        scalars=1,
-    )[0]
-
-
-def arrange_kernel(cut, where_ref, *refs):
-    z, x = where_ref[0], where_ref[1]
-    if cut:
-        ka, ga, *outs = refs
-        firsts, seconds = [(v, slice(0, 2)) for v in (ka, ga)], [(v, slice(2, 4)) for v in (ka, ga)]
-    else:
-        ka, ga, kb, gb, *outs = refs
-        firsts, seconds = [(v, slice(None)) for v in (ka, ga)], [(v, slice(None)) for v in (kb, gb)]
-    for d in range(4):
-        for o in range(4):
-            there = o * 4 + lax.rem(x + d, 4)
-            (keep, part), (got, _) = firsts
-            outs[d][o] = (keep[there, part].astype(F32) + got[there, part].astype(F32)).astype(BF16)
-            there = lax.rem(z + d, 4) * 4 + o
-            (keep, part), (got, _) = seconds
-            outs[4 + d][o] = (keep[there, part].astype(F32) + got[there, part].astype(F32)).astype(BF16)
-
-
-def arrange(where, pairs):
-    cut = len(pairs) == 2
-    dims = (4, 2, 48, D) if cut else (4, 48, D)
-    outs = call(
-        partial(arrange_kernel, cut), [shape(dims, BF16)] * 8, [where, *pairs], "arrange", 0, scalars=1
-    )
-    return outs[:4], outs[4:]
-
-
-def add_up_kernel(where_ref, *refs):
-    z, x = where_ref[0], where_ref[1]
-    for half, here in ((0, z), (1, x)):
-        blocks, outs = refs[4 * half : 4 * half + 4], refs[8 + 4 * half : 12 + 4 * half]
-        for d in range(4):
-            there = lax.rem(here + d, 4)
-            total = blocks[0][there].astype(F32)
-            for other in blocks[1:]:
-                total = total + other[there].astype(F32)
-            outs[d][...] = total.astype(BF16)
-
-
-def add_up(where, firsts, seconds):
-    dims = firsts[0].shape[1:]
-    outs = call(
-        add_up_kernel, [shape(dims, BF16)] * 8, [where, *firsts, *seconds], "add_up", 0, scalars=1
-    )
-    return outs[:4], outs[4:]
-
-
-def last_kernel(*refs):
-    for half in range(2):
-        total = refs[4 * half][...].astype(F32)
-        for d in (1, 2, 3):
-            total = total + refs[4 * half + d][...].astype(F32)
-        refs[8][half] = total.astype(BF16)
-
-
-def last(firsts, seconds):
-    dims = firsts[0].shape
-    return call(last_kernel, [shape((2,) + dims, BF16)], [*firsts, *seconds], "last", 0)[0]
-
-
-def scatter_pair(where, *pairs):
-    firsts, seconds = arrange(where, pairs)
-    firsts, seconds = add_up(where, along_ring(firsts, "x"), along_ring(seconds, "z"))
-    return last(along_ring(firsts, "z"), along_ring(seconds, "x"))
+def unpack(whole):
+    return call(unpack_kernel, [shape((D, 640), BF16), shape((192, D), BF16)], [whole], "unpack")
 
 
 def middle_kernel(
-    extra, me_ref, x_ref, g0, g1, g2, g3, w_ref, router_ref, gain_ref, route_ref, *refs
+    extra, me_ref, x_ref, g0, g1, g2, g3, w0, w1, w2, w3, router_ref, gain_ref, route_ref, *refs
 ):
     me = me_ref[0]
     if extra:
         d_out_ref, *refs = refs
     residual_ref, normed_ref, gates_ref, chosen_ref, high_ref, low_ref, *sent = refs
     residual = x_ref[...].astype(F32)
-    for d, ref in enumerate((g0, g1, g2, g3)):
-        residual = residual + dot(ref[...], w_ref[d], 1, 0)
+    for ref, w_ref in zip((g0, g1, g2, g3), (w0, w1, w2, w3)):
+        residual = residual + dot(ref[...], w_ref[...], 1, 0)
     residual_ref[...] = residual
     n, _ = norm_parts(residual)
     normed = (n * gain_ref[5:6, :]).astype(BF16)
@@ -416,9 +271,8 @@
             shape((ROWS, 320), BF16),
         ]
         + [shape(sent, BF16)] * 4,
-        [me, x, *gathered, w_back, router, gains, route_ids] + ([d_out] if extra else []),
+        [me, x, *gathered, *w_back, router, gains, route_ids] + ([d_out] if extra else []),
         "middle",
-        2 * ROWS * D * (D + 320),
         scalars=1,
     )
     return *outs[:6], outs[6:]
@@ -460,8 +314,7 @@
     return pl.BlockSpec((N_SHARD, 2, 48, 768), lambda i: (0, i, 0, 0))
 
 
-def grid_call(body, outs, out_specs, ins, in_specs, name, flops, scratch):
-    moved = sum(math.prod(v.shape) * v.dtype.itemsize for v in list(ins) + outs)
+def grid_call(body, outs, out_specs, ins, in_specs, name, scratch):
     return pl.pallas_call(
         body,
         grid=(2,),
@@ -470,7 +323,6 @@
         out_specs=out_specs,
         scratch_shapes=scratch,
         name=name,
-        cost_estimate=pl.CostEstimate(flops=flops, bytes_accessed=moved, transcendentals=0),
         compiler_params=pltpu.CompilerParams(
             vmem_limit_bytes=LIMIT, dimension_semantics=("arbitrary",)
         ),
@@ -485,7 +337,6 @@
         [*blocks, *packs],
         [whole_block((CAP, D))] * 4 + [pack_block()] * 2,
         "expert",
-        4 * 320 * D * FF,
         [pltpu.VMEM((320, D), BF16), pltpu.VMEM((320, D), F32)],
     )
 
@@ -542,31 +393,41 @@
         [*blocks, *packs],
         [block] * len(blocks) + [pack_block()] * 2,
         "expert_back",
-        8 * 320 * D * FF,
         [pltpu.VMEM((320, D), F32)] * 2,
     )
     return outs[:4], *outs[4:]
 
 
-def expert_grad_kernel(rows_ref, d_result_ref, act_ref, dh_ref, out_ref):
-    grad = dot(rows_ref[...], dh_ref[...], 0, 0).astype(BF16)
-    out_ref[:, 0] = grad.reshape(N_SHARD, 48, 768)
-    grad = dot(act_ref[...], d_result_ref[...], 0, 0).astype(BF16)
-    out_ref[:, 1] = grad.reshape(N_SHARD, 48, 768)
-
-
-def expert_grad(rows, d_result, active, d_hidden):
-    half = pl.BlockSpec((320, 768), lambda i: (0, i))
-    return grid_call(
-        expert_grad_kernel,
-        [shape((N_SHARD, 4, 48, 768), BF16)],
-        [pack_block()],
-        [rows, d_result, active, d_hidden],
-        [whole_block((320, D))] * 2 + [half] * 2,
-        "expert_grad",
-        2 * 320 * D * FF,
-        [],
-    )[0]
+def expert_grads_kernel(core_ref, rows_ref, d_result_ref, act_own, dh_own, act_other, dh_other, out_ref):
+    for place, act_ref, dh_ref in ((0, act_own, dh_own), (1, act_other, dh_other)):
+        @pl.when(pl.program_id(0) == place)
+        def _():
+            grad = dot(rows_ref[...], dh_ref[...], 0, 0).astype(BF16)
+            out_ref[0, :, 0] = grad.reshape(N_SHARD, 48, 768)
+            grad = dot(act_ref[...], d_result_ref[...], 0, 0).astype(BF16)
+            out_ref[0, :, 1] = grad.reshape(N_SHARD, 48, 768)
+
+
+def expert_grads(core, rows, d_result, act_own, dh_own, act_other, dh_other):
+    whole = pl.BlockSpec((320, D), lambda h, i, c: (0, 0))
+    mine = pl.BlockSpec((320, 768), lambda h, i, c: (0, jnp.where(h == 0, i, 1)))
+    theirs = pl.BlockSpec((320, 768), lambda h, i, c: (0, jnp.where(h == 0, 0, i)))
+    return pl.pallas_call(
+        expert_grads_kernel,
+        out_shape=shape((2, N_SHARD, 4, 48, D), BF16),
+        grid_spec=pltpu.PrefetchScalarGridSpec(
+            num_scalar_prefetch=1,
+            grid=(2, 2),
+            in_specs=[whole, whole, mine, mine, theirs, theirs],
+            out_specs=pl.BlockSpec(
+                (1, N_SHARD, 2, 48, D), lambda h, i, c: (jnp.where(h == 0, c[0], 1 - c[0]), 0, i, 0, 0)
+            ),
+        ),
+        name="expert_grads",
+        compiler_params=pltpu.CompilerParams(
+            vmem_limit_bytes=LIMIT, dimension_semantics=("arbitrary", "arbitrary")
+        ),
+    )(core, rows, d_result, act_own, dh_own, act_other, dh_other)
 
 
 def combine_kernel(residual_ref, high_ref, low_ref, r0, r1, r2, r3, out_ref, rows_ref):
@@ -583,7 +444,6 @@
         [shape((ROWS, D), BF16)],
         [residual, high, low, *blocks],
         "combine",
-        4 * ROWS * D * 320,
         scratch=[pltpu.VMEM((320, D), BF16)],
     )[0]
 
@@ -594,7 +454,7 @@
     blocks, refs = refs[:count], refs[count:]
     gathered, refs = refs[:4], refs[4:]
     (
-        chosen_ref, gates_ref, residual_ref, normed_ref, gain_ref, w_ref,
+        chosen_ref, gates_ref, residual_ref, normed_ref, gain_ref, w0, w1, w2, w3,
         d_residual_ref, small_ref, grad_ref, m0, m1, m2, m3, rows_ref, d_rows_ref, back_ref,
     ) = refs
     for d in range(N_SEQ):
@@ -621,11 +481,11 @@
     d_residual = d_out.astype(F32) + norm_back(n, inverse, gain_ref[5:6, :], d_normed)
     d_residual_ref[...] = d_residual
     d_branch = d_residual.astype(BF16)
-    for d, ref in enumerate((m0, m1, m2, m3)):
+    for d, (ref, w_ref) in enumerate(zip((m0, m1, m2, m3), (w0, w1, w2, w3))):
         group = lax.rem(me - d + N_SEQ, N_SEQ)
-        ref[...] = dot(d_branch, w_ref[d], 1, 1).astype(BF16)
+        ref[...] = dot(d_branch, w_ref[...], 1, 1).astype(BF16)
         back_ref[group] = dot(gathered[d][...], d_branch, 0, 0).astype(BF16)
-    grad_ref[...] = by_shard(back_ref[...].reshape(D, D))
+    grad_ref[...] = back_ref[...].reshape(D, D)
     high, low = two_parts(d_logits)
     small = dot(normed_ref[...], high, 0, 0) + dot(normed_ref[...], low, 0, 0)
     column = (lax.broadcasted_iota(jnp.int32, (ROWS, 128), 1) == 5).astype(BF16)
@@ -643,9 +503,8 @@
             shape((D, D), BF16),
         ]
         + [shape((ROWS, 192), BF16)] * 4,
-        [me, d_out, *blocks, *gathered, chosen, gates, residual, normed, gains, w_back],
+        [me, d_out, *blocks, *gathered, chosen, gates, residual, normed, gains, *w_back],
         "middle_back",
-        2 * ROWS * D * (2 * D + 640),
         scalars=1,
         scratch=[pltpu.VMEM((320, D), BF16)] * 2 + [pltpu.VMEM((N_SEQ, 192, D), BF16)],
     )
@@ -674,12 +533,11 @@
         [shape((ROWS, D), BF16)] + [shape((CAP, D), BF16)] * (4 if further else 0),
         [d_residual, x, gains, *blocks] + (list(weights) if further else []),
         "finish",
-        4 * ROWS * D * 320,
     )
     return outs[0], outs[1:]
 
 
-def attention_weights(where, w_qkv, w_proj, w_route, gain_attn, gain_ffn):
+def attention_weights(w_qkv, w_proj, w_route, gain_attn, gain_ffn):
     mine = w_qkv.reshape(12, 3, N_SEQ, 192).transpose(2, 0, 1, 3).reshape(N_SEQ, 12, 576)
     small = jnp.concatenate(
         [w_route, gain_attn[:, None], gain_ffn[:, None], jnp.zeros((12, 58), BF16)], axis=1
@@ -688,8 +546,8 @@
     arrived = lax.all_to_all(mine, "seq", 0, 0, tiled=True).reshape(48, 640)
     back = w_proj.reshape(12, N_SEQ, 192).transpose(1, 0, 2).reshape(48, 192)
     pack = jnp.concatenate([arrived, back], axis=1)
-    near = jnp.stack(from_ring(pack, "x"))
-    return unpack(where, from_ring(near, "z"))
+    whole = lax.all_gather(pack, "shard", axis=0, tiled=False)
+    return whole, *unpack(whole)
 
 
 def both_layers(mine):
@@ -708,49 +566,44 @@
     return [jnp.where(core == s, mine, arrived) for s in range(2)]
 
 
-def join_experts(own, other):
-    return (own.astype(F32) + swap(other).astype(F32)).astype(BF16)
-
-
-def scatter_beside(v):
-    return lax.psum_scatter(v, "shard", scatter_dimension=0, tiled=True)[0]
-
-
 def shards(images_in, out_grad, routes, w_qkv, w_proj, w_route, gain_attn, gain_ffn, w_in, w_out):
     core = lax.axis_index("section")
     me = lax.axis_index("seq").astype(jnp.int32).reshape(1)
+    core_index = core.astype(jnp.int32).reshape(1)
     own_routes = routes[0, :, 0]
     mine = pick(own_routes, core)
     arrived = swap(pick(own_routes, 1 - core))
     route_of = (jnp.where(core == 0, mine, arrived), jnp.where(core == 0, arrived, mine))
     x0 = pick(images_in, core)[0]
     d_last = pick(out_grad, core)[0]
-    where = where_shard()
     halves = half_packs(w_in[0, 0], w_out[0, 0])
-    near_a = jnp.stack(from_ring(halves[0][0:2], "x"))
-    near_b = jnp.stack(from_ring(halves[0][2:4], "z"))
-    rows, back_rows = attention_weights(
-        where, w_qkv[0], w_proj[0], w_route[0], gain_attn[0], gain_ffn[0]
-    )
-    near_a, near_b, rows = lax.optimization_barrier((near_a, near_b, rows))
-    own = order(where, from_ring(near_a, "z"), from_ring(near_b, "x"))
-    experts = [(own, swap(own)), None]
+    whole, rows, back_rows = attention_weights(
+        w_qkv[0], w_proj[0], w_route[0], gain_attn[0], gain_ffn[0]
+    )
+    own = lax.all_gather(tie(halves[0], whole), "shard", axis=0, tiled=False)
+    x_blocks = [x0] + [turn(x0, -d) for d in (1, 2, 3)]
     attn_rows = both_layers(rows)
+    back_rows = both_layers(back_rows)
+    attn_rows[0], attn_rows[1], back_rows[0], back_rows[1] = lax.optimization_barrier(
+        (attn_rows[0], attn_rows[1], back_rows[0], back_rows[1])
+    )
     w_mix = [v[:, :576] for v in attn_rows]
     routers = [jnp.pad(v[:, 576:], ((0, 0), (0, 64))) for v in attn_rows]
     tables = [v[:, 576:584].T.astype(F32) for v in attn_rows]
-    w_back = both_layers(jnp.stack([back_rows] + [turn(back_rows, d) for d in (1, 2, 3)]))
+    w_back = [[back_rows[0]] + [turn(back_rows[0], d) for d in (1, 2, 3)], None]
+    experts = [None, None]
 
     saved = []
     x = x0
     layer_outs = []
     for s in range(2):
-        mixture, x_all, packed, logs = attend([x] + [turn(x, -d) for d in (1, 2, 3)], w_mix[s], tables[s])
+        if s == 1:
+            x_blocks = [x] + [turn(x, -d) for d in (1, 2, 3)]
+        mixture, x_all, packed, logs = attend(x_blocks, w_mix[s], tables[s])
         if s == 0:
-            later = tie(halves[1], (mixture[0], own))
-            later = lax.all_gather(later, "shard", axis=0, tiled=False)
+            w_back[0], mixture = lax.optimization_barrier((w_back[0], mixture))
         else:
-            later = tie(later, mixture[0])
+            later, mixture[0] = lax.optimization_barrier((later, mixture[0]))
             experts[1] = (later, swap(later))
         gathered = send_out(mixture)
         d_out = d_last if s == 1 else None
@@ -760,7 +613,14 @@
         blocks = send_out(buffer)
         kept = (x, x_all, packed, logs, gathered, residual, normed, gates, chosen, high, low, blocks)
         if s == 0:
-            returned = send_back(expert_run(blocks, experts[s]))
+            own, blocks[1] = lax.optimization_barrier((own, blocks[1]))
+            experts[0] = (own, swap(own))
+            later = lax.all_gather(tie(halves[1], own), "shard", axis=0, tiled=False)
+            later_back = tie(back_rows[1], blocks[1])
+            w_back[1] = [later_back] + [turn(later_back, d) for d in (1, 2, 3)]
+            result = expert_run(blocks, experts[s])
+            w_back[1], result = lax.optimization_barrier((w_back[1], result))
+            returned = send_back(result)
             x = combine(residual, high, low, returned)
             layer_outs.append(x)
             saved.append((kept, returned))
@@ -778,41 +638,33 @@
         if s == 1:
             sent, *states = expert_back(blocks, experts[s], True)
             arrived = send_back(sent)
-            first_arrival = arrived[1]
             layer_outs.append(combine(residual, high, low, [v[0] for v in arrived]))
         else:
             sent, *states = expert_back([*blocks, *send_out(d_buffer)], experts[s], False)
-            back = send_back(sent)
-            first_arrival = back[1]
-            arrived = [*returned, *back]
-        rows, d_result, act_own, act_other, dh_own, dh_other = states
-        if s == 1:
-            rows = tie(rows, first_arrival)
-        other = swap(expert_grad(rows, d_result, act_other, dh_other))
+            arrived = [*returned, *send_back(sent)]
         d_residual, small, grad_back, d_mixture = middle_back(
             me, d_out, arrived, gathered, chosen, gates, residual, normed, tables[s], w_back[s], s == 1
         )
         d_heads = send_back(d_mixture)
+        rows, d_result, act_own, act_other, dh_own, dh_other = states
         if s == 1:
-            rows = tie(rows, d_heads[1])
-        own = expert_grad(rows, d_result, act_own, dh_own)
-        if s == 1:
-            expert_sums[s] = scatter_beside((own.astype(F32) + other.astype(F32)).astype(BF16))
-        else:
-            expert_sums[s] = scatter_pair(where, own, other)
-            expert_sums[s] = expert_sums[s].reshape(4, 48, D)
+            rows = tie(rows, d_residual)
+        both = expert_grads(core_index, rows, d_result, act_own, dh_own, act_other, dh_other)
+        both = both.reshape(2 * N_SHARD, 4, 48, D)
+        expert_sums[s] = lax.psum_scatter(both, ("section", "shard"), scatter_dimension=0, tiled=True)[0]
         d_normed, grad_mix = attend_back(x_all, w_mix[s], tables[s], packed, logs, d_heads, small)
         d_parts = send_out(d_normed)
         keep = jnp.where(core == 0, grad_mix, grad_back)
         give = jnp.where(core == 0, grad_back, grad_mix)
-        attn_grads[s] = (keep.reshape(N_SHARD, 48, D), swap(give).reshape(N_SHARD, 48, D))
+        attn_grads[s] = (keep.astype(F32) + swap(give).astype(F32)).astype(BF16)
         weights = saved[0][0][9:11] if s == 1 else None
         d_out, d_buffer = finish(d_residual, x, tables[s], d_parts, weights)
         in_grads[s] = d_out
 
-    attn_sum = scatter_pair(where, *attn_grads[0], *attn_grads[1])
-    attn_sum = attn_sum.reshape(2, N_SEQ, 12, D).transpose(1, 2, 0, 3).reshape(N_SEQ, 12, 2 * D)
-    attn_sum = lax.all_to_all(attn_sum, "seq", 0, 0, tiled=True).astype(F32)
+    pair = jnp.concatenate(attn_grads, axis=1).reshape(N_SEQ * N_SHARD, 12, 2 * D)
+    pair = tie(pair, d_parts)
+    arrived = lax.all_to_all(pair, ("seq", "shard"), 0, 0, tiled=True)
+    attn_sum = jnp.sum(arrived.reshape(N_SEQ, N_SHARD, 12, 2 * D).astype(F32), axis=1)
     attn_sums = [attn_sum[:, :, :D], attn_sum[:, :, D:]]
 
     def settle(pair):

time: 581 us -> 502 us (0.86)
  starting transfers between devices: 150 us -> 94.4 us
  Pallas kernels: 150 us -> 115 us
  waiting for transfers between devices: 191 us -> 208 us
  other arithmetic: 23.7 us -> 17 us
    ppermute x42 -> x0, waiting for transfers between devices: 81.9 us -> none  [hop(): return lax.ppermute(v, 'shard', route)]
    ppermute x42 -> x0, starting transfers between devices: 55.4 us -> none  [hop(): return lax.ppermute(v, 'shard', route)]
    all_to_all x1, waiting for transfers between devices: 0.01 us -> 38.7 us  [shards(): arrived = lax.all_to_all(pair, ('seq', 'shard'), 0, 0, tiled=True)]
    all_gather x1 -> x3, waiting for transfers between devices: 0.01 us -> 37.8 us  [the longest x1 37.8 us: attention_weights(): whole = lax.all_gather(pack, 'shard', axis=0, tiled=False)]
    pallas_call x20 -> x13, Pallas kernels: 96.6 us -> 65.8 us  [call(): pl.pallas_call(body, out_shape=outs, in_specs=specs, out_specs=[vmem()] *...]
    pallas_call x7 -> x3, Pallas kernels: 52.9 us -> 29.2 us  [grid_call(): pl.pallas_call(body, grid=(2,), out_shape=outs, in_specs=in_specs, out_sp...]
    pallas_call x0 -> x2, Pallas kernels: none -> 19.8 us  [expert_grads(): pl.pallas_call(expert_grads_kernel, out_shape=shape((2, N_SHARD, 4, 48, D...]
    reduce_scatter x0 -> x2, waiting for transfers between devices: none -> 18.6 us  [shards(): lax.psum_scatter(both, ('section', 'shard'), scatter_dimension=0, tiled=T...]
  transfers between devices with their start and end apart: 105 -> 67, of which waited for: 54 -> 40; matrix products, arithmetic and copies ran while one was open for 6% -> 7% of each run, Pallas kernels for 21% -> 18%
where the time goes in v5:
time: 502 us; the launch traced here: 493 us
  waiting for transfers between devices  208 us (41%)
  Pallas kernels  115 us (23%)
  starting transfers between devices  94.4 us (19%)
  local copies, waits for them, and re-layouts  43.7 us (9%)
  other arithmetic  17 us (3%)
  between operations  14.8 us (3%)
    ppermute x48, waiting for transfers between devices, turn(): return lax.ppermute(v, 'seq', [(i, (i + d) % N_SEQ) for i in range(N_SEQ)])  108 us
    pallas_call x13, Pallas kernels, call(): pl.pallas_call(body, out_shape=outs, in_specs=specs, out_specs=[vmem()] *...  65.8 us
    ppermute x48, starting transfers between devices, turn(): return lax.ppermute(v, 'seq', [(i, (i + d) % N_SEQ) for i in range(N_SEQ)])  50.3 us
    all_to_all x1, waiting for transfers between devices, shards(): arrived = lax.all_to_all(pair, ('seq', 'shard'), 0, 0, tiled=True)  38.7 us
    all_gather x1, waiting for transfers between devices, attention_weights(): whole = lax.all_gather(pack, 'shard', axis=0, tiled=False)  37.8 us
    ppermute x12, starting transfers between devices, swap(): return lax.ppermute(v, 'section', [(0, 1), (1, 0)])  30.7 us
    pallas_call x3, Pallas kernels, grid_call(): pl.pallas_call(body, grid=(2,), out_shape=outs, in_specs=in_specs, out_sp...  29.2 us
    pallas_call x2, Pallas kernels, expert_grads(): pl.pallas_call(expert_grads_kernel, out_shape=shape((2, N_SHARD, 4, 48, D...  19.8 us
  transfers between devices with their start and end apart: 67, of which 40 were waited for; matrix products, arithmetic and copies ran while one was open for 7% of the time, Pallas kernels for 18%

profile of v5, /device:TPU:1, one launch (start us, length us, event | category | flops | bytes accessed | tf_op | source)
XLA Modules:
  0.0 492.7 jit_solution(13611607426686133387)
XLA Ops:
  11.7 5.0 %all-to-all-start = ((bf16[4,12,640]{2,1,0:T(8,128)(2,1)}), bf16[4,12,640]{2,1,0:T(8,128)(2,1)S(1)}, u32[]{:S(2)}, u32[]{:S(2)}) async-start(bf16[4,12,640]{2,1,0:T(8,128)(2,1)} %copy.103), calls=%async_computation | async-start | bytes 163840 | tf_op jit(solution)/shard_map/all_to_all | solution.py:546
  28.1 37.8 %all-gather.7.cloned.1.call-done = bf16[768,832]{1,0:T(8,128)(2,1)} async-done(((bf16[48,832]{1,0:T(8,128)(2,1)}), bf16[768,832]{1,0:T(8,128)(2,1)}) %all-gather.7.cloned.1.call-update) | async-done | bytes 1277968 | tf_op jit(solution)/shard_map/all_gather | solution.py:549
  92.7 8.0 %collective-permute-done.5.x1 = bf16[144,768]{1,0:T(8,128)(2,1)S(1)} collective-permute-done((bf16[144,768]{1,0:T(8,128)(2,1)}, bf16[144,768]{1,0:T(8,128)(2,1)S(1)}, u32[]{:S(2)}, u32[]{:S(2)}) %collective-permute-start.5) | collective-permute-done | bytes 221216 | tf_op jit(solution)/shard_map/ppermute | solution.py:35
  101.3 6.0 %attention.2 = (bf16[144,192]{1,0:T(8,128)(2,1)}, bf16[144,192]{1,0:T(8,128)(2,1)}, bf16[144,192]{1,0:T(8,128)(2,1)}, bf16[144,192]{1,0:T(8,128)(2,1)}, bf16[576...) custom-call(bf16[144,768]{1,0:T(8,128)(2,1)} %dynamic-slice_bitcast_fusion.2.x0.x_ref, ...), custom_call_target="tpu_custom_call" | custom-call | tf_op jit(solution)/shard_map/attention/pallas_call | solution.py:92
  120.6 4.7 collective-permute-done.13.r1.refs_1_
  133.4 15.0 %collective-permute-done.17.r2.refs_2_ = bf16[80,768]{1,0:T(8,128)(2,1)S(1)} collective-permute-done((bf16[80,768]{1,0:T(8,128)(2,1)}, bf16[80,768]{1,0:T(8,128)(2,1)S(1)}, u32[]{:S(2)}, u32[]{:S(2)}) %collective-permute-start.17) | collective-permute-done | bytes 122912 | tf_op jit(solution)/shard_map/ppermute | solution.py:35
  154.5 7.0 %expert.1 = (bf16[80,768]{1,0:T(8,128)(2,1)}, bf16[80,768]{1,0:T(8,128)(2,1)}, bf16[80,768]{1,0:T(8,128)(2,1)}, bf16[80,768]{1,0:T(8,128)(2,1)}) custom-call(bf16[80,768]{1,0:T(8,128)(2,1)} %get-tuple-element.151.r0.refs_0_, bf16[80,768]{1,0:T(8,128)(2,1)} %copy-done.20, bf16[80,768]{1,0:T(8,128)(2,1)} %copy-done.21, bf16[80,768]{1,0:T(8,128)(2,1)} %copy-done.22, ...), custom_call_target="tpu_custom_call" | custom-call | tf_op jit(solution)/shard_map/expert/pallas_call | solution.py:318
  176.3 6.4 %collective-permute-done.25.x3 = bf16[144,768]{1,0:T(8,128)(2,1)S(1)} collective-permute-done((bf16[144,768]{1,0:T(8,128)(2,1)}, bf16[144,768]{1,0:T(8,128)(2,1)S(1)}, u32[]{:S(2)}, u32[]{:S(2)}) %collective-permute-start.25) | collective-permute-done | bytes 221216 | tf_op jit(solution)/shard_map/ppermute | solution.py:35
  184.1 6.1 %attention.3 = (bf16[144,192]{1,0:T(8,128)(2,1)}, bf16[144,192]{1,0:T(8,128)(2,1)}, bf16[144,192]{1,0:T(8,128)(2,1)}, bf16[144,192]{1,0:T(8,128)(2,1)}, bf16[576...) custom-call(bf16[144,768]{1,0:T(8,128)(2,1)} %combine.2.x0.x_ref, bf16[144,768]{1,0:T(8,128)(2,1)} %copy-done.47, ...), custom_call_target="tpu_custom_call" | custom-call | tf_op jit(solution)/shard_map/attention/pallas_call | solution.py:92
  215.4 6.8 %collective-permute-done.30.refs_2_ = bf16[2,80,768]{2,1,0:T(8,128)(2,1)S(1)} collective-permute-done((bf16[2,80,768]{2,1,0:T(8,128)(2,1)}, bf16[2,80,768]{2,1,0:T(8,128)(2,1)S(1)}, u32[]{:S(2)}, u32[]{:S(2)}) %collective-permute-start.30) | collective-permute-done | bytes 245792 | tf_op jit(solution)/shard_map/ppermute | solution.py:35
  223.0 11.6 %expert_back.2 = (bf16[2,80,768]{2,1,0:T(8,128)(2,1)}, bf16[2,80,768]{2,1,0:T(8,128)(2,1)}, bf16[2,80,768]{2,1,0:T(8,128)(2,1)}, bf16[2,80,768]{2,1,0:T(8,128)(2...) custom-call(bf16[2,80,768]{2,1,0:T(8,128)(2,1)} %get-tuple-element.1, ...), custom_call_target="tpu_custom_call" | custom-call | tf_op jit(solution)/shard_map/expert_back/pallas_call | solution.py:318
  238.3 9.2 %collective-permute-done.33.refs_1_ = bf16[2,80,768]{2,1,0:T(8,128)(2,1)S(1)} collective-permute-done((bf16[2,80,768]{2,1,0:T(8,128)(2,1)}, bf16[2,80,768]{2,1,0:T(8,128)(2,1)S(1)}, u32[]{:S(2)}, u32[]{:S(2)}) %collective-permute-start.33) | collective-permute-done | bytes 245792 | tf_op jit(solution)/shard_map/ppermute | solution.py:35
  252.8 5.6 %middle_back.2 = (f32[144,768]{1,0:T(8,128)}, f32[768,64]{1,0:T(8,128)}, bf16[768,768]{1,0:T(8,128)(2,1)}, bf16[144,192]{1,0:T(8,128)(2,1)}, bf16[144,192]{1,0:T...) custom-call(s32[1]{0:T(128)} %bitcast.me_ref, ...), custom_call_target="tpu_custom_call" | custom-call | tf_op jit(solution)/shard_map/middle_back/pallas_call | solution.py:92
  258.4 9.9 %expert_grads.3 = bf16[2,16,4,48,768]{4,3,2,1,0:T(8,128)(2,1)} custom-call(s32[1]{0:T(128)} %bitcast.34.core_ref, bf16[320,768]{1,0:T(8,128)(2,1)} %get-tuple-element.239.rows_ref, bf16[320,768]{1,0:T(8,128)(2,1)} %get-tuple-element.240.d_result_ref, bf16[320,1536]{1,0:T(8,128)(2,1)} %get-tuple-element.241.act_own, ...), custom_call_target="tpu_custom_call" | custom-call | tf_op jit(solution)/shard_map/expert_grads/pallas_call | solution.py:415
  276.3 10.0 %attention_back.2 = (bf16[144,768]{1,0:T(8,128)(2,1)}, bf16[144,768]{1,0:T(8,128)(2,1)}, bf16[144,768]{1,0:T(8,128)(2,1)}, bf16[144,768]{1,0:T(8,128)(2,1)}, bf16[768,768]{1,0:T(8,128)(2,1)}) custom-call(bf16[576,768]{1,0:T(8,128)(2,1)} %get-tuple-element.190.x_ref, bf16[768,576]{1,0:T(8,128)(2,1)} %copy.113.w_ref, ...), custom_call_target="tpu_custom_call" | custom-call | tf_op jit(solution)/shard_map/attention_back/pallas_call | solution.py:92
  289.1 5.2 %collective-permute-done.40.b1 = bf16[144,768]{1,0:T(8,128)(2,1)S(1)} collective-permute-done((bf16[144,768]{1,0:T(8,128)(2,1)}, bf16[144,768]{1,0:T(8,128)(2,1)S(1)}, u32[]{:S(2)}, u32[]{:S(2)}) %collective-permute-start.40) | collective-permute-done | bytes 221216 | tf_op jit(solution)/shard_map/ppermute | solution.py:35
  313.5 10.6 %expert_back.3 = (bf16[80,768]{1,0:T(8,128)(2,1)}, bf16[80,768]{1,0:T(8,128)(2,1)}, bf16[80,768]{1,0:T(8,128)(2,1)}, bf16[80,768]{1,0:T(8,128)(2,1)}, bf16[320,7...) custom-call(bf16[80,768]{1,0:T(8,128)(2,1)} %get-tuple-element.151.r, ...), custom_call_target="tpu_custom_call" | custom-call | tf_op jit(solution)/shard_map/expert_back/pallas_call | solution.py:318
  324.1 10.0 %expert_grads.2 = bf16[2,16,4,48,768]{4,3,2,1,0:T(8,128)(2,1)} custom-call(s32[1]{0:T(128)} %bitcast.34.core_ref, bf16[320,768]{1,0:T(8,128)(2,1)} %get-tuple-element.232.rows_ref, bf16[320,768]{1,0:T(8,128)(2,1)} %get-tuple-element.233.d_result_ref, bf16[320,1536]{1,0:T(8,128)(2,1)} %get-tuple-element.234.act_own, ...), custom_call_target="tpu_custom_call" | custom-call | tf_op jit(solution)/shard_map/expert_grads/pallas_call | solution.py:415
  343.2 5.6 %middle_back.3 = (f32[144,768]{1,0:T(8,128)}, f32[768,64]{1,0:T(8,128)}, bf16[768,768]{1,0:T(8,128)(2,1)}, bf16[144,192]{1,0:T(8,128)(2,1)}, bf16[144,192]{1,0:T...) custom-call(s32[1]{0:T(128)} %bitcast.me_ref, bf16[144,768]{1,0:T(8,128)(2,1)} %get-tuple-element.202.d_out_ref, ...), custom_call_target="tpu_custom_call" | custom-call | tf_op jit(solution)/shard_map/middle_back/pallas_call | solution.py:92
  351.0 4.7 collective-permute-start.57
  356.6 9.9 %attention_back.3 = (bf16[144,768]{1,0:T(8,128)(2,1)}, bf16[144,768]{1,0:T(8,128)(2,1)}, bf16[144,768]{1,0:T(8,128)(2,1)}, bf16[144,768]{1,0:T(8,128)(2,1)}, bf16[768,768]{1,0:T(8,128)(2,1)}) custom-call(bf16[576,768]{1,0:T(8,128)(2,1)} %get-tuple-element.215.x_ref, bf16[768,576]{1,0:T(8,128)(2,1)} %copy.108.w_ref, ...), custom_call_target="tpu_custom_call" | custom-call | tf_op jit(solution)/shard_map/attention_back/pallas_call | solution.py:92
  385.4 8.3 %all-to-all-start.1 = ((bf16[64,12,1536]{2,1,0:T(8,128)(2,1)}), bf16[64,12,1536]{2,1,0:T(8,128)(2,1)}, u32[]{:S(2)}, u32[]{:S(2)}) async-start(bf16[64,12,1536]{2,1,0:T(8,128)(2,1)} %reshape.189), calls=%async_computation.1 | async-start | bytes 6291456 | tf_op jit(solution)/shard_map/all_to_all | solution.py:666
  404.7 38.7 %all-to-all-done.1 = bf16[64,12,1536]{2,1,0:T(8,128)(2,1)} async-done(((bf16[64,12,1536]{2,1,0:T(8,128)(2,1)}), bf16[64,12,1536]{2,1,0:T(8,128)(2,1)}, u32[]{:S(2)}, u32[]{:S(2)}) %all-to-all-start.1) | async-done | bytes 2359328 | tf_op jit(solution)/shard_map/all_to_all | solution.py:666
  452.4 18.6 %reduce-scatter.3.cloned.1.call-done = bf16[1,4,48,768]{3,2,1,0:T(8,128)(2,1)} async-done(((bf16[32,4,48,768]{3,2,1,0:T(8,128)(2,1)}), bf16[1,4,48,768]{3,2,1,0:T(8,128)(2,1)}) %reduce-scatter.3.cloned.1.call-update) | async-done | bytes 294928 | tf_op jit(solution)/shard_map/reduce_scatter | solution.py:654
  (350 shorter events, 217.3 us)
Async XLA Ops:
  16.7 49.2 %all-gather.7.cloned.1.call-start = ((), (), s32[]{:S(2)}) async-start(), calls=%async_computation.6 | async-start | bytes 1462272 | tf_op jit(solution)/shard_map/all_gather | solution.py:549
  21.9 103.4 %all-gather.9.cloned.1.call-start = ((), (), s32[]{:S(2)}) async-start(), calls=%async_computation.7 | async-start | bytes 5013504 | tf_op jit(solution)/shard_map/all_gather | solution.py:583
  65.9 124.3 %all-gather.11.cloned.1.call-start = ((), (), s32[]{:S(2)}) async-start(), calls=%async_computation.8 | async-start | bytes 5013504 | tf_op jit(solution)/shard_map/all_gather | solution.py:618
  80.5 26.8 %collective-permute-start.4 = (bf16[192,768]{1,0:T(8,128)(2,1)}, bf16[192,768]{1,0:T(8,128)(2,1)}, u32[]{:S(2)}, u32[]{:S(2)}) collective-permute-start(bf16[192,768]{1,0:T(8,128)(2,1)} %get-tuple-element.139.w0.refs_17_), channel_id=1, source_target_pairs={{0,48},{16,0},{32,16},{48,32},{1,49},{17,1},{33,17},{49,33},{2,50}... | collective-permute-start | bytes 884744 | tf_op jit(solution)/shard_map/ppermute | solution.py:35
  81.7 25.7 %collective-permute-start.3 = (bf16[192,768]{1,0:T(8,128)(2,1)}, bf16[192,768]{1,0:T(8,128)(2,1)}, u32[]{:S(2)}, u32[]{:S(2)}) collective-permute-start(bf16[192,768]{1,0:T(8,128)(2,1)} %get-tuple-element.139.w0.refs_17_), channel_id=1, source_target_pairs={{0,32},{16,48},{32,0},{48,16},{1,33},{17,49},{33,1},{49,17},{2,34}... | collective-permute-start | bytes 884744 | tf_op jit(solution)/shard_map/ppermute | solution.py:35
  82.0 25.4 %collective-permute-start.2 = (bf16[192,768]{1,0:T(8,128)(2,1)}, bf16[192,768]{1,0:T(8,128)(2,1)}, u32[]{:S(2)}, u32[]{:S(2)}) collective-permute-start(bf16[192,768]{1,0:T(8,128)(2,1)} %get-tuple-element.139.w0.refs_17_), channel_id=1, source_target_pairs={{0,16},{16,32},{32,48},{48,0},{1,17},{17,33},{33,49},{49,1},{2,18}... | collective-permute-start | bytes 884744 | tf_op jit(solution)/shard_map/ppermute | solution.py:35
  82.7 17.9 %collective-permute-start.5 = (bf16[144,768]{1,0:T(8,128)(2,1)}, bf16[144,768]{1,0:T(8,128)(2,1)S(1)}, u32[]{:S(2)}, u32[]{:S(2)}) collective-permute-start(bf16[144,768]{1,0:T(8,128)(2,1)} %dynamic-slice_bitcast_fusion.2.x0.x_ref), channel_id=1, source_target_pairs={{0,48},{16,0},{32,16},{48,32},{1,49},{17,1},{33,17},{49,33},{2,50}... | collective-permute-start | bytes 663560 | tf_op jit(solution)/shard_map/ppermute | solution.py:35
  88.5 24.4 %collective-permute-start.11 = (s32[144,2]{1,0:T(8,128)S(1)}, s32[144,2]{1,0:T(8,128)}, u32[]{:S(2)}, u32[]{:S(2)}) collective-permute-start(s32[144,2]{1,0:T(8,128)S(1)} %bitcast.105), channel_id=1, source_target_pairs={{0,64},{64,0},{1,65},{65,1},{2,66},{66,2},{3,67},{67,3},{4,68},{68... | collective-permute-start | bytes 3464 | tf_op jit(solution)/shard_map/ppermute | solution.py:31
  125.3 327.1 %reduce-scatter.5.cloned.1.call-start = ((), (), s32[]{:S(2)}) async-start(), calls=%async_computation.5 | async-start | bytes 9732096 | tf_op jit(solution)/shard_map/reduce_scatter | solution.py:654
  125.4 27.0 %collective-permute-start.19 = (bf16[16,4,48,768]{3,2,1,0:T(8,128)(2,1)}, bf16[16,4,48,768]{3,2,1,0:T(8,128)(2,1)S(1)}, u32[]{:S(2)}, u32[]{:S(2)}) collective-permute-start(bf16[16,4,48,768]{3,2,1,0:T(8,128)(2,1)} %bitcast.84), channel_id=1, source_target_pairs={{0,64},{64,0},{1,65},{65,1},{2,66},{66,2},{3,67},{67,3},{4,68},{68... | collective-permute-start | bytes 14155784 | tf_op jit(solution)/shard_map/ppermute | solution.py:31
  128.3 33.2 %collective-permute-start.16 = (bf16[192,768]{1,0:T(8,128)(2,1)S(1)}, bf16[192,768]{1,0:T(8,128)(2,1)S(1)}, u32[]{:S(2)}, u32[]{:S(2)}) collective-permute-start(bf16[192,768]{1,0:T(8,128)(2,1)S(1)} %get-tuple-element.170.w0.refs_13_), channel_id=1, source_target_pairs={{0,48},{16,0},{32,16},{48,32},{1,49},{17,1},{33,17},{49,33},{2,50}... | collective-permute-start | bytes 884744 | tf_op jit(solution)/shard_map/ppermute | solution.py:35
  129.7 31.9 %collective-permute-start.15 = (bf16[192,768]{1,0:T(8,128)(2,1)S(1)}, bf16[192,768]{1,0:T(8,128)(2,1)S(1)}, u32[]{:S(2)}, u32[]{:S(2)}) collective-permute-start(bf16[192,768]{1,0:T(8,128)(2,1)S(1)} %get-tuple-element.170.w0.refs_13_), channel_id=1, source_target_pairs={{0,32},{16,48},{32,0},{48,16},{1,33},{17,49},{33,1},{49,17},{2,34}... | collective-permute-start | bytes 884744 | tf_op jit(solution)/shard_map/ppermute | solution.py:35
  129.7 31.9 %collective-permute-start.14 = (bf16[192,768]{1,0:T(8,128)(2,1)S(1)}, bf16[192,768]{1,0:T(8,128)(2,1)S(1)}, u32[]{:S(2)}, u32[]{:S(2)}) collective-permute-start(bf16[192,768]{1,0:T(8,128)(2,1)S(1)} %get-tuple-element.170.w0.refs_13_), channel_id=1, source_target_pairs={{0,16},{16,32},{32,48},{48,0},{1,17},{17,33},{33,49},{49,1},{2,18}... | collective-permute-start | bytes 884744 | tf_op jit(solution)/shard_map/ppermute | solution.py:35
  130.2 18.2 %collective-permute-start.17 = (bf16[80,768]{1,0:T(8,128)(2,1)}, bf16[80,768]{1,0:T(8,128)(2,1)S(1)}, u32[]{:S(2)}, u32[]{:S(2)}) collective-permute-start(bf16[80,768]{1,0:T(8,128)(2,1)} %get-tuple-element.152), channel_id=1, source_target_pairs={{0,32},{16,48},{32,0},{48,16},{1,33},{17,49},{33,1},{49,17},{2,34}... | collective-permute-start | bytes 368648 | tf_op jit(solution)/shard_map/ppermute | solution.py:35
  190.2 32.0 %collective-permute-start.32 = (bf16[16,4,48,768]{3,2,1,0:T(8,128)(2,1)}, bf16[16,4,48,768]{3,2,1,0:T(8,128)(2,1)}, u32[]{:S(2)}, u32[]{:S(2)}) collective-permute-start(bf16[16,4,48,768]{3,2,1,0:T(8,128)(2,1)} %bitcast.89), channel_id=1, source_target_pairs={{0,64},{64,0},{1,65},{65,1},{2,66},{66,2},{3,67},{67,3},{4,68},{68... | collective-permute-start | bytes 14155784 | tf_op jit(solution)/shard_map/ppermute | solution.py:31
  207.2 15.0 %collective-permute-start.30 = (bf16[2,80,768]{2,1,0:T(8,128)(2,1)}, bf16[2,80,768]{2,1,0:T(8,128)(2,1)S(1)}, u32[]{:S(2)}, u32[]{:S(2)}) collective-permute-start(bf16[2,80,768]{2,1,0:T(8,128)(2,1)} %get-tuple-element.179), channel_id=1, source_target_pairs={{0,32},{16,48},{32,0},{48,16},{1,33},{17,49},{33,1},{49,17},{2,34}... | collective-permute-start | bytes 737288 | tf_op jit(solution)/shard_map/ppermute | solution.py:35
  234.6 12.9 %collective-permute-start.33 = (bf16[2,80,768]{2,1,0:T(8,128)(2,1)}, bf16[2,80,768]{2,1,0:T(8,128)(2,1)S(1)}, u32[]{:S(2)}, u32[]{:S(2)}) collective-permute-start(bf16[2,80,768]{2,1,0:T(8,128)(2,1)} %get-tuple-element.183), channel_id=1, source_target_pairs={{0,48},{16,0},{32,16},{48,32},{1,49},{17,1},{33,17},{49,33},{2,50}... | collective-permute-start | bytes 737288 | tf_op jit(solution)/shard_map/ppermute | solution.py:35
  237.3 14.9 %collective-permute-start.35 = (bf16[2,80,768]{2,1,0:T(8,128)(2,1)}, bf16[2,80,768]{2,1,0:T(8,128)(2,1)S(1)}, u32[]{:S(2)}, u32[]{:S(2)}) collective-permute-start(bf16[2,80,768]{2,1,0:T(8,128)(2,1)} %get-tuple-element.185), channel_id=1, source_target_pairs={{0,16},{16,32},{32,48},{48,0},{1,17},{17,33},{33,49},{49,1},{2,18}... | collective-permute-start | bytes 737288 | tf_op jit(solution)/shard_map/ppermute | solution.py:35
  268.3 202.7 %reduce-scatter.3.cloned.1.call-start = ((), (), s32[]{:S(2)}) async-start(), calls=%async_computation.4 | async-start | bytes 9732096 | tf_op jit(solution)/shard_map/reduce_scatter | solution.py:654
  351.0 23.5 %collective-permute-start.57 = (bf16[768,768]{1,0:T(8,128)(2,1)S(1)}, bf16[768,768]{1,0:T(8,128)(2,1)S(1)}, u32[]{:S(2)}, u32[]{:S(2)}) collective-permute-start(bf16[768,768]{1,0:T(8,128)(2,1)S(1)} %broadcast_select_fusion), channel_id=1, source_target_pairs={{0,64},{64,0},{1,65},{65,1},{2,66},{66,2},{3,67},{67,3},{4,68},{68... | collective-permute-start | bytes 3538952 | tf_op jit(solution)/shard_map/ppermute | solution.py:31
  371.7 12.8 %collective-permute-start.53 = (bf16[144,768]{1,0:T(8,128)(2,1)S(1)}, bf16[144,768]{1,0:T(8,128)(2,1)S(1)}, u32[]{:S(2)}, u32[]{:S(2)}) collective-permute-start(bf16[144,768]{1,0:T(8,128)(2,1)S(1)} %copy-done.63), channel_id=1, source_target_pairs={{0,32},{16,48},{32,0},{48,16},{1,33},{17,49},{33,1},{49,17},{2,34}... | collective-permute-start | bytes 663560 | tf_op jit(solution)/shard_map/ppermute | solution.py:35
  385.4 58.0 %all-to-all-start.1 = ((bf16[64,12,1536]{2,1,0:T(8,128)(2,1)}), bf16[64,12,1536]{2,1,0:T(8,128)(2,1)}, u32[]{:S(2)}, u32[]{:S(2)}) async-start(bf16[64,12,1536]{2,1,0:T(8,128)(2,1)} %reshape.189), calls=%async_computation.1 | async-start | bytes 6291456 | tf_op jit(solution)/shard_map/all_to_all | solution.py:666
  399.8 50.9 %collective-permute-start.36 = (bf16[144,768]{1,0:T(8,128)(2,1)S(1)}, bf16[144,768]{1,0:T(8,128)(2,1)S(1)}, u32[]{:S(2)}, u32[]{:S(2)}) collective-permute-start(bf16[144,768]{1,0:T(8,128)(2,1)S(1)} %get-tuple-element.287), channel_id=1, source_target_pairs={{0,64},{64,0},{1,65},{65,1},{2,66},{66,2},{3,67},{67,3},{4,68},{68... | collective-permute-start | bytes 663560 | tf_op jit(solution)/shard_map/ppermute | solution.py:31
  404.3 47.2 %collective-permute-start.55 = (bf16[144,768]{1,0:T(8,128)(2,1)S(1)}, bf16[144,768]{1,0:T(8,128)(2,1)S(1)}, u32[]{:S(2)}, u32[]{:S(2)}) collective-permute-start(bf16[144,768]{1,0:T(8,128)(2,1)S(1)} %get-tuple-element.285), channel_id=1, source_target_pairs={{0,64},{64,0},{1,65},{65,1},{2,66},{66,2},{3,67},{67,3},{4,68},{68... | collective-permute-start | bytes 663560 | tf_op jit(solution)/shard_map/ppermute | solution.py:31
  (113 other events, 676.2 us)
Sparse Core Ops, SparseCore 0:
  22.0 43.8 all-gather.6
  68.6 55.1 all-gather.8
  126.5 53.7 all-gather.10
  268.4 90.8 reduce-scatter.4
  363.3 107.6 reduce-scatter.2

commit v6 on v5

--- a/solution.py
+++ b/solution.py
@@ -33,6 +33,19 @@
 
 def turn(v, d):
     return lax.ppermute(v, "seq", [(i, (i + d) % N_SEQ) for i in range(N_SEQ)])
+
+
+def hop(v, axis, d):
+    route = []
+    for z in range(4):
+        for x in range(4):
+            to = ((z + d) % 4) * 4 + x if axis == "z" else z * 4 + (x + d) % 4
+            route.append((z * 4 + x, to))
+    return lax.ppermute(v, "shard", route)
+
+
+def from_ring(v, axis):
+    return [v] + [hop(v, axis, -d) for d in (1, 2, 3)]
 
 
 def pick(v, i):
@@ -191,7 +204,11 @@
     return (lax.broadcasted_iota(jnp.int32, (D, D), 1) == source).astype(BF16)
 
 
-def unpack_kernel(all_ref, rows_ref, back_ref):
+def unpack_kernel(where_ref, b0, b1, b2, b3, rows_ref, back_ref, all_ref):
+    z, x = where_ref[0], where_ref[1]
+    for dz, ref in enumerate((b0, b1, b2, b3)):
+        for dx in range(4):
+            all_ref[lax.rem(z + dz, 4) * 4 + lax.rem(x + dx, 4)] = ref[dx]
     whole = all_ref[...].reshape(D, 832)
     ordered = dot(order_rows(N_SHARD, N_SEQ), whole, 1, 0).astype(BF16)
     rows_ref[...] = ordered[:, :640]
@@ -199,20 +216,59 @@
         back_ref[:, 192 * chunk : 192 * (chunk + 1)] = ordered[192 * chunk : 192 * (chunk + 1), 640:]
 
 
-def unpack(whole):
-    return call(unpack_kernel, [shape((D, 640), BF16), shape((192, D), BF16)], [whole], "unpack")
+def unpack(blocks):
+    i = lax.axis_index("shard").astype(jnp.int32)
+    return call(
+        unpack_kernel,
+        [shape((D, 640), BF16), shape((192, D), BF16)],
+        [jnp.stack([i // 4, lax.rem(i, 4)]), *blocks],
+        "unpack",
+        scalars=1,
+        scratch=[pltpu.VMEM((N_SHARD, 48, 832), BF16)],
+    )
+
+
+def reorder_kernel(core_ref, keep_ref, got_ref, in_ref, out_ref):
+    def write(halves):
+        columns = []
+        for shard in range(N_SHARD):
+            for p in range(4):
+                block = halves[p // 2][2 * (p % 2)]
+                columns.append(block[:, 48 * shard : 48 * (shard + 1)])
+        in_ref[...] = jnp.concatenate(columns, axis=1).astype(F32)
+        for p in range(4):
+            out_ref[48 * p : 48 * (p + 1)] = halves[p // 2][2 * (p % 2) + 1].astype(F32)
+
+    @pl.when(core_ref[0] == 0)
+    def _():
+        write((keep_ref, got_ref))
+
+    @pl.when(core_ref[0] == 1)
+    def _():
+        write((got_ref, keep_ref))
+
+
+def reorder(core, keep, got):
+    return call(
+        reorder_kernel,
+        [shape((48, FF), F32), shape((192, D), F32)],
+        [core, keep, got],
+        "reorder",
+        scalars=1,
+    )
 
 
 def middle_kernel(
-    extra, me_ref, x_ref, g0, g1, g2, g3, w0, w1, w2, w3, router_ref, gain_ref, route_ref, *refs
+    layer, me_ref, x_ref, g0, g1, g2, g3, w0, w1, w2, w3, router_ref, gain_ref, route_ref, *refs
 ):
     me = me_ref[0]
+    extra = layer == 1
     if extra:
         d_out_ref, *refs = refs
     residual_ref, normed_ref, gates_ref, chosen_ref, high_ref, low_ref, *sent = refs
     residual = x_ref[...].astype(F32)
     for ref, w_ref in zip((g0, g1, g2, g3), (w0, w1, w2, w3)):
-        residual = residual + dot(ref[...], w_ref[...], 1, 0)
+        residual = residual + dot(ref[...], w_ref[layer], 1, 0)
     residual_ref[...] = residual
     n, _ = norm_parts(residual)
     normed = (n * gain_ref[5:6, :]).astype(BF16)
@@ -261,7 +317,7 @@
     extra = d_out is not None
     sent = (2, CAP, D) if extra else (CAP, D)
     outs = call(
-        partial(middle_kernel, extra),
+        partial(middle_kernel, int(extra)),
         [
             shape((ROWS, D), F32),
             shape((ROWS, D), BF16),
@@ -398,11 +454,17 @@
     return outs[:4], *outs[4:]
 
 
-def expert_grads_kernel(core_ref, rows_ref, d_result_ref, act_own, dh_own, act_other, dh_other, out_ref):
+def expert_grads_kernel(
+    core_ref, rows_ref, d_result_ref, act_own, dh_own, act_other, dh_other, out_ref, turned_ref
+):
+    @pl.when((pl.program_id(0) == 0) & (pl.program_id(1) == 0))
+    def _():
+        turned_ref[...] = rows_ref[...].T
+
     for place, act_ref, dh_ref in ((0, act_own, dh_own), (1, act_other, dh_other)):
         @pl.when(pl.program_id(0) == place)
         def _():
-            grad = dot(rows_ref[...], dh_ref[...], 0, 0).astype(BF16)
+            grad = dot(turned_ref[...], dh_ref[...], 1, 0).astype(BF16)
             out_ref[0, :, 0] = grad.reshape(N_SHARD, 48, 768)
             grad = dot(act_ref[...], d_result_ref[...], 0, 0).astype(BF16)
             out_ref[0, :, 1] = grad.reshape(N_SHARD, 48, 768)
@@ -422,6 +484,7 @@
             out_specs=pl.BlockSpec(
                 (1, N_SHARD, 2, 48, D), lambda h, i, c: (jnp.where(h == 0, c[0], 1 - c[0]), 0, i, 0, 0)
             ),
+            scratch_shapes=[pltpu.VMEM((D, 320), BF16)],
         ),
         name="expert_grads",
         compiler_params=pltpu.CompilerParams(
@@ -483,7 +546,7 @@
     d_branch = d_residual.astype(BF16)
     for d, (ref, w_ref) in enumerate(zip((m0, m1, m2, m3), (w0, w1, w2, w3))):
         group = lax.rem(me - d + N_SEQ, N_SEQ)
-        ref[...] = dot(d_branch, w_ref[...], 1, 1).astype(BF16)
+        ref[...] = dot(d_branch, w_ref[int(paired)], 1, 1).astype(BF16)
         back_ref[group] = dot(gathered[d][...], d_branch, 0, 0).astype(BF16)
     grad_ref[...] = back_ref[...].reshape(D, D)
     high, low = two_parts(d_logits)
@@ -537,7 +600,7 @@
     return outs[0], outs[1:]
 
 
-def attention_weights(w_qkv, w_proj, w_route, gain_attn, gain_ffn):
+def attention_weights(x_blocks, w_qkv, w_proj, w_route, gain_attn, gain_ffn):
     mine = w_qkv.reshape(12, 3, N_SEQ, 192).transpose(2, 0, 1, 3).reshape(N_SEQ, 12, 576)
     small = jnp.concatenate(
         [w_route, gain_attn[:, None], gain_ffn[:, None], jnp.zeros((12, 58), BF16)], axis=1
@@ -546,8 +609,9 @@
     arrived = lax.all_to_all(mine, "seq", 0, 0, tiled=True).reshape(48, 640)
     back = w_proj.reshape(12, N_SEQ, 192).transpose(1, 0, 2).reshape(48, 192)
     pack = jnp.concatenate([arrived, back], axis=1)
-    whole = lax.all_gather(pack, "shard", axis=0, tiled=False)
-    return whole, *unpack(whole)
+    near = jnp.stack(from_ring(tie(pack, x_blocks), "x"))
+    far = from_ring(near, "z")
+    return far, *unpack(far)
 
 
 def both_layers(mine):
@@ -577,11 +641,11 @@
     x0 = pick(images_in, core)[0]
     d_last = pick(out_grad, core)[0]
     halves = half_packs(w_in[0, 0], w_out[0, 0])
-    whole, rows, back_rows = attention_weights(
-        w_qkv[0], w_proj[0], w_route[0], gain_attn[0], gain_ffn[0]
-    )
-    own = lax.all_gather(tie(halves[0], whole), "shard", axis=0, tiled=False)
     x_blocks = [x0] + [turn(x0, -d) for d in (1, 2, 3)]
+    far, rows, back_rows = attention_weights(
+        x_blocks, w_qkv[0], w_proj[0], w_route[0], gain_attn[0], gain_ffn[0]
+    )
+    own = lax.all_gather(tie(halves[0], far), "shard", axis=0, tiled=False)
     attn_rows = both_layers(rows)
     back_rows = both_layers(back_rows)
     attn_rows[0], attn_rows[1], back_rows[0], back_rows[1] = lax.optimization_barrier(
@@ -590,7 +654,8 @@
     w_mix = [v[:, :576] for v in attn_rows]
     routers = [jnp.pad(v[:, 576:], ((0, 0), (0, 64))) for v in attn_rows]
     tables = [v[:, 576:584].T.astype(F32) for v in attn_rows]
-    w_back = [[back_rows[0]] + [turn(back_rows[0], d) for d in (1, 2, 3)], None]
+    back_rows = jnp.stack(back_rows)
+    w_back = [back_rows] + [turn(back_rows, d) for d in (1, 2, 3)]
     experts = [None, None]
 
     saved = []
@@ -601,14 +666,14 @@
             x_blocks = [x] + [turn(x, -d) for d in (1, 2, 3)]
         mixture, x_all, packed, logs = attend(x_blocks, w_mix[s], tables[s])
         if s == 0:
-            w_back[0], mixture = lax.optimization_barrier((w_back[0], mixture))
+            w_back, mixture = lax.optimization_barrier((w_back, mixture))
         else:
             later, mixture[0] = lax.optimization_barrier((later, mixture[0]))
             experts[1] = (later, swap(later))
         gathered = send_out(mixture)
         d_out = d_last if s == 1 else None
         residual, normed, gates, chosen, high, low, buffer = middle(
-            me, x, gathered, w_back[s], routers[s], tables[s], route_of[s], d_out
+            me, x, gathered, w_back, routers[s], tables[s], route_of[s], d_out
         )
         blocks = send_out(buffer)
         kept = (x, x_all, packed, logs, gathered, residual, normed, gates, chosen, high, low, blocks)
@@ -616,11 +681,7 @@
             own, blocks[1] = lax.optimization_barrier((own, blocks[1]))
             experts[0] = (own, swap(own))
             later = lax.all_gather(tie(halves[1], own), "shard", axis=0, tiled=False)
-            later_back = tie(back_rows[1], blocks[1])
-            w_back[1] = [later_back] + [turn(later_back, d) for d in (1, 2, 3)]
-            result = expert_run(blocks, experts[s])
-            w_back[1], result = lax.optimization_barrier((w_back[1], result))
-            returned = send_back(result)
+            returned = send_back(expert_run(blocks, experts[s]))
             x = combine(residual, high, low, returned)
             layer_outs.append(x)
             saved.append((kept, returned))
@@ -643,12 +704,10 @@
             sent, *states = expert_back([*blocks, *send_out(d_buffer)], experts[s], False)
             arrived = [*returned, *send_back(sent)]
         d_residual, small, grad_back, d_mixture = middle_back(
-            me, d_out, arrived, gathered, chosen, gates, residual, normed, tables[s], w_back[s], s == 1
+            me, d_out, arrived, gathered, chosen, gates, residual, normed, tables[s], w_back, s == 1
         )
         d_heads = send_back(d_mixture)
         rows, d_result, act_own, act_other, dh_own, dh_other = states
-        if s == 1:
-            rows = tie(rows, d_residual)
         both = expert_grads(core_index, rows, d_result, act_own, dh_own, act_other, dh_other)
         both = both.reshape(2 * N_SHARD, 4, 48, D)
         expert_sums[s] = lax.psum_scatter(both, ("section", "shard"), scatter_dimension=0, tiled=True)[0]
@@ -677,11 +736,8 @@
 
     layer_out = in_order(*settle(layer_outs))
     in_grad = in_order(*settle(in_grads))
-    expert_sum = in_order(*settle(expert_sums)).astype(F32)
+    grad_in, grad_out = reorder(core_index, *settle(expert_sums))
     attn_sum = in_order(*settle(attn_sums))
-    quarters = expert_sum.reshape(4, 2, 48, 768)
-    grad_in = quarters[:, 0].reshape(4, 48, N_SHARD, 48).transpose(1, 2, 0, 3).reshape(48, FF)
-    grad_out = quarters[:, 1].reshape(192, D)
     mix = attn_sum[0]
     back = jnp.sum(attn_sum[1], axis=0)
     grad_qkv = mix[:, :, :576].reshape(N_SEQ, 12, 3, 192).transpose(1, 2, 0, 3).reshape(12, 3 * D)

time: 502 us -> 474 us (0.944)
  waiting for transfers between devices: 208 us -> 176 us
  starting transfers between devices: 94.4 us -> 100 us
    all_gather x2 -> x1, waiting for transfers between devices: 37.8 us -> 0.01 us  [shards(): own = lax.all_gather(tie(halves[0], far), 'shard', axis=0, tiled=False)]
    ppermute x0 -> x6, waiting for transfers between devices: none -> 13.3 us  [hop(): return lax.ppermute(v, 'shard', route)]
    ppermute x0 -> x6, starting transfers between devices: none -> 10.6 us  [hop(): return lax.ppermute(v, 'shard', route)]
    all_to_all x1, waiting for transfers between devices: 38.7 us -> 47 us  [shards(): arrived = lax.all_to_all(pair, ('seq', 'shard'), 0, 0, tiled=True)]
    ppermute x48 -> x45, waiting for transfers between devices: 108 us -> 100 us  [turn(): return lax.ppermute(v, 'seq', [(i, (i + d) % N_SEQ) for i in range(N_SEQ)])]
    reduce_scatter x2, waiting for transfers between devices: 18.6 us -> 11.9 us  [shards(): lax.psum_scatter(both, ('section', 'shard'), scatter_dimension=0, tiled=T...]
    pallas_call x13 -> x14, Pallas kernels: 65.8 us -> 69.5 us  [call(): pl.pallas_call(body, out_shape=outs, in_specs=specs, out_specs=[vmem()] *...]
    unnamed x142 -> x160, local copies, waits for them, and re-layouts: 13.4 us -> 15.3 us
  transfers between devices with their start and end apart: 67 -> 69, of which waited for: 40 -> 40; matrix products, arithmetic and copies ran while one was open for 7% -> 9% of each run, Pallas kernels for 18% -> 20%
where the time goes in v6:
time: 474 us; the launch traced here: 466 us
  waiting for transfers between devices  176 us (37%)
  Pallas kernels  119 us (25%)
  starting transfers between devices  100 us (21%)
  local copies, waits for them, and re-layouts  40.1 us (8%)
  other arithmetic  16.7 us (4%)
  between operations  14.7 us (3%)
    ppermute x45, waiting for transfers between devices, turn(): return lax.ppermute(v, 'seq', [(i, (i + d) % N_SEQ) for i in range(N_SEQ)])  100 us
    pallas_call x14, Pallas kernels, call(): pl.pallas_call(body, out_shape=outs, in_specs=specs, out_specs=[vmem()] *...  69.5 us
    ppermute x45, starting transfers between devices, turn(): return lax.ppermute(v, 'seq', [(i, (i + d) % N_SEQ) for i in range(N_SEQ)])  49.9 us
    all_to_all x1, waiting for transfers between devices, shards(): arrived = lax.all_to_all(pair, ('seq', 'shard'), 0, 0, tiled=True)  47 us
    pallas_call x3, Pallas kernels, grid_call(): pl.pallas_call(body, grid=(2,), out_shape=outs, in_specs=in_specs, out_sp...  29.3 us
    ppermute x12, starting transfers between devices, swap(): return lax.ppermute(v, 'section', [(0, 1), (1, 0)])  26.2 us
    pallas_call x2, Pallas kernels, expert_grads(): pl.pallas_call(expert_grads_kernel, out_shape=shape((2, N_SHARD, 4, 48, D...  20 us
    unnamed x160, local copies, waits for them, and re-layouts  15.3 us
  transfers between devices with their start and end apart: 69, of which 40 were waited for; matrix products, arithmetic and copies ran while one was open for 9% of the time, Pallas kernels for 20%

profile of v6, /device:TPU:1, one launch (start us, length us, event | category | flops | bytes accessed | tf_op | source)
XLA Modules:
  0.0 466.1 jit_solution(18063268929526669616)
XLA Ops:
  42.3 7.6 %collective-permute-done.7.b2 = bf16[4,48,832]{2,1,0:T(8,128)(2,1)S(1)} collective-permute-done((bf16[4,48,832]{2,1,0:T(8,128)(2,1)S(1)}, bf16[4,48,832]{2,1,0:T(8,128)(2,1)S(1)}, u32[]{:S(2)}, u32[]{:S(2)}) %collective-permute-start.7) | collective-permute-done | bytes 319520 | tf_op jit(solution)/shard_map/ppermute | solution.py:44
  77.5 6.0 %attention.2 = (bf16[144,192]{1,0:T(8,128)(2,1)}, bf16[144,192]{1,0:T(8,128)(2,1)}, bf16[144,192]{1,0:T(8,128)(2,1)}, bf16[144,192]{1,0:T(8,128)(2,1)}, bf16[576...) custom-call(bf16[144,768]{1,0:T(8,128)(2,1)} %copy-done.13, ...), custom_call_target="tpu_custom_call" | custom-call | tf_op jit(solution)/shard_map/attention/pallas_call | solution.py:105
  83.6 9.9 %collective-permute-done.13.w3.refs_16_.refs_20_ = bf16[2,192,768]{2,1,0:T(8,128)(2,1)S(1)} collective-permute-done((bf16[2,192,768]{2,1,0:T(8,128)(2,1)S(1)}, bf16[2,192,768]{2,1,0:T(8,128)(2,1)S(1)}, u32[]{:S(2)}, u32[]{:S(2)}) %collective-permute-start.13) | collective-permute-done | bytes 589856 | tf_op jit(solution)/shard_map/ppermute | solution.py:35
  93.5 4.7 collective-permute-done.11.w1.refs_14_.refs_18_
  119.3 4.9 %collective-permute-done.20.r2.refs_2_ = bf16[80,768]{1,0:T(8,128)(2,1)S(1)} collective-permute-done((bf16[80,768]{1,0:T(8,128)(2,1)}, bf16[80,768]{1,0:T(8,128)(2,1)S(1)}, u32[]{:S(2)}, u32[]{:S(2)}) %collective-permute-start.20) | collective-permute-done | bytes 122912 | tf_op jit(solution)/shard_map/ppermute | solution.py:35
  127.5 7.1 %expert.1 = (bf16[80,768]{1,0:T(8,128)(2,1)}, bf16[80,768]{1,0:T(8,128)(2,1)}, bf16[80,768]{1,0:T(8,128)(2,1)}, bf16[80,768]{1,0:T(8,128)(2,1)}) custom-call(bf16[80,768]{1,0:T(8,128)(2,1)} %get-tuple-element.141.r0.refs_0_, bf16[80,768]{1,0:T(8,128)(2,1)} %copy-done.23, bf16[80,768]{1,0:T(8,128)(2,1)} %copy-done.24, bf16[80,768]{1,0:T(8,128)(2,1)} %copy-done.25, ...), custom_call_target="tpu_custom_call" | custom-call | tf_op jit(solution)/shard_map/expert/pallas_call | solution.py:374
  153.4 9.2 %collective-permute-done.28.x3 = bf16[144,768]{1,0:T(8,128)(2,1)S(1)} collective-permute-done((bf16[144,768]{1,0:T(8,128)(2,1)}, bf16[144,768]{1,0:T(8,128)(2,1)S(1)}, u32[]{:S(2)}, u32[]{:S(2)}) %collective-permute-start.28) | collective-permute-done | bytes 221216 | tf_op jit(solution)/shard_map/ppermute | solution.py:35
  164.1 6.0 %attention.3 = (bf16[144,192]{1,0:T(8,128)(2,1)}, bf16[144,192]{1,0:T(8,128)(2,1)}, bf16[144,192]{1,0:T(8,128)(2,1)}, bf16[144,192]{1,0:T(8,128)(2,1)}, bf16[576...) custom-call(bf16[144,768]{1,0:T(8,128)(2,1)} %combine.2.x0.x_ref, bf16[144,768]{1,0:T(8,128)(2,1)} %copy-done.55, ...), custom_call_target="tpu_custom_call" | custom-call | tf_op jit(solution)/shard_map/attention/pallas_call | solution.py:105
  179.3 4.6 middle.3
  191.7 7.2 %collective-permute-done.33.refs_2_ = bf16[2,80,768]{2,1,0:T(8,128)(2,1)S(1)} collective-permute-done((bf16[2,80,768]{2,1,0:T(8,128)(2,1)}, bf16[2,80,768]{2,1,0:T(8,128)(2,1)S(1)}, u32[]{:S(2)}, u32[]{:S(2)}) %collective-permute-start.33) | collective-permute-done | bytes 245792 | tf_op jit(solution)/shard_map/ppermute | solution.py:35
  199.7 11.6 %expert_back.2 = (bf16[2,80,768]{2,1,0:T(8,128)(2,1)}, bf16[2,80,768]{2,1,0:T(8,128)(2,1)}, bf16[2,80,768]{2,1,0:T(8,128)(2,1)}, bf16[2,80,768]{2,1,0:T(8,128)(2...) custom-call(bf16[2,80,768]{2,1,0:T(8,128)(2,1)} %get-tuple-element.1, ...), custom_call_target="tpu_custom_call" | custom-call | tf_op jit(solution)/shard_map/expert_back/pallas_call | solution.py:374
  211.3 9.9 %expert_grads.3 = bf16[2,16,4,48,768]{4,3,2,1,0:T(8,128)(2,1)} custom-call(s32[1]{0:T(128)} %bitcast.41.core_ref, bf16[320,768]{1,0:T(8,128)(2,1)} %get-tuple-element.223.rows_ref, bf16[320,768]{1,0:T(8,128)(2,1)} %get-tuple-element.224.d_result_ref, bf16[320,1536]{1,0:T(8,128)(2,1)} %get-tuple-element.225.act_own, ...), custom_call_target="tpu_custom_call" | custom-call | tf_op jit(solution)/shard_map/expert_grads/pallas_call | solution.py:477
  225.5 9.3 %collective-permute-done.36.refs_1_ = bf16[2,80,768]{2,1,0:T(8,128)(2,1)S(1)} collective-permute-done((bf16[2,80,768]{2,1,0:T(8,128)(2,1)S(1)}, bf16[2,80,768]{2,1,0:T(8,128)(2,1)S(1)}, u32[]{:S(2)}, u32[]{:S(2)}) %collective-permute-start.36) | collective-permute-done | bytes 245792 | tf_op jit(solution)/shard_map/ppermute | solution.py:35
  239.8 6.2 %middle_back.2 = (f32[144,768]{1,0:T(8,128)}, f32[768,64]{1,0:T(8,128)}, bf16[768,768]{1,0:T(8,128)(2,1)}, bf16[144,192]{1,0:T(8,128)(2,1)}, bf16[144,192]{1,0:T...) custom-call(s32[1]{0:T(128)} %bitcast.me_ref, ...), custom_call_target="tpu_custom_call" | custom-call | tf_op jit(solution)/shard_map/middle_back/pallas_call | solution.py:105
  252.7 9.9 %attention_back.2 = (bf16[144,768]{1,0:T(8,128)(2,1)}, bf16[144,768]{1,0:T(8,128)(2,1)}, bf16[144,768]{1,0:T(8,128)(2,1)}, bf16[144,768]{1,0:T(8,128)(2,1)}, bf16[768,768]{1,0:T(8,128)(2,1)}) custom-call(bf16[576,768]{1,0:T(8,128)(2,1)} %get-tuple-element.175.x_ref, bf16[768,576]{1,0:T(8,128)(2,1)} %copy.111.w_ref, ...), custom_call_target="tpu_custom_call" | custom-call | tf_op jit(solution)/shard_map/attention_back/pallas_call | solution.py:105
  268.8 6.2 %collective-permute-done.44.b2 = bf16[144,768]{1,0:T(8,128)(2,1)S(1)} collective-permute-done((bf16[144,768]{1,0:T(8,128)(2,1)}, bf16[144,768]{1,0:T(8,128)(2,1)S(1)}, u32[]{:S(2)}, u32[]{:S(2)}) %collective-permute-start.44) | collective-permute-done | bytes 221216 | tf_op jit(solution)/shard_map/ppermute | solution.py:35
  289.3 10.5 %expert_back.3 = (bf16[80,768]{1,0:T(8,128)(2,1)}, bf16[80,768]{1,0:T(8,128)(2,1)}, bf16[80,768]{1,0:T(8,128)(2,1)}, bf16[80,768]{1,0:T(8,128)(2,1)}, bf16[320,7...) custom-call(bf16[80,768]{1,0:T(8,128)(2,1)} %get-tuple-element.141.r, ...), custom_call_target="tpu_custom_call" | custom-call | tf_op jit(solution)/shard_map/expert_back/pallas_call | solution.py:374
  299.9 10.0 %expert_grads.2 = bf16[2,16,4,48,768]{4,3,2,1,0:T(8,128)(2,1)} custom-call(s32[1]{0:T(128)} %bitcast.41.core_ref, bf16[320,768]{1,0:T(8,128)(2,1)} %get-tuple-element.217.rows_ref, bf16[320,768]{1,0:T(8,128)(2,1)} %get-tuple-element.218.d_result_ref, bf16[320,1536]{1,0:T(8,128)(2,1)} %get-tuple-element.219.act_own, ...), custom_call_target="tpu_custom_call" | custom-call | tf_op jit(solution)/shard_map/expert_grads/pallas_call | solution.py:477
  318.4 6.0 %middle_back.3 = (f32[144,768]{1,0:T(8,128)}, f32[768,64]{1,0:T(8,128)}, bf16[768,768]{1,0:T(8,128)(2,1)}, bf16[144,192]{1,0:T(8,128)(2,1)}, bf16[144,192]{1,0:T...) custom-call(s32[1]{0:T(128)} %bitcast.me_ref, bf16[144,768]{1,0:T(8,128)(2,1)} %get-tuple-element.187.d_out_ref, ...), custom_call_target="tpu_custom_call" | custom-call | tf_op jit(solution)/shard_map/middle_back/pallas_call | solution.py:105
  327.1 5.0 %collective-permute-start.60 = (bf16[768,768]{1,0:T(8,128)(2,1)S(1)}, bf16[768,768]{1,0:T(8,128)(2,1)S(1)}, u32[]{:S(2)}, u32[]{:S(2)}) collective-permute-start(bf16[768,768]{1,0:T(8,128)(2,1)S(1)} %broadcast_select_fusion), channel_id=1, source_target_pairs={{0,64},{64,0},{1,65},{65,1},{2,66},{66,2},{3,67},{67,3},{4,68},{68... | collective-permute-start | bytes 3538952 | tf_op jit(solution)/shard_map/ppermute | solution.py:31
  332.8 10.0 %attention_back.3 = (bf16[144,768]{1,0:T(8,128)(2,1)}, bf16[144,768]{1,0:T(8,128)(2,1)}, bf16[144,768]{1,0:T(8,128)(2,1)}, bf16[144,768]{1,0:T(8,128)(2,1)}, bf16[768,768]{1,0:T(8,128)(2,1)}) custom-call(bf16[576,768]{1,0:T(8,128)(2,1)} %get-tuple-element.200.x_ref, bf16[768,576]{1,0:T(8,128)(2,1)} %copy.106.w_ref, ...), custom_call_target="tpu_custom_call" | custom-call | tf_op jit(solution)/shard_map/attention_back/pallas_call | solution.py:105
  362.0 9.8 %all-to-all-start.1 = ((bf16[64,12,1536]{2,1,0:T(8,128)(2,1)}), bf16[64,12,1536]{2,1,0:T(8,128)(2,1)}, u32[]{:S(2)}, u32[]{:S(2)}) async-start(bf16[64,12,1536]{2,1,0:T(8,128)(2,1)} %reshape.184), calls=%async_computation.1 | async-start | bytes 6291456 | tf_op jit(solution)/shard_map/all_to_all | solution.py:725
  382.6 47.0 %all-to-all-done.1 = bf16[64,12,1536]{2,1,0:T(8,128)(2,1)} async-done(((bf16[64,12,1536]{2,1,0:T(8,128)(2,1)}), bf16[64,12,1536]{2,1,0:T(8,128)(2,1)}, u32[]{:S(2)}, u32[]{:S(2)}) %all-to-all-start.1) | async-done | bytes 2359328 | tf_op jit(solution)/shard_map/all_to_all | solution.py:725
  437.0 11.9 %reduce-scatter.3.cloned.1.call-done = bf16[1,4,48,768]{3,2,1,0:T(8,128)(2,1)} async-done(((bf16[32,4,48,768]{3,2,1,0:T(8,128)(2,1)}), bf16[1,4,48,768]{3,2,1,0:T(8,128)(2,1)}) %reduce-scatter.3.cloned.1.call-update) | async-done | bytes 294928 | tf_op jit(solution)/shard_map/reduce_scatter | solution.py:713
  (370 shorter events, 220.7 us)
Async XLA Ops:
  8.2 18.1 %collective-permute-start.2 = (bf16[144,768]{1,0:T(8,128)(2,1)S(1)}, bf16[144,768]{1,0:T(8,128)(2,1)S(1)}, u32[]{:S(2)}, u32[]{:S(2)}) collective-permute-start(bf16[144,768]{1,0:T(8,128)(2,1)S(1)} %dynamic-slice_bitcast_fusion.2.x0.x_ref), channel_id=1, source_target_pairs={{0,16},{16,32},{32,48},{48,0},{1,17},{17,33},{33,49},{49,1},{2,18}... | collective-permute-start | bytes 663560 | tf_op jit(solution)/shard_map/ppermute | solution.py:35
  10.4 16.0 %collective-permute-start.1 = (bf16[144,768]{1,0:T(8,128)(2,1)S(1)}, bf16[144,768]{1,0:T(8,128)(2,1)S(1)}, u32[]{:S(2)}, u32[]{:S(2)}) collective-permute-start(bf16[144,768]{1,0:T(8,128)(2,1)S(1)} %dynamic-slice_bitcast_fusion.2.x0.x_ref), channel_id=1, source_target_pairs={{0,32},{16,48},{32,0},{48,16},{1,33},{17,49},{33,1},{49,17},{2,34}... | collective-permute-start | bytes 663560 | tf_op jit(solution)/shard_map/ppermute | solution.py:35
  13.0 13.4 %collective-permute-start = (bf16[144,768]{1,0:T(8,128)(2,1)S(1)}, bf16[144,768]{1,0:T(8,128)(2,1)}, u32[]{:S(2)}, u32[]{:S(2)}) collective-permute-start(bf16[144,768]{1,0:T(8,128)(2,1)S(1)} %dynamic-slice_bitcast_fusion.2.x0.x_ref), channel_id=1, source_target_pairs={{0,48},{16,0},{32,16},{48,32},{1,49},{17,1},{33,17},{49,33},{2,50}... | collective-permute-start | bytes 663560 | tf_op jit(solution)/shard_map/ppermute | solution.py:35
  21.8 93.2 %all-gather.5.cloned.1.call-start = ((), (), s32[]{:S(2)}) async-start(), calls=%async_computation.6 | async-start | bytes 5013504 | tf_op jit(solution)/shard_map/all_gather | solution.py:648
  23.7 15.9 %collective-permute-start.18 = (bf16[4,48,768]{2,1,0:T(8,128)(2,1)S(1)}, bf16[4,48,768]{2,1,0:T(8,128)(2,1)S(1)}, u32[]{:S(2)}, u32[]{:S(2)}) collective-permute-start(bf16[4,48,768]{2,1,0:T(8,128)(2,1)S(1)} %dynamic-slice_bitcast_fusion), channel_id=1, source_target_pairs={{0,64},{64,0},{1,65},{65,1},{2,66},{66,2},{3,67},{67,3},{4,68},{68... | collective-permute-start | bytes 884744 | tf_op jit(solution)/shard_map/ppermute | solution.py:31
  35.6 14.4 %collective-permute-start.7 = (bf16[4,48,832]{2,1,0:T(8,128)(2,1)S(1)}, bf16[4,48,832]{2,1,0:T(8,128)(2,1)S(1)}, u32[]{:S(2)}, u32[]{:S(2)}) collective-permute-start(bf16[4,48,832]{2,1,0:T(8,128)(2,1)S(1)} %pad_maximum_fusion.3.b0), channel_id=1, source_target_pairs={{0,8},{1,9},{2,10},{3,11},{4,12},{5,13},{6,14},{7,15},{8,0},{9,1},... | collective-permute-start | bytes 958472 | tf_op jit(solution)/shard_map/ppermute | solution.py:44
  51.4 118.8 %all-gather.7.cloned.1.call-start = ((), (), s32[]{:S(2)}) async-start(), calls=%async_computation.7 | async-start | bytes 5013504 | tf_op jit(solution)/shard_map/all_gather | solution.py:683
  66.0 27.5 %collective-permute-start.13 = (bf16[2,192,768]{2,1,0:T(8,128)(2,1)S(1)}, bf16[2,192,768]{2,1,0:T(8,128)(2,1)S(1)}, u32[]{:S(2)}, u32[]{:S(2)}) collective-permute-start(bf16[2,192,768]{2,1,0:T(8,128)(2,1)S(1)} %pad_maximum_fusion.1.w0.refs_13_.refs_17_), channel_id=1, source_target_pairs={{0,48},{16,0},{32,16},{48,32},{1,49},{17,1},{33,17},{49,33},{2,50}... | collective-permute-start | bytes 1769480 | tf_op jit(solution)/shard_map/ppermute | solution.py:35
  68.7 24.8 %collective-permute-start.12 = (bf16[2,192,768]{2,1,0:T(8,128)(2,1)S(1)}, bf16[2,192,768]{2,1,0:T(8,128)(2,1)S(1)}, u32[]{:S(2)}, u32[]{:S(2)}) collective-permute-start(bf16[2,192,768]{2,1,0:T(8,128)(2,1)S(1)} %pad_maximum_fusion.1.w0.refs_13_.refs_17_), channel_id=1, source_target_pairs={{0,32},{16,48},{32,0},{48,16},{1,33},{17,49},{33,1},{49,17},{2,34}... | collective-permute-start | bytes 1769480 | tf_op jit(solution)/shard_map/ppermute | solution.py:35
  69.3 28.9 %collective-permute-start.11 = (bf16[2,192,768]{2,1,0:T(8,128)(2,1)S(1)}, bf16[2,192,768]{2,1,0:T(8,128)(2,1)S(1)}, u32[]{:S(2)}, u32[]{:S(2)}) collective-permute-start(bf16[2,192,768]{2,1,0:T(8,128)(2,1)S(1)} %pad_maximum_fusion.1.w0.refs_13_.refs_17_), channel_id=1, source_target_pairs={{0,16},{16,32},{32,48},{48,0},{1,17},{17,33},{33,49},{49,1},{2,18}... | collective-permute-start | bytes 1769480 | tf_op jit(solution)/shard_map/ppermute | solution.py:35
  70.2 30.7 %collective-permute-start.17 = (s32[144,2]{1,0:T(8,128)S(1)}, s32[144,2]{1,0:T(8,128)S(1)}, u32[]{:S(2)}, u32[]{:S(2)}) collective-permute-start(s32[144,2]{1,0:T(8,128)S(1)} %bitcast.110), channel_id=1, source_target_pairs={{0,64},{64,0},{1,65},{65,1},{2,66},{66,2},{3,67},{67,3},{4,68},{68... | collective-permute-start | bytes 3464 | tf_op jit(solution)/shard_map/ppermute | solution.py:31
  115.0 322.0 %reduce-scatter.5.cloned.1.call-start = ((), (), s32[]{:S(2)}) async-start(), calls=%async_computation.5 | async-start | bytes 9732096 | tf_op jit(solution)/shard_map/reduce_scatter | solution.py:713
  149.8 12.9 %collective-permute-start.28 = (bf16[144,768]{1,0:T(8,128)(2,1)}, bf16[144,768]{1,0:T(8,128)(2,1)S(1)}, u32[]{:S(2)}, u32[]{:S(2)}) collective-permute-start(bf16[144,768]{1,0:T(8,128)(2,1)} %combine.2.x0.x_ref), channel_id=1, source_target_pairs={{0,16},{16,32},{32,48},{48,0},{1,17},{17,33},{33,49},{49,1},{2,18}... | collective-permute-start | bytes 663560 | tf_op jit(solution)/shard_map/ppermute | solution.py:35
  149.8 12.9 %collective-permute-start.27 = (bf16[144,768]{1,0:T(8,128)(2,1)}, bf16[144,768]{1,0:T(8,128)(2,1)S(1)}, u32[]{:S(2)}, u32[]{:S(2)}) collective-permute-start(bf16[144,768]{1,0:T(8,128)(2,1)} %combine.2.x0.x_ref), channel_id=1, source_target_pairs={{0,32},{16,48},{32,0},{48,16},{1,33},{17,49},{33,1},{49,17},{2,34}... | collective-permute-start | bytes 663560 | tf_op jit(solution)/shard_map/ppermute | solution.py:35
  170.1 28.8 %collective-permute-start.35 = (bf16[16,4,48,768]{3,2,1,0:T(8,128)(2,1)}, bf16[16,4,48,768]{3,2,1,0:T(8,128)(2,1)}, u32[]{:S(2)}, u32[]{:S(2)}) collective-permute-start(bf16[16,4,48,768]{3,2,1,0:T(8,128)(2,1)} %bitcast.91), channel_id=1, source_target_pairs={{0,64},{64,0},{1,65},{65,1},{2,66},{66,2},{3,67},{67,3},{4,68},{68... | collective-permute-start | bytes 14155784 | tf_op jit(solution)/shard_map/ppermute | solution.py:31
  184.4 14.5 %collective-permute-start.33 = (bf16[2,80,768]{2,1,0:T(8,128)(2,1)}, bf16[2,80,768]{2,1,0:T(8,128)(2,1)S(1)}, u32[]{:S(2)}, u32[]{:S(2)}) collective-permute-start(bf16[2,80,768]{2,1,0:T(8,128)(2,1)} %get-tuple-element.164), channel_id=1, source_target_pairs={{0,32},{16,48},{32,0},{48,16},{1,33},{17,49},{33,1},{49,17},{2,34}... | collective-permute-start | bytes 737288 | tf_op jit(solution)/shard_map/ppermute | solution.py:35
  221.3 227.6 %reduce-scatter.3.cloned.1.call-start = ((), (), s32[]{:S(2)}) async-start(), calls=%async_computation.4 | async-start | bytes 9732096 | tf_op jit(solution)/shard_map/reduce_scatter | solution.py:713
  222.2 12.6 %collective-permute-start.36 = (bf16[2,80,768]{2,1,0:T(8,128)(2,1)S(1)}, bf16[2,80,768]{2,1,0:T(8,128)(2,1)S(1)}, u32[]{:S(2)}, u32[]{:S(2)}) collective-permute-start(bf16[2,80,768]{2,1,0:T(8,128)(2,1)S(1)} %copy-done.73), channel_id=1, source_target_pairs={{0,48},{16,0},{32,16},{48,32},{1,49},{17,1},{33,17},{49,33},{2,50}... | collective-permute-start | bytes 737288 | tf_op jit(solution)/shard_map/ppermute | solution.py:35
  224.8 14.2 %collective-permute-start.38 = (bf16[2,80,768]{2,1,0:T(8,128)(2,1)S(1)}, bf16[2,80,768]{2,1,0:T(8,128)(2,1)S(1)}, u32[]{:S(2)}, u32[]{:S(2)}) collective-permute-start(bf16[2,80,768]{2,1,0:T(8,128)(2,1)S(1)} %copy-done.71), channel_id=1, source_target_pairs={{0,16},{16,32},{32,48},{48,0},{1,17},{17,33},{33,49},{49,1},{2,18}... | collective-permute-start | bytes 737288 | tf_op jit(solution)/shard_map/ppermute | solution.py:35
  327.1 23.8 %collective-permute-start.60 = (bf16[768,768]{1,0:T(8,128)(2,1)S(1)}, bf16[768,768]{1,0:T(8,128)(2,1)S(1)}, u32[]{:S(2)}, u32[]{:S(2)}) collective-permute-start(bf16[768,768]{1,0:T(8,128)(2,1)S(1)} %broadcast_select_fusion), channel_id=1, source_target_pairs={{0,64},{64,0},{1,65},{65,1},{2,66},{66,2},{3,67},{67,3},{4,68},{68... | collective-permute-start | bytes 3538952 | tf_op jit(solution)/shard_map/ppermute | solution.py:31
  348.3 12.8 %collective-permute-start.56 = (bf16[144,768]{1,0:T(8,128)(2,1)S(1)}, bf16[144,768]{1,0:T(8,128)(2,1)S(1)}, u32[]{:S(2)}, u32[]{:S(2)}) collective-permute-start(bf16[144,768]{1,0:T(8,128)(2,1)S(1)} %copy-done.75), channel_id=1, source_target_pairs={{0,32},{16,48},{32,0},{48,16},{1,33},{17,49},{33,1},{49,17},{2,34}... | collective-permute-start | bytes 663560 | tf_op jit(solution)/shard_map/ppermute | solution.py:35
  362.0 67.6 %all-to-all-start.1 = ((bf16[64,12,1536]{2,1,0:T(8,128)(2,1)}), bf16[64,12,1536]{2,1,0:T(8,128)(2,1)}, u32[]{:S(2)}, u32[]{:S(2)}) async-start(bf16[64,12,1536]{2,1,0:T(8,128)(2,1)} %reshape.184), calls=%async_computation.1 | async-start | bytes 6291456 | tf_op jit(solution)/shard_map/all_to_all | solution.py:725
  377.9 57.4 %collective-permute-start.39 = (bf16[144,768]{1,0:T(8,128)(2,1)S(1)}, bf16[144,768]{1,0:T(8,128)(2,1)S(1)}, u32[]{:S(2)}, u32[]{:S(2)}) collective-permute-start(bf16[144,768]{1,0:T(8,128)(2,1)S(1)} %get-tuple-element.271), channel_id=1, source_target_pairs={{0,64},{64,0},{1,65},{65,1},{2,66},{66,2},{3,67},{67,3},{4,68},{68... | collective-permute-start | bytes 663560 | tf_op jit(solution)/shard_map/ppermute | solution.py:31
  382.3 53.9 %collective-permute-start.58 = (bf16[144,768]{1,0:T(8,128)(2,1)S(1)}, bf16[144,768]{1,0:T(8,128)(2,1)S(1)}, u32[]{:S(2)}, u32[]{:S(2)}) collective-permute-start(bf16[144,768]{1,0:T(8,128)(2,1)S(1)} %get-tuple-element.269), channel_id=1, source_target_pairs={{0,64},{64,0},{1,65},{65,1},{2,66},{66,2},{3,67},{67,3},{4,68},{68... | collective-permute-start | bytes 663560 | tf_op jit(solution)/shard_map/ppermute | solution.py:31
  (124 other events, 719.6 us)
Sparse Core Ops, SparseCore 0:
  51.5 57.6 all-gather.4
  115.2 53.8 all-gather.6
  221.4 93.7 reduce-scatter.4
  319.3 129.5 reduce-scatter.2

commit v7 on v6

--- a/solution.py
+++ b/solution.py
@@ -118,7 +118,7 @@
         x_ref[ROWS * d : ROWS * (d + 1)] = ref[...]
     n, _ = norm_parts(x_ref[...].astype(F32))
     normed = (n * gain_ref[4:5, :]).astype(BF16)
-    packed_ref[...] = dot(normed, w_ref[...], 1, 0).astype(BF16)
+    packed_ref[...] = dot(normed, w_ref[:, 0:576], 1, 0).astype(BF16)
     lane = lax.broadcasted_iota(jnp.int32, (SEQ, 128), 1)
     logs = jnp.zeros((SEQ, 128), F32)
     outs = []
@@ -173,7 +173,7 @@
     n, _ = norm_parts(x_ref[...].astype(F32))
     normed = (n * gain_ref[4:5, :]).astype(BF16)
     d_packed = d_packed_ref[...]
-    d_normed = dot(d_packed, w_ref[...], 1, 1)
+    d_normed = dot(d_packed, w_ref[:, 0:576], 1, 1)
     for d, ref in enumerate((n0, n1, n2, n3)):
         ref[...] = d_normed[ROWS * d : ROWS * (d + 1)].astype(BF16)
     column = (lax.broadcasted_iota(jnp.int32, (SEQ, 64), 1) == 4).astype(BF16)
@@ -268,13 +268,13 @@
     residual_ref, normed_ref, gates_ref, chosen_ref, high_ref, low_ref, *sent = refs
     residual = x_ref[...].astype(F32)
     for ref, w_ref in zip((g0, g1, g2, g3), (w0, w1, w2, w3)):
-        residual = residual + dot(ref[...], w_ref[layer], 1, 0)
+        residual = residual + dot(ref[...], w_ref[...], 1, 0)
     residual_ref[...] = residual
     n, _ = norm_parts(residual)
     normed = (n * gain_ref[5:6, :]).astype(BF16)
     normed_ref[...] = normed
-    lane = lax.broadcasted_iota(jnp.int32, (ROWS, 128), 1)
-    logits = jnp.where(lane < 4, dot(normed, router_ref[...], 1, 0), -1e30)
+    lane = lax.broadcasted_iota(jnp.int32, (ROWS, 64), 1)
+    logits = jnp.where(lane < 4, dot(normed, router_ref[:, 576:640], 1, 0), -1e30)
     logits = logits - jnp.max(logits, axis=1, keepdims=True)
     gates = jnp.exp(logits)
     gates = gates / jnp.sum(gates, axis=1, keepdims=True)
@@ -321,7 +321,7 @@
         [
             shape((ROWS, D), F32),
             shape((ROWS, D), BF16),
-            shape((ROWS, 128), F32),
+            shape((ROWS, 64), F32),
             shape((ROWS, 320), BF16),
             shape((ROWS, 320), BF16),
             shape((ROWS, 320), BF16),
@@ -397,9 +397,10 @@
     )
 
 
-def expert_back_kernel(forward, *refs):
+def expert_back_kernel(forward, me_ref, *refs):
+    me = me_ref[0]
     ins, (own_ref, other_ref), refs = refs[: 4 if forward else 8], refs[4 if forward else 8 :][:2], refs[6 if forward else 10 :]
-    sent, refs = refs[:4], refs[4:]
+    sent, refs = (refs[0], refs[1:]) if forward else (refs[:4], refs[4:])
     rows_out, d_result_out, act_own, act_other, dh_own, dh_other, d_total, total = refs
     step = pl.program_id(0)
 
@@ -432,26 +433,27 @@
         for d in range(N_SEQ):
             there = pl.ds(CAP * d, CAP)
             if forward:
-                sent[d][0] = total[there].astype(BF16)
-                sent[d][1] = d_total[there].astype(BF16)
+                to = lax.rem(me - d + N_SEQ, N_SEQ)
+                sent[to, 0] = total[there].astype(BF16)
+                sent[to, 1] = d_total[there].astype(BF16)
             else:
                 sent[d][...] = d_total[there].astype(BF16)
 
 
-def expert_back(blocks, packs, forward):
+def expert_back(me, blocks, packs, forward):
+    count, sent = (1, (N_SEQ, 2, CAP, D)) if forward else (4, (CAP, D))
     half = pl.BlockSpec((320, 768), lambda i: (0, i))
     block = whole_block((2, CAP, D)) if forward else whole_block((CAP, D))
-    sent = (2, CAP, D) if forward else (CAP, D)
     outs = grid_call(
         partial(expert_back_kernel, forward),
-        [shape(sent, BF16)] * 4 + [shape((320, D), BF16)] * 2 + [shape((320, 1536), BF16)] * 4,
-        [whole_block(sent)] * 4 + [whole_block((320, D))] * 2 + [half] * 4,
-        [*blocks, *packs],
-        [block] * len(blocks) + [pack_block()] * 2,
+        [shape(sent, BF16)] * count + [shape((320, D), BF16)] * 2 + [shape((320, 1536), BF16)] * 4,
+        [whole_block(sent)] * count + [whole_block((320, D))] * 2 + [half] * 4,
+        [me, *blocks, *packs],
+        [smem()] + [block] * len(blocks) + [pack_block()] * 2,
         "expert_back",
         [pltpu.VMEM((320, D), F32)] * 2,
     )
-    return outs[:4], *outs[4:]
+    return outs[:count], *outs[count:]
 
 
 def expert_grads_kernel(
@@ -493,27 +495,30 @@
     )(core, rows, d_result, act_own, dh_own, act_other, dh_other)
 
 
-def combine_kernel(residual_ref, high_ref, low_ref, r0, r1, r2, r3, out_ref, rows_ref):
-    for d, ref in enumerate((r0, r1, r2, r3)):
-        rows_ref[CAP * d : CAP * (d + 1)] = ref[...]
+def combine_kernel(whole, me_ref, residual_ref, high_ref, low_ref, *refs):
+    *blocks, out_ref, rows_ref = refs
+    for d in range(N_SEQ):
+        rows = blocks[0][lax.rem(me_ref[0] + d, N_SEQ), 0] if whole else blocks[d][...]
+        rows_ref[CAP * d : CAP * (d + 1)] = rows
     rows = rows_ref[...]
     total = residual_ref[...] + dot(high_ref[...], rows, 1, 0) + dot(low_ref[...], rows, 1, 0)
     out_ref[...] = total.astype(BF16)
 
 
-def combine(residual, high, low, blocks):
+def combine(me, residual, high, low, blocks):
     return call(
-        combine_kernel,
+        partial(combine_kernel, len(blocks) == 1),
         [shape((ROWS, D), BF16)],
-        [residual, high, low, *blocks],
+        [me, residual, high, low, *blocks],
         "combine",
+        scalars=1,
         scratch=[pltpu.VMEM((320, D), BF16)],
     )[0]
 
 
 def middle_back_kernel(paired, me_ref, d_out_ref, *refs):
     me = me_ref[0]
-    count = 4 if paired else 8
+    count = 1 if paired else 8
     blocks, refs = refs[:count], refs[count:]
     gathered, refs = refs[:4], refs[4:]
     (
@@ -522,8 +527,9 @@
     ) = refs
     for d in range(N_SEQ):
         there = pl.ds(CAP * d, CAP)
-        rows_ref[there] = blocks[d][0] if paired else blocks[d][...]
-        d_rows_ref[there] = blocks[d][1] if paired else blocks[4 + d][...]
+        origin = lax.rem(me + d, N_SEQ)
+        rows_ref[there] = blocks[0][origin, 0] if paired else blocks[d][...]
+        d_rows_ref[there] = blocks[0][origin, 1] if paired else blocks[4 + d][...]
     d_out = d_out_ref[...]
     chosen = chosen_ref[...]
     gates = gates_ref[...]
@@ -531,8 +537,8 @@
     slot = lax.broadcasted_iota(jnp.int32, (ROWS, 320), 1)
     own = jnp.where(slot >= 160, jnp.where(slot >= 240, 3, 2), jnp.where(slot >= 80, 1, 0))
     own = lax.rem(own + me, N_SEQ)
-    lane = lax.broadcasted_iota(jnp.int32, (ROWS, 128), 1)
-    d_gates = jnp.zeros((ROWS, 128), F32)
+    lane = lax.broadcasted_iota(jnp.int32, (ROWS, 64), 1)
+    d_gates = jnp.zeros((ROWS, 64), F32)
     for e in range(N_SEQ):
         part = jnp.sum(jnp.where(own == e, products, 0.0), axis=1, keepdims=True)
         d_gates = jnp.where(lane == e, part, d_gates)
@@ -546,15 +552,15 @@
     d_branch = d_residual.astype(BF16)
     for d, (ref, w_ref) in enumerate(zip((m0, m1, m2, m3), (w0, w1, w2, w3))):
         group = lax.rem(me - d + N_SEQ, N_SEQ)
-        ref[...] = dot(d_branch, w_ref[int(paired)], 1, 1).astype(BF16)
+        ref[...] = dot(d_branch, w_ref[...], 1, 1).astype(BF16)
         back_ref[group] = dot(gathered[d][...], d_branch, 0, 0).astype(BF16)
     grad_ref[...] = back_ref[...].reshape(D, D)
     high, low = two_parts(d_logits)
     small = dot(normed_ref[...], high, 0, 0) + dot(normed_ref[...], low, 0, 0)
-    column = (lax.broadcasted_iota(jnp.int32, (ROWS, 128), 1) == 5).astype(BF16)
+    column = (lax.broadcasted_iota(jnp.int32, (ROWS, 64), 1) == 5).astype(BF16)
     high, low = two_parts(d_normed * n)
     small = small + dot(high, column, 0, 0) + dot(low, column, 0, 0)
-    small_ref[...] = small[:, 0:64]
+    small_ref[...] = small
 
 
 def middle_back(me, d_out, blocks, gathered, chosen, gates, residual, normed, gains, w_back, paired):
@@ -600,18 +606,21 @@
     return outs[0], outs[1:]
 
 
-def attention_weights(x_blocks, w_qkv, w_proj, w_route, gain_attn, gain_ffn):
+def attention_weights(x, w_qkv, w_proj, w_route, gain_attn, gain_ffn):
     mine = w_qkv.reshape(12, 3, N_SEQ, 192).transpose(2, 0, 1, 3).reshape(N_SEQ, 12, 576)
     small = jnp.concatenate(
         [w_route, gain_attn[:, None], gain_ffn[:, None], jnp.zeros((12, 58), BF16)], axis=1
     )
     mine = jnp.concatenate([mine, jnp.broadcast_to(small, (N_SEQ, 12, 64))], axis=2)
+    mine, x = lax.optimization_barrier((mine, x))
+    x_blocks = [x] + [turn(x, -d) for d in (1, 2, 3)]
     arrived = lax.all_to_all(mine, "seq", 0, 0, tiled=True).reshape(48, 640)
     back = w_proj.reshape(12, N_SEQ, 192).transpose(1, 0, 2).reshape(48, 192)
     pack = jnp.concatenate([arrived, back], axis=1)
-    near = jnp.stack(from_ring(tie(pack, x_blocks), "x"))
+    near = jnp.stack(from_ring(pack, "x"))
+    near, x_blocks = lax.optimization_barrier((near, x_blocks))
     far = from_ring(near, "z")
-    return far, *unpack(far)
+    return far, x_blocks, *unpack(far)
 
 
 def both_layers(mine):
@@ -641,9 +650,8 @@
     x0 = pick(images_in, core)[0]
     d_last = pick(out_grad, core)[0]
     halves = half_packs(w_in[0, 0], w_out[0, 0])
-    x_blocks = [x0] + [turn(x0, -d) for d in (1, 2, 3)]
-    far, rows, back_rows = attention_weights(
-        x_blocks, w_qkv[0], w_proj[0], w_route[0], gain_attn[0], gain_ffn[0]
+    far, x_blocks, rows, back_rows = attention_weights(
+        x0, w_qkv[0], w_proj[0], w_route[0], gain_attn[0], gain_ffn[0]
     )
     own = lax.all_gather(tie(halves[0], far), "shard", axis=0, tiled=False)
     attn_rows = both_layers(rows)
@@ -651,11 +659,8 @@
     attn_rows[0], attn_rows[1], back_rows[0], back_rows[1] = lax.optimization_barrier(
         (attn_rows[0], attn_rows[1], back_rows[0], back_rows[1])
     )
-    w_mix = [v[:, :576] for v in attn_rows]
-    routers = [jnp.pad(v[:, 576:], ((0, 0), (0, 64))) for v in attn_rows]
     tables = [v[:, 576:584].T.astype(F32) for v in attn_rows]
-    back_rows = jnp.stack(back_rows)
-    w_back = [back_rows] + [turn(back_rows, d) for d in (1, 2, 3)]
+    w_back = [[back_rows[0]] + [turn(back_rows[0], d) for d in (1, 2, 3)], None]
     experts = [None, None]
 
     saved = []
@@ -664,25 +669,30 @@
     for s in range(2):
         if s == 1:
             x_blocks = [x] + [turn(x, -d) for d in (1, 2, 3)]
-        mixture, x_all, packed, logs = attend(x_blocks, w_mix[s], tables[s])
+        mixture, x_all, packed, logs = attend(x_blocks, attn_rows[s], tables[s])
         if s == 0:
-            w_back, mixture = lax.optimization_barrier((w_back, mixture))
+            w_back[0], mixture = lax.optimization_barrier((w_back[0], mixture))
         else:
             later, mixture[0] = lax.optimization_barrier((later, mixture[0]))
             experts[1] = (later, swap(later))
         gathered = send_out(mixture)
+        if s == 0:
+            later_back = tie(back_rows[1], gathered)
+            w_back[1] = [later_back] + [turn(later_back, d) for d in (1, 2, 3)]
         d_out = d_last if s == 1 else None
         residual, normed, gates, chosen, high, low, buffer = middle(
-            me, x, gathered, w_back, routers[s], tables[s], route_of[s], d_out
+            me, x, gathered, w_back[s], attn_rows[s], tables[s], route_of[s], d_out
         )
         blocks = send_out(buffer)
         kept = (x, x_all, packed, logs, gathered, residual, normed, gates, chosen, high, low, blocks)
         if s == 0:
-            own, blocks[1] = lax.optimization_barrier((own, blocks[1]))
+            own = tie(own, buffer[0])
             experts[0] = (own, swap(own))
             later = lax.all_gather(tie(halves[1], own), "shard", axis=0, tiled=False)
-            returned = send_back(expert_run(blocks, experts[s]))
-            x = combine(residual, high, low, returned)
+            result = expert_run(blocks, experts[s])
+            w_back[1], result = lax.optimization_barrier((w_back[1], result))
+            returned = send_back(result)
+            x = combine(me, residual, high, low, returned)
             layer_outs.append(x)
             saved.append((kept, returned))
         else:
@@ -697,21 +707,21 @@
         kept, returned = saved[s]
         x, x_all, packed, logs, gathered, residual, normed, gates, chosen, high, low, blocks = kept
         if s == 1:
-            sent, *states = expert_back(blocks, experts[s], True)
-            arrived = send_back(sent)
-            layer_outs.append(combine(residual, high, low, [v[0] for v in arrived]))
+            sent, *states = expert_back(me, blocks, experts[s], True)
+            arrived = [lax.all_to_all(sent[0], "seq", 0, 0, tiled=True)]
+            layer_outs.append(combine(me, residual, high, low, arrived))
         else:
-            sent, *states = expert_back([*blocks, *send_out(d_buffer)], experts[s], False)
+            sent, *states = expert_back(me, [*blocks, *send_out(d_buffer)], experts[s], False)
             arrived = [*returned, *send_back(sent)]
         d_residual, small, grad_back, d_mixture = middle_back(
-            me, d_out, arrived, gathered, chosen, gates, residual, normed, tables[s], w_back, s == 1
+            me, d_out, arrived, gathered, chosen, gates, residual, normed, tables[s], w_back[s], s == 1
         )
         d_heads = send_back(d_mixture)
         rows, d_result, act_own, act_other, dh_own, dh_other = states
         both = expert_grads(core_index, rows, d_result, act_own, dh_own, act_other, dh_other)
         both = both.reshape(2 * N_SHARD, 4, 48, D)
         expert_sums[s] = lax.psum_scatter(both, ("section", "shard"), scatter_dimension=0, tiled=True)[0]
-        d_normed, grad_mix = attend_back(x_all, w_mix[s], tables[s], packed, logs, d_heads, small)
+        d_normed, grad_mix = attend_back(x_all, attn_rows[s], tables[s], packed, logs, d_heads, small)
         d_parts = send_out(d_normed)
         keep = jnp.where(core == 0, grad_mix, grad_back)
         give = jnp.where(core == 0, grad_back, grad_mix)
@@ -720,10 +730,12 @@
         d_out, d_buffer = finish(d_residual, x, tables[s], d_parts, weights)
         in_grads[s] = d_out
 
-    pair = jnp.concatenate(attn_grads, axis=1).reshape(N_SEQ * N_SHARD, 12, 2 * D)
+    pair = jnp.concatenate(attn_grads, axis=1).reshape(N_SEQ * N_SHARD, 12, 12, 128)
+    pair = pair.transpose(0, 2, 1, 3).reshape(N_SEQ * N_SHARD, 144, 128)
     pair = tie(pair, d_parts)
     arrived = lax.all_to_all(pair, ("seq", "shard"), 0, 0, tiled=True)
-    attn_sum = jnp.sum(arrived.reshape(N_SEQ, N_SHARD, 12, 2 * D).astype(F32), axis=1)
+    attn_sum = jnp.sum(arrived.reshape(N_SEQ, N_SHARD, 144, 128).astype(F32), axis=1)
+    attn_sum = attn_sum.reshape(N_SEQ, 12, 12, 128).transpose(0, 2, 1, 3).reshape(N_SEQ, 12, 2 * D)
     attn_sums = [attn_sum[:, :, :D], attn_sum[:, :, D:]]
 
     def settle(pair):

time: 474 us -> 483 us (1.019)
  blocking collectives: 0 us -> 17.4 us
  waiting for transfers between devices: 176 us -> 171 us
    all_to_all x0 -> x1, blocking collectives: none -> 17.4 us  [shards(): arrived = [lax.all_to_all(sent[0], 'seq', 0, 0, tiled=True)]]
    ppermute x45, waiting for transfers between devices: 100 us -> 85.3 us  [turn(): return lax.ppermute(v, 'seq', [(i, (i + d) % N_SEQ) for i in range(N_SEQ)])]
    all_gather x1, waiting for transfers between devices: 0.01 us -> 12.4 us  [shards(): own = lax.all_gather(tie(halves[0], far), 'shard', axis=0, tiled=False)]
    slice x6 -> x0, local copies, waits for them, and re-layouts: 6.74 us -> none  [the longest x4 5.83 us: shards(): w_mix = [v[:, :576] for v in attn_rows]]
    all_to_all x1, waiting for transfers between devices: 47 us -> 40.6 us  [shards(): arrived = lax.all_to_all(pair, ('seq', 'shard'), 0, 0, tiled=True)]
    optimization_barrier x0 -> x4, local copies, waits for them, and re-layouts: none -> 6.36 us  [the longest x1 2.97 us: tie(): return lax.optimization_barrier((value, other))[0]]
    unnamed x160 -> x151, local copies, waits for them, and re-layouts: 15.3 us -> 16.2 us
  transfers between devices with their start and end apart: 69 -> 69, of which waited for: 40 -> 39; matrix products, arithmetic and copies ran while one was open for 9% -> 7% of each run, Pallas kernels for 20% -> 20%
where the time goes in v7:
time: 483 us; the launch traced here: 474 us
  waiting for transfers between devices  171 us (35%)
  Pallas kernels  118 us (24%)
  starting transfers between devices  95.8 us (20%)
  local copies, waits for them, and re-layouts  40.4 us (8%)
  blocking collectives  17.4 us (4%)
  other arithmetic  17 us (4%)
  between operations  14.6 us (3%)
    ppermute x45, waiting for transfers between devices, turn(): return lax.ppermute(v, 'seq', [(i, (i + d) % N_SEQ) for i in range(N_SEQ)])  85.3 us
    pallas_call x14, Pallas kernels, call(): pl.pallas_call(body, out_shape=outs, in_specs=specs, out_specs=[vmem()] *...  69.3 us
    ppermute x45, starting transfers between devices, turn(): return lax.ppermute(v, 'seq', [(i, (i + d) % N_SEQ) for i in range(N_SEQ)])  47.1 us
    all_to_all x1, waiting for transfers between devices, shards(): arrived = lax.all_to_all(pair, ('seq', 'shard'), 0, 0, tiled=True)  40.6 us
    pallas_call x3, Pallas kernels, grid_call(): pl.pallas_call(body, grid=(2,), out_shape=outs, in_specs=in_specs, out_sp...  29 us
    ppermute x12, starting transfers between devices, swap(): return lax.ppermute(v, 'section', [(0, 1), (1, 0)])  24.6 us
    pallas_call x2, Pallas kernels, expert_grads(): pl.pallas_call(expert_grads_kernel, out_shape=shape((2, N_SHARD, 4, 48, D...  19.9 us
    all_to_all x1, blocking collectives, shards(): arrived = [lax.all_to_all(sent[0], 'seq', 0, 0, tiled=True)]  17.4 us
  transfers between devices with their start and end apart: 69, of which 39 were waited for; matrix products, arithmetic and copies ran while one was open for 7% of the time, Pallas kernels for 20%

profile of v7, /device:TPU:1, one launch (start us, length us, event | category | flops | bytes accessed | tf_op | source)
XLA Modules:
  0.0 474.4 jit_solution(14621879725638708934)
XLA Ops:
  34.4 6.5 %collective-permute-done.5.x3 = bf16[144,768]{1,0:T(8,128)(2,1)S(1)} collective-permute-done((bf16[144,768]{1,0:T(8,128)(2,1)S(1)}, bf16[144,768]{1,0:T(8,128)(2,1)S(1)}, u32[]{:S(2)}, u32[]{:S(2)}) %collective-permute-start.5) | collective-permute-done | bytes 221216 | tf_op jit(solution)/shard_map/ppermute | solution.py:35
  54.2 8.2 %collective-permute-done.7.b2 = bf16[4,48,832]{2,1,0:T(8,128)(2,1)S(1)} collective-permute-done((bf16[4,48,832]{2,1,0:T(8,128)(2,1)S(1)}, bf16[4,48,832]{2,1,0:T(8,128)(2,1)S(1)}, u32[]{:S(2)}, u32[]{:S(2)}) %collective-permute-start.7) | collective-permute-done | bytes 319520 | tf_op jit(solution)/shard_map/ppermute | solution.py:44
  79.9 6.0 %attention.2 = (bf16[144,192]{1,0:T(8,128)(2,1)}, bf16[144,192]{1,0:T(8,128)(2,1)}, bf16[144,192]{1,0:T(8,128)(2,1)}, bf16[144,192]{1,0:T(8,128)(2,1)}, bf16[576...) custom-call(bf16[144,768]{1,0:T(8,128)(2,1)} %copy-done.9, bf16[144,768]{1,0:T(8,128)(2,1)} %copy-done.51, ...), custom_call_target="tpu_custom_call" | custom-call | tf_op jit(solution)/shard_map/attention/pallas_call | solution.py:105
  86.0 6.0 %collective-permute-done.11.w1.refs_18_ = bf16[192,768]{1,0:T(8,128)(2,1)S(1)} collective-permute-done((bf16[192,768]{1,0:T(8,128)(2,1)S(1)}, bf16[192,768]{1,0:T(8,128)(2,1)S(1)}, u32[]{:S(2)}, u32[]{:S(2)}) %collective-permute-start.11) | collective-permute-done | bytes 294944 | tf_op jit(solution)/shard_map/ppermute | solution.py:35
  103.0 12.4 %all-gather.5.cloned.1.call-done = bf16[64,48,768]{2,1,0:T(8,128)(2,1)} async-done(((bf16[4,48,768]{2,1,0:T(8,128)(2,1)}), bf16[64,48,768]{2,1,0:T(8,128)(2,1)}) %all-gather.5.cloned.1.call-update) | async-done | bytes 4718608 | tf_op jit(solution)/shard_map/all_gather | solution.py:656
  124.1 14.8 %collective-permute-done.22.r2.refs_2_ = bf16[80,768]{1,0:T(8,128)(2,1)S(1)} collective-permute-done((bf16[80,768]{1,0:T(8,128)(2,1)}, bf16[80,768]{1,0:T(8,128)(2,1)S(1)}, u32[]{:S(2)}, u32[]{:S(2)}) %collective-permute-start.22) | collective-permute-done | bytes 122912 | tf_op jit(solution)/shard_map/ppermute | solution.py:35
  145.6 7.0 %expert.1 = (bf16[80,768]{1,0:T(8,128)(2,1)}, bf16[80,768]{1,0:T(8,128)(2,1)}, bf16[80,768]{1,0:T(8,128)(2,1)}, bf16[80,768]{1,0:T(8,128)(2,1)}) custom-call(bf16[80,768]{1,0:T(8,128)(2,1)} %get-tuple-element.159.r0.refs_0_, bf16[80,768]{1,0:T(8,128)(2,1)} %copy-done.24, bf16[80,768]{1,0:T(8,128)(2,1)} %copy-done.25, bf16[80,768]{1,0:T(8,128)(2,1)} %copy-done.26, ...), custom_call_target="tpu_custom_call" | custom-call | tf_op jit(solution)/shard_map/expert/pallas_call | solution.py:374
  177.6 6.1 %attention.3 = (bf16[144,192]{1,0:T(8,128)(2,1)}, bf16[144,192]{1,0:T(8,128)(2,1)}, bf16[144,192]{1,0:T(8,128)(2,1)}, bf16[144,192]{1,0:T(8,128)(2,1)}, bf16[576...) custom-call(bf16[144,768]{1,0:T(8,128)(2,1)} %combine.2.x0.x_ref, bf16[144,768]{1,0:T(8,128)(2,1)} %copy-done.54, ...), custom_call_target="tpu_custom_call" | custom-call | tf_op jit(solution)/shard_map/attention/pallas_call | solution.py:105
  206.9 7.0 %collective-permute-done.36.refs_2_ = bf16[2,80,768]{2,1,0:T(8,128)(2,1)S(1)} collective-permute-done((bf16[2,80,768]{2,1,0:T(8,128)(2,1)}, bf16[2,80,768]{2,1,0:T(8,128)(2,1)S(1)}, u32[]{:S(2)}, u32[]{:S(2)}) %collective-permute-start.36) | collective-permute-done | bytes 245792 | tf_op jit(solution)/shard_map/ppermute | solution.py:35
  216.3 11.5 %expert_back.2 = (bf16[4,2,80,768]{3,2,1,0:T(8,128)(2,1)}, bf16[320,768]{1,0:T(8,128)(2,1)}, bf16[320,768]{1,0:T(8,128)(2,1)}, bf16[320,1536]{1,0:T(8,128)(2,1)}...) custom-call(s32[1]{0:T(128)} %bitcast.me_ref, ...), custom_call_target="tpu_custom_call" | custom-call | tf_op jit(solution)/shard_map/expert_back/pallas_call | solution.py:374
  227.8 9.9 %expert_grads.3 = bf16[2,16,4,48,768]{4,3,2,1,0:T(8,128)(2,1)} custom-call(s32[1]{0:T(128)} %bitcast.39.core_ref, bf16[320,768]{1,0:T(8,128)(2,1)} %get-tuple-element.245.rows_ref, bf16[320,768]{1,0:T(8,128)(2,1)} %get-tuple-element.246.d_result_ref, bf16[320,1536]{1,0:T(8,128)(2,1)} %get-tuple-element.247.act_own, ...), custom_call_target="tpu_custom_call" | custom-call | tf_op jit(solution)/shard_map/expert_grads/pallas_call | solution.py:479
  238.9 17.4 %all_to_all.15.refs_0_ = bf16[4,2,80,768]{3,2,1,0:T(8,128)(2,1)} all-to-all(bf16[4,2,80,768]{3,2,1,0:T(8,128)(2,1)S(1)} %copy-done.19), channel_id=1, replica_groups=mesh['section'=2,'seq'=4,'shard'=16] {'seq'}, dimensions={0} | all-to-all | bytes 1966080 | tf_op jit(solution)/shard_map/all_to_all | solution.py:711
  256.4 5.6 %middle_back.2 = (f32[144,768]{1,0:T(8,128)}, f32[768,64]{1,0:T(8,128)}, bf16[768,768]{1,0:T(8,128)(2,1)}, bf16[144,192]{1,0:T(8,128)(2,1)}, bf16[144,192]{1,0:T...) custom-call(s32[1]{0:T(128)} %bitcast.me_ref, ...), custom_call_target="tpu_custom_call" | custom-call | tf_op jit(solution)/shard_map/middle_back/pallas_call | solution.py:105
  269.6 10.0 %attention_back.2 = (bf16[144,768]{1,0:T(8,128)(2,1)}, bf16[144,768]{1,0:T(8,128)(2,1)}, bf16[144,768]{1,0:T(8,128)(2,1)}, bf16[144,768]{1,0:T(8,128)(2,1)}, bf16[768,768]{1,0:T(8,128)(2,1)}) custom-call(bf16[576,768]{1,0:T(8,128)(2,1)} %get-tuple-element.197.x_ref, bf16[768,640]{1,0:T(8,128)(2,1)} %copy.140.w_ref.router_ref, ...), custom_call_target="tpu_custom_call" | custom-call | tf_op jit(solution)/shard_map/attention_back/pallas_call | solution.py:105
  282.5 5.6 %collective-permute-done.43.b1 = bf16[144,768]{1,0:T(8,128)(2,1)S(1)} collective-permute-done((bf16[144,768]{1,0:T(8,128)(2,1)}, bf16[144,768]{1,0:T(8,128)(2,1)S(1)}, u32[]{:S(2)}, u32[]{:S(2)}) %collective-permute-start.43) | collective-permute-done | bytes 221216 | tf_op jit(solution)/shard_map/ppermute | solution.py:35
  293.9 5.4 %collective-permute-start.47 = (bf16[80,768]{1,0:T(8,128)(2,1)}, bf16[80,768]{1,0:T(8,128)(2,1)S(1)}, u32[]{:S(2)}, u32[]{:S(2)}) collective-permute-start(bf16[80,768]{1,0:T(8,128)(2,1)} %get-tuple-element.212), channel_id=1, source_target_pairs={{0,32},{16,48},{32,0},{48,16},{1,33},{17,49},{33,1},{49,17},{2,34}... | collective-permute-start | bytes 368648 | tf_op jit(solution)/shard_map/ppermute | solution.py:35
  304.7 10.5 %expert_back.3 = (bf16[80,768]{1,0:T(8,128)(2,1)}, bf16[80,768]{1,0:T(8,128)(2,1)}, bf16[80,768]{1,0:T(8,128)(2,1)}, bf16[80,768]{1,0:T(8,128)(2,1)}, bf16[320,7...) custom-call(s32[1]{0:T(128)} %bitcast.me_ref, ...), custom_call_target="tpu_custom_call" | custom-call | tf_op jit(solution)/shard_map/expert_back/pallas_call | solution.py:374
  315.2 10.0 %expert_grads.2 = bf16[2,16,4,48,768]{4,3,2,1,0:T(8,128)(2,1)} custom-call(s32[1]{0:T(128)} %bitcast.39.core_ref, bf16[320,768]{1,0:T(8,128)(2,1)} %get-tuple-element.239.rows_ref, bf16[320,768]{1,0:T(8,128)(2,1)} %get-tuple-element.240.d_result_ref, bf16[320,1536]{1,0:T(8,128)(2,1)} %get-tuple-element.241.act_own, ...), custom_call_target="tpu_custom_call" | custom-call | tf_op jit(solution)/shard_map/expert_grads/pallas_call | solution.py:479
  334.4 5.6 %middle_back.3 = (f32[144,768]{1,0:T(8,128)}, f32[768,64]{1,0:T(8,128)}, bf16[768,768]{1,0:T(8,128)(2,1)}, bf16[144,192]{1,0:T(8,128)(2,1)}, bf16[144,192]{1,0:T...) custom-call(s32[1]{0:T(128)} %bitcast.me_ref, bf16[144,768]{1,0:T(8,128)(2,1)} %get-tuple-element.209.d_out_ref, ...), custom_call_target="tpu_custom_call" | custom-call | tf_op jit(solution)/shard_map/middle_back/pallas_call | solution.py:105
  342.2 6.0 %collective-permute-start.60 = (bf16[768,768]{1,0:T(8,128)(2,1)S(1)}, bf16[768,768]{1,0:T(8,128)(2,1)S(1)}, u32[]{:S(2)}, u32[]{:S(2)}) collective-permute-start(bf16[768,768]{1,0:T(8,128)(2,1)S(1)} %broadcast_select_fusion), channel_id=1, source_target_pairs={{0,64},{64,0},{1,65},{65,1},{2,66},{66,2},{3,67},{67,3},{4,68},{68... | collective-permute-start | bytes 3538952 | tf_op jit(solution)/shard_map/ppermute | solution.py:31
  348.9 10.0 %attention_back.3 = (bf16[144,768]{1,0:T(8,128)(2,1)}, bf16[144,768]{1,0:T(8,128)(2,1)}, bf16[144,768]{1,0:T(8,128)(2,1)}, bf16[144,768]{1,0:T(8,128)(2,1)}, bf16[768,768]{1,0:T(8,128)(2,1)}) custom-call(bf16[576,768]{1,0:T(8,128)(2,1)} %get-tuple-element.222.x_ref, bf16[768,640]{1,0:T(8,128)(2,1)} %copy.135.w_ref.router_ref, ...), custom_call_target="tpu_custom_call" | custom-call | tf_op jit(solution)/shard_map/attention_back/pallas_call | solution.py:105
  380.1 8.5 %all-to-all-start.2 = ((bf16[64,144,128]{2,1,0:T(8,128)(2,1)}), bf16[64,144,128]{2,1,0:T(8,128)(2,1)S(1)}, u32[]{:S(2)}, u32[]{:S(2)}) async-start(bf16[64,144,128]{2,1,0:T(8,128)(2,1)} %copy.145), calls=%async_computation.2 | async-start | bytes 4718592 | tf_op jit(solution)/shard_map/all_to_all | solution.py:736
  397.8 40.6 %all-to-all-done.2 = bf16[64,144,128]{2,1,0:T(8,128)(2,1)S(1)} async-done(((bf16[64,144,128]{2,1,0:T(8,128)(2,1)}), bf16[64,144,128]{2,1,0:T(8,128)(2,1)S(1)}, u32[]{:S(2)}, u32[]{:S(2)}) %all-to-all-start.2) | async-done | bytes 2359328 | tf_op jit(solution)/shard_map/all_to_all | solution.py:736
  445.5 11.8 %reduce-scatter.3.cloned.1.call-done = bf16[1,4,48,768]{3,2,1,0:T(8,128)(2,1)} async-done(((bf16[32,4,48,768]{3,2,1,0:T(8,128)(2,1)}), bf16[1,4,48,768]{3,2,1,0:T(8,128)(2,1)}) %reduce-scatter.3.cloned.1.call-update) | async-done | bytes 294928 | tf_op jit(solution)/shard_map/reduce_scatter | solution.py:723
  (354 shorter events, 217.3 us)
Async XLA Ops:
  16.8 98.7 %all-gather.5.cloned.1.call-start = ((), (), s32[]{:S(2)}) async-start(), calls=%async_computation.7 | async-start | bytes 5013504 | tf_op jit(solution)/shard_map/all_gather | solution.py:656
  25.1 23.4 %collective-permute-start.24 = (bf16[4,48,768]{2,1,0:T(8,128)(2,1)S(1)}, bf16[4,48,768]{2,1,0:T(8,128)(2,1)S(1)}, u32[]{:S(2)}, u32[]{:S(2)}) collective-permute-start(bf16[4,48,768]{2,1,0:T(8,128)(2,1)S(1)} %dynamic-slice_bitcast_fusion), channel_id=1, source_target_pairs={{0,64},{64,0},{1,65},{65,1},{2,66},{66,2},{3,67},{67,3},{4,68},{68... | collective-permute-start | bytes 884744 | tf_op jit(solution)/shard_map/ppermute | solution.py:31
  27.9 12.9 %collective-permute-start.5 = (bf16[144,768]{1,0:T(8,128)(2,1)S(1)}, bf16[144,768]{1,0:T(8,128)(2,1)S(1)}, u32[]{:S(2)}, u32[]{:S(2)}) collective-permute-start(bf16[144,768]{1,0:T(8,128)(2,1)S(1)} %dynamic-slice_bitcast_fusion.2.x0.x_ref), channel_id=1, source_target_pairs={{0,16},{16,32},{32,48},{48,0},{1,17},{17,33},{33,49},{49,1},{2,18}... | collective-permute-start | bytes 663560 | tf_op jit(solution)/shard_map/ppermute | solution.py:35
  28.2 12.7 %collective-permute-start.4 = (bf16[144,768]{1,0:T(8,128)(2,1)S(1)}, bf16[144,768]{1,0:T(8,128)(2,1)S(1)}, u32[]{:S(2)}, u32[]{:S(2)}) collective-permute-start(bf16[144,768]{1,0:T(8,128)(2,1)S(1)} %dynamic-slice_bitcast_fusion.2.x0.x_ref), channel_id=1, source_target_pairs={{0,32},{16,48},{32,0},{48,16},{1,33},{17,49},{33,1},{49,17},{2,34}... | collective-permute-start | bytes 663560 | tf_op jit(solution)/shard_map/ppermute | solution.py:35
  30.0 12.2 %collective-permute-start.3 = (bf16[144,768]{1,0:T(8,128)(2,1)S(1)}, bf16[144,768]{1,0:T(8,128)(2,1)S(1)}, u32[]{:S(2)}, u32[]{:S(2)}) collective-permute-start(bf16[144,768]{1,0:T(8,128)(2,1)S(1)} %dynamic-slice_bitcast_fusion.2.x0.x_ref), channel_id=1, source_target_pairs={{0,48},{16,0},{32,16},{48,32},{1,49},{17,1},{33,17},{49,33},{2,50}... | collective-permute-start | bytes 663560 | tf_op jit(solution)/shard_map/ppermute | solution.py:35
  44.5 17.9 %collective-permute-start.7 = (bf16[4,48,832]{2,1,0:T(8,128)(2,1)S(1)}, bf16[4,48,832]{2,1,0:T(8,128)(2,1)S(1)}, u32[]{:S(2)}, u32[]{:S(2)}) collective-permute-start(bf16[4,48,832]{2,1,0:T(8,128)(2,1)S(1)} %pad_maximum_fusion.2.b0), channel_id=1, source_target_pairs={{0,8},{1,9},{2,10},{3,11},{4,12},{5,13},{6,14},{7,15},{8,0},{9,1},... | collective-permute-start | bytes 958472 | tf_op jit(solution)/shard_map/ppermute | solution.py:44
  47.8 14.6 %collective-permute-start.6 = (bf16[4,48,832]{2,1,0:T(8,128)(2,1)S(1)}, bf16[4,48,832]{2,1,0:T(8,128)(2,1)S(1)}, u32[]{:S(2)}, u32[]{:S(2)}) collective-permute-start(bf16[4,48,832]{2,1,0:T(8,128)(2,1)S(1)} %pad_maximum_fusion.2.b0), channel_id=1, source_target_pairs={{0,12},{1,13},{2,14},{3,15},{4,0},{5,1},{6,2},{7,3},{8,4},{9,5},{1... | collective-permute-start | bytes 958472 | tf_op jit(solution)/shard_map/ppermute | solution.py:44
  62.5 121.2 %all-gather.7.cloned.1.call-start = ((), (), s32[]{:S(2)}) async-start(), calls=%async_computation.8 | async-start | bytes 5013504 | tf_op jit(solution)/shard_map/all_gather | solution.py:691
  75.8 16.1 %collective-permute-start.11 = (bf16[192,768]{1,0:T(8,128)(2,1)S(1)}, bf16[192,768]{1,0:T(8,128)(2,1)S(1)}, u32[]{:S(2)}, u32[]{:S(2)}) collective-permute-start(bf16[192,768]{1,0:T(8,128)(2,1)S(1)} %get-tuple-element.150.w0.refs_17_), channel_id=1, source_target_pairs={{0,16},{16,32},{32,48},{48,0},{1,17},{17,33},{33,49},{49,1},{2,18}... | collective-permute-start | bytes 884744 | tf_op jit(solution)/shard_map/ppermute | solution.py:35
  76.6 18.0 %collective-permute-start.17 = (s32[144,2]{1,0:T(8,128)S(1)}, s32[144,2]{1,0:T(8,128)}, u32[]{:S(2)}, u32[]{:S(2)}) collective-permute-start(s32[144,2]{1,0:T(8,128)S(1)} %bitcast.109), channel_id=1, source_target_pairs={{0,64},{64,0},{1,65},{65,1},{2,66},{66,2},{3,67},{67,3},{4,68},{68... | collective-permute-start | bytes 3464 | tf_op jit(solution)/shard_map/ppermute | solution.py:31
  115.5 330.1 %reduce-scatter.5.cloned.1.call-start = ((), (), s32[]{:S(2)}) async-start(), calls=%async_computation.6 | async-start | bytes 9732096 | tf_op jit(solution)/shard_map/reduce_scatter | solution.py:723
  115.5 27.3 %collective-permute-start.25 = (bf16[16,4,48,768]{3,2,1,0:T(8,128)(2,1)}, bf16[16,4,48,768]{3,2,1,0:T(8,128)(2,1)S(1)}, u32[]{:S(2)}, u32[]{:S(2)}) collective-permute-start(bf16[16,4,48,768]{3,2,1,0:T(8,128)(2,1)} %bitcast.87), channel_id=1, source_target_pairs={{0,64},{64,0},{1,65},{65,1},{2,66},{66,2},{3,67},{67,3},{4,68},{68... | collective-permute-start | bytes 14155784 | tf_op jit(solution)/shard_map/ppermute | solution.py:31
  117.5 35.1 %collective-permute-start.20 = (bf16[192,768]{1,0:T(8,128)(2,1)S(1)}, bf16[192,768]{1,0:T(8,128)(2,1)S(1)}, u32[]{:S(2)}, u32[]{:S(2)}) collective-permute-start(bf16[192,768]{1,0:T(8,128)(2,1)S(1)} %copy-done.11), channel_id=1, source_target_pairs={{0,48},{16,0},{32,16},{48,32},{1,49},{17,1},{33,17},{49,33},{2,50}... | collective-permute-start | bytes 884744 | tf_op jit(solution)/shard_map/ppermute | solution.py:35
  119.0 33.7 %collective-permute-start.19 = (bf16[192,768]{1,0:T(8,128)(2,1)S(1)}, bf16[192,768]{1,0:T(8,128)(2,1)S(1)}, u32[]{:S(2)}, u32[]{:S(2)}) collective-permute-start(bf16[192,768]{1,0:T(8,128)(2,1)S(1)} %copy-done.11), channel_id=1, source_target_pairs={{0,32},{16,48},{32,0},{48,16},{1,33},{17,49},{33,1},{49,17},{2,34}... | collective-permute-start | bytes 884744 | tf_op jit(solution)/shard_map/ppermute | solution.py:35
  120.5 32.2 %collective-permute-start.18 = (bf16[192,768]{1,0:T(8,128)(2,1)S(1)}, bf16[192,768]{1,0:T(8,128)(2,1)S(1)}, u32[]{:S(2)}, u32[]{:S(2)}) collective-permute-start(bf16[192,768]{1,0:T(8,128)(2,1)S(1)} %copy-done.11), channel_id=1, source_target_pairs={{0,16},{16,32},{32,48},{48,0},{1,17},{17,33},{33,49},{49,1},{2,18}... | collective-permute-start | bytes 884744 | tf_op jit(solution)/shard_map/ppermute | solution.py:35
  122.6 16.3 %collective-permute-start.22 = (bf16[80,768]{1,0:T(8,128)(2,1)}, bf16[80,768]{1,0:T(8,128)(2,1)S(1)}, u32[]{:S(2)}, u32[]{:S(2)}) collective-permute-start(bf16[80,768]{1,0:T(8,128)(2,1)} %get-tuple-element.161), channel_id=1, source_target_pairs={{0,32},{16,48},{32,0},{48,16},{1,33},{17,49},{33,1},{49,17},{2,34}... | collective-permute-start | bytes 368648 | tf_op jit(solution)/shard_map/ppermute | solution.py:35
  183.7 30.2 %collective-permute-start.38 = (bf16[16,4,48,768]{3,2,1,0:T(8,128)(2,1)}, bf16[16,4,48,768]{3,2,1,0:T(8,128)(2,1)S(1)}, u32[]{:S(2)}, u32[]{:S(2)}) collective-permute-start(bf16[16,4,48,768]{3,2,1,0:T(8,128)(2,1)} %bitcast.92), channel_id=1, source_target_pairs={{0,64},{64,0},{1,65},{65,1},{2,66},{66,2},{3,67},{67,3},{4,68},{68... | collective-permute-start | bytes 14155784 | tf_op jit(solution)/shard_map/ppermute | solution.py:31
  199.8 14.2 %collective-permute-start.36 = (bf16[2,80,768]{2,1,0:T(8,128)(2,1)}, bf16[2,80,768]{2,1,0:T(8,128)(2,1)S(1)}, u32[]{:S(2)}, u32[]{:S(2)}) collective-permute-start(bf16[2,80,768]{2,1,0:T(8,128)(2,1)} %get-tuple-element.189), channel_id=1, source_target_pairs={{0,32},{16,48},{32,0},{48,16},{1,33},{17,49},{33,1},{49,17},{2,34}... | collective-permute-start | bytes 737288 | tf_op jit(solution)/shard_map/ppermute | solution.py:35
  237.8 219.5 %reduce-scatter.3.cloned.1.call-start = ((), (), s32[]{:S(2)}) async-start(), calls=%async_computation.5 | async-start | bytes 9732096 | tf_op jit(solution)/shard_map/reduce_scatter | solution.py:723
  342.2 24.8 %collective-permute-start.60 = (bf16[768,768]{1,0:T(8,128)(2,1)S(1)}, bf16[768,768]{1,0:T(8,128)(2,1)S(1)}, u32[]{:S(2)}, u32[]{:S(2)}) collective-permute-start(bf16[768,768]{1,0:T(8,128)(2,1)S(1)} %broadcast_select_fusion), channel_id=1, source_target_pairs={{0,64},{64,0},{1,65},{65,1},{2,66},{66,2},{3,67},{67,3},{4,68},{68... | collective-permute-start | bytes 3538952 | tf_op jit(solution)/shard_map/ppermute | solution.py:31
  364.1 12.8 %collective-permute-start.56 = (bf16[144,768]{1,0:T(8,128)(2,1)S(1)}, bf16[144,768]{1,0:T(8,128)(2,1)S(1)}, u32[]{:S(2)}, u32[]{:S(2)}) collective-permute-start(bf16[144,768]{1,0:T(8,128)(2,1)S(1)} %copy-done.71), channel_id=1, source_target_pairs={{0,32},{16,48},{32,0},{48,16},{1,33},{17,49},{33,1},{49,17},{2,34}... | collective-permute-start | bytes 663560 | tf_op jit(solution)/shard_map/ppermute | solution.py:35
  380.1 58.3 %all-to-all-start.2 = ((bf16[64,144,128]{2,1,0:T(8,128)(2,1)}), bf16[64,144,128]{2,1,0:T(8,128)(2,1)S(1)}, u32[]{:S(2)}, u32[]{:S(2)}) async-start(bf16[64,144,128]{2,1,0:T(8,128)(2,1)} %copy.145), calls=%async_computation.2 | async-start | bytes 4718592 | tf_op jit(solution)/shard_map/all_to_all | solution.py:736
  392.7 49.0 %collective-permute-start.39 = (bf16[144,768]{1,0:T(8,128)(2,1)S(1)}, bf16[144,768]{1,0:T(8,128)(2,1)}, u32[]{:S(2)}, u32[]{:S(2)}) collective-permute-start(bf16[144,768]{1,0:T(8,128)(2,1)S(1)} %get-tuple-element.302), channel_id=1, source_target_pairs={{0,64},{64,0},{1,65},{65,1},{2,66},{66,2},{3,67},{67,3},{4,68},{68... | collective-permute-start | bytes 663560 | tf_op jit(solution)/shard_map/ppermute | solution.py:31
  397.8 45.7 %collective-permute-start.58 = (bf16[144,768]{1,0:T(8,128)(2,1)}, bf16[144,768]{1,0:T(8,128)(2,1)}, u32[]{:S(2)}, u32[]{:S(2)}) collective-permute-start(bf16[144,768]{1,0:T(8,128)(2,1)} %get-tuple-element.300), channel_id=1, source_target_pairs={{0,64},{64,0},{1,65},{65,1},{2,66},{66,2},{3,67},{67,3},{4,68},{68... | collective-permute-start | bytes 663560 | tf_op jit(solution)/shard_map/ppermute | solution.py:31
  (120 other events, 662.4 us)
Sparse Core Ops, SparseCore 0:
  62.6 52.7 all-gather.4
  117.6 53.6 all-gather.6
  237.9 93.2 reduce-scatter.4
  335.3 121.9 reduce-scatter.2

commit v8 on v6

--- a/solution.py
+++ b/solution.py
@@ -118,7 +118,7 @@
         x_ref[ROWS * d : ROWS * (d + 1)] = ref[...]
     n, _ = norm_parts(x_ref[...].astype(F32))
     normed = (n * gain_ref[4:5, :]).astype(BF16)
-    packed_ref[...] = dot(normed, w_ref[...], 1, 0).astype(BF16)
+    packed_ref[...] = dot(normed, w_ref[:, 0:576], 1, 0).astype(BF16)
     lane = lax.broadcasted_iota(jnp.int32, (SEQ, 128), 1)
     logs = jnp.zeros((SEQ, 128), F32)
     outs = []
@@ -173,7 +173,7 @@
     n, _ = norm_parts(x_ref[...].astype(F32))
     normed = (n * gain_ref[4:5, :]).astype(BF16)
     d_packed = d_packed_ref[...]
-    d_normed = dot(d_packed, w_ref[...], 1, 1)
+    d_normed = dot(d_packed, w_ref[:, 0:576], 1, 1)
     for d, ref in enumerate((n0, n1, n2, n3)):
         ref[...] = d_normed[ROWS * d : ROWS * (d + 1)].astype(BF16)
     column = (lax.broadcasted_iota(jnp.int32, (SEQ, 64), 1) == 4).astype(BF16)
@@ -268,13 +268,13 @@
     residual_ref, normed_ref, gates_ref, chosen_ref, high_ref, low_ref, *sent = refs
     residual = x_ref[...].astype(F32)
     for ref, w_ref in zip((g0, g1, g2, g3), (w0, w1, w2, w3)):
-        residual = residual + dot(ref[...], w_ref[layer], 1, 0)
+        residual = residual + dot(ref[...], w_ref[...], 1, 0)
     residual_ref[...] = residual
     n, _ = norm_parts(residual)
     normed = (n * gain_ref[5:6, :]).astype(BF16)
     normed_ref[...] = normed
-    lane = lax.broadcasted_iota(jnp.int32, (ROWS, 128), 1)
-    logits = jnp.where(lane < 4, dot(normed, router_ref[...], 1, 0), -1e30)
+    lane = lax.broadcasted_iota(jnp.int32, (ROWS, 64), 1)
+    logits = jnp.where(lane < 4, dot(normed, router_ref[:, 576:640], 1, 0), -1e30)
     logits = logits - jnp.max(logits, axis=1, keepdims=True)
     gates = jnp.exp(logits)
     gates = gates / jnp.sum(gates, axis=1, keepdims=True)
@@ -321,7 +321,7 @@
         [
             shape((ROWS, D), F32),
             shape((ROWS, D), BF16),
-            shape((ROWS, 128), F32),
+            shape((ROWS, 64), F32),
             shape((ROWS, 320), BF16),
             shape((ROWS, 320), BF16),
             shape((ROWS, 320), BF16),
@@ -493,6 +493,31 @@
     )(core, rows, d_result, act_own, dh_own, act_other, dh_other)
 
 
+def expert_grad_kernel(rows_ref, d_result_ref, act_ref, dh_ref, *refs):
+    *extra, out_ref = refs
+    for i, grad in enumerate((
+        dot(rows_ref[...], dh_ref[...], 0, 0),
+        dot(act_ref[...], d_result_ref[...], 0, 0),
+    )):
+        grad = grad.reshape(N_SHARD, 48, 768)
+        if extra:
+            grad = grad + extra[0][:, i].astype(F32)
+        out_ref[:, i] = grad.astype(BF16)
+
+
+def expert_grad(rows, d_result, active, d_hidden, extra=()):
+    half = pl.BlockSpec((320, 768), lambda i: (0, i))
+    return grid_call(
+        expert_grad_kernel,
+        [shape((N_SHARD, 4, 48, 768), BF16)],
+        [pack_block()],
+        [rows, d_result, active, d_hidden, *extra],
+        [whole_block((320, D))] * 2 + [half] * 2 + [pack_block()] * len(extra),
+        "expert_grad",
+        [],
+    )[0]
+
+
 def combine_kernel(residual_ref, high_ref, low_ref, r0, r1, r2, r3, out_ref, rows_ref):
     for d, ref in enumerate((r0, r1, r2, r3)):
         rows_ref[CAP * d : CAP * (d + 1)] = ref[...]
@@ -531,8 +556,8 @@
     slot = lax.broadcasted_iota(jnp.int32, (ROWS, 320), 1)
     own = jnp.where(slot >= 160, jnp.where(slot >= 240, 3, 2), jnp.where(slot >= 80, 1, 0))
     own = lax.rem(own + me, N_SEQ)
-    lane = lax.broadcasted_iota(jnp.int32, (ROWS, 128), 1)
-    d_gates = jnp.zeros((ROWS, 128), F32)
+    lane = lax.broadcasted_iota(jnp.int32, (ROWS, 64), 1)
+    d_gates = jnp.zeros((ROWS, 64), F32)
     for e in range(N_SEQ):
         part = jnp.sum(jnp.where(own == e, products, 0.0), axis=1, keepdims=True)
         d_gates = jnp.where(lane == e, part, d_gates)
@@ -546,15 +571,15 @@
     d_branch = d_residual.astype(BF16)
     for d, (ref, w_ref) in enumerate(zip((m0, m1, m2, m3), (w0, w1, w2, w3))):
         group = lax.rem(me - d + N_SEQ, N_SEQ)
-        ref[...] = dot(d_branch, w_ref[int(paired)], 1, 1).astype(BF16)
+        ref[...] = dot(d_branch, w_ref[...], 1, 1).astype(BF16)
         back_ref[group] = dot(gathered[d][...], d_branch, 0, 0).astype(BF16)
     grad_ref[...] = back_ref[...].reshape(D, D)
     high, low = two_parts(d_logits)
     small = dot(normed_ref[...], high, 0, 0) + dot(normed_ref[...], low, 0, 0)
-    column = (lax.broadcasted_iota(jnp.int32, (ROWS, 128), 1) == 5).astype(BF16)
+    column = (lax.broadcasted_iota(jnp.int32, (ROWS, 64), 1) == 5).astype(BF16)
     high, low = two_parts(d_normed * n)
     small = small + dot(high, column, 0, 0) + dot(low, column, 0, 0)
-    small_ref[...] = small[:, 0:64]
+    small_ref[...] = small
 
 
 def middle_back(me, d_out, blocks, gathered, chosen, gates, residual, normed, gains, w_back, paired):
@@ -651,11 +676,8 @@
     attn_rows[0], attn_rows[1], back_rows[0], back_rows[1] = lax.optimization_barrier(
         (attn_rows[0], attn_rows[1], back_rows[0], back_rows[1])
     )
-    w_mix = [v[:, :576] for v in attn_rows]
-    routers = [jnp.pad(v[:, 576:], ((0, 0), (0, 64))) for v in attn_rows]
     tables = [v[:, 576:584].T.astype(F32) for v in attn_rows]
-    back_rows = jnp.stack(back_rows)
-    w_back = [back_rows] + [turn(back_rows, d) for d in (1, 2, 3)]
+    w_back = [[back_rows[0]] + [turn(back_rows[0], d) for d in (1, 2, 3)], None]
     experts = [None, None]
 
     saved = []
@@ -664,24 +686,28 @@
     for s in range(2):
         if s == 1:
             x_blocks = [x] + [turn(x, -d) for d in (1, 2, 3)]
-        mixture, x_all, packed, logs = attend(x_blocks, w_mix[s], tables[s])
+        mixture, x_all, packed, logs = attend(x_blocks, attn_rows[s], tables[s])
         if s == 0:
-            w_back, mixture = lax.optimization_barrier((w_back, mixture))
+            w_back[0], mixture = lax.optimization_barrier((w_back[0], mixture))
         else:
             later, mixture[0] = lax.optimization_barrier((later, mixture[0]))
             experts[1] = (later, swap(later))
         gathered = send_out(mixture)
         d_out = d_last if s == 1 else None
         residual, normed, gates, chosen, high, low, buffer = middle(
-            me, x, gathered, w_back, routers[s], tables[s], route_of[s], d_out
+            me, x, gathered, w_back[s], attn_rows[s], tables[s], route_of[s], d_out
         )
         blocks = send_out(buffer)
         kept = (x, x_all, packed, logs, gathered, residual, normed, gates, chosen, high, low, blocks)
         if s == 0:
-            own, blocks[1] = lax.optimization_barrier((own, blocks[1]))
+            own = tie(own, blocks)
             experts[0] = (own, swap(own))
             later = lax.all_gather(tie(halves[1], own), "shard", axis=0, tiled=False)
-            returned = send_back(expert_run(blocks, experts[s]))
+            later_back = tie(back_rows[1], blocks)
+            w_back[1] = [later_back] + [turn(later_back, d) for d in (1, 2, 3)]
+            result = expert_run(blocks, experts[s])
+            w_back[1], result = lax.optimization_barrier((w_back[1], result))
+            returned = send_back(result)
             x = combine(residual, high, low, returned)
             layer_outs.append(x)
             saved.append((kept, returned))
@@ -704,14 +730,20 @@
             sent, *states = expert_back([*blocks, *send_out(d_buffer)], experts[s], False)
             arrived = [*returned, *send_back(sent)]
         d_residual, small, grad_back, d_mixture = middle_back(
-            me, d_out, arrived, gathered, chosen, gates, residual, normed, tables[s], w_back, s == 1
+            me, d_out, arrived, gathered, chosen, gates, residual, normed, tables[s], w_back[s], s == 1
         )
         d_heads = send_back(d_mixture)
         rows, d_result, act_own, act_other, dh_own, dh_other = states
-        both = expert_grads(core_index, rows, d_result, act_own, dh_own, act_other, dh_other)
-        both = both.reshape(2 * N_SHARD, 4, 48, D)
-        expert_sums[s] = lax.psum_scatter(both, ("section", "shard"), scatter_dimension=0, tiled=True)[0]
-        d_normed, grad_mix = attend_back(x_all, w_mix[s], tables[s], packed, logs, d_heads, small)
+        if s == 1:
+            both = expert_grads(core_index, rows, d_result, act_own, dh_own, act_other, dh_other)
+            both = both.reshape(2 * N_SHARD, 4, 48, D)
+            group = ("section", "shard")
+        else:
+            other = swap(expert_grad(rows, d_result, act_other, dh_other))
+            both = expert_grad(rows, d_result, act_own, dh_own, (other,))
+            group = "shard"
+        expert_sums[s] = lax.psum_scatter(both, group, scatter_dimension=0, tiled=True)[0]
+        d_normed, grad_mix = attend_back(x_all, attn_rows[s], tables[s], packed, logs, d_heads, small)
         d_parts = send_out(d_normed)
         keep = jnp.where(core == 0, grad_mix, grad_back)
         give = jnp.where(core == 0, grad_back, grad_mix)
@@ -720,10 +752,12 @@
         d_out, d_buffer = finish(d_residual, x, tables[s], d_parts, weights)
         in_grads[s] = d_out
 
-    pair = jnp.concatenate(attn_grads, axis=1).reshape(N_SEQ * N_SHARD, 12, 2 * D)
+    pair = jnp.concatenate(attn_grads, axis=1).reshape(N_SEQ * N_SHARD, 12, 12, 128)
+    pair = pair.transpose(0, 2, 1, 3).reshape(N_SEQ * N_SHARD, 144, 128)
     pair = tie(pair, d_parts)
     arrived = lax.all_to_all(pair, ("seq", "shard"), 0, 0, tiled=True)
-    attn_sum = jnp.sum(arrived.reshape(N_SEQ, N_SHARD, 12, 2 * D).astype(F32), axis=1)
+    attn_sum = jnp.sum(arrived.reshape(N_SEQ, N_SHARD, 144, 128).astype(F32), axis=1)
+    attn_sum = attn_sum.reshape(N_SEQ, 12, 12, 128).transpose(0, 2, 1, 3).reshape(N_SEQ, 12, 2 * D)
     attn_sums = [attn_sum[:, :, :D], attn_sum[:, :, D:]]
 
     def settle(pair):

time: 474 us -> 450 us (0.949)
  waiting for transfers between devices: 176 us -> 153 us
  starting transfers between devices: 100 us -> 92 us
  local copies, waits for them, and re-layouts: 40.1 us -> 45.4 us
    all_to_all x1, waiting for transfers between devices: 47 us -> 24.2 us  [shards(): arrived = lax.all_to_all(pair, ('seq', 'shard'), 0, 0, tiled=True)]
    pallas_call x3 -> x5, Pallas kernels: 29.3 us -> 41.7 us  [grid_call(): pl.pallas_call(body, grid=(2,), out_shape=outs, in_specs=in_specs, out_sp...]
    reduce_scatter x2 -> x1, waiting for transfers between devices: 11.9 us -> 0.02 us  [shards(): lax.psum_scatter(both, group, scatter_dimension=0, tiled=True)[0]]
    ppermute x12 -> x13, waiting for transfers between devices: 2.54 us -> 14.4 us  [swap(): return lax.ppermute(v, 'section', [(0, 1), (1, 0)])]
    ppermute x12 -> x13, starting transfers between devices: 26.2 us -> 15.5 us  [swap(): return lax.ppermute(v, 'section', [(0, 1), (1, 0)])]
    pallas_call x2 -> x1, Pallas kernels: 20 us -> 9.98 us  [expert_grads(): pl.pallas_call(expert_grads_kernel, out_shape=shape((2, N_SHARD, 4, 48, D...]
    ppermute x45 -> x48, waiting for transfers between devices: 100 us -> 93 us  [turn(): return lax.ppermute(v, 'seq', [(i, (i + d) % N_SEQ) for i in range(N_SEQ)])]
    slice x6 -> x0, local copies, waits for them, and re-layouts: 6.74 us -> none  [the longest x4 5.83 us: shards(): w_mix = [v[:, :576] for v in attn_rows]]
  transfers between devices with their start and end apart: 69 -> 73, of which waited for: 40 -> 48; matrix products, arithmetic and copies ran while one was open for 9% -> 9% of each run, Pallas kernels for 20% -> 22%
where the time goes in v8:
time: 450 us; the launch traced here: 442 us
  waiting for transfers between devices  153 us (34%)
  Pallas kernels  120 us (27%)
  starting transfers between devices  92 us (20%)
  local copies, waits for them, and re-layouts  45.4 us (10%)
  other arithmetic  16 us (4%)
  between operations  15 us (3%)
    ppermute x48, waiting for transfers between devices, turn(): return lax.ppermute(v, 'seq', [(i, (i + d) % N_SEQ) for i in range(N_SEQ)])  93 us
    pallas_call x14, Pallas kernels, call(): pl.pallas_call(body, out_shape=outs, in_specs=specs, out_specs=[vmem()] *...  68.7 us
    ppermute x48, starting transfers between devices, turn(): return lax.ppermute(v, 'seq', [(i, (i + d) % N_SEQ) for i in range(N_SEQ)])  54 us
    pallas_call x5, Pallas kernels, grid_call(): pl.pallas_call(body, grid=(2,), out_shape=outs, in_specs=in_specs, out_sp...  41.7 us
    all_to_all x1, waiting for transfers between devices, shards(): arrived = lax.all_to_all(pair, ('seq', 'shard'), 0, 0, tiled=True)  24.2 us
    unnamed x168, local copies, waits for them, and re-layouts  18 us
    ppermute x13, starting transfers between devices, swap(): return lax.ppermute(v, 'section', [(0, 1), (1, 0)])  15.5 us
    ppermute x13, waiting for transfers between devices, swap(): return lax.ppermute(v, 'section', [(0, 1), (1, 0)])  14.4 us
  transfers between devices with their start and end apart: 73, of which 48 were waited for; matrix products, arithmetic and copies ran while one was open for 9% of the time, Pallas kernels for 22%

profile of v8, /device:TPU:1, one launch (start us, length us, event | category | flops | bytes accessed | tf_op | source)
XLA Modules:
  0.0 441.9 jit_solution(16107612069476684720)
XLA Ops:
  42.3 7.6 %collective-permute-done.7.b2 = bf16[4,48,832]{2,1,0:T(8,128)(2,1)S(1)} collective-permute-done((bf16[4,48,832]{2,1,0:T(8,128)(2,1)S(1)}, bf16[4,48,832]{2,1,0:T(8,128)(2,1)S(1)}, u32[]{:S(2)}, u32[]{:S(2)}) %collective-permute-start.7) | collective-permute-done | bytes 319520 | tf_op jit(solution)/shard_map/ppermute | solution.py:44
  73.3 6.0 %attention.2 = (bf16[144,192]{1,0:T(8,128)(2,1)}, bf16[144,192]{1,0:T(8,128)(2,1)}, bf16[144,192]{1,0:T(8,128)(2,1)}, bf16[144,192]{1,0:T(8,128)(2,1)}, bf16[576...) custom-call(bf16[144,768]{1,0:T(8,128)(2,1)} %copy-done.10, bf16[144,768]{1,0:T(8,128)(2,1)} %copy-done.57, ...), custom_call_target="tpu_custom_call" | custom-call | tf_op jit(solution)/shard_map/attention/pallas_call | solution.py:105
  80.2 4.5 %collective-permute-done.11.w1.refs_18_ = bf16[192,768]{1,0:T(8,128)(2,1)S(1)} collective-permute-done((bf16[192,768]{1,0:T(8,128)(2,1)S(1)}, bf16[192,768]{1,0:T(8,128)(2,1)S(1)}, u32[]{:S(2)}, u32[]{:S(2)}) %collective-permute-start.11) | collective-permute-done | bytes 294944 | tf_op jit(solution)/shard_map/ppermute | solution.py:35
  104.2 5.0 %all-gather.5.cloned.1.call-done = bf16[64,48,768]{2,1,0:T(8,128)(2,1)} async-done(((bf16[4,48,768]{2,1,0:T(8,128)(2,1)}), bf16[64,48,768]{2,1,0:T(8,128)(2,1)}) %all-gather.5.cloned.1.call-update) | async-done | bytes 4718608 | tf_op jit(solution)/shard_map/all_gather | solution.py:673
  119.9 7.3 %expert.1 = (bf16[80,768]{1,0:T(8,128)(2,1)}, bf16[80,768]{1,0:T(8,128)(2,1)}, bf16[80,768]{1,0:T(8,128)(2,1)}, bf16[80,768]{1,0:T(8,128)(2,1)}) custom-call(bf16[80,768]{1,0:T(8,128)(2,1)} %get-tuple-element.149.r0.refs_0_, bf16[80,768]{1,0:T(8,128)(2,1)} %copy-done.27, bf16[80,768]{1,0:T(8,128)(2,1)} %copy-done.28, bf16[80,768]{1,0:T(8,128)(2,1)} %copy-done.29, ...), custom_call_target="tpu_custom_call" | custom-call | tf_op jit(solution)/shard_map/expert/pallas_call | solution.py:374
  145.9 9.5 %collective-permute-done.31.x3 = bf16[144,768]{1,0:T(8,128)(2,1)S(1)} collective-permute-done((bf16[144,768]{1,0:T(8,128)(2,1)}, bf16[144,768]{1,0:T(8,128)(2,1)S(1)}, u32[]{:S(2)}, u32[]{:S(2)}) %collective-permute-start.31) | collective-permute-done | bytes 221216 | tf_op jit(solution)/shard_map/ppermute | solution.py:35
  156.8 6.1 %attention.3 = (bf16[144,192]{1,0:T(8,128)(2,1)}, bf16[144,192]{1,0:T(8,128)(2,1)}, bf16[144,192]{1,0:T(8,128)(2,1)}, bf16[144,192]{1,0:T(8,128)(2,1)}, bf16[576...) custom-call(bf16[144,768]{1,0:T(8,128)(2,1)} %combine.2.x0.x_ref, bf16[144,768]{1,0:T(8,128)(2,1)} %copy-done.60, ...), custom_call_target="tpu_custom_call" | custom-call | tf_op jit(solution)/shard_map/attention/pallas_call | solution.py:105
  174.3 4.5 %middle.3 = (f32[144,768]{1,0:T(8,128)}, bf16[144,768]{1,0:T(8,128)(2,1)}, f32[144,64]{1,0:T(8,128)}, bf16[144,320]{1,0:T(8,128)(2,1)}, bf16[144,320]{1,0:T(8,12...) custom-call(s32[1]{0:T(128)} %bitcast.me_ref, ...), custom_call_target="tpu_custom_call" | custom-call | tf_op jit(solution)/shard_map/middle/pallas_call | solution.py:105
  183.1 4.6 %collective-permute-done.35.refs_1_ = bf16[2,80,768]{2,1,0:T(8,128)(2,1)S(1)} collective-permute-done((bf16[2,80,768]{2,1,0:T(8,128)(2,1)}, bf16[2,80,768]{2,1,0:T(8,128)(2,1)S(1)}, u32[]{:S(2)}, u32[]{:S(2)}) %collective-permute-start.35) | collective-permute-done | bytes 245792 | tf_op jit(solution)/shard_map/ppermute | solution.py:35
  195.3 11.6 %expert_back.2 = (bf16[2,80,768]{2,1,0:T(8,128)(2,1)}, bf16[2,80,768]{2,1,0:T(8,128)(2,1)}, bf16[2,80,768]{2,1,0:T(8,128)(2,1)}, bf16[2,80,768]{2,1,0:T(8,128)(2...) custom-call(bf16[2,80,768]{2,1,0:T(8,128)(2,1)} %get-tuple-element.1, ...), custom_call_target="tpu_custom_call" | custom-call | tf_op jit(solution)/shard_map/expert_back/pallas_call | solution.py:374
  206.8 10.0 %expert_grads.1 = bf16[2,16,4,48,768]{4,3,2,1,0:T(8,128)(2,1)} custom-call(s32[1]{0:T(128)} %bitcast.43.core_ref, bf16[320,768]{1,0:T(8,128)(2,1)} %get-tuple-element.239.rows_ref, bf16[320,768]{1,0:T(8,128)(2,1)} %get-tuple-element.240.d_result_ref, bf16[320,1536]{1,0:T(8,128)(2,1)} %get-tuple-element.241.act_own, ...), custom_call_target="tpu_custom_call" | custom-call | tf_op jit(solution)/shard_map/expert_grads/pallas_call | solution.py:477
  221.9 5.0 %collective-permute-done.39.refs_1_ = bf16[2,80,768]{2,1,0:T(8,128)(2,1)S(1)} collective-permute-done((bf16[2,80,768]{2,1,0:T(8,128)(2,1)S(1)}, bf16[2,80,768]{2,1,0:T(8,128)(2,1)S(1)}, u32[]{:S(2)}, u32[]{:S(2)}) %collective-permute-start.39) | collective-permute-done | bytes 245792 | tf_op jit(solution)/shard_map/ppermute | solution.py:35
  229.4 6.4 %collective-permute-done.41.refs_3_ = bf16[2,80,768]{2,1,0:T(8,128)(2,1)S(1)} collective-permute-done((bf16[2,80,768]{2,1,0:T(8,128)(2,1)S(1)}, bf16[2,80,768]{2,1,0:T(8,128)(2,1)S(1)}, u32[]{:S(2)}, u32[]{:S(2)}) %collective-permute-start.41) | collective-permute-done | bytes 245792 | tf_op jit(solution)/shard_map/ppermute | solution.py:35
  236.4 5.8 %middle_back.2 = (f32[144,768]{1,0:T(8,128)}, f32[768,64]{1,0:T(8,128)}, bf16[768,768]{1,0:T(8,128)(2,1)}, bf16[144,192]{1,0:T(8,128)(2,1)}, bf16[144,192]{1,0:T...) custom-call(s32[1]{0:T(128)} %bitcast.me_ref, ...), custom_call_target="tpu_custom_call" | custom-call | tf_op jit(solution)/shard_map/middle_back/pallas_call | solution.py:105
  250.3 10.0 %attention_back.2 = (bf16[144,768]{1,0:T(8,128)(2,1)}, bf16[144,768]{1,0:T(8,128)(2,1)}, bf16[144,768]{1,0:T(8,128)(2,1)}, bf16[144,768]{1,0:T(8,128)(2,1)}, bf16[768,768]{1,0:T(8,128)(2,1)}) custom-call(bf16[576,768]{1,0:T(8,128)(2,1)} %get-tuple-element.191.x_ref, bf16[768,640]{1,0:T(8,128)(2,1)} %copy.140.w_ref.router_ref, ...), custom_call_target="tpu_custom_call" | custom-call | tf_op jit(solution)/shard_map/attention_back/pallas_call | solution.py:105
  262.9 6.3 %collective-permute-done.46.b1 = bf16[144,768]{1,0:T(8,128)(2,1)S(1)} collective-permute-done((bf16[144,768]{1,0:T(8,128)(2,1)}, bf16[144,768]{1,0:T(8,128)(2,1)S(1)}, u32[]{:S(2)}, u32[]{:S(2)}) %collective-permute-start.46) | collective-permute-done | bytes 221216 | tf_op jit(solution)/shard_map/ppermute | solution.py:35
  287.7 10.5 %expert_back.3 = (bf16[80,768]{1,0:T(8,128)(2,1)}, bf16[80,768]{1,0:T(8,128)(2,1)}, bf16[80,768]{1,0:T(8,128)(2,1)}, bf16[80,768]{1,0:T(8,128)(2,1)}, bf16[320,7...) custom-call(bf16[80,768]{1,0:T(8,128)(2,1)} %get-tuple-element.149.r, ...), custom_call_target="tpu_custom_call" | custom-call | tf_op jit(solution)/shard_map/expert_back/pallas_call | solution.py:374
  298.2 5.9 %expert_grad.2 = bf16[16,4,48,768]{3,2,1,0:T(8,128)(2,1)} custom-call(bf16[320,768]{1,0:T(8,128)(2,1)} %get-tuple-element.233.rows_ref, bf16[320,768]{1,0:T(8,128)(2,1)} %get-tuple-element.234.d_result_ref, bf16[320,1536]{1,0:T(8,128)(2,1)} %get-tuple-element.237.act_ref, bf16[320,1536]{1,0:T(8,128)(2,1)} %get-tuple-element.238.dh_ref), custom_call_target="tpu_custom_call" | custom-call | tf_op jit(solution)/shard_map/expert_grad/pallas_call | solution.py:374
  305.5 7.7 %collective-permute-done.65.refs_0_ = bf16[16,4,48,768]{3,2,1,0:T(8,128)(2,1)S(1)} collective-permute-done((bf16[16,4,48,768]{3,2,1,0:T(8,128)(2,1)}, bf16[16,4,48,768]{3,2,1,0:T(8,128)(2,1)S(1)}, u32[]{:S(2)}, u32[]{:S(2)}) %collective-permute-start.65) | collective-permute-done | bytes 4718624 | tf_op jit(solution)/shard_map/ppermute | solution.py:31
  315.4 6.5 %expert_grad.3 = bf16[16,4,48,768]{3,2,1,0:T(8,128)(2,1)} custom-call(bf16[320,768]{1,0:T(8,128)(2,1)} %get-tuple-element.233.rows_ref, bf16[320,768]{1,0:T(8,128)(2,1)} %get-tuple-element.234.d_result_ref, bf16[320,1536]{1,0:T(8,128)(2,1)} %get-tuple-element.235.act_ref, bf16[320,1536]{1,0:T(8,128)(2,1)} %get-tuple-element.236.dh_ref, ...), custom_call_target="tpu_custom_call" | custom-call | tf_op jit(solution)/shard_map/expert_grad/pallas_call | solution.py:374
  334.1 5.7 %middle_back.3 = (f32[144,768]{1,0:T(8,128)}, f32[768,64]{1,0:T(8,128)}, bf16[768,768]{1,0:T(8,128)(2,1)}, bf16[144,192]{1,0:T(8,128)(2,1)}, bf16[144,192]{1,0:T...) custom-call(s32[1]{0:T(128)} %bitcast.me_ref, bf16[144,768]{1,0:T(8,128)(2,1)} %get-tuple-element.203.d_out_ref, ...), custom_call_target="tpu_custom_call" | custom-call | tf_op jit(solution)/shard_map/middle_back/pallas_call | solution.py:105
  346.5 9.9 %attention_back.3 = (bf16[144,768]{1,0:T(8,128)(2,1)}, bf16[144,768]{1,0:T(8,128)(2,1)}, bf16[144,768]{1,0:T(8,128)(2,1)}, bf16[144,768]{1,0:T(8,128)(2,1)}, bf16[768,768]{1,0:T(8,128)(2,1)}) custom-call(bf16[576,768]{1,0:T(8,128)(2,1)} %get-tuple-element.216.x_ref, bf16[768,640]{1,0:T(8,128)(2,1)} %copy.135.w_ref.router_ref, ...), custom_call_target="tpu_custom_call" | custom-call | tf_op jit(solution)/shard_map/attention_back/pallas_call | solution.py:105
  375.9 8.5 %all-to-all-start.1 = ((bf16[64,144,128]{2,1,0:T(8,128)(2,1)}), bf16[64,144,128]{2,1,0:T(8,128)(2,1)S(1)}, u32[]{:S(2)}, u32[]{:S(2)}) async-start(bf16[64,144,128]{2,1,0:T(8,128)(2,1)} %copy.145), calls=%async_computation.1 | async-start | bytes 4718592 | tf_op jit(solution)/shard_map/all_to_all | solution.py:758
  396.5 24.2 %all-to-all-done.1 = bf16[64,144,128]{2,1,0:T(8,128)(2,1)S(1)} async-done(((bf16[64,144,128]{2,1,0:T(8,128)(2,1)}), bf16[64,144,128]{2,1,0:T(8,128)(2,1)S(1)}, u32[]{:S(2)}, u32[]{:S(2)}) %all-to-all-start.1) | async-done | bytes 2359328 | tf_op jit(solution)/shard_map/all_to_all | solution.py:758
  (383 shorter events, 238.1 us)
Async XLA Ops:
  8.2 18.1 %collective-permute-start.2 = (bf16[144,768]{1,0:T(8,128)(2,1)S(1)}, bf16[144,768]{1,0:T(8,128)(2,1)S(1)}, u32[]{:S(2)}, u32[]{:S(2)}) collective-permute-start(bf16[144,768]{1,0:T(8,128)(2,1)S(1)} %dynamic-slice_bitcast_fusion.2.x0.x_ref), channel_id=1, source_target_pairs={{0,16},{16,32},{32,48},{48,0},{1,17},{17,33},{33,49},{49,1},{2,18}... | collective-permute-start | bytes 663560 | tf_op jit(solution)/shard_map/ppermute | solution.py:35
  10.4 16.0 %collective-permute-start.1 = (bf16[144,768]{1,0:T(8,128)(2,1)S(1)}, bf16[144,768]{1,0:T(8,128)(2,1)S(1)}, u32[]{:S(2)}, u32[]{:S(2)}) collective-permute-start(bf16[144,768]{1,0:T(8,128)(2,1)S(1)} %dynamic-slice_bitcast_fusion.2.x0.x_ref), channel_id=1, source_target_pairs={{0,32},{16,48},{32,0},{48,16},{1,33},{17,49},{33,1},{49,17},{2,34}... | collective-permute-start | bytes 663560 | tf_op jit(solution)/shard_map/ppermute | solution.py:35
  13.0 13.4 %collective-permute-start = (bf16[144,768]{1,0:T(8,128)(2,1)S(1)}, bf16[144,768]{1,0:T(8,128)(2,1)S(1)}, u32[]{:S(2)}, u32[]{:S(2)}) collective-permute-start(bf16[144,768]{1,0:T(8,128)(2,1)S(1)} %dynamic-slice_bitcast_fusion.2.x0.x_ref), channel_id=1, source_target_pairs={{0,48},{16,0},{32,16},{48,32},{1,49},{17,1},{33,17},{49,33},{2,50}... | collective-permute-start | bytes 663560 | tf_op jit(solution)/shard_map/ppermute | solution.py:35
  21.8 87.4 %all-gather.5.cloned.1.call-start = ((), (), s32[]{:S(2)}) async-start(), calls=%async_computation.5 | async-start | bytes 5013504 | tf_op jit(solution)/shard_map/all_gather | solution.py:673
  23.7 15.9 %collective-permute-start.24 = (bf16[4,48,768]{2,1,0:T(8,128)(2,1)S(1)}, bf16[4,48,768]{2,1,0:T(8,128)(2,1)S(1)}, u32[]{:S(2)}, u32[]{:S(2)}) collective-permute-start(bf16[4,48,768]{2,1,0:T(8,128)(2,1)S(1)} %dynamic-slice_bitcast_fusion), channel_id=1, source_target_pairs={{0,64},{64,0},{1,65},{65,1},{2,66},{66,2},{3,67},{67,3},{4,68},{68... | collective-permute-start | bytes 884744 | tf_op jit(solution)/shard_map/ppermute | solution.py:31
  35.6 14.4 %collective-permute-start.7 = (bf16[4,48,832]{2,1,0:T(8,128)(2,1)S(1)}, bf16[4,48,832]{2,1,0:T(8,128)(2,1)S(1)}, u32[]{:S(2)}, u32[]{:S(2)}) collective-permute-start(bf16[4,48,832]{2,1,0:T(8,128)(2,1)S(1)} %pad_maximum_fusion.2.b0), channel_id=1, source_target_pairs={{0,8},{1,9},{2,10},{3,11},{4,12},{5,13},{6,14},{7,15},{8,0},{9,1},... | collective-permute-start | bytes 958472 | tf_op jit(solution)/shard_map/ppermute | solution.py:44
  38.9 12.5 %collective-permute-start.6 = (bf16[4,48,832]{2,1,0:T(8,128)(2,1)S(1)}, bf16[4,48,832]{2,1,0:T(8,128)(2,1)S(1)}, u32[]{:S(2)}, u32[]{:S(2)}) collective-permute-start(bf16[4,48,832]{2,1,0:T(8,128)(2,1)S(1)} %pad_maximum_fusion.2.b0), channel_id=1, source_target_pairs={{0,12},{1,13},{2,14},{3,15},{4,0},{5,1},{6,2},{7,3},{8,4},{9,5},{1... | collective-permute-start | bytes 958472 | tf_op jit(solution)/shard_map/ppermute | solution.py:44
  51.4 113.7 %all-gather.7.cloned.1.call-start = ((), (), s32[]{:S(2)}) async-start(), calls=%async_computation.6 | async-start | bytes 5013504 | tf_op jit(solution)/shard_map/all_gather | solution.py:705
  65.3 14.9 %collective-permute-start.13 = (bf16[192,768]{1,0:T(8,128)(2,1)S(1)}, bf16[192,768]{1,0:T(8,128)(2,1)S(1)}, u32[]{:S(2)}, u32[]{:S(2)}) collective-permute-start(bf16[192,768]{1,0:T(8,128)(2,1)S(1)} %get-tuple-element.141.w0.refs_17_), channel_id=1, source_target_pairs={{0,48},{16,0},{32,16},{48,32},{1,49},{17,1},{33,17},{49,33},{2,50}... | collective-permute-start | bytes 884744 | tf_op jit(solution)/shard_map/ppermute | solution.py:35
  68.6 16.2 %collective-permute-start.11 = (bf16[192,768]{1,0:T(8,128)(2,1)S(1)}, bf16[192,768]{1,0:T(8,128)(2,1)S(1)}, u32[]{:S(2)}, u32[]{:S(2)}) collective-permute-start(bf16[192,768]{1,0:T(8,128)(2,1)S(1)} %get-tuple-element.141.w0.refs_17_), channel_id=1, source_target_pairs={{0,16},{16,32},{32,48},{48,0},{1,17},{17,33},{33,49},{49,1},{2,18}... | collective-permute-start | bytes 884744 | tf_op jit(solution)/shard_map/ppermute | solution.py:35
  69.5 18.0 %collective-permute-start.17 = (s32[144,2]{1,0:T(8,128)S(1)}, s32[144,2]{1,0:T(8,128)S(1)}, u32[]{:S(2)}, u32[]{:S(2)}) collective-permute-start(s32[144,2]{1,0:T(8,128)S(1)} %bitcast.116), channel_id=1, source_target_pairs={{0,64},{64,0},{1,65},{65,1},{2,66},{66,2},{3,67},{67,3},{4,68},{68... | collective-permute-start | bytes 3464 | tf_op jit(solution)/shard_map/ppermute | solution.py:31
  109.2 317.5 %reduce-scatter.5.cloned.1.call-start = ((), (), s32[]{:S(2)}) async-start(), calls=%async_computation.4 | async-start | bytes 9732096 | tf_op jit(solution)/shard_map/reduce_scatter | solution.py:745
  110.0 17.2 %collective-permute-start.23 = (bf16[192,768]{1,0:T(8,128)(2,1)S(1)}, bf16[192,768]{1,0:T(8,128)(2,1)S(1)}, u32[]{:S(2)}, u32[]{:S(2)}) collective-permute-start(bf16[192,768]{1,0:T(8,128)(2,1)S(1)} %copy-done.12), channel_id=1, source_target_pairs={{0,48},{16,0},{32,16},{48,32},{1,49},{17,1},{33,17},{49,33},{2,50}... | collective-permute-start | bytes 884744 | tf_op jit(solution)/shard_map/ppermute | solution.py:35
  112.5 14.7 %collective-permute-start.22 = (bf16[192,768]{1,0:T(8,128)(2,1)S(1)}, bf16[192,768]{1,0:T(8,128)(2,1)S(1)}, u32[]{:S(2)}, u32[]{:S(2)}) collective-permute-start(bf16[192,768]{1,0:T(8,128)(2,1)S(1)} %copy-done.12), channel_id=1, source_target_pairs={{0,32},{16,48},{32,0},{48,16},{1,33},{17,49},{33,1},{49,17},{2,34}... | collective-permute-start | bytes 884744 | tf_op jit(solution)/shard_map/ppermute | solution.py:35
  113.0 16.2 %collective-permute-start.21 = (bf16[192,768]{1,0:T(8,128)(2,1)S(1)}, bf16[192,768]{1,0:T(8,128)(2,1)S(1)}, u32[]{:S(2)}, u32[]{:S(2)}) collective-permute-start(bf16[192,768]{1,0:T(8,128)(2,1)S(1)} %copy-done.12), channel_id=1, source_target_pairs={{0,16},{16,32},{32,48},{48,0},{1,17},{17,33},{33,49},{49,1},{2,18}... | collective-permute-start | bytes 884744 | tf_op jit(solution)/shard_map/ppermute | solution.py:35
  142.4 13.0 %collective-permute-start.31 = (bf16[144,768]{1,0:T(8,128)(2,1)}, bf16[144,768]{1,0:T(8,128)(2,1)S(1)}, u32[]{:S(2)}, u32[]{:S(2)}) collective-permute-start(bf16[144,768]{1,0:T(8,128)(2,1)} %combine.2.x0.x_ref), channel_id=1, source_target_pairs={{0,16},{16,32},{32,48},{48,0},{1,17},{17,33},{33,49},{49,1},{2,18}... | collective-permute-start | bytes 663560 | tf_op jit(solution)/shard_map/ppermute | solution.py:35
  142.6 12.8 %collective-permute-start.30 = (bf16[144,768]{1,0:T(8,128)(2,1)}, bf16[144,768]{1,0:T(8,128)(2,1)S(1)}, u32[]{:S(2)}, u32[]{:S(2)}) collective-permute-start(bf16[144,768]{1,0:T(8,128)(2,1)} %combine.2.x0.x_ref), channel_id=1, source_target_pairs={{0,32},{16,48},{32,0},{48,16},{1,33},{17,49},{33,1},{49,17},{2,34}... | collective-permute-start | bytes 663560 | tf_op jit(solution)/shard_map/ppermute | solution.py:35
  165.1 28.0 %collective-permute-start.38 = (bf16[16,4,48,768]{3,2,1,0:T(8,128)(2,1)}, bf16[16,4,48,768]{3,2,1,0:T(8,128)(2,1)S(1)}, u32[]{:S(2)}, u32[]{:S(2)}) collective-permute-start(bf16[16,4,48,768]{3,2,1,0:T(8,128)(2,1)} %bitcast.99), channel_id=1, source_target_pairs={{0,64},{64,0},{1,65},{65,1},{2,66},{66,2},{3,67},{67,3},{4,68},{68... | collective-permute-start | bytes 14155784 | tf_op jit(solution)/shard_map/ppermute | solution.py:31
  216.9 209.9 %reduce-scatter.7.cloned.1.call-start = ((), (), s32[]{:S(2)}) async-start(), calls=%async_computation.7 | async-start | bytes 5013504
  221.9 13.9 %collective-permute-start.41 = (bf16[2,80,768]{2,1,0:T(8,128)(2,1)S(1)}, bf16[2,80,768]{2,1,0:T(8,128)(2,1)S(1)}, u32[]{:S(2)}, u32[]{:S(2)}) collective-permute-start(bf16[2,80,768]{2,1,0:T(8,128)(2,1)S(1)} %copy-done.76), channel_id=1, source_target_pairs={{0,16},{16,32},{32,48},{48,0},{1,17},{17,33},{33,49},{49,1},{2,18}... | collective-permute-start | bytes 737288 | tf_op jit(solution)/shard_map/ppermute | solution.py:35
  341.5 20.7 %collective-permute-start.63 = (bf16[768,768]{1,0:T(8,128)(2,1)S(1)}, bf16[768,768]{1,0:T(8,128)(2,1)S(1)}, u32[]{:S(2)}, u32[]{:S(2)}) collective-permute-start(bf16[768,768]{1,0:T(8,128)(2,1)S(1)} %broadcast_select_fusion), channel_id=1, source_target_pairs={{0,64},{64,0},{1,65},{65,1},{2,66},{66,2},{3,67},{67,3},{4,68},{68... | collective-permute-start | bytes 3538952 | tf_op jit(solution)/shard_map/ppermute | solution.py:31
  375.9 44.7 %all-to-all-start.1 = ((bf16[64,144,128]{2,1,0:T(8,128)(2,1)}), bf16[64,144,128]{2,1,0:T(8,128)(2,1)S(1)}, u32[]{:S(2)}, u32[]{:S(2)}) async-start(bf16[64,144,128]{2,1,0:T(8,128)(2,1)} %copy.145), calls=%async_computation.1 | async-start | bytes 4718592 | tf_op jit(solution)/shard_map/all_to_all | solution.py:758
  391.4 31.5 %collective-permute-start.42 = (bf16[144,768]{1,0:T(8,128)(2,1)S(1)}, bf16[144,768]{1,0:T(8,128)(2,1)}, u32[]{:S(2)}, u32[]{:S(2)}) collective-permute-start(bf16[144,768]{1,0:T(8,128)(2,1)S(1)} %get-tuple-element.296), channel_id=1, source_target_pairs={{0,64},{64,0},{1,65},{65,1},{2,66},{66,2},{3,67},{67,3},{4,68},{68... | collective-permute-start | bytes 663560 | tf_op jit(solution)/shard_map/ppermute | solution.py:31
  396.5 28.3 %collective-permute-start.61 = (bf16[144,768]{1,0:T(8,128)(2,1)}, bf16[144,768]{1,0:T(8,128)(2,1)}, u32[]{:S(2)}, u32[]{:S(2)}) collective-permute-start(bf16[144,768]{1,0:T(8,128)(2,1)} %get-tuple-element.294), channel_id=1, source_target_pairs={{0,64},{64,0},{1,65},{65,1},{2,66},{66,2},{3,67},{67,3},{4,68},{68... | collective-permute-start | bytes 663560 | tf_op jit(solution)/shard_map/ppermute | solution.py:31
  (133 other events, 868.9 us)
Sparse Core Ops, SparseCore 0:
  51.5 57.6 all-gather.4
  111.3 53.6 all-gather.6
  217.0 93.8 reduce-scatter.4
  322.0 96.4 reduce-scatter.6

commit v9 on v8

--- a/solution.py
+++ b/solution.py
@@ -343,18 +343,24 @@
     return ref[:, i].reshape(768, D)
 
 
-def expert_kernel(r0, r1, r2, r3, own_ref, other_ref, o0, o1, o2, o3, rows_ref, total):
+def expert_first_kernel(r0, r1, r2, r3, pack, rows_ref, total):
     @pl.when(pl.program_id(0) == 0)
     def _():
         for d, ref in enumerate((r0, r1, r2, r3)):
             rows_ref[CAP * d : CAP * (d + 1)] = ref[...]
         total[...] = jnp.zeros_like(total)
 
-    rows = rows_ref[...]
-    for pack in (own_ref, other_ref):
-        hidden = dot(rows, quarter(pack, 0), 1, 0)
-        active = gelu_of(hidden)[0].astype(BF16)
-        total[...] += dot(active, quarter(pack, 1), 1, 0)
+    active = gelu_of(dot(rows_ref[...], quarter(pack, 0), 1, 0))[0].astype(BF16)
+    total[...] += dot(active, quarter(pack, 1), 1, 0)
+
+
+def expert_second_kernel(rows_ref, first_ref, pack, o0, o1, o2, o3, total):
+    @pl.when(pl.program_id(0) == 0)
+    def _():
+        total[...] = first_ref[...]
+
+    active = gelu_of(dot(rows_ref[...], quarter(pack, 0), 1, 0))[0].astype(BF16)
+    total[...] += dot(active, quarter(pack, 1), 1, 0)
 
     @pl.when(pl.program_id(0) == 1)
     def _():
@@ -385,15 +391,24 @@
     )(*ins)
 
 
-def expert_run(blocks, packs):
+def expert_run(blocks, own, other):
+    rows, first = grid_call(
+        expert_first_kernel,
+        [shape((320, D), BF16), shape((320, D), F32)],
+        [whole_block((320, D))] * 2,
+        [*blocks, own],
+        [whole_block((CAP, D))] * 4 + [pack_block()],
+        "expert_first",
+        [],
+    )
     return grid_call(
-        expert_kernel,
+        expert_second_kernel,
         [shape((CAP, D), BF16)] * 4,
         [whole_block((CAP, D))] * 4,
-        [*blocks, *packs],
-        [whole_block((CAP, D))] * 4 + [pack_block()] * 2,
-        "expert",
-        [pltpu.VMEM((320, D), BF16), pltpu.VMEM((320, D), F32)],
+        [rows, first, other],
+        [whole_block((320, D))] * 2 + [pack_block()],
+        "expert_second",
+        [pltpu.VMEM((320, D), F32)],
     )
 
 
@@ -705,7 +720,7 @@
             later = lax.all_gather(tie(halves[1], own), "shard", axis=0, tiled=False)
             later_back = tie(back_rows[1], blocks)
             w_back[1] = [later_back] + [turn(later_back, d) for d in (1, 2, 3)]
-            result = expert_run(blocks, experts[s])
+            result = expert_run(blocks, *experts[s])
             w_back[1], result = lax.optimization_barrier((w_back[1], result))
             returned = send_back(result)
             x = combine(residual, high, low, returned)
@@ -728,7 +743,8 @@
             layer_outs.append(combine(residual, high, low, [v[0] for v in arrived]))
         else:
             sent, *states = expert_back([*blocks, *send_out(d_buffer)], experts[s], False)
-            arrived = [*returned, *send_back(sent)]
+            back = send_back(sent)
+            arrived = [*returned, *back]
         d_residual, small, grad_back, d_mixture = middle_back(
             me, d_out, arrived, gathered, chosen, gates, residual, normed, tables[s], w_back[s], s == 1
         )
@@ -740,7 +756,7 @@
             group = ("section", "shard")
         else:
             other = swap(expert_grad(rows, d_result, act_other, dh_other))
-            both = expert_grad(rows, d_result, act_own, dh_own, (other,))
+            both = expert_grad(rows, d_result, act_own, dh_own, (tie(other, back),))
             group = "shard"
         expert_sums[s] = lax.psum_scatter(both, group, scatter_dimension=0, tiled=True)[0]
         d_normed, grad_mix = attend_back(x_all, attn_rows[s], tables[s], packed, logs, d_heads, small)
@@ -757,8 +773,7 @@
     pair = tie(pair, d_parts)
     arrived = lax.all_to_all(pair, ("seq", "shard"), 0, 0, tiled=True)
     attn_sum = jnp.sum(arrived.reshape(N_SEQ, N_SHARD, 144, 128).astype(F32), axis=1)
-    attn_sum = attn_sum.reshape(N_SEQ, 12, 12, 128).transpose(0, 2, 1, 3).reshape(N_SEQ, 12, 2 * D)
-    attn_sums = [attn_sum[:, :, :D], attn_sum[:, :, D:]]
+    attn_sums = [attn_sum[:, :72], attn_sum[:, 72:]]
 
     def settle(pair):
         keep = jnp.where(core == 0, pair[0], pair[1])
@@ -771,7 +786,8 @@
     layer_out = in_order(*settle(layer_outs))
     in_grad = in_order(*settle(in_grads))
     grad_in, grad_out = reorder(core_index, *settle(expert_sums))
-    attn_sum = in_order(*settle(attn_sums))
+    attn_sum = in_order(*settle(attn_sums)).reshape(2, N_SEQ, 6, 12, 128)
+    attn_sum = attn_sum.transpose(0, 1, 3, 2, 4).reshape(2, N_SEQ, 12, D)
     mix = attn_sum[0]
     back = jnp.sum(attn_sum[1], axis=0)
     grad_qkv = mix[:, :, :576].reshape(N_SEQ, 12, 3, 192).transpose(1, 2, 0, 3).reshape(12, 3 * D)

time: 450 us -> 440 us (0.978)
  waiting for transfers between devices: 153 us -> 140 us
    ppermute x13, waiting for transfers between devices: 14.4 us -> 2.54 us  [swap(): return lax.ppermute(v, 'section', [(0, 1), (1, 0)])]
    all_to_all x1, waiting for transfers between devices: 24.2 us -> 19.5 us  [shards(): arrived = lax.all_to_all(pair, ('seq', 'shard'), 0, 0, tiled=True)]
    pallas_call x5 -> x6, Pallas kernels: 41.7 us -> 44.7 us  [grid_call(): pl.pallas_call(body, grid=(2,), out_shape=outs, in_specs=in_specs, out_sp...]
  transfers between devices with their start and end apart: 73 -> 73, of which waited for: 48 -> 48; matrix products, arithmetic and copies ran while one was open for 9% -> 10% of each run, Pallas kernels for 22% -> 23%
where the time goes in v9:
time: 440 us; the launch traced here: 433 us
  waiting for transfers between devices  140 us (32%)
  Pallas kernels  123 us (28%)
  starting transfers between devices  94.6 us (22%)
  local copies, waits for them, and re-layouts  43.7 us (10%)
  other arithmetic  16 us (4%)
  between operations  15 us (3%)
    ppermute x48, waiting for transfers between devices, turn(): return lax.ppermute(v, 'seq', [(i, (i + d) % N_SEQ) for i in range(N_SEQ)])  93.2 us
    pallas_call x14, Pallas kernels, call(): pl.pallas_call(body, out_shape=outs, in_specs=specs, out_specs=[vmem()] *...  68.6 us
    ppermute x48, starting transfers between devices, turn(): return lax.ppermute(v, 'seq', [(i, (i + d) % N_SEQ) for i in range(N_SEQ)])  53.8 us
    pallas_call x6, Pallas kernels, grid_call(): pl.pallas_call(body, grid=(2,), out_shape=outs, in_specs=in_specs, out_sp...  44.7 us
    all_to_all x1, waiting for transfers between devices, shards(): arrived = lax.all_to_all(pair, ('seq', 'shard'), 0, 0, tiled=True)  19.5 us
    ppermute x13, starting transfers between devices, swap(): return lax.ppermute(v, 'section', [(0, 1), (1, 0)])  18.2 us
    unnamed x168, local copies, waits for them, and re-layouts  16.2 us
    ppermute x6, waiting for transfers between devices, hop(): return lax.ppermute(v, 'shard', route)  13.3 us
  transfers between devices with their start and end apart: 73, of which 48 were waited for; matrix products, arithmetic and copies ran while one was open for 10% of the time, Pallas kernels for 23%

profile of v9, /device:TPU:1, one launch (start us, length us, event | category | flops | bytes accessed | tf_op | source)
XLA Modules:
  0.0 432.5 jit_solution(10569722537104641166)
XLA Ops:
  42.3 7.6 %collective-permute-done.7.b2 = bf16[4,48,832]{2,1,0:T(8,128)(2,1)S(1)} collective-permute-done((bf16[4,48,832]{2,1,0:T(8,128)(2,1)S(1)}, bf16[4,48,832]{2,1,0:T(8,128)(2,1)S(1)}, u32[]{:S(2)}, u32[]{:S(2)}) %collective-permute-start.7) | collective-permute-done | bytes 319520 | tf_op jit(solution)/shard_map/ppermute | solution.py:44
  73.3 6.0 %attention.2 = (bf16[144,192]{1,0:T(8,128)(2,1)}, bf16[144,192]{1,0:T(8,128)(2,1)}, bf16[144,192]{1,0:T(8,128)(2,1)}, bf16[144,192]{1,0:T(8,128)(2,1)}, bf16[576...) custom-call(bf16[144,768]{1,0:T(8,128)(2,1)} %copy-done.10, bf16[144,768]{1,0:T(8,128)(2,1)} %copy-done.57, ...), custom_call_target="tpu_custom_call" | custom-call | tf_op jit(solution)/shard_map/attention/pallas_call | solution.py:105
  80.2 4.5 %collective-permute-done.11.w1.refs_18_ = bf16[192,768]{1,0:T(8,128)(2,1)S(1)} collective-permute-done((bf16[192,768]{1,0:T(8,128)(2,1)S(1)}, bf16[192,768]{1,0:T(8,128)(2,1)S(1)}, u32[]{:S(2)}, u32[]{:S(2)}) %collective-permute-start.11) | collective-permute-done | bytes 294944 | tf_op jit(solution)/shard_map/ppermute | solution.py:35
  104.2 5.0 %all-gather.5.cloned.1.call-done = bf16[64,48,768]{2,1,0:T(8,128)(2,1)} async-done(((bf16[4,48,768]{2,1,0:T(8,128)(2,1)}), bf16[64,48,768]{2,1,0:T(8,128)(2,1)}) %all-gather.5.cloned.1.call-update) | async-done | bytes 4718608 | tf_op jit(solution)/shard_map/all_gather | solution.py:688
  113.7 5.0 %expert_first.1 = (bf16[320,768]{1,0:T(8,128)(2,1)}, f32[320,768]{1,0:T(8,128)}) custom-call(bf16[80,768]{1,0:T(8,128)(2,1)} %get-tuple-element.152.r0.refs_0_, bf16[80,768]{1,0:T(8,128)(2,1)} %copy-done.27, bf16[80,768]{1,0:T(8,128)(2,1)} %copy-done.28, bf16[80,768]{1,0:T(8,128)(2,1)} %copy-done.29, bf16[16,4,48,768]{3,2,1,0:T(8,128)(2,1)} %bitcast.89), custom_call_target="tpu_custom_call" | custom-call | tf_op jit(solution)/shard_map/expert_first/pallas_call | solution.py:380
  120.8 5.2 %expert_second.1 = (bf16[80,768]{1,0:T(8,128)(2,1)}, bf16[80,768]{1,0:T(8,128)(2,1)}, bf16[80,768]{1,0:T(8,128)(2,1)}, bf16[80,768]{1,0:T(8,128)(2,1)}) custom-call(bf16[320,768]{1,0:T(8,128)(2,1)} %get-tuple-element.159.rows_ref, f32[320,768]{1,0:T(8,128)} %get-tuple-element.160.first_ref, bf16[16,4,48,768]{3,2,1,0:T(8,128)(2,1)} %copy-done.2), custom_call_target="tpu_custom_call" | custom-call | tf_op jit(solution)/shard_map/expert_second/pallas_call | solution.py:380
  145.1 6.4 %collective-permute-done.31.x3 = bf16[144,768]{1,0:T(8,128)(2,1)S(1)} collective-permute-done((bf16[144,768]{1,0:T(8,128)(2,1)}, bf16[144,768]{1,0:T(8,128)(2,1)S(1)}, u32[]{:S(2)}, u32[]{:S(2)}) %collective-permute-start.31) | collective-permute-done | bytes 221216 | tf_op jit(solution)/shard_map/ppermute | solution.py:35
  155.3 6.1 %attention.3 = (bf16[144,192]{1,0:T(8,128)(2,1)}, bf16[144,192]{1,0:T(8,128)(2,1)}, bf16[144,192]{1,0:T(8,128)(2,1)}, bf16[144,192]{1,0:T(8,128)(2,1)}, bf16[576...) custom-call(bf16[144,768]{1,0:T(8,128)(2,1)} %combine.2.x0.x_ref, bf16[144,768]{1,0:T(8,128)(2,1)} %copy-done.60, ...), custom_call_target="tpu_custom_call" | custom-call | tf_op jit(solution)/shard_map/attention/pallas_call | solution.py:105
  174.3 4.5 %middle.3 = (f32[144,768]{1,0:T(8,128)}, bf16[144,768]{1,0:T(8,128)(2,1)}, f32[144,64]{1,0:T(8,128)}, bf16[144,320]{1,0:T(8,128)(2,1)}, bf16[144,320]{1,0:T(8,12...) custom-call(s32[1]{0:T(128)} %bitcast.me_ref, ...), custom_call_target="tpu_custom_call" | custom-call | tf_op jit(solution)/shard_map/middle/pallas_call | solution.py:105
  183.1 4.5 %collective-permute-done.35.refs_1_ = bf16[2,80,768]{2,1,0:T(8,128)(2,1)S(1)} collective-permute-done((bf16[2,80,768]{2,1,0:T(8,128)(2,1)}, bf16[2,80,768]{2,1,0:T(8,128)(2,1)S(1)}, u32[]{:S(2)}, u32[]{:S(2)}) %collective-permute-start.35) | collective-permute-done | bytes 245792 | tf_op jit(solution)/shard_map/ppermute | solution.py:35
  195.3 11.6 %expert_back.2 = (bf16[2,80,768]{2,1,0:T(8,128)(2,1)}, bf16[2,80,768]{2,1,0:T(8,128)(2,1)}, bf16[2,80,768]{2,1,0:T(8,128)(2,1)}, bf16[2,80,768]{2,1,0:T(8,128)(2...) custom-call(bf16[2,80,768]{2,1,0:T(8,128)(2,1)} %get-tuple-element.1, ...), custom_call_target="tpu_custom_call" | custom-call | tf_op jit(solution)/shard_map/expert_back/pallas_call | solution.py:380
  206.8 10.0 %expert_grads.1 = bf16[2,16,4,48,768]{4,3,2,1,0:T(8,128)(2,1)} custom-call(s32[1]{0:T(128)} %bitcast.41.core_ref, bf16[320,768]{1,0:T(8,128)(2,1)} %get-tuple-element.245.rows_ref, bf16[320,768]{1,0:T(8,128)(2,1)} %get-tuple-element.246.d_result_ref, bf16[320,1536]{1,0:T(8,128)(2,1)} %get-tuple-element.247.act_own, ...), custom_call_target="tpu_custom_call" | custom-call | tf_op jit(solution)/shard_map/expert_grads/pallas_call | solution.py:492
  221.9 5.0 %collective-permute-done.39.refs_1_ = bf16[2,80,768]{2,1,0:T(8,128)(2,1)S(1)} collective-permute-done((bf16[2,80,768]{2,1,0:T(8,128)(2,1)S(1)}, bf16[2,80,768]{2,1,0:T(8,128)(2,1)S(1)}, u32[]{:S(2)}, u32[]{:S(2)}) %collective-permute-start.39) | collective-permute-done | bytes 245792 | tf_op jit(solution)/shard_map/ppermute | solution.py:35
  229.4 6.3 %collective-permute-done.41.refs_3_ = bf16[2,80,768]{2,1,0:T(8,128)(2,1)S(1)} collective-permute-done((bf16[2,80,768]{2,1,0:T(8,128)(2,1)S(1)}, bf16[2,80,768]{2,1,0:T(8,128)(2,1)S(1)}, u32[]{:S(2)}, u32[]{:S(2)}) %collective-permute-start.41) | collective-permute-done | bytes 245792 | tf_op jit(solution)/shard_map/ppermute | solution.py:35
  236.4 5.8 %middle_back.2 = (f32[144,768]{1,0:T(8,128)}, f32[768,64]{1,0:T(8,128)}, bf16[768,768]{1,0:T(8,128)(2,1)}, bf16[144,192]{1,0:T(8,128)(2,1)}, bf16[144,192]{1,0:T...) custom-call(s32[1]{0:T(128)} %bitcast.me_ref, ...), custom_call_target="tpu_custom_call" | custom-call | tf_op jit(solution)/shard_map/middle_back/pallas_call | solution.py:105
  250.2 10.0 %attention_back.2 = (bf16[144,768]{1,0:T(8,128)(2,1)}, bf16[144,768]{1,0:T(8,128)(2,1)}, bf16[144,768]{1,0:T(8,128)(2,1)}, bf16[144,768]{1,0:T(8,128)(2,1)}, bf16[768,768]{1,0:T(8,128)(2,1)}) custom-call(bf16[576,768]{1,0:T(8,128)(2,1)} %get-tuple-element.196.x_ref, bf16[768,640]{1,0:T(8,128)(2,1)} %copy.142.w_ref.router_ref, ...), custom_call_target="tpu_custom_call" | custom-call | tf_op jit(solution)/shard_map/attention_back/pallas_call | solution.py:105
  262.9 6.2 %collective-permute-done.46.b1 = bf16[144,768]{1,0:T(8,128)(2,1)S(1)} collective-permute-done((bf16[144,768]{1,0:T(8,128)(2,1)}, bf16[144,768]{1,0:T(8,128)(2,1)S(1)}, u32[]{:S(2)}, u32[]{:S(2)}) %collective-permute-start.46) | collective-permute-done | bytes 221216 | tf_op jit(solution)/shard_map/ppermute | solution.py:35
  287.6 10.5 %expert_back.3 = (bf16[80,768]{1,0:T(8,128)(2,1)}, bf16[80,768]{1,0:T(8,128)(2,1)}, bf16[80,768]{1,0:T(8,128)(2,1)}, bf16[80,768]{1,0:T(8,128)(2,1)}, bf16[320,7...) custom-call(bf16[80,768]{1,0:T(8,128)(2,1)} %get-tuple-element.152.r, ...), custom_call_target="tpu_custom_call" | custom-call | tf_op jit(solution)/shard_map/expert_back/pallas_call | solution.py:380
  298.2 6.0 %expert_grad.2 = bf16[16,4,48,768]{3,2,1,0:T(8,128)(2,1)} custom-call(bf16[320,768]{1,0:T(8,128)(2,1)} %get-tuple-element.238.rows_ref, bf16[320,768]{1,0:T(8,128)(2,1)} %get-tuple-element.239.d_result_ref, bf16[320,1536]{1,0:T(8,128)(2,1)} %get-tuple-element.242.act_ref, bf16[320,1536]{1,0:T(8,128)(2,1)} %get-tuple-element.243.dh_ref), custom_call_target="tpu_custom_call" | custom-call | tf_op jit(solution)/shard_map/expert_grad/pallas_call | solution.py:380
  318.4 6.4 %expert_grad.3 = bf16[16,4,48,768]{3,2,1,0:T(8,128)(2,1)} custom-call(bf16[320,768]{1,0:T(8,128)(2,1)} %get-tuple-element.238.rows_ref, bf16[320,768]{1,0:T(8,128)(2,1)} %get-tuple-element.239.d_result_ref, bf16[320,1536]{1,0:T(8,128)(2,1)} %get-tuple-element.240.act_ref, bf16[320,1536]{1,0:T(8,128)(2,1)} %get-tuple-element.241.dh_ref, ...), custom_call_target="tpu_custom_call" | custom-call | tf_op jit(solution)/shard_map/expert_grad/pallas_call | solution.py:380
  324.8 5.7 %middle_back.3 = (f32[144,768]{1,0:T(8,128)}, f32[768,64]{1,0:T(8,128)}, bf16[768,768]{1,0:T(8,128)(2,1)}, bf16[144,192]{1,0:T(8,128)(2,1)}, bf16[144,192]{1,0:T...) custom-call(s32[1]{0:T(128)} %bitcast.me_ref, bf16[144,768]{1,0:T(8,128)(2,1)} %get-tuple-element.208.d_out_ref, ...), custom_call_target="tpu_custom_call" | custom-call | tf_op jit(solution)/shard_map/middle_back/pallas_call | solution.py:105
  337.4 9.8 %attention_back.3 = (bf16[144,768]{1,0:T(8,128)(2,1)}, bf16[144,768]{1,0:T(8,128)(2,1)}, bf16[144,768]{1,0:T(8,128)(2,1)}, bf16[144,768]{1,0:T(8,128)(2,1)}, bf16[768,768]{1,0:T(8,128)(2,1)}) custom-call(bf16[576,768]{1,0:T(8,128)(2,1)} %get-tuple-element.221.x_ref, bf16[768,640]{1,0:T(8,128)(2,1)} %copy.137.w_ref.router_ref, ...), custom_call_target="tpu_custom_call" | custom-call | tf_op jit(solution)/shard_map/attention_back/pallas_call | solution.py:105
  366.8 8.5 %all-to-all-start.1 = ((bf16[64,144,128]{2,1,0:T(8,128)(2,1)}), bf16[64,144,128]{2,1,0:T(8,128)(2,1)S(1)}, u32[]{:S(2)}, u32[]{:S(2)}) async-start(bf16[64,144,128]{2,1,0:T(8,128)(2,1)} %copy.147), calls=%async_computation.1 | async-start | bytes 4718592 | tf_op jit(solution)/shard_map/all_to_all | solution.py:774
  387.4 19.5 %all-to-all-done.1 = bf16[64,144,128]{2,1,0:T(8,128)(2,1)S(1)} async-done(((bf16[64,144,128]{2,1,0:T(8,128)(2,1)}), bf16[64,144,128]{2,1,0:T(8,128)(2,1)S(1)}, u32[]{:S(2)}, u32[]{:S(2)}) %all-to-all-start.1) | async-done | bytes 2359328 | tf_op jit(solution)/shard_map/all_to_all | solution.py:774
  (387 shorter events, 241.4 us)
Async XLA Ops:
  8.2 18.1 %collective-permute-start.2 = (bf16[144,768]{1,0:T(8,128)(2,1)S(1)}, bf16[144,768]{1,0:T(8,128)(2,1)S(1)}, u32[]{:S(2)}, u32[]{:S(2)}) collective-permute-start(bf16[144,768]{1,0:T(8,128)(2,1)S(1)} %dynamic-slice_bitcast_fusion.2.x0.x_ref), channel_id=1, source_target_pairs={{0,16},{16,32},{32,48},{48,0},{1,17},{17,33},{33,49},{49,1},{2,18}... | collective-permute-start | bytes 663560 | tf_op jit(solution)/shard_map/ppermute | solution.py:35
  10.4 16.0 %collective-permute-start.1 = (bf16[144,768]{1,0:T(8,128)(2,1)S(1)}, bf16[144,768]{1,0:T(8,128)(2,1)S(1)}, u32[]{:S(2)}, u32[]{:S(2)}) collective-permute-start(bf16[144,768]{1,0:T(8,128)(2,1)S(1)} %dynamic-slice_bitcast_fusion.2.x0.x_ref), channel_id=1, source_target_pairs={{0,32},{16,48},{32,0},{48,16},{1,33},{17,49},{33,1},{49,17},{2,34}... | collective-permute-start | bytes 663560 | tf_op jit(solution)/shard_map/ppermute | solution.py:35
  13.0 13.4 %collective-permute-start = (bf16[144,768]{1,0:T(8,128)(2,1)S(1)}, bf16[144,768]{1,0:T(8,128)(2,1)S(1)}, u32[]{:S(2)}, u32[]{:S(2)}) collective-permute-start(bf16[144,768]{1,0:T(8,128)(2,1)S(1)} %dynamic-slice_bitcast_fusion.2.x0.x_ref), channel_id=1, source_target_pairs={{0,48},{16,0},{32,16},{48,32},{1,49},{17,1},{33,17},{49,33},{2,50}... | collective-permute-start | bytes 663560 | tf_op jit(solution)/shard_map/ppermute | solution.py:35
  21.8 87.4 %all-gather.5.cloned.1.call-start = ((), (), s32[]{:S(2)}) async-start(), calls=%async_computation.5 | async-start | bytes 5013504 | tf_op jit(solution)/shard_map/all_gather | solution.py:688
  23.7 15.9 %collective-permute-start.24 = (bf16[4,48,768]{2,1,0:T(8,128)(2,1)S(1)}, bf16[4,48,768]{2,1,0:T(8,128)(2,1)S(1)}, u32[]{:S(2)}, u32[]{:S(2)}) collective-permute-start(bf16[4,48,768]{2,1,0:T(8,128)(2,1)S(1)} %dynamic-slice_bitcast_fusion), channel_id=1, source_target_pairs={{0,64},{64,0},{1,65},{65,1},{2,66},{66,2},{3,67},{67,3},{4,68},{68... | collective-permute-start | bytes 884744 | tf_op jit(solution)/shard_map/ppermute | solution.py:31
  35.6 14.4 %collective-permute-start.7 = (bf16[4,48,832]{2,1,0:T(8,128)(2,1)S(1)}, bf16[4,48,832]{2,1,0:T(8,128)(2,1)S(1)}, u32[]{:S(2)}, u32[]{:S(2)}) collective-permute-start(bf16[4,48,832]{2,1,0:T(8,128)(2,1)S(1)} %pad_maximum_fusion.2.b0), channel_id=1, source_target_pairs={{0,8},{1,9},{2,10},{3,11},{4,12},{5,13},{6,14},{7,15},{8,0},{9,1},... | collective-permute-start | bytes 958472 | tf_op jit(solution)/shard_map/ppermute | solution.py:44
  38.9 12.5 %collective-permute-start.6 = (bf16[4,48,832]{2,1,0:T(8,128)(2,1)S(1)}, bf16[4,48,832]{2,1,0:T(8,128)(2,1)S(1)}, u32[]{:S(2)}, u32[]{:S(2)}) collective-permute-start(bf16[4,48,832]{2,1,0:T(8,128)(2,1)S(1)} %pad_maximum_fusion.2.b0), channel_id=1, source_target_pairs={{0,12},{1,13},{2,14},{3,15},{4,0},{5,1},{6,2},{7,3},{8,4},{9,5},{1... | collective-permute-start | bytes 958472 | tf_op jit(solution)/shard_map/ppermute | solution.py:44
  51.4 113.8 %all-gather.7.cloned.1.call-start = ((), (), s32[]{:S(2)}) async-start(), calls=%async_computation.6 | async-start | bytes 5013504 | tf_op jit(solution)/shard_map/all_gather | solution.py:720
  65.3 14.9 %collective-permute-start.13 = (bf16[192,768]{1,0:T(8,128)(2,1)S(1)}, bf16[192,768]{1,0:T(8,128)(2,1)S(1)}, u32[]{:S(2)}, u32[]{:S(2)}) collective-permute-start(bf16[192,768]{1,0:T(8,128)(2,1)S(1)} %get-tuple-element.144.w0.refs_17_), channel_id=1, source_target_pairs={{0,48},{16,0},{32,16},{48,32},{1,49},{17,1},{33,17},{49,33},{2,50}... | collective-permute-start | bytes 884744 | tf_op jit(solution)/shard_map/ppermute | solution.py:35
  68.0 12.2 %collective-permute-start.12 = (bf16[192,768]{1,0:T(8,128)(2,1)S(1)}, bf16[192,768]{1,0:T(8,128)(2,1)S(1)}, u32[]{:S(2)}, u32[]{:S(2)}) collective-permute-start(bf16[192,768]{1,0:T(8,128)(2,1)S(1)} %get-tuple-element.144.w0.refs_17_), channel_id=1, source_target_pairs={{0,32},{16,48},{32,0},{48,16},{1,33},{17,49},{33,1},{49,17},{2,34}... | collective-permute-start | bytes 884744 | tf_op jit(solution)/shard_map/ppermute | solution.py:35
  68.6 16.2 %collective-permute-start.11 = (bf16[192,768]{1,0:T(8,128)(2,1)S(1)}, bf16[192,768]{1,0:T(8,128)(2,1)S(1)}, u32[]{:S(2)}, u32[]{:S(2)}) collective-permute-start(bf16[192,768]{1,0:T(8,128)(2,1)S(1)} %get-tuple-element.144.w0.refs_17_), channel_id=1, source_target_pairs={{0,16},{16,32},{32,48},{48,0},{1,17},{17,33},{33,49},{49,1},{2,18}... | collective-permute-start | bytes 884744 | tf_op jit(solution)/shard_map/ppermute | solution.py:35
  69.5 18.0 %collective-permute-start.17 = (s32[144,2]{1,0:T(8,128)S(1)}, s32[144,2]{1,0:T(8,128)S(1)}, u32[]{:S(2)}, u32[]{:S(2)}) collective-permute-start(s32[144,2]{1,0:T(8,128)S(1)} %bitcast.109), channel_id=1, source_target_pairs={{0,64},{64,0},{1,65},{65,1},{2,66},{66,2},{3,67},{67,3},{4,68},{68... | collective-permute-start | bytes 3464 | tf_op jit(solution)/shard_map/ppermute | solution.py:31
  109.2 305.0 %reduce-scatter.5.cloned.1.call-start = ((), (), s32[]{:S(2)}) async-start(), calls=%async_computation.4 | async-start | bytes 9732096 | tf_op jit(solution)/shard_map/reduce_scatter | solution.py:761
  110.0 16.0 %collective-permute-start.23 = (bf16[192,768]{1,0:T(8,128)(2,1)S(1)}, bf16[192,768]{1,0:T(8,128)(2,1)S(1)}, u32[]{:S(2)}, u32[]{:S(2)}) collective-permute-start(bf16[192,768]{1,0:T(8,128)(2,1)S(1)} %copy-done.12), channel_id=1, source_target_pairs={{0,48},{16,0},{32,16},{48,32},{1,49},{17,1},{33,17},{49,33},{2,50}... | collective-permute-start | bytes 884744 | tf_op jit(solution)/shard_map/ppermute | solution.py:35
  112.5 13.5 %collective-permute-start.22 = (bf16[192,768]{1,0:T(8,128)(2,1)S(1)}, bf16[192,768]{1,0:T(8,128)(2,1)S(1)}, u32[]{:S(2)}, u32[]{:S(2)}) collective-permute-start(bf16[192,768]{1,0:T(8,128)(2,1)S(1)} %copy-done.12), channel_id=1, source_target_pairs={{0,32},{16,48},{32,0},{48,16},{1,33},{17,49},{33,1},{49,17},{2,34}... | collective-permute-start | bytes 884744 | tf_op jit(solution)/shard_map/ppermute | solution.py:35
  113.0 16.2 %collective-permute-start.21 = (bf16[192,768]{1,0:T(8,128)(2,1)S(1)}, bf16[192,768]{1,0:T(8,128)(2,1)S(1)}, u32[]{:S(2)}, u32[]{:S(2)}) collective-permute-start(bf16[192,768]{1,0:T(8,128)(2,1)S(1)} %copy-done.12), channel_id=1, source_target_pairs={{0,16},{16,32},{32,48},{48,0},{1,17},{17,33},{33,49},{49,1},{2,18}... | collective-permute-start | bytes 884744 | tf_op jit(solution)/shard_map/ppermute | solution.py:35
  165.2 27.9 %collective-permute-start.38 = (bf16[16,4,48,768]{3,2,1,0:T(8,128)(2,1)}, bf16[16,4,48,768]{3,2,1,0:T(8,128)(2,1)S(1)}, u32[]{:S(2)}, u32[]{:S(2)}) collective-permute-start(bf16[16,4,48,768]{3,2,1,0:T(8,128)(2,1)} %bitcast.93), channel_id=1, source_target_pairs={{0,64},{64,0},{1,65},{65,1},{2,66},{66,2},{3,67},{67,3},{4,68},{68... | collective-permute-start | bytes 14155784 | tf_op jit(solution)/shard_map/ppermute | solution.py:31
  216.9 199.1 %reduce-scatter.7.cloned.1.call-start = ((), (), s32[]{:S(2)}) async-start(), calls=%async_computation.7 | async-start | bytes 5013504
  221.9 13.8 %collective-permute-start.41 = (bf16[2,80,768]{2,1,0:T(8,128)(2,1)S(1)}, bf16[2,80,768]{2,1,0:T(8,128)(2,1)S(1)}, u32[]{:S(2)}, u32[]{:S(2)}) collective-permute-start(bf16[2,80,768]{2,1,0:T(8,128)(2,1)S(1)} %copy-done.76), channel_id=1, source_target_pairs={{0,16},{16,32},{32,48},{48,0},{1,17},{17,33},{33,49},{49,1},{2,18}... | collective-permute-start | bytes 737288 | tf_op jit(solution)/shard_map/ppermute | solution.py:35
  332.2 20.8 %collective-permute-start.63 = (bf16[768,768]{1,0:T(8,128)(2,1)S(1)}, bf16[768,768]{1,0:T(8,128)(2,1)S(1)}, u32[]{:S(2)}, u32[]{:S(2)}) collective-permute-start(bf16[768,768]{1,0:T(8,128)(2,1)S(1)} %broadcast_select_fusion), channel_id=1, source_target_pairs={{0,64},{64,0},{1,65},{65,1},{2,66},{66,2},{3,67},{67,3},{4,68},{68... | collective-permute-start | bytes 3538952 | tf_op jit(solution)/shard_map/ppermute | solution.py:31
  349.9 12.5 %collective-permute-start.59 = (bf16[144,768]{1,0:T(8,128)(2,1)S(1)}, bf16[144,768]{1,0:T(8,128)(2,1)S(1)}, u32[]{:S(2)}, u32[]{:S(2)}) collective-permute-start(bf16[144,768]{1,0:T(8,128)(2,1)S(1)} %copy-done.80), channel_id=1, source_target_pairs={{0,32},{16,48},{32,0},{48,16},{1,33},{17,49},{33,1},{49,17},{2,34}... | collective-permute-start | bytes 663560 | tf_op jit(solution)/shard_map/ppermute | solution.py:35
  366.8 40.1 %all-to-all-start.1 = ((bf16[64,144,128]{2,1,0:T(8,128)(2,1)}), bf16[64,144,128]{2,1,0:T(8,128)(2,1)S(1)}, u32[]{:S(2)}, u32[]{:S(2)}) async-start(bf16[64,144,128]{2,1,0:T(8,128)(2,1)} %copy.147), calls=%async_computation.1 | async-start | bytes 4718592 | tf_op jit(solution)/shard_map/all_to_all | solution.py:774
  382.2 28.1 %collective-permute-start.42 = (bf16[144,768]{1,0:T(8,128)(2,1)S(1)}, bf16[144,768]{1,0:T(8,128)(2,1)}, u32[]{:S(2)}, u32[]{:S(2)}) collective-permute-start(bf16[144,768]{1,0:T(8,128)(2,1)S(1)} %get-tuple-element.302), channel_id=1, source_target_pairs={{0,64},{64,0},{1,65},{65,1},{2,66},{66,2},{3,67},{67,3},{4,68},{68... | collective-permute-start | bytes 663560 | tf_op jit(solution)/shard_map/ppermute | solution.py:31
  387.3 24.9 %collective-permute-start.61 = (bf16[144,768]{1,0:T(8,128)(2,1)}, bf16[144,768]{1,0:T(8,128)(2,1)}, u32[]{:S(2)}, u32[]{:S(2)}) collective-permute-start(bf16[144,768]{1,0:T(8,128)(2,1)} %get-tuple-element.300), channel_id=1, source_target_pairs={{0,64},{64,0},{1,65},{65,1},{2,66},{66,2},{3,67},{67,3},{4,68},{68... | collective-permute-start | bytes 663560 | tf_op jit(solution)/shard_map/ppermute | solution.py:31
  (133 other events, 905.4 us)
Sparse Core Ops, SparseCore 0:
  51.5 57.6 all-gather.4
  111.3 53.7 all-gather.6
  217.0 93.7 reduce-scatter.4
  324.9 90.9 reduce-scatter.6

commit v10 on v9

--- a/solution.py
+++ b/solution.py
@@ -640,7 +640,7 @@
     return outs[0], outs[1:]
 
 
-def attention_weights(x_blocks, w_qkv, w_proj, w_route, gain_attn, gain_ffn):
+def attention_weights(x, w_qkv, w_proj, w_route, gain_attn, gain_ffn):
     mine = w_qkv.reshape(12, 3, N_SEQ, 192).transpose(2, 0, 1, 3).reshape(N_SEQ, 12, 576)
     small = jnp.concatenate(
         [w_route, gain_attn[:, None], gain_ffn[:, None], jnp.zeros((12, 58), BF16)], axis=1
@@ -649,9 +649,11 @@
     arrived = lax.all_to_all(mine, "seq", 0, 0, tiled=True).reshape(48, 640)
     back = w_proj.reshape(12, N_SEQ, 192).transpose(1, 0, 2).reshape(48, 192)
     pack = jnp.concatenate([arrived, back], axis=1)
-    near = jnp.stack(from_ring(tie(pack, x_blocks), "x"))
+    near, x = lax.optimization_barrier((jnp.stack(from_ring(pack, "x")), x))
     far = from_ring(near, "z")
-    return far, *unpack(far)
+    x_blocks = [x] + [turn(x, -d) for d in (1, 2, 3)]
+    far, x_blocks = lax.optimization_barrier((far, x_blocks))
+    return far, x_blocks, *unpack(far)
 
 
 def both_layers(mine):
@@ -681,9 +683,8 @@
     x0 = pick(images_in, core)[0]
     d_last = pick(out_grad, core)[0]
     halves = half_packs(w_in[0, 0], w_out[0, 0])
-    x_blocks = [x0] + [turn(x0, -d) for d in (1, 2, 3)]
-    far, rows, back_rows = attention_weights(
-        x_blocks, w_qkv[0], w_proj[0], w_route[0], gain_attn[0], gain_ffn[0]
+    far, x_blocks, rows, back_rows = attention_weights(
+        x0, w_qkv[0], w_proj[0], w_route[0], gain_attn[0], gain_ffn[0]
     )
     own = lax.all_gather(tie(halves[0], far), "shard", axis=0, tiled=False)
     attn_rows = both_layers(rows)

time: 440 us -> 436 us (level)
    ppermute x6, waiting for transfers between devices: 13.3 us -> 5.35 us  [hop(): return lax.ppermute(v, 'shard', route)]
    unnamed x168 -> x169, local copies, waits for them, and re-layouts: 16.2 us -> 15.2 us
  transfers between devices with their start and end apart: 73 -> 73, of which waited for: 48 -> 48; matrix products, arithmetic and copies ran while one was open for 10% -> 9% of each run, Pallas kernels for 23% -> 23%
where the time goes in v10:
time: 436 us; the launch traced here: 429 us
  waiting for transfers between devices  136 us (31%)
  Pallas kernels  123 us (28%)
  starting transfers between devices  95.4 us (22%)
  local copies, waits for them, and re-layouts  42.8 us (10%)
  other arithmetic  16 us (4%)
  between operations  15 us (3%)
    ppermute x48, waiting for transfers between devices, turn(): return lax.ppermute(v, 'seq', [(i, (i + d) % N_SEQ) for i in range(N_SEQ)])  96.8 us
    pallas_call x14, Pallas kernels, call(): pl.pallas_call(body, out_shape=outs, in_specs=specs, out_specs=[vmem()] *...  68.6 us
    ppermute x48, starting transfers between devices, turn(): return lax.ppermute(v, 'seq', [(i, (i + d) % N_SEQ) for i in range(N_SEQ)])  53.3 us
    pallas_call x6, Pallas kernels, grid_call(): pl.pallas_call(body, grid=(2,), out_shape=outs, in_specs=in_specs, out_sp...  44.7 us
    all_to_all x1, waiting for transfers between devices, shards(): arrived = lax.all_to_all(pair, ('seq', 'shard'), 0, 0, tiled=True)  19.5 us
    ppermute x13, starting transfers between devices, swap(): return lax.ppermute(v, 'section', [(0, 1), (1, 0)])  18 us
    unnamed x169, local copies, waits for them, and re-layouts  15.2 us
    ppermute x6, starting transfers between devices, hop(): return lax.ppermute(v, 'shard', route)  10.6 us
  transfers between devices with their start and end apart: 73, of which 48 were waited for; matrix products, arithmetic and copies ran while one was open for 9% of the time, Pallas kernels for 23%

profile of v10, /device:TPU:1, one launch (start us, length us, event | category | flops | bytes accessed | tf_op | source)
XLA Modules:
  0.0 428.9 jit_solution(5558503705872278460)
XLA Ops:
  11.7 5.0 %all-to-all-start = ((bf16[4,12,640]{2,1,0:T(8,128)(2,1)}), bf16[4,12,640]{2,1,0:T(8,128)(2,1)S(1)}, u32[]{:S(2)}, u32[]{:S(2)}) async-start(bf16[4,12,640]{2,1,0:T(8,128)(2,1)} %copy.132), calls=%async_computation | async-start | bytes 163840 | tf_op jit(solution)/shard_map/all_to_all | solution.py:649
  68.2 6.0 %attention.2 = (bf16[144,192]{1,0:T(8,128)(2,1)}, bf16[144,192]{1,0:T(8,128)(2,1)}, bf16[144,192]{1,0:T(8,128)(2,1)}, bf16[144,192]{1,0:T(8,128)(2,1)}, bf16[576...) custom-call(bf16[144,768]{1,0:T(8,128)(2,1)} %copy-done.10, bf16[144,768]{1,0:T(8,128)(2,1)} %copy-done.57, ...), custom_call_target="tpu_custom_call" | custom-call | tf_op jit(solution)/shard_map/attention/pallas_call | solution.py:105
  74.3 5.4 %collective-permute-done.11.w1.refs_18_ = bf16[192,768]{1,0:T(8,128)(2,1)S(1)} collective-permute-done((bf16[192,768]{1,0:T(8,128)(2,1)S(1)}, bf16[192,768]{1,0:T(8,128)(2,1)S(1)}, u32[]{:S(2)}, u32[]{:S(2)}) %collective-permute-start.11) | collective-permute-done | bytes 294944 | tf_op jit(solution)/shard_map/ppermute | solution.py:35
  99.9 4.3 %all-gather.5.cloned.1.call-done = bf16[64,48,768]{2,1,0:T(8,128)(2,1)} async-done(((bf16[4,48,768]{2,1,0:T(8,128)(2,1)}), bf16[64,48,768]{2,1,0:T(8,128)(2,1)}) %all-gather.5.cloned.1.call-update) | async-done | bytes 4718608 | tf_op jit(solution)/shard_map/all_gather | solution.py:689
  108.7 5.0 %expert_first.1 = (bf16[320,768]{1,0:T(8,128)(2,1)}, f32[320,768]{1,0:T(8,128)}) custom-call(bf16[80,768]{1,0:T(8,128)(2,1)} %get-tuple-element.170.r0.refs_0_, bf16[80,768]{1,0:T(8,128)(2,1)} %copy-done.27, bf16[80,768]{1,0:T(8,128)(2,1)} %copy-done.28, bf16[80,768]{1,0:T(8,128)(2,1)} %copy-done.29, bf16[16,4,48,768]{3,2,1,0:T(8,128)(2,1)} %bitcast.89), custom_call_target="tpu_custom_call" | custom-call | tf_op jit(solution)/shard_map/expert_first/pallas_call | solution.py:380
  115.8 5.2 %expert_second.1 = (bf16[80,768]{1,0:T(8,128)(2,1)}, bf16[80,768]{1,0:T(8,128)(2,1)}, bf16[80,768]{1,0:T(8,128)(2,1)}, bf16[80,768]{1,0:T(8,128)(2,1)}) custom-call(bf16[320,768]{1,0:T(8,128)(2,1)} %get-tuple-element.177.rows_ref, f32[320,768]{1,0:T(8,128)} %get-tuple-element.178.first_ref, bf16[16,4,48,768]{3,2,1,0:T(8,128)(2,1)} %copy-done.2), custom_call_target="tpu_custom_call" | custom-call | tf_op jit(solution)/shard_map/expert_second/pallas_call | solution.py:380
  140.1 6.4 %collective-permute-done.31.x3 = bf16[144,768]{1,0:T(8,128)(2,1)S(1)} collective-permute-done((bf16[144,768]{1,0:T(8,128)(2,1)}, bf16[144,768]{1,0:T(8,128)(2,1)S(1)}, u32[]{:S(2)}, u32[]{:S(2)}) %collective-permute-start.31) | collective-permute-done | bytes 221216 | tf_op jit(solution)/shard_map/ppermute | solution.py:35
  150.3 6.1 %attention.3 = (bf16[144,192]{1,0:T(8,128)(2,1)}, bf16[144,192]{1,0:T(8,128)(2,1)}, bf16[144,192]{1,0:T(8,128)(2,1)}, bf16[144,192]{1,0:T(8,128)(2,1)}, bf16[576...) custom-call(bf16[144,768]{1,0:T(8,128)(2,1)} %combine.2.x0.x_ref, bf16[144,768]{1,0:T(8,128)(2,1)} %copy-done.60, ...), custom_call_target="tpu_custom_call" | custom-call | tf_op jit(solution)/shard_map/attention/pallas_call | solution.py:105
  169.3 4.5 %middle.3 = (f32[144,768]{1,0:T(8,128)}, bf16[144,768]{1,0:T(8,128)(2,1)}, f32[144,64]{1,0:T(8,128)}, bf16[144,320]{1,0:T(8,128)(2,1)}, bf16[144,320]{1,0:T(8,12...) custom-call(s32[1]{0:T(128)} %bitcast.me_ref, ...), custom_call_target="tpu_custom_call" | custom-call | tf_op jit(solution)/shard_map/middle/pallas_call | solution.py:105
  178.1 4.5 %collective-permute-done.35.refs_1_ = bf16[2,80,768]{2,1,0:T(8,128)(2,1)S(1)} collective-permute-done((bf16[2,80,768]{2,1,0:T(8,128)(2,1)}, bf16[2,80,768]{2,1,0:T(8,128)(2,1)S(1)}, u32[]{:S(2)}, u32[]{:S(2)}) %collective-permute-start.35) | collective-permute-done | bytes 245792 | tf_op jit(solution)/shard_map/ppermute | solution.py:35
  190.3 11.6 %expert_back.2 = (bf16[2,80,768]{2,1,0:T(8,128)(2,1)}, bf16[2,80,768]{2,1,0:T(8,128)(2,1)}, bf16[2,80,768]{2,1,0:T(8,128)(2,1)}, bf16[2,80,768]{2,1,0:T(8,128)(2...) custom-call(bf16[2,80,768]{2,1,0:T(8,128)(2,1)} %get-tuple-element.2, ...), custom_call_target="tpu_custom_call" | custom-call | tf_op jit(solution)/shard_map/expert_back/pallas_call | solution.py:380
  201.8 10.0 %expert_grads.1 = bf16[2,16,4,48,768]{4,3,2,1,0:T(8,128)(2,1)} custom-call(s32[1]{0:T(128)} %bitcast.41.core_ref, bf16[320,768]{1,0:T(8,128)(2,1)} %get-tuple-element.263.rows_ref, bf16[320,768]{1,0:T(8,128)(2,1)} %get-tuple-element.264.d_result_ref, bf16[320,1536]{1,0:T(8,128)(2,1)} %get-tuple-element.265.act_own, ...), custom_call_target="tpu_custom_call" | custom-call | tf_op jit(solution)/shard_map/expert_grads/pallas_call | solution.py:492
  216.9 5.0 %collective-permute-done.39.refs_1_ = bf16[2,80,768]{2,1,0:T(8,128)(2,1)S(1)} collective-permute-done((bf16[2,80,768]{2,1,0:T(8,128)(2,1)S(1)}, bf16[2,80,768]{2,1,0:T(8,128)(2,1)S(1)}, u32[]{:S(2)}, u32[]{:S(2)}) %collective-permute-start.39) | collective-permute-done | bytes 245792 | tf_op jit(solution)/shard_map/ppermute | solution.py:35
  224.4 6.3 %collective-permute-done.41.refs_3_ = bf16[2,80,768]{2,1,0:T(8,128)(2,1)S(1)} collective-permute-done((bf16[2,80,768]{2,1,0:T(8,128)(2,1)S(1)}, bf16[2,80,768]{2,1,0:T(8,128)(2,1)S(1)}, u32[]{:S(2)}, u32[]{:S(2)}) %collective-permute-start.41) | collective-permute-done | bytes 245792 | tf_op jit(solution)/shard_map/ppermute | solution.py:35
  231.4 5.8 %middle_back.2 = (f32[144,768]{1,0:T(8,128)}, f32[768,64]{1,0:T(8,128)}, bf16[768,768]{1,0:T(8,128)(2,1)}, bf16[144,192]{1,0:T(8,128)(2,1)}, bf16[144,192]{1,0:T...) custom-call(s32[1]{0:T(128)} %bitcast.me_ref, ...), custom_call_target="tpu_custom_call" | custom-call | tf_op jit(solution)/shard_map/middle_back/pallas_call | solution.py:105
  245.2 10.0 %attention_back.2 = (bf16[144,768]{1,0:T(8,128)(2,1)}, bf16[144,768]{1,0:T(8,128)(2,1)}, bf16[144,768]{1,0:T(8,128)(2,1)}, bf16[144,768]{1,0:T(8,128)(2,1)}, bf16[768,768]{1,0:T(8,128)(2,1)}) custom-call(bf16[576,768]{1,0:T(8,128)(2,1)} %get-tuple-element.214.x_ref, bf16[768,640]{1,0:T(8,128)(2,1)} %copy.142.w_ref.router_ref, ...), custom_call_target="tpu_custom_call" | custom-call | tf_op jit(solution)/shard_map/attention_back/pallas_call | solution.py:105
  257.9 6.2 %collective-permute-done.46.b1 = bf16[144,768]{1,0:T(8,128)(2,1)S(1)} collective-permute-done((bf16[144,768]{1,0:T(8,128)(2,1)}, bf16[144,768]{1,0:T(8,128)(2,1)S(1)}, u32[]{:S(2)}, u32[]{:S(2)}) %collective-permute-start.46) | collective-permute-done | bytes 221216 | tf_op jit(solution)/shard_map/ppermute | solution.py:35
  282.7 10.5 %expert_back.3 = (bf16[80,768]{1,0:T(8,128)(2,1)}, bf16[80,768]{1,0:T(8,128)(2,1)}, bf16[80,768]{1,0:T(8,128)(2,1)}, bf16[80,768]{1,0:T(8,128)(2,1)}, bf16[320,7...) custom-call(bf16[80,768]{1,0:T(8,128)(2,1)} %get-tuple-element.170.r, ...), custom_call_target="tpu_custom_call" | custom-call | tf_op jit(solution)/shard_map/expert_back/pallas_call | solution.py:380
  293.2 6.0 %expert_grad.2 = bf16[16,4,48,768]{3,2,1,0:T(8,128)(2,1)} custom-call(bf16[320,768]{1,0:T(8,128)(2,1)} %get-tuple-element.256.rows_ref, bf16[320,768]{1,0:T(8,128)(2,1)} %get-tuple-element.257.d_result_ref, bf16[320,1536]{1,0:T(8,128)(2,1)} %get-tuple-element.260.act_ref, bf16[320,1536]{1,0:T(8,128)(2,1)} %get-tuple-element.261.dh_ref), custom_call_target="tpu_custom_call" | custom-call | tf_op jit(solution)/shard_map/expert_grad/pallas_call | solution.py:380
  313.4 6.4 %expert_grad.3 = bf16[16,4,48,768]{3,2,1,0:T(8,128)(2,1)} custom-call(bf16[320,768]{1,0:T(8,128)(2,1)} %get-tuple-element.256.rows_ref, bf16[320,768]{1,0:T(8,128)(2,1)} %get-tuple-element.257.d_result_ref, bf16[320,1536]{1,0:T(8,128)(2,1)} %get-tuple-element.258.act_ref, bf16[320,1536]{1,0:T(8,128)(2,1)} %get-tuple-element.259.dh_ref, ...), custom_call_target="tpu_custom_call" | custom-call | tf_op jit(solution)/shard_map/expert_grad/pallas_call | solution.py:380
  319.9 5.7 %middle_back.3 = (f32[144,768]{1,0:T(8,128)}, f32[768,64]{1,0:T(8,128)}, bf16[768,768]{1,0:T(8,128)(2,1)}, bf16[144,192]{1,0:T(8,128)(2,1)}, bf16[144,192]{1,0:T...) custom-call(s32[1]{0:T(128)} %bitcast.me_ref, bf16[144,768]{1,0:T(8,128)(2,1)} %get-tuple-element.226.d_out_ref, ...), custom_call_target="tpu_custom_call" | custom-call | tf_op jit(solution)/shard_map/middle_back/pallas_call | solution.py:105
  332.4 9.8 %attention_back.3 = (bf16[144,768]{1,0:T(8,128)(2,1)}, bf16[144,768]{1,0:T(8,128)(2,1)}, bf16[144,768]{1,0:T(8,128)(2,1)}, bf16[144,768]{1,0:T(8,128)(2,1)}, bf16[768,768]{1,0:T(8,128)(2,1)}) custom-call(bf16[576,768]{1,0:T(8,128)(2,1)} %get-tuple-element.239.x_ref, bf16[768,640]{1,0:T(8,128)(2,1)} %copy.137.w_ref.router_ref, ...), custom_call_target="tpu_custom_call" | custom-call | tf_op jit(solution)/shard_map/attention_back/pallas_call | solution.py:105
  361.8 8.5 %all-to-all-start.1 = ((bf16[64,144,128]{2,1,0:T(8,128)(2,1)}), bf16[64,144,128]{2,1,0:T(8,128)(2,1)S(1)}, u32[]{:S(2)}, u32[]{:S(2)}) async-start(bf16[64,144,128]{2,1,0:T(8,128)(2,1)} %copy.147), calls=%async_computation.1 | async-start | bytes 4718592 | tf_op jit(solution)/shard_map/all_to_all | solution.py:775
  382.4 19.5 %all-to-all-done.1 = bf16[64,144,128]{2,1,0:T(8,128)(2,1)S(1)} async-done(((bf16[64,144,128]{2,1,0:T(8,128)(2,1)}), bf16[64,144,128]{2,1,0:T(8,128)(2,1)S(1)}, u32[]{:S(2)}, u32[]{:S(2)}) %all-to-all-start.1) | async-done | bytes 2359328 | tf_op jit(solution)/shard_map/all_to_all | solution.py:775
  (388 shorter events, 240.3 us)
Async XLA Ops:
  16.7 87.6 %all-gather.5.cloned.1.call-start = ((), (), s32[]{:S(2)}) async-start(), calls=%async_computation.5 | async-start | bytes 5013504 | tf_op jit(solution)/shard_map/all_gather | solution.py:689
  18.5 16.2 %collective-permute-start.24 = (bf16[4,48,768]{2,1,0:T(8,128)(2,1)S(1)}, bf16[4,48,768]{2,1,0:T(8,128)(2,1)S(1)}, u32[]{:S(2)}, u32[]{:S(2)}) collective-permute-start(bf16[4,48,768]{2,1,0:T(8,128)(2,1)S(1)} %dynamic-slice_bitcast_fusion), channel_id=1, source_target_pairs={{0,64},{64,0},{1,65},{65,1},{2,66},{66,2},{3,67},{67,3},{4,68},{68... | collective-permute-start | bytes 884744 | tf_op jit(solution)/shard_map/ppermute | solution.py:31
  29.1 14.6 %collective-permute-start.5 = (bf16[4,48,832]{2,1,0:T(8,128)(2,1)S(1)}, bf16[4,48,832]{2,1,0:T(8,128)(2,1)S(1)}, u32[]{:S(2)}, u32[]{:S(2)}) collective-permute-start(bf16[4,48,832]{2,1,0:T(8,128)(2,1)S(1)} %pad_maximum_fusion.2.b0), channel_id=1, source_target_pairs={{0,4},{1,5},{2,6},{3,7},{4,8},{5,9},{6,10},{7,11},{8,12},{9,13},{1... | collective-permute-start | bytes 958472 | tf_op jit(solution)/shard_map/ppermute | solution.py:44
  30.7 15.0 %collective-permute-start.4 = (bf16[4,48,832]{2,1,0:T(8,128)(2,1)S(1)}, bf16[4,48,832]{2,1,0:T(8,128)(2,1)S(1)}, u32[]{:S(2)}, u32[]{:S(2)}) collective-permute-start(bf16[4,48,832]{2,1,0:T(8,128)(2,1)S(1)} %pad_maximum_fusion.2.b0), channel_id=1, source_target_pairs={{0,8},{1,9},{2,10},{3,11},{4,12},{5,13},{6,14},{7,15},{8,0},{9,1},... | collective-permute-start | bytes 958472 | tf_op jit(solution)/shard_map/ppermute | solution.py:44
  34.0 12.6 %collective-permute-start.3 = (bf16[4,48,832]{2,1,0:T(8,128)(2,1)S(1)}, bf16[4,48,832]{2,1,0:T(8,128)(2,1)S(1)}, u32[]{:S(2)}, u32[]{:S(2)}) collective-permute-start(bf16[4,48,832]{2,1,0:T(8,128)(2,1)S(1)} %pad_maximum_fusion.2.b0), channel_id=1, source_target_pairs={{0,12},{1,13},{2,14},{3,15},{4,0},{5,1},{6,2},{7,3},{8,4},{9,5},{1... | collective-permute-start | bytes 958472 | tf_op jit(solution)/shard_map/ppermute | solution.py:44
  46.7 113.5 %all-gather.7.cloned.1.call-start = ((), (), s32[]{:S(2)}) async-start(), calls=%async_computation.6 | async-start | bytes 5013504 | tf_op jit(solution)/shard_map/all_gather | solution.py:721
  60.4 13.8 %collective-permute-start.13 = (bf16[192,768]{1,0:T(8,128)(2,1)S(1)}, bf16[192,768]{1,0:T(8,128)(2,1)S(1)}, u32[]{:S(2)}, u32[]{:S(2)}) collective-permute-start(bf16[192,768]{1,0:T(8,128)(2,1)S(1)} %get-tuple-element.162.w0.refs_17_), channel_id=1, source_target_pairs={{0,48},{16,0},{32,16},{48,32},{1,49},{17,1},{33,17},{49,33},{2,50}... | collective-permute-start | bytes 884744 | tf_op jit(solution)/shard_map/ppermute | solution.py:35
  64.2 15.4 %collective-permute-start.11 = (bf16[192,768]{1,0:T(8,128)(2,1)S(1)}, bf16[192,768]{1,0:T(8,128)(2,1)S(1)}, u32[]{:S(2)}, u32[]{:S(2)}) collective-permute-start(bf16[192,768]{1,0:T(8,128)(2,1)S(1)} %get-tuple-element.162.w0.refs_17_), channel_id=1, source_target_pairs={{0,16},{16,32},{32,48},{48,0},{1,17},{17,33},{33,49},{49,1},{2,18}... | collective-permute-start | bytes 884744 | tf_op jit(solution)/shard_map/ppermute | solution.py:35
  64.4 18.6 %collective-permute-start.17 = (s32[144,2]{1,0:T(8,128)S(1)}, s32[144,2]{1,0:T(8,128)S(1)}, u32[]{:S(2)}, u32[]{:S(2)}) collective-permute-start(s32[144,2]{1,0:T(8,128)S(1)} %bitcast.109), channel_id=1, source_target_pairs={{0,64},{64,0},{1,65},{65,1},{2,66},{66,2},{3,67},{67,3},{4,68},{68... | collective-permute-start | bytes 3464 | tf_op jit(solution)/shard_map/ppermute | solution.py:31
  104.2 305.1 %reduce-scatter.5.cloned.1.call-start = ((), (), s32[]{:S(2)}) async-start(), calls=%async_computation.4 | async-start | bytes 9732096 | tf_op jit(solution)/shard_map/reduce_scatter | solution.py:762
  105.1 16.0 %collective-permute-start.23 = (bf16[192,768]{1,0:T(8,128)(2,1)S(1)}, bf16[192,768]{1,0:T(8,128)(2,1)S(1)}, u32[]{:S(2)}, u32[]{:S(2)}) collective-permute-start(bf16[192,768]{1,0:T(8,128)(2,1)S(1)} %copy-done.12), channel_id=1, source_target_pairs={{0,48},{16,0},{32,16},{48,32},{1,49},{17,1},{33,17},{49,33},{2,50}... | collective-permute-start | bytes 884744 | tf_op jit(solution)/shard_map/ppermute | solution.py:35
  107.5 13.5 %collective-permute-start.22 = (bf16[192,768]{1,0:T(8,128)(2,1)S(1)}, bf16[192,768]{1,0:T(8,128)(2,1)S(1)}, u32[]{:S(2)}, u32[]{:S(2)}) collective-permute-start(bf16[192,768]{1,0:T(8,128)(2,1)S(1)} %copy-done.12), channel_id=1, source_target_pairs={{0,32},{16,48},{32,0},{48,16},{1,33},{17,49},{33,1},{49,17},{2,34}... | collective-permute-start | bytes 884744 | tf_op jit(solution)/shard_map/ppermute | solution.py:35
  108.1 16.2 %collective-permute-start.21 = (bf16[192,768]{1,0:T(8,128)(2,1)S(1)}, bf16[192,768]{1,0:T(8,128)(2,1)S(1)}, u32[]{:S(2)}, u32[]{:S(2)}) collective-permute-start(bf16[192,768]{1,0:T(8,128)(2,1)S(1)} %copy-done.12), channel_id=1, source_target_pairs={{0,16},{16,32},{32,48},{48,0},{1,17},{17,33},{33,49},{49,1},{2,18}... | collective-permute-start | bytes 884744 | tf_op jit(solution)/shard_map/ppermute | solution.py:35
  160.2 27.9 %collective-permute-start.38 = (bf16[16,4,48,768]{3,2,1,0:T(8,128)(2,1)}, bf16[16,4,48,768]{3,2,1,0:T(8,128)(2,1)S(1)}, u32[]{:S(2)}, u32[]{:S(2)}) collective-permute-start(bf16[16,4,48,768]{3,2,1,0:T(8,128)(2,1)} %bitcast.93), channel_id=1, source_target_pairs={{0,64},{64,0},{1,65},{65,1},{2,66},{66,2},{3,67},{67,3},{4,68},{68... | collective-permute-start | bytes 14155784 | tf_op jit(solution)/shard_map/ppermute | solution.py:31
  174.2 12.1 %collective-permute-start.36 = (bf16[2,80,768]{2,1,0:T(8,128)(2,1)}, bf16[2,80,768]{2,1,0:T(8,128)(2,1)S(1)}, u32[]{:S(2)}, u32[]{:S(2)}) collective-permute-start(bf16[2,80,768]{2,1,0:T(8,128)(2,1)} %get-tuple-element.203), channel_id=1, source_target_pairs={{0,32},{16,48},{32,0},{48,16},{1,33},{17,49},{33,1},{49,17},{2,34}... | collective-permute-start | bytes 737288 | tf_op jit(solution)/shard_map/ppermute | solution.py:35
  176.6 11.5 %collective-permute-start.37 = (bf16[2,80,768]{2,1,0:T(8,128)(2,1)}, bf16[2,80,768]{2,1,0:T(8,128)(2,1)S(1)}, u32[]{:S(2)}, u32[]{:S(2)}) collective-permute-start(bf16[2,80,768]{2,1,0:T(8,128)(2,1)} %get-tuple-element.204), channel_id=1, source_target_pairs={{0,48},{16,0},{32,16},{48,32},{1,49},{17,1},{33,17},{49,33},{2,50}... | collective-permute-start | bytes 737288 | tf_op jit(solution)/shard_map/ppermute | solution.py:35
  211.9 200.0 %reduce-scatter.7.cloned.1.call-start = ((), (), s32[]{:S(2)}) async-start(), calls=%async_computation.7 | async-start | bytes 5013504
  216.9 13.8 %collective-permute-start.41 = (bf16[2,80,768]{2,1,0:T(8,128)(2,1)S(1)}, bf16[2,80,768]{2,1,0:T(8,128)(2,1)S(1)}, u32[]{:S(2)}, u32[]{:S(2)}) collective-permute-start(bf16[2,80,768]{2,1,0:T(8,128)(2,1)S(1)} %copy-done.76), channel_id=1, source_target_pairs={{0,16},{16,32},{32,48},{48,0},{1,17},{17,33},{33,49},{49,1},{2,18}... | collective-permute-start | bytes 737288 | tf_op jit(solution)/shard_map/ppermute | solution.py:35
  299.2 12.1 %collective-permute-start.65 = (bf16[16,4,48,768]{3,2,1,0:T(8,128)(2,1)}, bf16[16,4,48,768]{3,2,1,0:T(8,128)(2,1)S(1)}, u32[]{:S(2)}, u32[]{:S(2)}) collective-permute-start(bf16[16,4,48,768]{3,2,1,0:T(8,128)(2,1)} %expert_grad.2), channel_id=1, source_target_pairs={{0,64},{64,0},{1,65},{65,1},{2,66},{66,2},{3,67},{67,3},{4,68},{68... | collective-permute-start | bytes 14155784 | tf_op jit(solution)/shard_map/ppermute | solution.py:31
  327.2 20.8 %collective-permute-start.63 = (bf16[768,768]{1,0:T(8,128)(2,1)S(1)}, bf16[768,768]{1,0:T(8,128)(2,1)S(1)}, u32[]{:S(2)}, u32[]{:S(2)}) collective-permute-start(bf16[768,768]{1,0:T(8,128)(2,1)S(1)} %broadcast_select_fusion), channel_id=1, source_target_pairs={{0,64},{64,0},{1,65},{65,1},{2,66},{66,2},{3,67},{67,3},{4,68},{68... | collective-permute-start | bytes 3538952 | tf_op jit(solution)/shard_map/ppermute | solution.py:31
  344.9 12.5 %collective-permute-start.59 = (bf16[144,768]{1,0:T(8,128)(2,1)S(1)}, bf16[144,768]{1,0:T(8,128)(2,1)S(1)}, u32[]{:S(2)}, u32[]{:S(2)}) collective-permute-start(bf16[144,768]{1,0:T(8,128)(2,1)S(1)} %copy-done.80), channel_id=1, source_target_pairs={{0,32},{16,48},{32,0},{48,16},{1,33},{17,49},{33,1},{49,17},{2,34}... | collective-permute-start | bytes 663560 | tf_op jit(solution)/shard_map/ppermute | solution.py:35
  361.8 40.1 %all-to-all-start.1 = ((bf16[64,144,128]{2,1,0:T(8,128)(2,1)}), bf16[64,144,128]{2,1,0:T(8,128)(2,1)S(1)}, u32[]{:S(2)}, u32[]{:S(2)}) async-start(bf16[64,144,128]{2,1,0:T(8,128)(2,1)} %copy.147), calls=%async_computation.1 | async-start | bytes 4718592 | tf_op jit(solution)/shard_map/all_to_all | solution.py:775
  377.2 28.1 %collective-permute-start.42 = (bf16[144,768]{1,0:T(8,128)(2,1)S(1)}, bf16[144,768]{1,0:T(8,128)(2,1)}, u32[]{:S(2)}, u32[]{:S(2)}) collective-permute-start(bf16[144,768]{1,0:T(8,128)(2,1)S(1)} %get-tuple-element.320), channel_id=1, source_target_pairs={{0,64},{64,0},{1,65},{65,1},{2,66},{66,2},{3,67},{67,3},{4,68},{68... | collective-permute-start | bytes 663560 | tf_op jit(solution)/shard_map/ppermute | solution.py:31
  382.3 24.9 %collective-permute-start.61 = (bf16[144,768]{1,0:T(8,128)(2,1)}, bf16[144,768]{1,0:T(8,128)(2,1)}, u32[]{:S(2)}, u32[]{:S(2)}) collective-permute-start(bf16[144,768]{1,0:T(8,128)(2,1)} %get-tuple-element.318), channel_id=1, source_target_pairs={{0,64},{64,0},{1,65},{65,1},{2,66},{66,2},{3,67},{67,3},{4,68},{68... | collective-permute-start | bytes 663560 | tf_op jit(solution)/shard_map/ppermute | solution.py:31
  (133 other events, 851.9 us)
Sparse Core Ops, SparseCore 0:
  46.8 57.4 all-gather.4
  106.4 53.7 all-gather.6
  212.0 93.7 reduce-scatter.4
  320.0 91.8 reduce-scatter.6
